TPU v7x, 32 devices: a whole 2x2x4 slice. The times are simulated.
32 devices in a mesh: blk: 8 (over z, core), grp: 4 (over y, x).
Axes of the slice: x: 2, y: 2, z: 4, core: 2. Of those that a mesh axis runs over, the one named last changes fastest.
Arguments:
- ratings: bfloat16 [2, 8, 4, 64, 256, 256], P(None, 'blk', 'grp'), may hold values from -6 to 6
- row_index: int32 [2, 8, 4, 64], P(None, 'blk', 'grp'), may hold values from 0 to 7
- col_index: int32 [2, 8, 4, 64], P(None, 'blk', 'grp'), may hold values from 0 to 63
- row_mask: int32 [2, 8, 4, 64, 256], P(None, 'blk', 'grp'), may hold values 0 or 1
- counts: int32 [2, 8, 4], P(None, 'blk', 'grp'), may hold values from 21 to 64, as said below
- owner_list: int32 [2, 8], P(None, 'blk'), may hold values from 0 to 3
- user_factors: float32 [65536, 128], P(('blk', 'grp'))
- item_factors: float32 [131072, 128], P('blk'), may hold values from -2 to 2
Outputs:
- user_final: float32 [65536, 128], P(('blk', 'grp'))
- item_final: float32 [131072, 128], P(('blk', 'grp'))
Inputs may be any that keep to these rules, and one draw needn't show every extreme that they name: `counts`: in every sub-epoch some device has exactly 64 live slots, and every device has at least a third of 64, rounded down.
All inputs are finite; a program needn't handle non-finite values. No bound on the sum of `row_mask` on one device may be relied on, other than what follows from the above.
Results may differ from a plain program's by a relative error of at most 0.02.
Values may be sent and summed in bfloat16 or wider, within the bound.
No kernel may reach another device: no remote copies, remote signals or barrier semaphores. Data moves between devices by JAX's collectives and lax.ppermute only.
A program may use at most 128 MiB of HBM per device.

v0:
```python
import jax
import jax.numpy as jnp
from jax import lax
from jax.sharding import PartitionSpec as P

SUB = 2


LEARN = 0.004
GRAM = 256.0
RIDGE = 1.0


def spread(value, axis, source):
    kept = jnp.where(lax.axis_index(axis) == source, value, 0).astype(value.dtype)
    return lax.psum(kept, axis)


def passed_along(shard, axis, by):
    length = lax.axis_size(axis)
    return lax.ppermute(shard, axis, [(i, (i + by) % length) for i in range(length)])


def inner_gram(matrix):
    return lax.dot_general(
        matrix, matrix, (((0,), (0,)), ((), ())), preferred_element_type=jnp.float32
    )


def local(ratings, row_index, col_index, row_mask, counts, owner_list, user_factors, item_factors):
    members = lax.axis_size("grp")
    member_id = lax.axis_index("grp")
    tile = ratings.shape[-1]
    rank = user_factors.shape[1]
    user_rows = user_factors.shape[0]
    identity = jnp.eye(rank, dtype=jnp.float32)
    item_block = item_factors
    users_now = user_factors
    for epoch in range(SUB):
        item_bf = item_block.astype(jnp.bfloat16)
        block_rows = item_bf.shape[0]
        user_bf = users_now.astype(jnp.bfloat16)
        user_tiles = user_bf.reshape(-1, tile, rank)
        item_tiles = item_bf.reshape(-1, tile, rank)
        tile_vals = ratings[epoch, 0, 0]
        rows_in = row_index[epoch, 0, 0]
        cols_in = col_index[epoch, 0, 0]
        mask_in = row_mask[epoch, 0, 0]

        def tile_step(slot, carry):
            grad_user, grad_item = carry
            row_tile = rows_in[slot]
            col_tile = cols_in[slot]
            user_part = user_tiles[row_tile]
            item_part = item_tiles[col_tile]
            predicted = lax.dot_general(
                user_part, item_part, (((1,), (1,)), ((), ())), preferred_element_type=jnp.float32
            )
            weights = mask_in[slot].astype(jnp.float32)[:, None]
            errors = (weights * (predicted - tile_vals[slot].astype(jnp.float32))).astype(
                jnp.bfloat16
            )
            user_add = jnp.dot(errors, item_part, preferred_element_type=jnp.float32)
            item_add = lax.dot_general(
                errors, user_part, (((0,), (0,)), ((), ())), preferred_element_type=jnp.float32
            )
            grad_user = grad_user.at[row_tile].add(user_add)
            grad_item = grad_item.at[col_tile].add(item_add)
            return (grad_user, grad_item)

        start_user = jnp.zeros(user_tiles.shape, jnp.float32)
        start_item = jnp.zeros(item_tiles.shape, jnp.float32)
        grad_user, grad_item = lax.fori_loop(
            0, counts[epoch, 0, 0], tile_step, (start_user, start_item)
        )
        own_gram = inner_gram(user_bf) * (GRAM / user_rows) + RIDGE * identity
        owner_now = owner_list[epoch, 0]
        owner_gram = spread(own_gram.astype(jnp.bfloat16), "grp", owner_now).astype(own_gram.dtype)
        item_gram = inner_gram(item_bf) * (GRAM / block_rows) + RIDGE * identity
        user_pull = jnp.dot(users_now, item_gram, precision=lax.Precision.HIGHEST)
        users_now = users_now - LEARN * (grad_user.reshape(users_now.shape) + user_pull)
        item_terms = grad_item.reshape(block_rows, rank)
        item_grad = lax.psum(item_terms.astype(jnp.bfloat16), "grp").astype(jnp.float32)
        item_pull = jnp.dot(item_block, owner_gram, precision=lax.Precision.HIGHEST)
        item_block = item_block - LEARN * (item_grad + item_pull)
        item_block = passed_along(item_block.astype(jnp.bfloat16), "blk", 1).astype(
            item_block.dtype
        )
    shard_rows = item_block.shape[0] // members
    item_final = lax.dynamic_slice_in_dim(item_block, member_id * shard_rows, shard_rows, 0)
    return (users_now, item_final)


def solution(mesh):
    in_specs = (
        P(None, "blk", "grp", None, None, None),
        P(None, "blk", "grp", None),
        P(None, "blk", "grp", None),
        P(None, "blk", "grp", None, None),
        P(None, "blk", "grp"),
        P(None, "blk"),
        P(("blk", "grp"), None),
        P("blk", None),
    )
    out_specs = (P(("blk", "grp"), None), P(("blk", "grp"), None))
    return jax.shard_map(local, mesh=mesh, in_specs=in_specs, out_specs=out_specs, check_vma=False)
```

profile of v0, /device:TPU:0, one launch (start us, length us, event | category | flops | bytes accessed | tf_op | source)
XLA Modules:
  0.0 1952.6 jit_solution(8182375525848994722)
XLA Ops:
  8.5 2.5 copy.11
  11.0 11.5 slice_bitcast_fusion
  22.6 5.1 convert_element_type.99
  28.4 4.8 fusion.53
  33.2 4.2 broadcast.83.clone
  37.6 436.5 %while.28 = (s32[]{:T(128)}, f32[8,256,128]{2,1,0:T(8,128)S(1)}, f32[64,256,128]{2,1,0:T(8,128)}, s32[]{:T(128)}, s32[64]{0:T(128)S(1)}, /*index=5*/s32[64,256]{...) while((s32[]{:T(128)}, f32[8,256,128]{2,1,0:T(8,128)S(1)}, ...), condition=%wide.region_3.0_spmd, body=%wide.region_0.0_spmd.sunk | while | flops 50725164 | bytes 1318217 | solution.py:73
  45.2 2.5 fusion.110
  57.0 2.5 fusion.110
  68.8 2.5 fusion.110
  80.5 2.5 fusion.110
  115.9 2.5 fusion.110
  139.4 2.5 fusion.110
  151.2 2.5 fusion.110
  163.0 2.5 fusion.110
  174.8 2.5 fusion.110
  186.6 2.5 fusion.110
  198.3 2.5 fusion.110
  210.1 2.5 fusion.110
  257.2 2.5 fusion.110
  280.8 2.5 fusion.110
  292.6 2.5 fusion.110
  304.4 2.5 fusion.110
  316.1 2.5 fusion.110
  327.9 2.5 fusion.110
  339.7 2.5 fusion.110
  386.8 2.5 fusion.110
  398.6 2.5 fusion.110
  410.4 2.5 fusion.110
  445.7 2.5 fusion.110
  457.5 2.5 fusion.110
  469.3 2.5 fusion.110
  478.2 2.7 fusion.60
  481.9 6.1 convert_element_type.102
  488.0 6.4 copy.26
  494.6 9.0 copy.13
  503.6 338.1 %all-reduce.9.cloned.1.call-done = (bf16[128,128]{1,0:T(8,128)(2,1)}, bf16[128,128]{1,0:T(8,128)(2,1)}) async-done(((bf16[128,128]{1,0:T(8,128)(2,1)}, bf16[128,128]{1,0:T(8,128)(2,1)}), (bf16[128,128]{1,0:T(8,128)(2,1)}, bf16[128,128]{1,0:T(8,128)(2,1)})) %all-reduce.9.cloned.1.call-update) | async-done | bytes 65552 | tf_op jit(solution)/shard_map/psum | solution.py:16
  841.7 107.5 %all-reduce.5.cloned.1.call-done = bf16[16384,128]{0,1:T(8,128)(2,1)} async-done(((bf16[16384,128]{0,1:T(8,128)(2,1)}), bf16[16384,128]{0,1:T(8,128)(2,1)}) %all-reduce.5.cloned.1.call-update) | async-done | bytes 4194320 | tf_op jit(solution)/shard_map/psum | solution.py:83
  949.2 14.4 fusion.44
  963.9 49.8 %collective-permute-done = bf16[16384,128]{0,1:T(8,128)(2,1)} collective-permute-done((bf16[16384,128]{0,1:T(8,128)(2,1)}, bf16[16384,128]{0,1:T(8,128)(2,1)}, u32[]{:S(2)}, u32[]{:S(2)}) %collective-permute-start) | collective-permute-done | bytes 4194336 | tf_op jit(solution)/shard_map/ppermute | solution.py:21
  1013.6 6.4 copy.27
  1020.1 4.3 broadcast.83
  1024.4 630.1 %while.29 = (s32[]{:T(128)}, f32[8,256,128]{2,1,0:T(8,128)S(1)}, f32[64,256,128]{2,1,0:T(8,128)}, s32[]{:T(128)}, s32[64]{0:T(128)S(1)}, /*index=5*/s32[64,256]{...) while((s32[]{:T(128)}, f32[8,256,128]{2,1,0:T(8,128)S(1)}, ...), condition=%wide.region_9.10_spmd, body=%wide.region_6.9_spmd.sunk | while | flops 50725164 | bytes 1318217 | solution.py:73
  1654.5 6.1 convert_element_type.108
  1660.5 6.4 copy.29
  1667.0 217.0 %all-reduce.7.cloned.1.call-done = bf16[16384,128]{0,1:T(8,128)(2,1)} async-done(((bf16[16384,128]{0,1:T(8,128)(2,1)}), bf16[16384,128]{0,1:T(8,128)(2,1)}) %all-reduce.7.cloned.1.call-update) | async-done | bytes 4194320 | tf_op jit(solution)/shard_map/psum | solution.py:83
  1884.0 8.8 subtract_convert_fusion
  1893.2 4.7 fusion.51
  1900.3 42.6 %collective-permute-done.1 = bf16[16384,128]{0,1:T(8,128)(2,1)} collective-permute-done((bf16[16384,128]{0,1:T(8,128)(2,1)}, bf16[16384,128]{0,1:T(8,128)(2,1)}, u32[]{:S(2)}, u32[]{:S(2)}) %collective-permute-start.1) | collective-permute-done | bytes 4194336 | tf_op jit(solution)/shard_map/ppermute | solution.py:21
  (654 shorter events, 604.3 us)
Async XLA Ops:
  7.2 834.5 %all-reduce.9.cloned.1.call-start = ((), (), s32[]{:S(2)}) async-start(), calls=%async_computation.2 | async-start | bytes 131072 | tf_op jit(solution)/shard_map/psum | solution.py:16
  22.6 5.2 copy-start.1
  22.6 5.2 copy-start.5
  27.7 5.4 copy-start.7
  27.7 5.4 copy-start.8
  33.2 4.4 copy-start.2
  33.2 4.4 copy-start.3
  33.2 442.2 %copy-start.6 = (s32[2,1]{0,1:T(1,128)S(1)}, s32[2,1]{0,1:T(1,128)}, u32[]{:S(2)}) copy-start(s32[2,1]{0,1:T(1,128)} %param.25) | copy-start | bytes 28
  33.2 445.0 %copy-start = (f32[2048,128]{1,0:T(8,128)S(1)}, f32[2048,128]{1,0:T(8,128)}, u32[]{:S(2)}) copy-start(f32[2048,128]{1,0:T(8,128)} %param.26) | copy-start | bytes 3145732
  481.9 467.4 %all-reduce.5.cloned.1.call-start = ((), (), s32[]{:S(2)}) async-start(), calls=%async_computation | async-start | bytes 8388608 | tf_op jit(solution)/shard_map/psum | solution.py:83
  494.4 1389.6 %all-reduce.7.cloned.1.call-start = ((), (), s32[]{:S(2)}) async-start(), calls=%async_computation.1 | async-start | bytes 8388608 | tf_op jit(solution)/shard_map/psum | solution.py:83
  963.6 50.0 %collective-permute-start = (bf16[16384,128]{0,1:T(8,128)(2,1)}, bf16[16384,128]{0,1:T(8,128)(2,1)}, u32[]{:S(2)}, u32[]{:S(2)}) collective-permute-start(bf16[16384,128]{0,1:T(8,128)(2,1)} %fusion.44), channel_id=1, source_target_pairs={{0,4},{4,8},{8,12},{12,16},{16,20},{20,24},{24,28},{28,0},{1,5},{5... | collective-permute-start | bytes 12582920 | tf_op jit(solution)/shard_map/ppermute | solution.py:21
  1660.5 223.5 %copy-start.4 = (bf16[128,128]{1,0:T(8,128)(2,1)S(1)}, bf16[128,128]{1,0:T(8,128)(2,1)}, u32[]{:S(2)}) copy-start(bf16[128,128]{1,0:T(8,128)(2,1)} %get-tuple-element.215) | copy-start | bytes 98308
  1892.8 50.0 %collective-permute-start.1 = (bf16[16384,128]{0,1:T(8,128)(2,1)}, bf16[16384,128]{0,1:T(8,128)(2,1)}, u32[]{:S(2)}, u32[]{:S(2)}) collective-permute-start(bf16[16384,128]{0,1:T(8,128)(2,1)} %subtract_convert_fusion), channel_id=1, source_target_pairs={{0,4},{4,8},{8,12},{12,16},{16,20},{20,24},{24,28},{28,0},{1,5},{5... | collective-permute-start | bytes 12582920 | tf_op jit(solution)/shard_map/ppermute | solution.py:21
Sparse Core Ops, SparseCore 0:
  482.0 359.6 all-reduce.8
  845.3 103.8 all-reduce.4
  1667.1 216.8 all-reduce.6
where the time goes:
time: 1980 us; the launch traced here: 1950 us
  waiting for transfers between devices  755 us (38%)
  matrix products  510 us (26%)
  loops' own time  413 us (21%)
  local copies, waits for them, and re-layouts  167 us (8%)
  other arithmetic  92.6 us (5%)
    another operation x2, loops' own time, local(): lax.fori_loop(0, counts[epoch, 0, 0], tile_step, (start_user, start_item))  413 us
    psum x1, waiting for transfers between devices, spread(): return lax.psum(kept, axis)  338 us
    psum x2, waiting for transfers between devices, local(): lax.psum(item_terms.astype(jnp.bfloat16), 'grp').astype(jnp.float32)  325 us
    dot_general x91, matrix products, tile_step(): lax.dot_general(errors, user_part, (((0,), (0,)), ((), ())), preferred_el...  219 us
    dot_general x91, matrix products, tile_step(): user_add = jnp.dot(errors, item_part, preferred_element_type=jnp.float32)  149 us
    dot_general x91, matrix products, tile_step(): lax.dot_general(user_part, item_part, (((1,), (1,)), ((), ())), preferred...  104 us
    ppermute x2, waiting for transfers between devices, passed_along(): lax.ppermute(shard, axis, [(i, (i + by) % length) for i in range(length)])  92.3 us
    another operation x91, other arithmetic  71.4 us
  transfers between devices with their start and end apart: 5, of which 5 were waited for; matrix products, arithmetic and copies ran while one was open for 1% of the time, Pallas kernels for 0%

commit v1 on v0

v1 whole, which is shorter than its diff:
```python
import functools

import jax
import jax.numpy as jnp
from jax import lax
from jax.experimental import pallas as pl
from jax.experimental.pallas import tpu as pltpu
from jax.sharding import PartitionSpec as P

SUB = 2
LEARN = 0.004
GRAM = 256.0
RIDGE = 1.0
CHUNKS = 4
F32 = jnp.float32
BF16 = jnp.bfloat16

ANY = pl.BlockSpec(memory_space=pl.ANY)
SMEM = pl.BlockSpec(memory_space=pltpu.SMEM)
VMEM = pl.BlockSpec(memory_space=pltpu.VMEM)


def params(mib):
    return pltpu.CompilerParams(vmem_limit_bytes=mib * 1024 * 1024)


def gram_of(matrix):
    return lax.dot_general(matrix, matrix, (((0,), (0,)), ((), ())), preferred_element_type=F32)


def owned_gram(users_bf, owner, me):
    rank = users_bf.shape[1]
    eye = (
        lax.broadcasted_iota(jnp.int32, (rank, rank), 0)
        == lax.broadcasted_iota(jnp.int32, (rank, rank), 1)
    )
    own = gram_of(users_bf) * (GRAM / users_bf.shape[0]) + jnp.where(eye, RIDGE, 0.0)
    return jnp.where(owner == me, own, 0.0).astype(BF16)


def tile_kernel(epoch, chunk, members, shard_tiles, tile, pieces, first, *refs):
    me_ref, row_ref, col_ref, count_ref, owner_ref, ratings, mask_ref, users = refs[:8]
    sources = refs[8:8 + pieces]
    refs = refs[8 + pieces:]
    if not first:
        grad_in, gram_in = refs[:2]
        refs = refs[2:]
    send_a, keep_a, send_b, keep_b, grad_user, gram_item = refs[:6]
    refs = refs[6:]
    if first and epoch == 0:
        own_gram = refs[0]
        refs = refs[1:]
    users_f, items, items_f, parts, held, slots, sem_tile, sem_item, sem_user, sem_prev = refs

    me = me_ref[0]
    chunk_tiles = shard_tiles // CHUNKS
    rows = chunk_tiles * tile
    half = rows // 2
    top = members // 2

    user_copy = pltpu.make_async_copy(users, users_f, sem_user)
    user_copy.start()
    copies = []
    if epoch == 0:
        for r in range(members):
            start = (me ^ r) * (shard_tiles * tile) + chunk * rows
            start = pl.multiple_of(start, rows)
            copies.append(
                pltpu.make_async_copy(
                    sources[0].at[pl.ds(start, rows)], items_f.at[pl.ds(r * rows, rows)], sem_item.at[r]
                )
            )
    else:
        at = 0
        for i, source in enumerate(sources):
            copies.append(
                pltpu.make_async_copy(source, items.at[pl.ds(at, source.shape[0])], sem_item.at[i])
            )
            at += source.shape[0]
    for copy in copies:
        copy.start()

    def pick(t, found):
        slots[found] = t
        here = lax.rem(col_ref[epoch, 0, 0, t], shard_tiles) // chunk_tiles == chunk
        live = t < count_ref[epoch, 0, 0]
        return found + jnp.where(here & live, 1, 0).astype(jnp.int32)

    total = lax.fori_loop(0, col_ref.shape[3], pick, jnp.int32(0))

    def fetch(i):
        return pltpu.make_async_copy(ratings.at[epoch, 0, 0, slots[i]], held.at[i], sem_tile.at[i])

    def begin(i, _):
        fetch(i).start()
        return 0

    lax.fori_loop(0, total, begin, 0)

    parts[...] = jnp.zeros_like(parts)
    if first:
        grad_user[...] = jnp.zeros_like(grad_user)
        gram_item[...] = jnp.zeros_like(gram_item)
    else:
        prev = pltpu.make_async_copy(grad_in, grad_user, sem_prev)
        prev.start()
        gram_item[...] = gram_in[...]
    user_copy.wait()
    if epoch == 0:
        for r in range(members):
            copies[r].wait()
            items[pl.ds(r * rows, rows)] = items_f[pl.ds(r * rows, rows)].astype(BF16)
    else:
        for copy in copies:
            copy.wait()
    if not first:
        prev.wait()

    def one(i, valid):
        t = slots[i]
        row = pl.multiple_of(row_ref[epoch, 0, 0, t] * tile, tile)
        col = col_ref[epoch, 0, 0, t]
        place = ((col // shard_tiles) ^ me) * chunk_tiles + lax.rem(col, chunk_tiles)
        place = pl.multiple_of(place * tile, tile)
        user_part = users_f[pl.ds(row, tile)].astype(BF16)
        item_part = items[pl.ds(place, tile)]
        predicted = lax.dot_general(
            user_part, item_part, (((1,), (1,)), ((), ())), preferred_element_type=F32
        )
        weight = mask_ref[epoch, 0, 0, pl.ds(t, 1), :].astype(F32)
        weight = jnp.where(valid, weight, 0.0)
        weight = jnp.broadcast_to(weight, (128, tile)).T
        weight = jnp.concatenate([weight] * (tile // 128), axis=1)
        error = jnp.where(weight > 0.5, predicted - held[i].astype(F32), 0.0).astype(BF16)
        user_add = jnp.dot(error, item_part, preferred_element_type=F32)
        item_add = lax.dot_general(
            error, user_part, (((0,), (0,)), ((), ())), preferred_element_type=F32
        )
        return row, place, user_add, item_add

    def pair(j, _):
        i = 2 * j
        valid = i + 1 < total
        other = jnp.where(valid, i + 1, i)
        fetch(i).wait()

        @pl.when(valid)
        def _():
            fetch(other).wait()

        first_out = one(i, True)
        second_out = one(other, valid)
        for row, place, user_add, item_add in (first_out, second_out):
            grad_user[pl.ds(row, tile)] += user_add
            parts[pl.ds(place, tile)] += item_add
        return 0

    lax.fori_loop(0, (total + 1) // 2, pair, 0)

    spot_sa = spot_ka = spot_sb = spot_kb = 0
    for r in range(members):
        upper = parts[pl.ds(r * rows, half)].astype(BF16)
        lower = parts[pl.ds(r * rows + half, rows - half)].astype(BF16)
        if r & 1:
            send_a[spot_sa] = upper
            spot_sa += 1
        else:
            keep_a[spot_ka] = upper
            spot_ka += 1
        if r & top:
            send_b[spot_sb] = lower
            spot_sb += 1
        else:
            keep_b[spot_kb] = lower
            spot_kb += 1

    def add_gram(j, _):
        gram_item[...] += gram_of(items[pl.ds(pl.multiple_of(j * tile, tile), tile)])
        return 0

    lax.fori_loop(0, members * chunk_tiles, add_gram, 0)
    if first and epoch == 0:
        own_gram[...] = owned_gram(users_f[...].astype(BF16), owner_ref[epoch, 0], me)


def tile_call(epoch, chunk, members, scalars, ratings, row_mask, users, sources, carried):
    tile = ratings.shape[-1]
    slots = ratings.shape[3]
    user_rows, rank = users.shape
    first = carried is None
    if epoch == 0:
        block_rows = sources[0].shape[0]
    else:
        block_rows = sum(s.shape[0] for s in sources) * CHUNKS
    shard_tiles = block_rows // members // tile
    rows = shard_tiles // CHUNKS * tile
    half = rows // 2
    sd = jax.ShapeDtypeStruct
    out_shape = [sd((members // 2, half, rank), BF16)] * 2 + [sd((members // 2, rows - half, rank), BF16)] * 2
    out_shape += [sd((user_rows, rank), F32), sd((rank, rank), F32)]
    if first and epoch == 0:
        out_shape.append(sd((rank, rank), BF16))
    in_specs = [SMEM] * 5 + [ANY, VMEM, ANY] + [ANY] * len(sources)
    operands = [*scalars, ratings, row_mask, users, *sources]
    if not first:
        in_specs += [ANY, VMEM]
        operands += list(carried)
    flops = slots * tile * tile * rank * 6 // CHUNKS
    return pl.pallas_call(
        functools.partial(
            tile_kernel, epoch, chunk, members, shard_tiles, tile, len(sources), first
        ),
        out_shape=out_shape,
        in_specs=in_specs,
        out_specs=[VMEM] * len(out_shape),
        scratch_shapes=[
            pltpu.VMEM((user_rows, rank), F32),
            pltpu.VMEM((members * rows, rank), BF16),
            pltpu.VMEM((members * rows if epoch == 0 else 8, rank), F32),
            pltpu.VMEM((members * rows, rank), F32),
            pltpu.VMEM((slots, tile, tile), BF16),
            pltpu.SMEM((slots + 1,), jnp.int32),
            pltpu.SemaphoreType.DMA((slots,)),
            pltpu.SemaphoreType.DMA((max(members, len(sources)),)),
            pltpu.SemaphoreType.DMA,
            pltpu.SemaphoreType.DMA,
        ],
        compiler_params=params(32),
        cost_estimate=pl.CostEstimate(flops=flops, bytes_accessed=4 << 20, transcendentals=0),
        name=f"tiles_{epoch}_{chunk}",
    )(*operands)


def user_kernel(epoch, block_rows, me_ref, owner_ref, users, grad, gram, *outs):
    rank = users.shape[1]
    eye = (
        lax.broadcasted_iota(jnp.int32, (rank, rank), 0)
        == lax.broadcasted_iota(jnp.int32, (rank, rank), 1)
    )
    full = gram[...] * (GRAM / block_rows) + jnp.where(eye, RIDGE, 0.0)
    pull = jnp.dot(users[...], full, precision=lax.Precision.HIGHEST, preferred_element_type=F32)
    new = users[...] - LEARN * (grad[...] + pull)
    outs[0][...] = new
    if len(outs) > 1:
        outs[1][...] = owned_gram(new.astype(BF16), owner_ref[epoch + 1, 0], me_ref[0])


def user_call(epoch, block_rows, me, owner_list, users, grad, gram):
    rank = users.shape[1]
    out_shape = [jax.ShapeDtypeStruct(users.shape, F32)]
    if epoch + 1 < SUB:
        out_shape.append(jax.ShapeDtypeStruct((rank, rank), BF16))
    return pl.pallas_call(
        functools.partial(user_kernel, epoch, block_rows),
        out_shape=out_shape,
        in_specs=[SMEM, SMEM, VMEM, VMEM, VMEM],
        out_specs=[VMEM] * len(out_shape),
        compiler_params=params(24),
        cost_estimate=pl.CostEstimate(
            flops=users.shape[0] * rank * rank * 14, bytes_accessed=4 << 20, transcendentals=0
        ),
        name=f"users_{epoch}",
    )(me, owner_list, users, grad, gram)


def item_kernel(epoch, chunk, count, shard_rows, me_ref, gram, items, *refs):
    terms_a = refs[:count]
    terms_b = refs[count:2 * count]
    out, held, sem = refs[2 * count:]
    rows = out.shape[0]
    if epoch == 0:
        start = pl.multiple_of(me_ref[0] * shard_rows + chunk * rows, rows)
        copy = pltpu.make_async_copy(items.at[pl.ds(start, rows)], held, sem)
        copy.start()
        copy.wait()
        old = held[...]
        high = old.astype(BF16)
        low = (old - high.astype(F32)).astype(BF16)
        pull = jnp.dot(high, gram[...], preferred_element_type=F32)
        pull += jnp.dot(low, gram[...], preferred_element_type=F32)
    else:
        old = items[...].astype(F32)
        pull = jnp.dot(items[...], gram[...], preferred_element_type=F32)
    sums = []
    for terms in (terms_a, terms_b):
        total = terms[0][0].astype(F32)
        for term in terms[1:]:
            total += term[0].astype(F32)
        sums.append(total)
    grad = jnp.concatenate(sums, axis=0)
    out[...] = (old - LEARN * (grad + pull)).astype(BF16)


def item_call(epoch, chunk, shard_rows, me, gram, items, terms_a, terms_b):
    rank = gram.shape[1]
    rows = shard_rows // CHUNKS
    return pl.pallas_call(
        functools.partial(item_kernel, epoch, chunk, len(terms_a), shard_rows),
        out_shape=jax.ShapeDtypeStruct((rows, rank), BF16),
        in_specs=[SMEM, VMEM, ANY if epoch == 0 else VMEM] + [VMEM] * (2 * len(terms_a)),
        out_specs=VMEM,
        scratch_shapes=[pltpu.VMEM((rows if epoch == 0 else 8, rank), F32), pltpu.SemaphoreType.DMA],
        compiler_params=params(24),
        cost_estimate=pl.CostEstimate(
            flops=rows * rank * rank * 4, bytes_accessed=2 << 20, transcendentals=0
        ),
        name=f"items_{epoch}_{chunk}",
    )(me, gram, items, *terms_a, *terms_b)


def swapped(value, bit):
    length = lax.axis_size("grp")
    return lax.ppermute(value, "grp", [(i, i ^ bit) for i in range(length)])


def moved(value, bit):
    length, blocks = lax.axis_size("grp"), lax.axis_size("blk")
    pairs = [
        (b * length + i, (b + 1) % blocks * length + (i ^ bit))
        for b in range(blocks)
        for i in range(length)
    ]
    return lax.ppermute(value, ("blk", "grp"), pairs)


def summed_over(value):
    length = lax.axis_size("grp")
    bit = 1
    while bit < length:
        value = value + swapped(value, bit)
        bit *= 2
    return value


def scattered(send, keep, order):
    length = lax.axis_size("grp")
    names = [r for r in range(length) if not r & order[0]]
    terms = [keep]
    arrived = swapped(send, order[0])
    for bit in order[1:]:
        terms.append(arrived)
        current = terms[0].astype(F32)
        for term in terms[1:]:
            current = current + term.astype(F32)
        going = [p for p, r in enumerate(names) if r & bit]
        staying = [p for p, r in enumerate(names) if not r & bit]
        send = jnp.stack([current[p] for p in going]).astype(BF16)
        if len(staying) < len(names):
            terms = [jnp.stack([t[p] for p in staying]) if len(staying) > 1 else t for t in terms]
        names = [names[p] for p in staying]
        arrived = swapped(send, bit)
    terms.append(arrived)
    return terms


def gathered(shard):
    length = lax.axis_size("grp")
    half = shard.shape[0] // 2
    known = {0: [moved(shard, 0)]}
    bit = 1
    while bit < length:
        known[bit] = [moved(shard, bit)]
        bit *= 2

    def cut(r, lower):
        pieces = known[r]
        if len(pieces) == 1:
            return pieces[0][half:] if lower else pieces[0][:half]
        return pieces[1] if lower else pieces[0]

    for r in range(1, length):
        if r in known:
            continue
        low = r & -r
        high = 1 << (r.bit_length() - 1)
        known[r] = [swapped(cut(r ^ high, False), high), swapped(cut(r ^ low, True), low)]
    return [piece for r in range(length) for piece in known[r]]


def local(ratings, row_index, col_index, row_mask, counts, owner_list, user_factors, item_factors):
    members = lax.axis_size("grp")
    block_rows = item_factors.shape[0]
    shard_rows = block_rows // members
    me = lax.axis_index("grp").astype(jnp.int32).reshape(1)
    scalars = (me, row_index, col_index, counts, owner_list)
    bits = [1 << i for i in range(members.bit_length() - 1)]
    users = user_factors
    chunks = [[item_factors]] * CHUNKS
    own_gram = None
    for epoch in range(SUB):
        carried = None
        outs = []
        for c in range(CHUNKS):
            out = tile_call(
                epoch, c, members, scalars, ratings, row_mask, users, chunks[c], carried
            )
            carried = out[4:6]
            if epoch == 0 and c == 0:
                own_gram = out[6]
            outs.append(out)
        owner_gram = summed_over(own_gram)
        new_users = user_call(epoch, block_rows, me, owner_list, users, *carried)
        shards = []
        for c in range(CHUNKS):
            send_a, keep_a, send_b, keep_b = outs[c][:4]
            terms_a = scattered(send_a, keep_a, bits)
            terms_b = scattered(send_b, keep_b, bits[::-1])
            shards.append(
                item_call(
                    epoch, c, shard_rows, me, owner_gram, chunks[c][0], terms_a, terms_b
                )
            )
        users = new_users[0]
        if epoch + 1 < SUB:
            own_gram = new_users[1]
            chunks = [gathered(shard) for shard in shards]
        else:
            chunks = [moved(shard, 0) for shard in shards]
    return users, jnp.concatenate(chunks, axis=0).astype(F32)


def solution(mesh):
    in_specs = (
        P(None, "blk", "grp", None, None, None),
        P(None, "blk", "grp", None),
        P(None, "blk", "grp", None),
        P(None, "blk", "grp", None, None),
        P(None, "blk", "grp"),
        P(None, "blk"),
        P(("blk", "grp"), None),
        P("blk", None),
    )
    out_specs = (P(("blk", "grp"), None), P(("blk", "grp"), None))
    return jax.shard_map(local, mesh=mesh, in_specs=in_specs, out_specs=out_specs, check_vma=False)
```

time: 1980 us -> 234 us (0.12); the launches traced: 1950 us -> 232 us
  waiting for transfers between devices: 755 us -> 56.8 us
  matrix products: 510 us -> 0 us
  loops' own time: 413 us -> 0 us
  local copies, waits for them, and re-layouts: 167 us -> 14.2 us
  other arithmetic: 92.6 us -> 2.11 us
  Pallas kernels: 0 us -> 88.2 us
  starting transfers between devices: 0.31 us -> 69.3 us
    psum x3 -> x0, waiting for transfers between devices: 663 us -> none  [the longest x1 338 us: spread(): return lax.psum(kept, axis)]
    dot_general x281 -> x0, matrix products: 510 us -> none  [the longest x91 219 us: tile_step(): lax.dot_general(errors, user_part, (((0,), (0,)), ((), ())), preferred_el...]
    another operation x2 -> x0, loops' own time: 413 us -> none  [local(): lax.fori_loop(0, counts[epoch, 0, 0], tile_step, (start_user, start_item))]
    dynamic_slice x182 -> x0, local copies, waits for them, and re-layouts: 110 us -> none  [the longest x91 56 us: tile_step(): row_tile = rows_in[slot]]
    pallas_call x0 -> x18, Pallas kernels: none -> 88.2 us  [the longest x8 81.3 us: tile_call(): pl.pallas_call(functools.partial(tile_kernel, epoch, chunk, members, shar...]
    another operation x91 -> x16, other arithmetic: 71.4 us -> 0.61 us
    ppermute x2 -> x60, starting transfers between devices: 0.01 us -> 69.3 us  [the longest x44 57.2 us: swapped(): return lax.ppermute(value, 'grp', [(i, i ^ bit) for i in range(length)])]
    ppermute x2 -> x60, waiting for transfers between devices: 92.3 us -> 56.8 us  [the longest x44 34.6 us: swapped(): return lax.ppermute(value, 'grp', [(i, i ^ bit) for i in range(length)])]
  transfers between devices with their start and end apart: 5 -> 60, of which waited for: 5 -> 24; matrix products, arithmetic and copies ran while one was open for 1% -> 0% of each run, Pallas kernels for 0% -> 34%
where the time goes in v1:
time: 234 us; the launch traced here: 232 us
  Pallas kernels  88.2 us (38%)
  starting transfers between devices  69.3 us (30%)
  waiting for transfers between devices  56.8 us (24%)
  local copies, waits for them, and re-layouts  14.2 us (6%)
    pallas_call x8, Pallas kernels, tile_call(): pl.pallas_call(functools.partial(tile_kernel, epoch, chunk, members, shar...  81.3 us
    ppermute x44, starting transfers between devices, swapped(): return lax.ppermute(value, 'grp', [(i, i ^ bit) for i in range(length)])  57.2 us
    ppermute x44, waiting for transfers between devices, swapped(): return lax.ppermute(value, 'grp', [(i, i ^ bit) for i in range(length)])  34.6 us
    ppermute x16, waiting for transfers between devices, moved(): return lax.ppermute(value, ('blk', 'grp'), pairs)  22.2 us
    unnamed x20, local copies, waits for them, and re-layouts  14.1 us
    ppermute x16, starting transfers between devices, moved(): return lax.ppermute(value, ('blk', 'grp'), pairs)  12.1 us
  transfers between devices with their start and end apart: 60, of which 24 were waited for; matrix products, arithmetic and copies ran while one was open for 0% of the time, Pallas kernels for 34%

profile of v1, /device:TPU:0, one launch (start us, length us, event | category | flops | bytes accessed | tf_op | source)
XLA Modules:
  0.0 231.9 jit_solution(18329845831940876960)
XLA Ops:
  2.1 3.4 %copy-done.1 = f32[16384,128]{1,0:T(8,128)S(1)} copy-done((f32[16384,128]{1,0:T(8,128)S(1)}, f32[16384,128]{1,0:T(8,128)}, u32[]{:S(2)}) %copy-start.1) | copy-done | bytes 8388632
  9.0 9.4 %tiles_0_0.1 = (bf16[2,512,128]{2,1,0:T(8,128)(2,1)S(1)}, bf16[2,512,128]{2,1,0:T(8,128)(2,1)S(1)}, bf16[2,512,128]{2,1,0:T(8,128)(2,1)S(1)}, bf16[2,512,128]{2,...) custom-call(s32[1]{0:T(128)} %bitcast.refs_0_.me_ref, ...), custom_call_target="tpu_custom_call" | custom-call | flops 805306368 | bytes 4194304 | tf_op jit(solution)/shard_map/tiles_0_0/pallas_call | solution.py:209
  18.4 3.0 %collective-permute-start = (bf16[128,128]{1,0:T(8,128)(2,1)S(1)}, bf16[128,128]{1,0:T(8,128)(2,1)S(1)}, u32[]{:S(2)}, u32[]{:S(2)}) collective-permute-start(bf16[128,128]{1,0:T(8,128)(2,1)S(1)} %get-tuple-element.62), channel_id=1, source_target_pairs={{0,1},{1,0},{2,3},{3,2},{4,5},{5,4},{6,7},{7,6},{8,9},{9,8},{10,11... | collective-permute-start | bytes 98312 | tf_op jit(solution)/shard_map/ppermute | solution.py:313
  21.5 2.1 collective-permute-start.31
  23.5 9.6 %tiles_0_1.1 = (bf16[2,512,128]{2,1,0:T(8,128)(2,1)S(1)}, bf16[2,512,128]{2,1,0:T(8,128)(2,1)S(1)}, bf16[2,512,128]{2,1,0:T(8,128)(2,1)S(1)}, bf16[2,512,128]{2,...) custom-call(s32[1]{0:T(128)} %bitcast.refs_0_.me_ref, s32[2,1,1,64]{3,2,1,0:T(1,128)S(1)} %copy-done.5, ...), custom_call_target="tpu_custom_call" | custom-call | flops 805306368 | bytes 4194304 | tf_op jit(solution)/shard_map/tiles_0_1/pallas_call | solution.py:209
  33.2 10.2 %tiles_0_2.1 = (bf16[2,512,128]{2,1,0:T(8,128)(2,1)S(1)}, bf16[2,512,128]{2,1,0:T(8,128)(2,1)S(1)}, bf16[2,512,128]{2,1,0:T(8,128)(2,1)S(1)}, bf16[2,512,128]{2,...) custom-call(s32[1]{0:T(128)} %bitcast.refs_0_.me_ref, s32[2,1,1,64]{3,2,1,0:T(1,128)S(1)} %copy-done.5, ...), custom_call_target="tpu_custom_call" | custom-call | flops 805306368 | bytes 4194304 | tf_op jit(solution)/shard_map/tiles_0_2/pallas_call | solution.py:209
  43.4 9.7 %tiles_0_3.1 = (bf16[2,512,128]{2,1,0:T(8,128)(2,1)S(1)}, bf16[2,512,128]{2,1,0:T(8,128)(2,1)S(1)}, bf16[2,512,128]{2,1,0:T(8,128)(2,1)S(1)}, bf16[2,512,128]{2,...) custom-call(s32[1]{0:T(128)} %bitcast.refs_0_.me_ref, s32[2,1,1,64]{3,2,1,0:T(1,128)S(1)} %copy-done.5, ...), custom_call_target="tpu_custom_call" | custom-call | flops 805306368 | bytes 4194304 | tf_op jit(solution)/shard_map/tiles_0_3/pallas_call | solution.py:209
  55.1 5.4 %collective-permute-start.38 = (bf16[128,128]{1,0:T(8,128)(2,1)S(1)}, bf16[128,128]{1,0:T(8,128)(2,1)S(1)}, u32[]{:S(2)}, u32[]{:S(2)}) collective-permute-start(bf16[128,128]{1,0:T(8,128)(2,1)S(1)} %get-tuple-element.87), channel_id=1, source_target_pairs={{0,1},{1,0},{2,3},{3,2},{4,5},{5,4},{6,7},{7,6},{8,9},{9,8},{10,11... | collective-permute-start | bytes 98312 | tf_op jit(solution)/shard_map/ppermute | solution.py:313
  60.7 2.1 collective-permute-start.13
  62.8 2.0 collective-permute-start.11
  64.9 4.9 %collective-permute-done.20.refs_1_ = bf16[2,512,128]{2,1,0:T(8,128)(2,1)S(1)} collective-permute-done((bf16[2,512,128]{2,1,0:T(8,128)(2,1)S(1)}, bf16[2,512,128]{2,1,0:T(8,128)(2,1)S(1)}, u32[]{:S(2)}, u32[]{:S(2)}) %collective-permute-start.20) | collective-permute-done | bytes 262176 | tf_op jit(solution)/shard_map/ppermute | solution.py:313
  71.7 2.6 %collective-permute-done.13.refs_4_ = bf16[2,512,128]{2,1,0:T(8,128)(2,1)S(1)} collective-permute-done((bf16[2,512,128]{2,1,0:T(8,128)(2,1)S(1)}, bf16[2,512,128]{2,1,0:T(8,128)(2,1)S(1)}, u32[]{:S(2)}, u32[]{:S(2)}) %collective-permute-start.13) | collective-permute-done | bytes 262176 | tf_op jit(solution)/shard_map/ppermute | solution.py:313
  75.3 2.1 collective-permute-start.32
  77.5 2.4 %collective-permute-done.4.refs_4_ = bf16[2,512,128]{2,1,0:T(8,128)(2,1)S(1)} collective-permute-done((bf16[2,512,128]{2,1,0:T(8,128)(2,1)S(1)}, bf16[2,512,128]{2,1,0:T(8,128)(2,1)S(1)}, u32[]{:S(2)}, u32[]{:S(2)}) %collective-permute-start.4) | collective-permute-done | bytes 262176 | tf_op jit(solution)/shard_map/ppermute | solution.py:313
  80.0 2.8 %collective-permute-done.30.refs_2_ = bf16[1,512,128]{2,1,0:T(8,128)(2,1)S(1)} collective-permute-done((bf16[1,512,128]{2,1,0:T(8,128)(2,1)S(1)}, bf16[1,512,128]{2,1,0:T(8,128)(2,1)S(1)}, u32[]{:S(2)}, u32[]{:S(2)}) %collective-permute-start.30) | collective-permute-done | bytes 131104 | tf_op jit(solution)/shard_map/ppermute | solution.py:313
  82.7 2.7 %collective-permute-start.23 = (bf16[1,512,128]{2,1,0:T(8,128)(2,1)S(1)}, bf16[1,512,128]{2,1,0:T(8,128)(2,1)S(1)}, u32[]{:S(2)}, u32[]{:S(2)}) collective-permute-start(bf16[1,512,128]{2,1,0:T(8,128)(2,1)S(1)} %add_convert_fusion.10), channel_id=1, source_target_pairs={{0,1},{1,0},{2,3},{3,2},{4,5},{5,4},{6,7},{7,6},{8,9},{9,8},{10,11... | collective-permute-start | bytes 393224 | tf_op jit(solution)/shard_map/ppermute | solution.py:313
  85.9 2.1 collective-permute-start.5
  90.0 4.8 %collective-permute-done.14.refs_5_ = bf16[1,512,128]{2,1,0:T(8,128)(2,1)S(1)} collective-permute-done((bf16[1,512,128]{2,1,0:T(8,128)(2,1)S(1)}, bf16[1,512,128]{2,1,0:T(8,128)(2,1)S(1)}, u32[]{:S(2)}, u32[]{:S(2)}) %collective-permute-start.14) | collective-permute-done | bytes 131104 | tf_op jit(solution)/shard_map/ppermute | solution.py:313
  95.2 3.0 %collective-permute-done.5.refs_5_ = bf16[1,512,128]{2,1,0:T(8,128)(2,1)S(1)} collective-permute-done((bf16[1,512,128]{2,1,0:T(8,128)(2,1)S(1)}, bf16[1,512,128]{2,1,0:T(8,128)(2,1)S(1)}, u32[]{:S(2)}, u32[]{:S(2)}) %collective-permute-start.5) | collective-permute-done | bytes 131104 | tf_op jit(solution)/shard_map/ppermute | solution.py:313
  101.4 2.0 collective-permute-done.35.refs_10_
  103.4 2.3 collective-permute-start.17
  107.6 4.2 %collective-permute-done.26.refs_10_ = bf16[1024,128]{1,0:T(8,128)(2,1)S(1)} collective-permute-done((bf16[1024,128]{1,0:T(8,128)(2,1)S(1)}, bf16[1024,128]{1,0:T(8,128)(2,1)S(1)}, u32[]{:S(2)}, u32[]{:S(2)}) %collective-permute-start.26) | collective-permute-done | bytes 262176 | tf_op jit(solution)/shard_map/ppermute | solution.py:323
  111.9 3.8 %collective-permute-done.16.refs_9_ = bf16[1024,128]{1,0:T(8,128)(2,1)S(1)} collective-permute-done((bf16[1024,128]{1,0:T(8,128)(2,1)S(1)}, bf16[1024,128]{1,0:T(8,128)(2,1)S(1)}, u32[]{:S(2)}, u32[]{:S(2)}) %collective-permute-start.16) | collective-permute-done | bytes 262176 | tf_op jit(solution)/shard_map/ppermute | solution.py:323
  115.7 4.5 %collective-permute-start.36 = (bf16[512,128]{1,0:T(8,128)(2,1)S(1)}, bf16[512,128]{1,0:T(8,128)(2,1)S(1)}, u32[]{:S(2)}, u32[]{:S(2)}) collective-permute-start(bf16[512,128]{1,0:T(8,128)(2,1)S(1)} %slice.134), channel_id=1, source_target_pairs={{0,2},{1,3},{2,0},{3,1},{4,6},{5,7},{6,4},{7,5},{8,10},{9,11},{10,... | collective-permute-start | bytes 393224 | tf_op jit(solution)/shard_map/ppermute | solution.py:313
  120.3 2.7 %collective-permute-start.37 = (bf16[512,128]{1,0:T(8,128)(2,1)S(1)}, bf16[512,128]{1,0:T(8,128)(2,1)S(1)}, u32[]{:S(2)}, u32[]{:S(2)}) collective-permute-start(bf16[512,128]{1,0:T(8,128)(2,1)S(1)} %slice.135), channel_id=1, source_target_pairs={{0,1},{1,0},{2,3},{3,2},{4,5},{5,4},{6,7},{7,6},{8,9},{9,8},{10,11... | collective-permute-start | bytes 393224 | tf_op jit(solution)/shard_map/ppermute | solution.py:313
  123.7 2.3 collective-permute-done.8.refs_10_
  126.0 2.7 %collective-permute-start.28 = (bf16[512,128]{1,0:T(8,128)(2,1)S(1)}, bf16[512,128]{1,0:T(8,128)(2,1)S(1)}, u32[]{:S(2)}, u32[]{:S(2)}) collective-permute-start(bf16[512,128]{1,0:T(8,128)(2,1)S(1)} %slice.129), channel_id=1, source_target_pairs={{0,1},{1,0},{2,3},{3,2},{4,5},{5,4},{6,7},{7,6},{8,9},{9,8},{10,11... | collective-permute-start | bytes 393224 | tf_op jit(solution)/shard_map/ppermute | solution.py:313
  128.7 2.8 %collective-permute-start.18 = (bf16[512,128]{1,0:T(8,128)(2,1)S(1)}, bf16[512,128]{1,0:T(8,128)(2,1)S(1)}, u32[]{:S(2)}, u32[]{:S(2)}) collective-permute-start(bf16[512,128]{1,0:T(8,128)(2,1)S(1)} %slice.122), channel_id=1, source_target_pairs={{0,2},{1,3},{2,0},{3,1},{4,6},{5,7},{6,4},{7,5},{8,10},{9,11},{10,... | collective-permute-start | bytes 393224 | tf_op jit(solution)/shard_map/ppermute | solution.py:313
  131.6 5.8 %copy-done = bf16[2,1,1,64,256,256]{5,4,3,2,1,0:T(8,128)(2,1)S(1)} copy-done((bf16[2,1,1,64,256,256]{5,4,3,2,1,0:T(8,128)(2,1)S(1)}, bf16[2,1,1,64,256,256]{5,4,3,2,1,0:T(8,128)(2,1)}, u32[]{:S(2)}) %copy-start) | copy-done | bytes 16777240
  137.4 9.4 %tiles_1_0.1 = (bf16[2,512,128]{2,1,0:T(8,128)(2,1)S(1)}, bf16[2,512,128]{2,1,0:T(8,128)(2,1)S(1)}, bf16[2,512,128]{2,1,0:T(8,128)(2,1)S(1)}, bf16[2,512,128]{2,...) custom-call(s32[1]{0:T(128)} %bitcast.refs_0_.me_ref, s32[2,1,1,64]{3,2,1,0:T(1,128)S(1)} %copy-done.5, ...), custom_call_target="tpu_custom_call" | custom-call | flops 805306368 | bytes 4194304 | tf_op jit(solution)/shard_map/tiles_1_0/pallas_call | solution.py:209
  147.7 3.2 %collective-permute-start.10 = (bf16[512,128]{1,0:T(8,128)(2,1)S(1)}, bf16[512,128]{1,0:T(8,128)(2,1)S(1)}, u32[]{:S(2)}, u32[]{:S(2)}) collective-permute-start(bf16[512,128]{1,0:T(8,128)(2,1)S(1)} %slice.117), channel_id=1, source_target_pairs={{0,1},{1,0},{2,3},{3,2},{4,5},{5,4},{6,7},{7,6},{8,9},{9,8},{10,11... | collective-permute-start | bytes 393224 | tf_op jit(solution)/shard_map/ppermute | solution.py:313
  150.9 2.0 collective-permute-start.9
  152.9 10.0 %tiles_1_1.1 = (bf16[2,512,128]{2,1,0:T(8,128)(2,1)S(1)}, bf16[2,512,128]{2,1,0:T(8,128)(2,1)S(1)}, bf16[2,512,128]{2,1,0:T(8,128)(2,1)S(1)}, bf16[2,512,128]{2,...) custom-call(s32[1]{0:T(128)} %bitcast.refs_0_.me_ref, s32[2,1,1,64]{3,2,1,0:T(1,128)S(1)} %copy-done.5, ...), custom_call_target="tpu_custom_call" | custom-call | flops 805306368 | bytes 4194304 | tf_op jit(solution)/shard_map/tiles_1_1/pallas_call | solution.py:209
  162.9 1.9 collective-permute-start.39
  164.8 11.1 %tiles_1_2.1 = (bf16[2,512,128]{2,1,0:T(8,128)(2,1)S(1)}, bf16[2,512,128]{2,1,0:T(8,128)(2,1)S(1)}, bf16[2,512,128]{2,1,0:T(8,128)(2,1)S(1)}, bf16[2,512,128]{2,...) custom-call(s32[1]{0:T(128)} %bitcast.refs_0_.me_ref, s32[2,1,1,64]{3,2,1,0:T(1,128)S(1)} %copy-done.5, ...), custom_call_target="tpu_custom_call" | custom-call | flops 805306368 | bytes 4194304 | tf_op jit(solution)/shard_map/tiles_1_2/pallas_call | solution.py:209
  178.1 12.0 %tiles_1_3.1 = (bf16[2,512,128]{2,1,0:T(8,128)(2,1)S(1)}, bf16[2,512,128]{2,1,0:T(8,128)(2,1)S(1)}, bf16[2,512,128]{2,1,0:T(8,128)(2,1)S(1)}, bf16[2,512,128]{2,...) custom-call(s32[1]{0:T(128)} %bitcast.refs_0_.me_ref, s32[2,1,1,64]{3,2,1,0:T(1,128)S(1)} %copy-done.5, ...), custom_call_target="tpu_custom_call" | custom-call | flops 805306368 | bytes 4194304 | tf_op jit(solution)/shard_map/tiles_1_3/pallas_call | solution.py:209
  190.5 1.9 collective-permute-start.57
  192.5 2.1 collective-permute-start.55
  194.6 3.9 %collective-permute-done.52.refs_4_ = bf16[2,512,128]{2,1,0:T(8,128)(2,1)S(1)} collective-permute-done((bf16[2,512,128]{2,1,0:T(8,128)(2,1)S(1)}, bf16[2,512,128]{2,1,0:T(8,128)(2,1)S(1)}, u32[]{:S(2)}, u32[]{:S(2)}) %collective-permute-start.52) | collective-permute-done | bytes 262176 | tf_op jit(solution)/shard_map/ppermute | solution.py:313
  199.5 2.0 collective-permute-start.41
  203.1 2.1 collective-permute-start.46
  205.2 2.0 collective-permute-done.43.refs_5_
  212.4 4.3 %collective-permute-start.49 = (bf16[1024,128]{1,0:T(8,128)(2,1)S(1)}, bf16[1024,128]{1,0:T(8,128)(2,1)S(1)}, u32[]{:S(2)}, u32[]{:S(2)}) collective-permute-start(bf16[1024,128]{1,0:T(8,128)(2,1)S(1)} %items_1_1.1), channel_id=1, source_target_pairs={{0,4},{1,5},{2,6},{3,7},{4,8},{5,9},{6,10},{7,11},{8,12},{9,13},{1... | collective-permute-start | bytes 786440 | tf_op jit(solution)/shard_map/ppermute | solution.py:323
  216.9 2.2 collective-permute-start.54
  220.1 2.5 %users_1.1 = f32[2048,128]{1,0:T(8,128)} custom-call(s32[1]{0:T(128)} %bitcast.refs_0_.me_ref, s32[2,1]{1,0:T(2,128)S(1)} %copy.27.refs_4_.owner_ref, f32[2048,128]{1,0:T(8,128)S(1)} %get-tuple-element.61.refs_7_.users, f32[2048,128]{1,0:T(8,128)S(1)} %get-tuple-element.85.grad, f32[128,128]{1,0:T(8,128)S(1)} %get-tuple-element.86.gram), custom_call_target="tpu_custom_call" | custom-call | flops 469762048 | bytes 4194304 | tf_op jit(solution)/shard_map/users_1/pallas_call | solution.py:253
  222.7 2.1 collective-permute-done.49
  224.8 2.8 %collective-permute-done.54 = bf16[1024,128]{1,0:T(8,128)(2,1)S(1)} collective-permute-done((bf16[1024,128]{1,0:T(8,128)(2,1)S(1)}, bf16[1024,128]{1,0:T(8,128)(2,1)S(1)}, u32[]{:S(2)}, u32[]{:S(2)}) %collective-permute-start.54) | collective-permute-done | bytes 262176 | tf_op jit(solution)/shard_map/ppermute | solution.py:323
  227.6 2.8 %collective-permute-done.59 = bf16[1024,128]{1,0:T(8,128)(2,1)S(1)} collective-permute-done((bf16[1024,128]{1,0:T(8,128)(2,1)S(1)}, bf16[1024,128]{1,0:T(8,128)(2,1)S(1)}, u32[]{:S(2)}, u32[]{:S(2)}) %collective-permute-start.59) | collective-permute-done | bytes 262176 | tf_op jit(solution)/shard_map/ppermute | solution.py:323
  (140 shorter events, 33.3 us)
Async XLA Ops:
  18.4 34.7 %collective-permute-start = (bf16[128,128]{1,0:T(8,128)(2,1)S(1)}, bf16[128,128]{1,0:T(8,128)(2,1)S(1)}, u32[]{:S(2)}, u32[]{:S(2)}) collective-permute-start(bf16[128,128]{1,0:T(8,128)(2,1)S(1)} %get-tuple-element.62), channel_id=1, source_target_pairs={{0,1},{1,0},{2,3},{3,2},{4,5},{5,4},{6,7},{7,6},{8,9},{9,8},{10,11... | collective-permute-start | bytes 98312 | tf_op jit(solution)/shard_map/ppermute | solution.py:313
  21.4 39.3 %collective-permute-start.29 = (bf16[2,512,128]{2,1,0:T(8,128)(2,1)S(1)}, bf16[2,512,128]{2,1,0:T(8,128)(2,1)S(1)}, u32[]{:S(2)}, u32[]{:S(2)}) collective-permute-start(bf16[2,512,128]{2,1,0:T(8,128)(2,1)S(1)} %get-tuple-element.76), channel_id=1, source_target_pairs={{0,1},{1,0},{2,3},{3,2},{4,5},{5,4},{6,7},{7,6},{8,9},{9,8},{10,11... | collective-permute-start | bytes 786440 | tf_op jit(solution)/shard_map/ppermute | solution.py:313
  21.5 41.3 %collective-permute-start.31 = (bf16[2,512,128]{2,1,0:T(8,128)(2,1)S(1)}, bf16[2,512,128]{2,1,0:T(8,128)(2,1)S(1)}, u32[]{:S(2)}, u32[]{:S(2)}) collective-permute-start(bf16[2,512,128]{2,1,0:T(8,128)(2,1)S(1)} %get-tuple-element.78), channel_id=1, source_target_pairs={{0,2},{1,3},{2,0},{3,1},{4,6},{5,7},{6,4},{7,5},{8,10},{9,11},{10,... | collective-permute-start | bytes 786440 | tf_op jit(solution)/shard_map/ppermute | solution.py:313
  55.1 30.7 %collective-permute-start.38 = (bf16[128,128]{1,0:T(8,128)(2,1)S(1)}, bf16[128,128]{1,0:T(8,128)(2,1)S(1)}, u32[]{:S(2)}, u32[]{:S(2)}) collective-permute-start(bf16[128,128]{1,0:T(8,128)(2,1)S(1)} %get-tuple-element.87), channel_id=1, source_target_pairs={{0,1},{1,0},{2,3},{3,2},{4,5},{5,4},{6,7},{7,6},{8,9},{9,8},{10,11... | collective-permute-start | bytes 98312 | tf_op jit(solution)/shard_map/ppermute | solution.py:313
  60.5 9.2 %collective-permute-start.20 = (bf16[2,512,128]{2,1,0:T(8,128)(2,1)S(1)}, bf16[2,512,128]{2,1,0:T(8,128)(2,1)S(1)}, u32[]{:S(2)}, u32[]{:S(2)}) collective-permute-start(bf16[2,512,128]{2,1,0:T(8,128)(2,1)S(1)} %get-tuple-element.72), channel_id=1, source_target_pairs={{0,1},{1,0},{2,3},{3,2},{4,5},{5,4},{6,7},{7,6},{8,9},{9,8},{10,11... | collective-permute-start | bytes 786440 | tf_op jit(solution)/shard_map/ppermute | solution.py:313
  60.6 9.1 %collective-permute-start.22 = (bf16[2,512,128]{2,1,0:T(8,128)(2,1)S(1)}, bf16[2,512,128]{2,1,0:T(8,128)(2,1)S(1)}, u32[]{:S(2)}, u32[]{:S(2)}) collective-permute-start(bf16[2,512,128]{2,1,0:T(8,128)(2,1)S(1)} %get-tuple-element.74), channel_id=1, source_target_pairs={{0,2},{1,3},{2,0},{3,1},{4,6},{5,7},{6,4},{7,5},{8,10},{9,11},{10,... | collective-permute-start | bytes 786440 | tf_op jit(solution)/shard_map/ppermute | solution.py:313
  60.7 13.6 %collective-permute-start.13 = (bf16[2,512,128]{2,1,0:T(8,128)(2,1)S(1)}, bf16[2,512,128]{2,1,0:T(8,128)(2,1)S(1)}, u32[]{:S(2)}, u32[]{:S(2)}) collective-permute-start(bf16[2,512,128]{2,1,0:T(8,128)(2,1)S(1)} %get-tuple-element.70), channel_id=1, source_target_pairs={{0,2},{1,3},{2,0},{3,1},{4,6},{5,7},{6,4},{7,5},{8,10},{9,11},{10,... | collective-permute-start | bytes 786440 | tf_op jit(solution)/shard_map/ppermute | solution.py:313
  62.8 12.5 %collective-permute-start.11 = (bf16[2,512,128]{2,1,0:T(8,128)(2,1)S(1)}, bf16[2,512,128]{2,1,0:T(8,128)(2,1)S(1)}, u32[]{:S(2)}, u32[]{:S(2)}) collective-permute-start(bf16[2,512,128]{2,1,0:T(8,128)(2,1)S(1)} %get-tuple-element.68), channel_id=1, source_target_pairs={{0,1},{1,0},{2,3},{3,2},{4,5},{5,4},{6,7},{7,6},{8,9},{9,8},{10,11... | collective-permute-start | bytes 786440 | tf_op jit(solution)/shard_map/ppermute | solution.py:313
  69.7 10.2 %collective-permute-start.4 = (bf16[2,512,128]{2,1,0:T(8,128)(2,1)S(1)}, bf16[2,512,128]{2,1,0:T(8,128)(2,1)S(1)}, u32[]{:S(2)}, u32[]{:S(2)}) collective-permute-start(bf16[2,512,128]{2,1,0:T(8,128)(2,1)S(1)} %get-tuple-element.66), channel_id=1, source_target_pairs={{0,2},{1,3},{2,0},{3,1},{4,6},{5,7},{6,4},{7,5},{8,10},{9,11},{10,... | collective-permute-start | bytes 786440 | tf_op jit(solution)/shard_map/ppermute | solution.py:313
  69.8 16.1 %collective-permute-start.2 = (bf16[2,512,128]{2,1,0:T(8,128)(2,1)S(1)}, bf16[2,512,128]{2,1,0:T(8,128)(2,1)S(1)}, u32[]{:S(2)}, u32[]{:S(2)}) collective-permute-start(bf16[2,512,128]{2,1,0:T(8,128)(2,1)S(1)} %get-tuple-element.64), channel_id=1, source_target_pairs={{0,1},{1,0},{2,3},{3,2},{4,5},{5,4},{6,7},{7,6},{8,9},{9,8},{10,11... | collective-permute-start | bytes 786440 | tf_op jit(solution)/shard_map/ppermute | solution.py:313
  75.3 10.0 %collective-permute-start.32 = (bf16[1,512,128]{2,1,0:T(8,128)(2,1)S(1)}, bf16[1,512,128]{2,1,0:T(8,128)(2,1)S(1)}, u32[]{:S(2)}, u32[]{:S(2)}) collective-permute-start(bf16[1,512,128]{2,1,0:T(8,128)(2,1)S(1)} %add_convert_fusion.8), channel_id=1, source_target_pairs={{0,1},{1,0},{2,3},{3,2},{4,5},{5,4},{6,7},{7,6},{8,9},{9,8},{10,11... | collective-permute-start | bytes 393224 | tf_op jit(solution)/shard_map/ppermute | solution.py:313
  85.4 9.4 %collective-permute-start.14 = (bf16[1,512,128]{2,1,0:T(8,128)(2,1)S(1)}, bf16[1,512,128]{2,1,0:T(8,128)(2,1)S(1)}, u32[]{:S(2)}, u32[]{:S(2)}) collective-permute-start(bf16[1,512,128]{2,1,0:T(8,128)(2,1)S(1)} %add_convert_fusion.12), channel_id=1, source_target_pairs={{0,1},{1,0},{2,3},{3,2},{4,5},{5,4},{6,7},{7,6},{8,9},{9,8},{10,11... | collective-permute-start | bytes 393224 | tf_op jit(solution)/shard_map/ppermute | solution.py:313
  85.8 9.0 %collective-permute-start.12 = (bf16[1,512,128]{2,1,0:T(8,128)(2,1)S(1)}, bf16[1,512,128]{2,1,0:T(8,128)(2,1)S(1)}, u32[]{:S(2)}, u32[]{:S(2)}) collective-permute-start(bf16[1,512,128]{2,1,0:T(8,128)(2,1)S(1)} %add_convert_fusion.13), channel_id=1, source_target_pairs={{0,2},{1,3},{2,0},{3,1},{4,6},{5,7},{6,4},{7,5},{8,10},{9,11},{10,... | collective-permute-start | bytes 393224 | tf_op jit(solution)/shard_map/ppermute | solution.py:313
  85.9 12.2 %collective-permute-start.5 = (bf16[1,512,128]{2,1,0:T(8,128)(2,1)S(1)}, bf16[1,512,128]{2,1,0:T(8,128)(2,1)S(1)}, u32[]{:S(2)}, u32[]{:S(2)}) collective-permute-start(bf16[1,512,128]{2,1,0:T(8,128)(2,1)S(1)} %add_convert_fusion.14), channel_id=1, source_target_pairs={{0,1},{1,0},{2,3},{3,2},{4,5},{5,4},{6,7},{7,6},{8,9},{9,8},{10,11... | collective-permute-start | bytes 393224 | tf_op jit(solution)/shard_map/ppermute | solution.py:313
  88.0 11.3 %collective-permute-start.34 = (bf16[1024,128]{1,0:T(8,128)(2,1)S(1)}, bf16[1024,128]{1,0:T(8,128)(2,1)S(1)}, u32[]{:S(2)}, u32[]{:S(2)}) collective-permute-start(bf16[1024,128]{1,0:T(8,128)(2,1)S(1)} %items_0_0.1), channel_id=1, source_target_pairs={{0,5},{1,4},{2,7},{3,6},{4,9},{5,8},{6,11},{7,10},{8,13},{9,12},{1... | collective-permute-start | bytes 786440 | tf_op jit(solution)/shard_map/ppermute | solution.py:323
  98.1 9.1 %collective-permute-start.25 = (bf16[1024,128]{1,0:T(8,128)(2,1)S(1)}, bf16[1024,128]{1,0:T(8,128)(2,1)S(1)}, u32[]{:S(2)}, u32[]{:S(2)}) collective-permute-start(bf16[1024,128]{1,0:T(8,128)(2,1)S(1)} %items_0_1.1), channel_id=1, source_target_pairs={{0,5},{1,4},{2,7},{3,6},{4,9},{5,8},{6,11},{7,10},{8,13},{9,12},{1... | collective-permute-start | bytes 786440 | tf_op jit(solution)/shard_map/ppermute | solution.py:323
  98.2 13.6 %collective-permute-start.26 = (bf16[1024,128]{1,0:T(8,128)(2,1)S(1)}, bf16[1024,128]{1,0:T(8,128)(2,1)S(1)}, u32[]{:S(2)}, u32[]{:S(2)}) collective-permute-start(bf16[1024,128]{1,0:T(8,128)(2,1)S(1)} %items_0_1.1), channel_id=1, source_target_pairs={{0,6},{1,7},{2,4},{3,5},{4,10},{5,11},{6,8},{7,9},{8,14},{9,15},{1... | collective-permute-start | bytes 786440 | tf_op jit(solution)/shard_map/ppermute | solution.py:323
  99.2 12.6 %collective-permute-start.24 = (bf16[1024,128]{1,0:T(8,128)(2,1)S(1)}, bf16[1024,128]{1,0:T(8,128)(2,1)S(1)}, u32[]{:S(2)}, u32[]{:S(2)}) collective-permute-start(bf16[1024,128]{1,0:T(8,128)(2,1)S(1)} %items_0_1.1), channel_id=1, source_target_pairs={{0,4},{1,5},{2,6},{3,7},{4,8},{5,9},{6,10},{7,11},{8,12},{9,13},{1... | collective-permute-start | bytes 786440 | tf_op jit(solution)/shard_map/ppermute | solution.py:323
  103.4 12.3 %collective-permute-start.16 = (bf16[1024,128]{1,0:T(8,128)(2,1)S(1)}, bf16[1024,128]{1,0:T(8,128)(2,1)S(1)}, u32[]{:S(2)}, u32[]{:S(2)}) collective-permute-start(bf16[1024,128]{1,0:T(8,128)(2,1)S(1)} %items_0_2.1), channel_id=1, source_target_pairs={{0,5},{1,4},{2,7},{3,6},{4,9},{5,8},{6,11},{7,10},{8,13},{9,12},{1... | collective-permute-start | bytes 786440 | tf_op jit(solution)/shard_map/ppermute | solution.py:323
  103.4 16.9 %collective-permute-start.17 = (bf16[1024,128]{1,0:T(8,128)(2,1)S(1)}, bf16[1024,128]{1,0:T(8,128)(2,1)S(1)}, u32[]{:S(2)}, u32[]{:S(2)}) collective-permute-start(bf16[1024,128]{1,0:T(8,128)(2,1)S(1)} %items_0_2.1), channel_id=1, source_target_pairs={{0,6},{1,7},{2,4},{3,5},{4,10},{5,11},{6,8},{7,9},{8,14},{9,15},{1... | collective-permute-start | bytes 786440 | tf_op jit(solution)/shard_map/ppermute | solution.py:323
  107.3 15.8 %collective-permute-start.15 = (bf16[1024,128]{1,0:T(8,128)(2,1)S(1)}, bf16[1024,128]{1,0:T(8,128)(2,1)S(1)}, u32[]{:S(2)}, u32[]{:S(2)}) collective-permute-start(bf16[1024,128]{1,0:T(8,128)(2,1)S(1)} %items_0_2.1), channel_id=1, source_target_pairs={{0,4},{1,5},{2,6},{3,7},{4,8},{5,9},{6,10},{7,11},{8,12},{9,13},{1... | collective-permute-start | bytes 786440 | tf_op jit(solution)/shard_map/ppermute | solution.py:323
  111.9 14.1 %collective-permute-start.8 = (bf16[1024,128]{1,0:T(8,128)(2,1)S(1)}, bf16[1024,128]{1,0:T(8,128)(2,1)S(1)}, u32[]{:S(2)}, u32[]{:S(2)}) collective-permute-start(bf16[1024,128]{1,0:T(8,128)(2,1)S(1)} %items_0_3.1), channel_id=1, source_target_pairs={{0,6},{1,7},{2,4},{3,5},{4,10},{5,11},{6,8},{7,9},{8,14},{9,15},{1... | collective-permute-start | bytes 786440 | tf_op jit(solution)/shard_map/ppermute | solution.py:323
  111.9 16.8 %collective-permute-start.7 = (bf16[1024,128]{1,0:T(8,128)(2,1)S(1)}, bf16[1024,128]{1,0:T(8,128)(2,1)S(1)}, u32[]{:S(2)}, u32[]{:S(2)}) collective-permute-start(bf16[1024,128]{1,0:T(8,128)(2,1)S(1)} %items_0_3.1), channel_id=1, source_target_pairs={{0,5},{1,4},{2,7},{3,6},{4,9},{5,8},{6,11},{7,10},{8,13},{9,12},{1... | collective-permute-start | bytes 786440 | tf_op jit(solution)/shard_map/ppermute | solution.py:323
  115.7 15.8 %collective-permute-start.36 = (bf16[512,128]{1,0:T(8,128)(2,1)S(1)}, bf16[512,128]{1,0:T(8,128)(2,1)S(1)}, u32[]{:S(2)}, u32[]{:S(2)}) collective-permute-start(bf16[512,128]{1,0:T(8,128)(2,1)S(1)} %slice.134), channel_id=1, source_target_pairs={{0,2},{1,3},{2,0},{3,1},{4,6},{5,7},{6,4},{7,5},{8,10},{9,11},{10,... | collective-permute-start | bytes 393224 | tf_op jit(solution)/shard_map/ppermute | solution.py:313
  120.3 11.2 %collective-permute-start.37 = (bf16[512,128]{1,0:T(8,128)(2,1)S(1)}, bf16[512,128]{1,0:T(8,128)(2,1)S(1)}, u32[]{:S(2)}, u32[]{:S(2)}) collective-permute-start(bf16[512,128]{1,0:T(8,128)(2,1)S(1)} %slice.135), channel_id=1, source_target_pairs={{0,1},{1,0},{2,3},{3,2},{4,5},{5,4},{6,7},{7,6},{8,9},{9,8},{10,11... | collective-permute-start | bytes 393224 | tf_op jit(solution)/shard_map/ppermute | solution.py:313
  123.0 23.8 %collective-permute-start.27 = (bf16[512,128]{1,0:T(8,128)(2,1)S(1)}, bf16[512,128]{1,0:T(8,128)(2,1)S(1)}, u32[]{:S(2)}, u32[]{:S(2)}) collective-permute-start(bf16[512,128]{1,0:T(8,128)(2,1)S(1)} %slice.128), channel_id=1, source_target_pairs={{0,2},{1,3},{2,0},{3,1},{4,6},{5,7},{6,4},{7,5},{8,10},{9,11},{10,... | collective-permute-start | bytes 393224 | tf_op jit(solution)/shard_map/ppermute | solution.py:313
  126.0 21.7 %collective-permute-start.28 = (bf16[512,128]{1,0:T(8,128)(2,1)S(1)}, bf16[512,128]{1,0:T(8,128)(2,1)S(1)}, u32[]{:S(2)}, u32[]{:S(2)}) collective-permute-start(bf16[512,128]{1,0:T(8,128)(2,1)S(1)} %slice.129), channel_id=1, source_target_pairs={{0,1},{1,0},{2,3},{3,2},{4,5},{5,4},{6,7},{7,6},{8,9},{9,8},{10,11... | collective-permute-start | bytes 393224 | tf_op jit(solution)/shard_map/ppermute | solution.py:313
  128.7 22.2 %collective-permute-start.18 = (bf16[512,128]{1,0:T(8,128)(2,1)S(1)}, bf16[512,128]{1,0:T(8,128)(2,1)S(1)}, u32[]{:S(2)}, u32[]{:S(2)}) collective-permute-start(bf16[512,128]{1,0:T(8,128)(2,1)S(1)} %slice.122), channel_id=1, source_target_pairs={{0,2},{1,3},{2,0},{3,1},{4,6},{5,7},{6,4},{7,5},{8,10},{9,11},{10,... | collective-permute-start | bytes 393224 | tf_op jit(solution)/shard_map/ppermute | solution.py:313
  131.5 44.4 %collective-permute-start.6 = (bf16[1024,128]{1,0:T(8,128)(2,1)S(1)}, bf16[1024,128]{1,0:T(8,128)(2,1)S(1)}, u32[]{:S(2)}, u32[]{:S(2)}) collective-permute-start(bf16[1024,128]{1,0:T(8,128)(2,1)S(1)} %items_0_3.1), channel_id=1, source_target_pairs={{0,4},{1,5},{2,6},{3,7},{4,8},{5,9},{6,10},{7,11},{8,12},{9,13},{1... | collective-permute-start | bytes 786440 | tf_op jit(solution)/shard_map/ppermute | solution.py:323
  131.5 31.3 %collective-permute-start.19 = (bf16[512,128]{1,0:T(8,128)(2,1)S(1)}, bf16[512,128]{1,0:T(8,128)(2,1)S(1)}, u32[]{:S(2)}, u32[]{:S(2)}) collective-permute-start(bf16[512,128]{1,0:T(8,128)(2,1)S(1)} %slice.123), channel_id=1, source_target_pairs={{0,1},{1,0},{2,3},{3,2},{4,5},{5,4},{6,7},{7,6},{8,9},{9,8},{10,11... | collective-permute-start | bytes 393224 | tf_op jit(solution)/shard_map/ppermute | solution.py:313
  146.8 43.3 %collective-permute-start.42 = (bf16[2,512,128]{2,1,0:T(8,128)(2,1)S(1)}, bf16[2,512,128]{2,1,0:T(8,128)(2,1)S(1)}, u32[]{:S(2)}, u32[]{:S(2)}) collective-permute-start(bf16[2,512,128]{2,1,0:T(8,128)(2,1)S(1)} %get-tuple-element.91), channel_id=1, source_target_pairs={{0,2},{1,3},{2,0},{3,1},{4,6},{5,7},{6,4},{7,5},{8,10},{9,11},{10,... | collective-permute-start | bytes 786440 | tf_op jit(solution)/shard_map/ppermute | solution.py:313
  147.7 28.3 %collective-permute-start.10 = (bf16[512,128]{1,0:T(8,128)(2,1)S(1)}, bf16[512,128]{1,0:T(8,128)(2,1)S(1)}, u32[]{:S(2)}, u32[]{:S(2)}) collective-permute-start(bf16[512,128]{1,0:T(8,128)(2,1)S(1)} %slice.117), channel_id=1, source_target_pairs={{0,1},{1,0},{2,3},{3,2},{4,5},{5,4},{6,7},{7,6},{8,9},{9,8},{10,11... | collective-permute-start | bytes 393224 | tf_op jit(solution)/shard_map/ppermute | solution.py:313
  150.9 25.3 %collective-permute-start.9 = (bf16[512,128]{1,0:T(8,128)(2,1)S(1)}, bf16[512,128]{1,0:T(8,128)(2,1)S(1)}, u32[]{:S(2)}, u32[]{:S(2)}) collective-permute-start(bf16[512,128]{1,0:T(8,128)(2,1)S(1)} %slice.116), channel_id=1, source_target_pairs={{0,2},{1,3},{2,0},{3,1},{4,6},{5,7},{6,4},{7,5},{8,10},{9,11},{10,... | collective-permute-start | bytes 393224 | tf_op jit(solution)/shard_map/ppermute | solution.py:313
  162.9 40.2 %collective-permute-start.39 = (bf16[128,128]{1,0:T(8,128)(2,1)S(1)}, bf16[128,128]{1,0:T(8,128)(2,1)S(1)}, u32[]{:S(2)}, u32[]{:S(2)}) collective-permute-start(bf16[128,128]{1,0:T(8,128)(2,1)S(1)} %add.70), channel_id=1, source_target_pairs={{0,2},{1,3},{2,0},{3,1},{4,6},{5,7},{6,4},{7,5},{8,10},{9,11},{10,... | collective-permute-start | bytes 98312 | tf_op jit(solution)/shard_map/ppermute | solution.py:313
  175.9 14.3 %collective-permute-start.40 = (bf16[2,512,128]{2,1,0:T(8,128)(2,1)S(1)}, bf16[2,512,128]{2,1,0:T(8,128)(2,1)S(1)}, u32[]{:S(2)}, u32[]{:S(2)}) collective-permute-start(bf16[2,512,128]{2,1,0:T(8,128)(2,1)S(1)} %get-tuple-element.89), channel_id=1, source_target_pairs={{0,1},{1,0},{2,3},{3,2},{4,5},{5,4},{6,7},{7,6},{8,9},{9,8},{10,11... | collective-permute-start | bytes 786440 | tf_op jit(solution)/shard_map/ppermute | solution.py:313
  176.0 14.5 %collective-permute-start.47 = (bf16[2,512,128]{2,1,0:T(8,128)(2,1)S(1)}, bf16[2,512,128]{2,1,0:T(8,128)(2,1)S(1)}, u32[]{:S(2)}, u32[]{:S(2)}) collective-permute-start(bf16[2,512,128]{2,1,0:T(8,128)(2,1)S(1)} %get-tuple-element.95), channel_id=1, source_target_pairs={{0,2},{1,3},{2,0},{3,1},{4,6},{5,7},{6,4},{7,5},{8,10},{9,11},{10,... | collective-permute-start | bytes 786440 | tf_op jit(solution)/shard_map/ppermute | solution.py:313
  176.2 16.3 %collective-permute-start.45 = (bf16[2,512,128]{2,1,0:T(8,128)(2,1)S(1)}, bf16[2,512,128]{2,1,0:T(8,128)(2,1)S(1)}, u32[]{:S(2)}, u32[]{:S(2)}) collective-permute-start(bf16[2,512,128]{2,1,0:T(8,128)(2,1)S(1)} %get-tuple-element.93), channel_id=1, source_target_pairs={{0,1},{1,0},{2,3},{3,2},{4,5},{5,4},{6,7},{7,6},{8,9},{9,8},{10,11... | collective-permute-start | bytes 786440 | tf_op jit(solution)/shard_map/ppermute | solution.py:313
  190.2 9.3 %collective-permute-start.50 = (bf16[2,512,128]{2,1,0:T(8,128)(2,1)S(1)}, bf16[2,512,128]{2,1,0:T(8,128)(2,1)S(1)}, u32[]{:S(2)}, u32[]{:S(2)}) collective-permute-start(bf16[2,512,128]{2,1,0:T(8,128)(2,1)S(1)} %get-tuple-element.97), channel_id=1, source_target_pairs={{0,1},{1,0},{2,3},{3,2},{4,5},{5,4},{6,7},{7,6},{8,9},{9,8},{10,11... | collective-permute-start | bytes 786440 | tf_op jit(solution)/shard_map/ppermute | solution.py:313
  190.5 12.2 %collective-permute-start.57 = (bf16[2,512,128]{2,1,0:T(8,128)(2,1)S(1)}, bf16[2,512,128]{2,1,0:T(8,128)(2,1)S(1)}, u32[]{:S(2)}, u32[]{:S(2)}) collective-permute-start(bf16[2,512,128]{2,1,0:T(8,128)(2,1)S(1)} %get-tuple-element.103), channel_id=1, source_target_pairs={{0,2},{1,3},{2,0},{3,1},{4,6},{5,7},{6,4},{7,5},{8,10},{9,11},{10,... | collective-permute-start | bytes 786440 | tf_op jit(solution)/shard_map/ppermute | solution.py:313
  192.5 12.7 %collective-permute-start.55 = (bf16[2,512,128]{2,1,0:T(8,128)(2,1)S(1)}, bf16[2,512,128]{2,1,0:T(8,128)(2,1)S(1)}, u32[]{:S(2)}, u32[]{:S(2)}) collective-permute-start(bf16[2,512,128]{2,1,0:T(8,128)(2,1)S(1)} %get-tuple-element.101), channel_id=1, source_target_pairs={{0,1},{1,0},{2,3},{3,2},{4,5},{5,4},{6,7},{7,6},{8,9},{9,8},{10,11... | collective-permute-start | bytes 786440 | tf_op jit(solution)/shard_map/ppermute | solution.py:313
  198.5 8.8 %collective-permute-start.43 = (bf16[1,512,128]{2,1,0:T(8,128)(2,1)S(1)}, bf16[1,512,128]{2,1,0:T(8,128)(2,1)S(1)}, u32[]{:S(2)}, u32[]{:S(2)}) collective-permute-start(bf16[1,512,128]{2,1,0:T(8,128)(2,1)S(1)} %add_convert_fusion.6), channel_id=1, source_target_pairs={{0,1},{1,0},{2,3},{3,2},{4,5},{5,4},{6,7},{7,6},{8,9},{9,8},{10,11... | collective-permute-start | bytes 393224 | tf_op jit(solution)/shard_map/ppermute | solution.py:313
  207.3 9.4 %collective-permute-start.51 = (bf16[1,512,128]{2,1,0:T(8,128)(2,1)S(1)}, bf16[1,512,128]{2,1,0:T(8,128)(2,1)S(1)}, u32[]{:S(2)}, u32[]{:S(2)}) collective-permute-start(bf16[1,512,128]{2,1,0:T(8,128)(2,1)S(1)} %add_convert_fusion.3), channel_id=1, source_target_pairs={{0,2},{1,3},{2,0},{3,1},{4,6},{5,7},{6,4},{7,5},{8,10},{9,11},{10,... | collective-permute-start | bytes 393224 | tf_op jit(solution)/shard_map/ppermute | solution.py:313
  207.3 11.8 %collective-permute-start.58 = (bf16[1,512,128]{2,1,0:T(8,128)(2,1)S(1)}, bf16[1,512,128]{2,1,0:T(8,128)(2,1)S(1)}, u32[]{:S(2)}, u32[]{:S(2)}) collective-permute-start(bf16[1,512,128]{2,1,0:T(8,128)(2,1)S(1)} %add_convert_fusion), channel_id=1, source_target_pairs={{0,1},{1,0},{2,3},{3,2},{4,5},{5,4},{6,7},{7,6},{8,9},{9,8},{10,11... | collective-permute-start | bytes 393224 | tf_op jit(solution)/shard_map/ppermute | solution.py:313
  210.1 9.0 %collective-permute-start.56 = (bf16[1,512,128]{2,1,0:T(8,128)(2,1)S(1)}, bf16[1,512,128]{2,1,0:T(8,128)(2,1)S(1)}, u32[]{:S(2)}, u32[]{:S(2)}) collective-permute-start(bf16[1,512,128]{2,1,0:T(8,128)(2,1)S(1)} %add_convert_fusion.1), channel_id=1, source_target_pairs={{0,2},{1,3},{2,0},{3,1},{4,6},{5,7},{6,4},{7,5},{8,10},{9,11},{10,... | collective-permute-start | bytes 393224 | tf_op jit(solution)/shard_map/ppermute | solution.py:313
  210.5 12.2 %collective-permute-start.44 = (bf16[1024,128]{1,0:T(8,128)(2,1)S(1)}, bf16[1024,128]{1,0:T(8,128)(2,1)S(1)}, u32[]{:S(2)}, u32[]{:S(2)}) collective-permute-start(bf16[1024,128]{1,0:T(8,128)(2,1)S(1)} %items_1_0.1), channel_id=1, source_target_pairs={{0,4},{1,5},{2,6},{3,7},{4,8},{5,9},{6,10},{7,11},{8,12},{9,13},{1... | collective-permute-start | bytes 786440 | tf_op jit(solution)/shard_map/ppermute | solution.py:323
  212.4 12.4 %collective-permute-start.49 = (bf16[1024,128]{1,0:T(8,128)(2,1)S(1)}, bf16[1024,128]{1,0:T(8,128)(2,1)S(1)}, u32[]{:S(2)}, u32[]{:S(2)}) collective-permute-start(bf16[1024,128]{1,0:T(8,128)(2,1)S(1)} %items_1_1.1), channel_id=1, source_target_pairs={{0,4},{1,5},{2,6},{3,7},{4,8},{5,9},{6,10},{7,11},{8,12},{9,13},{1... | collective-permute-start | bytes 786440 | tf_op jit(solution)/shard_map/ppermute | solution.py:323
  216.9 10.7 %collective-permute-start.54 = (bf16[1024,128]{1,0:T(8,128)(2,1)S(1)}, bf16[1024,128]{1,0:T(8,128)(2,1)S(1)}, u32[]{:S(2)}, u32[]{:S(2)}) collective-permute-start(bf16[1024,128]{1,0:T(8,128)(2,1)S(1)} %items_1_2.1), channel_id=1, source_target_pairs={{0,4},{1,5},{2,6},{3,7},{4,8},{5,9},{6,10},{7,11},{8,12},{9,13},{1... | collective-permute-start | bytes 786440 | tf_op jit(solution)/shard_map/ppermute | solution.py:323
  219.4 11.1 %collective-permute-start.59 = (bf16[1024,128]{1,0:T(8,128)(2,1)S(1)}, bf16[1024,128]{1,0:T(8,128)(2,1)S(1)}, u32[]{:S(2)}, u32[]{:S(2)}) collective-permute-start(bf16[1024,128]{1,0:T(8,128)(2,1)S(1)} %items_1_3.1), channel_id=1, source_target_pairs={{0,4},{1,5},{2,6},{3,7},{4,8},{5,9},{6,10},{7,11},{8,12},{9,13},{1... | collective-permute-start | bytes 786440 | tf_op jit(solution)/shard_map/ppermute | solution.py:323
  (21 other events, 221.7 us)

commit v2 on v1

v2 whole, which is shorter than its diff:
```python
import functools

import jax
import jax.numpy as jnp
from jax import lax
from jax.experimental import pallas as pl
from jax.experimental.pallas import tpu as pltpu
from jax.sharding import PartitionSpec as P

SUB = 2
LEARN = 0.004
GRAM = 256.0
RIDGE = 1.0
CHUNKS = 2
F32 = jnp.float32
BF16 = jnp.bfloat16
BIG = float(jnp.finfo(jnp.bfloat16).max)

ANY = pl.BlockSpec(memory_space=pl.ANY)
HBM = pl.BlockSpec(memory_space=pltpu.HBM)
VMEM = pl.BlockSpec(memory_space=pltpu.VMEM)


def params(mib):
    return pltpu.CompilerParams(vmem_limit_bytes=mib * 1024 * 1024)


def cost(flops, bytes_accessed):
    return pl.CostEstimate(flops=flops, bytes_accessed=bytes_accessed, transcendentals=0)


def over_rows(a, b):
    return lax.dot_general(a, b, (((1,), (1,)), ((), ())), preferred_element_type=F32)


def over_columns(a, b):
    return lax.dot_general(a, b, (((0,), (0,)), ((), ())), preferred_element_type=F32)


def ridge(rank):
    down = lax.broadcasted_iota(jnp.int32, (rank, rank), 0)
    across = lax.broadcasted_iota(jnp.int32, (rank, rank), 1)
    return jnp.where(down == across, RIDGE, 0.0)


def owned(gram, rows, owner):
    full = gram * (GRAM / rows) + ridge(gram.shape[0])
    return jnp.where(owner == lax.axis_index("grp"), full, 0.0).astype(BF16)


def without(members, bit):
    return [r for r in range(members) if not r & bit]


def tile_kernel(epoch, chunk, members, shard_tiles, tile, pieces, first, *refs):
    row_hbm, col_hbm, count_hbm, owner_hbm, ratings, mask_hbm, users = refs[:7]
    sources = refs[7:7 + pieces]
    refs = refs[7 + pieces:]
    if not first:
        grad_in, gram_in = refs[:2]
        refs = refs[2:]
    elif epoch > 0:
        own_in = refs[0]
        refs = refs[1:]
    send_a, keep_a, send_b, keep_b, grad_user, gram_item = refs[:6]
    (row_ref, col_ref, count_ref, owner_ref, mask, users_f, user_bf, user_t, items, items_f, parts,
     held, errors, slots, slot_row, slot_place, sem_tile, sem_item, sem_small) = refs[6:]

    me = lax.axis_index("grp")
    chunk_tiles = shard_tiles // CHUNKS
    rows = chunk_tiles * tile
    half = rows // 2
    bits_tile = chunk_tiles.bit_length() - 1
    bits_shard = shard_tiles.bit_length() - 1

    small = [
        pltpu.make_async_copy(src, dst, sem_small.at[i])
        for i, (src, dst) in enumerate(
            [(row_hbm, row_ref), (col_hbm, col_ref), (count_hbm, count_ref), (owner_hbm, owner_ref),
             (mask_hbm.at[epoch, 0, 0], mask), (users, users_f)]
        )
    ]
    for copy in small:
        copy.start()
    if not first:
        prev = pltpu.make_async_copy(grad_in, grad_user, sem_small.at[6])
        prev.start()
    copies = []
    if epoch == 0:
        for r in range(members):
            start = pl.multiple_of((me ^ r) * (shard_tiles * tile) + chunk * rows, rows)
            copies.append(
                pltpu.make_async_copy(
                    sources[0].at[pl.ds(start, rows)], items_f.at[pl.ds(r * rows, rows)], sem_item.at[r]
                )
            )
    else:
        at = 0
        for i, source in enumerate(sources):
            width = source.shape[1]
            copies.append(
                pltpu.make_async_copy(source, items.at[:, pl.ds(at, width)], sem_item.at[i])
            )
            at += width
    for copy in copies:
        copy.start()
    for copy in small[:4]:
        copy.wait()

    count = count_ref[epoch, 0, 0]

    def pick(t, found):
        col = col_ref[epoch, 0, 0, t]
        slots[found] = t
        slot_row[found] = row_ref[epoch, 0, 0, t]
        slot_place[found] = ((col >> bits_shard) ^ me) * chunk_tiles + (col & (chunk_tiles - 1))
        here = ((col >> bits_tile) & (CHUNKS - 1)) == chunk
        return found + jnp.where(here & (t < count), 1, 0).astype(jnp.int32)

    total = lax.fori_loop(0, col_ref.shape[3], pick, jnp.int32(0), unroll=8)

    def fetch(i):
        return pltpu.make_async_copy(ratings.at[epoch, 0, 0, slots[i]], held.at[i], sem_tile.at[i])

    def begin(i, _):
        fetch(i).start()
        return 0

    lax.fori_loop(0, total, begin, 0)

    parts[...] = jnp.zeros_like(parts)
    if first:
        grad_user[...] = jnp.zeros_like(grad_user)
    for copy in small[4:]:
        copy.wait()

    def user_tile(j, _):
        spot = pl.ds(pl.multiple_of(j * tile, tile), tile)
        part = users_f[spot]
        user_bf[spot] = part.astype(BF16)
        user_t[:, spot] = part.T
        return 0

    lax.fori_loop(0, users_f.shape[0] // tile, user_tile, 0, unroll=2)

    def item_tile(j, _):
        spot = pl.ds(pl.multiple_of(j * tile, tile), tile)
        items[:, spot] = items_f[spot].T.astype(BF16)
        return 0

    for i, copy in enumerate(copies):
        copy.wait()
        if epoch == 0:
            lax.fori_loop(i * chunk_tiles, (i + 1) * chunk_tiles, item_tile, 0, unroll=2)
    if not first:
        prev.wait()

    def spots(i):
        row = pl.multiple_of(slot_row[i] * tile, tile)
        place = pl.multiple_of(slot_place[i] * tile, tile)
        return pl.ds(row, tile), pl.ds(place, tile)

    def front(j):
        buffer = 2 * (j & 1)
        for k in range(2):
            i = 2 * j + k

            @pl.when(i < total)
            def _():
                fetch(i).wait()

        for k in range(2):
            i = jnp.minimum(2 * j + k, total - 1)
            row, place = spots(i)
            predicted = jnp.dot(user_bf[row], items[:, place], preferred_element_type=F32)
            error = (predicted - held[i].astype(F32)).astype(BF16)
            errors[buffer + k] = jnp.clip(error, -BIG, BIG)

    def back(j):
        buffer = 2 * (j & 1)
        adds = []
        for k in range(2):
            valid = 2 * j + k < total
            i = jnp.minimum(2 * j + k, total - 1)
            row, place = spots(i)
            weight = mask[pl.ds(slots[i], 1), :].astype(F32)
            weight = jnp.where(valid, weight, 0.0)
            error = errors[buffer + k]
            user_add = over_rows(items[:, place], error)
            item_add = jnp.dot(
                (user_t[:, row] * weight).astype(BF16), error, preferred_element_type=F32
            )
            adds.append((row, place, jnp.where(weight > 0.5, user_add, 0.0), item_add))
        for row, place, user_add, item_add in adds:
            grad_user[:, row] += user_add
            parts[:, place] += item_add

    pairs = (total + 1) // 2

    @pl.when(total > 0)
    def _():
        front(0)

    def step(j, _):
        front(jnp.minimum(j + 1, pairs))
        back(j)
        return 0

    lax.fori_loop(0, pairs, step, 0)

    for bit, send, keep, start, width in (
        (1, send_a, keep_a, 0, half), (members // 2, send_b, keep_b, half, rows - half)
    ):
        for k, r in enumerate(without(members, bit)):
            keep[:, k * width:(k + 1) * width] = parts[:, pl.ds(r * rows + start, width)].astype(BF16)
            r = r | bit
            send[:, k * width:(k + 1) * width] = parts[:, pl.ds(r * rows + start, width)].astype(BF16)
    gram = over_rows(items[...], items[...])
    if first:
        gram_item[...] = gram
        if epoch == 0:
            own = owned(
                over_columns(user_bf[...], user_bf[...]), users_f.shape[0], owner_ref[epoch, 0]
            )
        else:
            own = own_in[...]
        send_a[:, members // 2 * half:] = own
    else:
        gram_item[...] = gram_in[...] + gram


def tile_call(epoch, chunk, members, scalars, ratings, row_mask, users, sources, carried, own):
    tile = ratings.shape[-1]
    slots = ratings.shape[3]
    user_rows, rank = users.shape
    first = chunk == 0
    if epoch == 0:
        block_rows = sources[0].shape[0]
    else:
        block_rows = sum(s.shape[1] for s in sources) * CHUNKS
    shard_tiles = block_rows // members // tile
    rows = shard_tiles // CHUNKS * tile
    half = rows // 2
    sd = jax.ShapeDtypeStruct
    wide_a, wide_b = members // 2 * half, members // 2 * (rows - half)
    extra = rank if first else 0
    out_shape = [
        sd((rank, wide_a + extra), BF16), sd((rank, wide_a), BF16),
        sd((rank, wide_b), BF16), sd((rank, wide_b), BF16),
        sd((rank, user_rows), F32), sd((rank, rank), F32),
    ]
    in_specs = [HBM] * 7 + [HBM if epoch == 0 else ANY] * len(sources)
    operands = [*scalars, ratings, row_mask, users, *sources]
    if not first:
        in_specs += [ANY, VMEM]
        operands += list(carried)
    elif epoch > 0:
        in_specs += [VMEM]
        operands += [own]
    return pl.pallas_call(
        functools.partial(
            tile_kernel, epoch, chunk, members, shard_tiles, tile, len(sources), first
        ),
        out_shape=out_shape,
        in_specs=in_specs,
        out_specs=[VMEM] * len(out_shape),
        scratch_shapes=[
            *[pltpu.SMEM(s.shape, jnp.int32) for s in scalars],
            pltpu.VMEM((slots, tile), jnp.int32),
            pltpu.VMEM((user_rows, rank), F32),
            pltpu.VMEM((user_rows, rank), BF16),
            pltpu.VMEM((rank, user_rows), F32),
            pltpu.VMEM((rank, members * rows), BF16),
            pltpu.VMEM((members * rows if epoch == 0 else 8, rank), F32),
            pltpu.VMEM((rank, members * rows), F32),
            pltpu.VMEM((slots, tile, tile), BF16),
            pltpu.VMEM((4, tile, tile), BF16),
            *[pltpu.SMEM((slots + 1,), jnp.int32)] * 3,
            pltpu.SemaphoreType.DMA((slots,)),
            pltpu.SemaphoreType.DMA((max(members, len(sources)),)),
            pltpu.SemaphoreType.DMA((7,)),
        ],
        compiler_params=params(44),
        cost_estimate=cost(1 << 20, 1 << 16),
        name=f"tiles_{epoch}_{chunk}",
    )(*operands)


def user_kernel(epoch, block_rows, owner_ref, users, grad, gram, *outs):
    full = gram[...] * (GRAM / block_rows) + ridge(users.shape[1])
    pull = jnp.dot(users[...], full, precision=lax.Precision.HIGHEST, preferred_element_type=F32)
    new = users[...] - LEARN * (grad[...].T + pull)
    outs[0][...] = new
    if len(outs) > 1:
        new = new.astype(BF16)
        outs[1][...] = owned(over_columns(new, new), users.shape[0], owner_ref[epoch + 1, 0])


def user_call(epoch, block_rows, owner_list, users, grad, gram):
    rank = users.shape[1]
    out_shape = [jax.ShapeDtypeStruct(users.shape, F32)]
    if epoch + 1 < SUB:
        out_shape.append(jax.ShapeDtypeStruct((rank, rank), BF16))
    return pl.pallas_call(
        functools.partial(user_kernel, epoch, block_rows),
        out_shape=out_shape,
        in_specs=[pl.BlockSpec(memory_space=pltpu.SMEM), VMEM, VMEM, VMEM],
        out_specs=[VMEM] * len(out_shape),
        compiler_params=params(44),
        cost_estimate=cost(1 << 20, 1 << 16),
        name=f"users_{epoch}",
    )(owner_list, users, grad, gram)


def summed(refs, names, r, width):
    total = None
    for ref, order in zip(refs, names):
        k = order.index(r)
        term = ref[:, k * width:(k + 1) * width].astype(F32)
        total = term if total is None else total + term
    return total


def mid_kernel(paths, grams, *refs):
    at = 0
    outs = refs[sum(len(names) for names, _, _ in paths) + grams:]
    gram_refs = refs[len(refs) - len(paths) - grams:len(refs) - len(paths)]
    for (names, going, width), out in zip(paths, outs):
        terms = refs[at:at + len(names)]
        at += len(names)
        for k, r in enumerate(going):
            out[:, k * width:(k + 1) * width] = summed(terms, names, r, width).astype(BF16)
    if grams:
        rank = outs[0].shape[0]
        total = gram_refs[0][:, gram_refs[0].shape[1] - rank:].astype(F32)
        for ref in gram_refs[1:]:
            total += ref[:, ref.shape[1] - rank:].astype(F32)
        outs[0][:, outs[0].shape[1] - rank:] = total.astype(BF16)


def mid_call(epoch, chunk, step, paths, grams):
    rank = paths[0][0][0][0].shape[0]
    specs, operands, out_shape = [], [], []
    for terms, going, width in paths:
        specs.append(([names for _, names in terms], going, width))
        operands += [array for array, _ in terms]
        extra = rank if grams and not out_shape else 0
        out_shape.append(jax.ShapeDtypeStruct((rank, len(going) * width + extra), BF16))
    operands += grams
    return pl.pallas_call(
        functools.partial(mid_kernel, specs, len(grams)),
        out_shape=out_shape,
        in_specs=[VMEM] * len(operands),
        out_specs=[VMEM] * len(out_shape),
        compiler_params=params(44),
        cost_estimate=cost(1 << 16, 1 << 16),
        name=f"mid_{epoch}_{chunk}_{step}",
    )(*operands)


def item_kernel(epoch, chunk, count, shard_rows, width, grams, items, *refs):
    terms_a, terms_b = refs[:count], refs[count:2 * count]
    gram_refs = refs[2 * count:2 * count + grams]
    refs = refs[2 * count + grams:]
    out = refs[0]
    rank = gram_refs[0].shape[0]
    gram = gram_refs[0][:, gram_refs[0].shape[1] - rank:]
    for ref in gram_refs[1:]:
        gram = (gram.astype(F32) + ref[:, ref.shape[1] - rank:].astype(F32)).astype(BF16)
    if grams > 1:
        refs[1][...] = gram
    rows = shard_rows // CHUNKS
    zero = [[0]] * count
    grad = jnp.concatenate(
        [summed(terms_a, zero, 0, width), summed(terms_b, zero, 0, rows - width)], axis=1
    )
    if epoch == 0:
        held, sem = refs[-2:]
        start = pl.multiple_of(lax.axis_index("grp") * shard_rows + chunk * rows, rows)
        copy = pltpu.make_async_copy(items.at[pl.ds(start, rows)], held, sem)
        copy.start()
        copy.wait()
        old = held[...]
        high = old.astype(BF16)
        low = (old - high.astype(F32)).astype(BF16)
        pull = jnp.dot(high, gram, preferred_element_type=F32)
        pull += jnp.dot(low, gram, preferred_element_type=F32)
        out[...] = (old - LEARN * (grad.T + pull)).T.astype(BF16)
    else:
        pull = over_columns(gram, items[...])
        out[...] = (items[...].astype(F32) - LEARN * (grad + pull)).T.astype(BF16)


def item_call(epoch, chunk, shard_rows, items, terms_a, terms_b, grams):
    rank = grams[0].shape[0]
    rows = shard_rows // CHUNKS
    last = epoch + 1 == SUB
    out_shape = [jax.ShapeDtypeStruct((rows, rank) if last else (rank, rows), BF16)]
    if len(grams) > 1:
        out_shape.append(jax.ShapeDtypeStruct((rank, rank), BF16))
    scratch = [pltpu.VMEM((rows, rank), F32), pltpu.SemaphoreType.DMA] if epoch == 0 else []
    out = pl.pallas_call(
        functools.partial(
            item_kernel, epoch, chunk, len(terms_a), shard_rows, rows // 2, len(grams)
        ),
        out_shape=out_shape,
        in_specs=[HBM if epoch == 0 else VMEM] + [VMEM] * (2 * len(terms_a) + len(grams)),
        out_specs=[VMEM] * len(out_shape),
        scratch_shapes=scratch,
        compiler_params=params(44),
        cost_estimate=cost(1 << 16, 1 << 16),
        name=f"items_{epoch}_{chunk}",
    )(items, *terms_a, *terms_b, *grams)
    return out[0], out[-1]


def swapped(value, bit):
    length = lax.axis_size("grp")
    return lax.ppermute(value, "grp", [(i, i ^ bit) for i in range(length)])


def moved(value, bit):
    length, blocks = lax.axis_size("grp"), lax.axis_size("blk")
    pairs = [
        (b * length + i, (b + 1) % blocks * length + (i ^ bit))
        for b in range(blocks)
        for i in range(length)
    ]
    return lax.ppermute(value, ("blk", "grp"), pairs)


def scattered(epoch, chunk, out, members, width_a, width_b):
    send_a, keep_a, send_b, keep_b = out[:4]
    bits = [1 << i for i in range(members.bit_length() - 1)]
    orders = (bits, bits[::-1])
    widths = (width_a, width_b)
    sends = [send_a, send_b]
    names = [without(members, order[0]) for order in orders]
    terms = [[(keep_a, names[0])], [(keep_b, names[1])]]
    grams = [send_a] if chunk == 0 else []
    for step in range(len(bits)):
        for p in range(2):
            arrived = swapped(sends[p], orders[p][step])
            terms[p].append((arrived, names[p]))
            if p == 0 and grams:
                grams.append(arrived)
        if step + 1 == len(bits):
            break
        paths = []
        for p in range(2):
            bit = orders[p][step + 1]
            paths.append((terms[p], [r for r in names[p] if r & bit], widths[p]))
            names[p] = [r for r in names[p] if not r & bit]
        sends = mid_call(epoch, chunk, step, paths, grams)
    return [a for a, _ in terms[0]], [a for a, _ in terms[1]], grams


def gathered(shard):
    length = lax.axis_size("grp")
    half = shard.shape[1] // 2
    known = {0: [moved(shard, 0)]}
    bit = 1
    while bit < length:
        known[bit] = [moved(shard, bit)]
        bit *= 2

    def cut(r, lower):
        pieces = known[r]
        if len(pieces) == 1:
            return pieces[0][:, half:] if lower else pieces[0][:, :half]
        return pieces[1] if lower else pieces[0]

    for r in range(1, length):
        if r in known:
            continue
        low = r & -r
        high = 1 << (r.bit_length() - 1)
        known[r] = [swapped(cut(r ^ high, False), high), swapped(cut(r ^ low, True), low)]
    return [piece for r in range(length) for piece in known[r]]


def local(ratings, row_index, col_index, row_mask, counts, owner_list, user_factors, item_factors):
    members = lax.axis_size("grp")
    block_rows = item_factors.shape[0]
    shard_rows = block_rows // members
    rows = shard_rows // CHUNKS
    scalars = (row_index, col_index, counts, owner_list)
    users = user_factors
    chunks = [[item_factors]] * CHUNKS
    own_gram = None
    for epoch in range(SUB):
        carried = None
        outs = []
        for c in range(CHUNKS):
            out = tile_call(
                epoch, c, members, scalars, ratings, row_mask, users, chunks[c], carried, own_gram
            )
            carried = out[4:6]
            outs.append(out)
        new_users = user_call(epoch, block_rows, owner_list, users, *carried)
        shards = []
        grams = None
        for c in range(CHUNKS):
            terms_a, terms_b, found = scattered(
                epoch, c, outs[c], members, rows // 2, rows - rows // 2
            )
            shard, gram = item_call(
                epoch, c, shard_rows, chunks[c][0], terms_a, terms_b, found or grams
            )
            if found:
                grams = [gram]
            shards.append(shard)
        users = new_users[0]
        if epoch + 1 < SUB:
            own_gram = new_users[1]
            chunks = [gathered(shard) for shard in shards]
        else:
            chunks = [moved(shard, 0) for shard in shards]
    return users, jnp.concatenate(chunks, axis=0).astype(F32)


def solution(mesh):
    in_specs = (
        P(None, "blk", "grp", None, None, None),
        P(None, "blk", "grp", None),
        P(None, "blk", "grp", None),
        P(None, "blk", "grp", None, None),
        P(None, "blk", "grp"),
        P(None, "blk"),
        P(("blk", "grp"), None),
        P("blk", None),
    )
    out_specs = (P(("blk", "grp"), None), P(("blk", "grp"), None))
    return jax.shard_map(local, mesh=mesh, in_specs=in_specs, out_specs=out_specs, check_vma=False)
```

time: 234 us -> 165 us (0.71)
  Pallas kernels: 88.2 us -> 53.4 us
  starting transfers between devices: 69.3 us -> 37.4 us
  waiting for transfers between devices: 56.8 us -> 66.6 us
  local copies, waits for them, and re-layouts: 14.2 us -> 5.06 us
    pallas_call x8 -> x4, Pallas kernels: 81.3 us -> 43.7 us  [tile_call(): pl.pallas_call(functools.partial(tile_kernel, epoch, chunk, members, shar...]
    ppermute x44 -> x20, starting transfers between devices: 57.2 us -> 31.1 us  [swapped(): return lax.ppermute(value, 'grp', [(i, i ^ bit) for i in range(length)])]
    ppermute x16 -> x8, waiting for transfers between devices: 22.2 us -> 31.5 us  [moved(): return lax.ppermute(value, ('blk', 'grp'), pairs)]
    unnamed x20 -> x18, local copies, waits for them, and re-layouts: 14.1 us -> 4.99 us
    ppermute x16 -> x8, starting transfers between devices: 12.1 us -> 6.31 us  [moved(): return lax.ppermute(value, ('blk', 'grp'), pairs)]
    pallas_call x8 -> x4, Pallas kernels: 2.47 us -> 4.72 us  [item_call(): pl.pallas_call(functools.partial(item_kernel, epoch, chunk, len(terms_a),...]
    ppermute x44 -> x20, waiting for transfers between devices: 34.6 us -> 35.1 us  [swapped(): return lax.ppermute(value, 'grp', [(i, i ^ bit) for i in range(length)])]
  transfers between devices with their start and end apart: 60 -> 28, of which waited for: 24 -> 17; matrix products, arithmetic and copies ran while one was open for 0% -> 0% of each run, Pallas kernels for 34% -> 26%
where the time goes in v2:
time: 165 us
  waiting for transfers between devices  66.6 us (40%)
  Pallas kernels  53.4 us (32%)
  starting transfers between devices  37.4 us (23%)
  local copies, waits for them, and re-layouts  5.06 us (3%)
    pallas_call x4, Pallas kernels, tile_call(): pl.pallas_call(functools.partial(tile_kernel, epoch, chunk, members, shar...  43.7 us
    ppermute x20, waiting for transfers between devices, swapped(): return lax.ppermute(value, 'grp', [(i, i ^ bit) for i in range(length)])  35.1 us
    ppermute x8, waiting for transfers between devices, moved(): return lax.ppermute(value, ('blk', 'grp'), pairs)  31.5 us
    ppermute x20, starting transfers between devices, swapped(): return lax.ppermute(value, 'grp', [(i, i ^ bit) for i in range(length)])  31.1 us
    ppermute x8, starting transfers between devices, moved(): return lax.ppermute(value, ('blk', 'grp'), pairs)  6.31 us
    unnamed x18, local copies, waits for them, and re-layouts  4.99 us
    pallas_call x4, Pallas kernels, item_call(): pl.pallas_call(functools.partial(item_kernel, epoch, chunk, len(terms_a),...  4.72 us
    pallas_call x2, Pallas kernels, user_call(): pl.pallas_call(functools.partial(user_kernel, epoch, block_rows), out_sha...  4.44 us
  transfers between devices with their start and end apart: 28, of which 17 were waited for; matrix products, arithmetic and copies ran while one was open for 0% of the time, Pallas kernels for 26%

profile of v2, /device:TPU:0, one launch (start us, length us, event | category | flops | bytes accessed | tf_op | source)
XLA Modules:
  0.0 164.8 jit_solution(1945957309301266278)
XLA Ops:
  0.6 0.7 copy.19.refs_3_.owner_ref
  1.4 0.7 copy.12.refs_2_
  2.1 1.2 copy-done
  3.3 0.9 copy-done.2
  4.2 0.7 copy-done.4
  4.9 0.7 copy-done.6
  5.6 9.3 %tiles_0_0.1 = (bf16[128,2176]{1,0:T(8,128)(2,1)S(1)}, bf16[128,2048]{1,0:T(8,128)(2,1)S(1)}, bf16[128,2048]{1,0:T(8,128)(2,1)S(1)}, bf16[128,2048]{1,0:T(8,128)...) custom-call(s32[2,1,1,64]{3,2,1,0:T(1,128)S(1)} %copy-done.4, s32[2,1,1,64]{3,2,1,0:T(1,128)S(1)} %copy-done.6, ...), custom_call_target="tpu_custom_call" | custom-call | flops 1048576 | bytes 65536 | tf_op jit(solution)/shard_map/tiles_0_0/pallas_call | solution.py:260
  14.9 2.5 %collective-permute-start.4 = (bf16[128,2176]{1,0:T(8,128)(2,1)S(1)}, bf16[128,2176]{1,0:T(8,128)(2,1)S(1)}, u32[]{:S(2)}, u32[]{:S(2)}) collective-permute-start(bf16[128,2176]{1,0:T(8,128)(2,1)S(1)} %get-tuple-element.52.refs_4_.refs_6_), channel_id=1, source_target_pairs={{0,1},{1,0},{2,3},{3,2},{4,5},{5,4},{6,7},{7,6},{8,9},{9,8},{10,11... | collective-permute-start | bytes 1671176 | tf_op jit(solution)/shard_map/ppermute | solution.py:419
  17.4 7.8 %collective-permute-start.5 = (bf16[128,2048]{1,0:T(8,128)(2,1)S(1)}, bf16[128,2048]{1,0:T(8,128)(2,1)S(1)}, u32[]{:S(2)}, u32[]{:S(2)}) collective-permute-start(bf16[128,2048]{1,0:T(8,128)(2,1)S(1)} %get-tuple-element.54), channel_id=1, source_target_pairs={{0,2},{1,3},{2,0},{3,1},{4,6},{5,7},{6,4},{7,5},{8,10},{9,11},{10,... | collective-permute-start | bytes 1572872 | tf_op jit(solution)/shard_map/ppermute | solution.py:419
  25.1 11.2 %tiles_0_1.1 = (bf16[128,2048]{1,0:T(8,128)(2,1)S(1)}, bf16[128,2048]{1,0:T(8,128)(2,1)S(1)}, bf16[128,2048]{1,0:T(8,128)(2,1)S(1)}, bf16[128,2048]{1,0:T(8,128)...) custom-call(s32[2,1,1,64]{3,2,1,0:T(1,128)S(1)} %copy-done.4, s32[2,1,1,64]{3,2,1,0:T(1,128)S(1)} %copy-done.6, ...), custom_call_target="tpu_custom_call" | custom-call | flops 1048576 | bytes 65536 | tf_op jit(solution)/shard_map/tiles_0_1/pallas_call | solution.py:260
  36.7 2.1 %collective-permute-start.6 = (bf16[128,1152]{1,0:T(8,128)(2,1)S(1)}, bf16[128,1152]{1,0:T(8,128)(2,1)S(1)}, u32[]{:S(2)}, u32[]{:S(2)}) collective-permute-start(bf16[128,1152]{1,0:T(8,128)(2,1)S(1)} %get-tuple-element.55), channel_id=1, source_target_pairs={{0,2},{1,3},{2,0},{3,1},{4,6},{5,7},{6,4},{7,5},{8,10},{9,11},{10,... | collective-permute-start | bytes 884744 | tf_op jit(solution)/shard_map/ppermute | solution.py:419
  38.8 1.9 %collective-permute-start.7 = (bf16[128,1024]{1,0:T(8,128)(2,1)S(1)}, bf16[128,1024]{1,0:T(8,128)(2,1)S(1)}, u32[]{:S(2)}, u32[]{:S(2)}) collective-permute-start(bf16[128,1024]{1,0:T(8,128)(2,1)S(1)} %get-tuple-element.56), channel_id=1, source_target_pairs={{0,1},{1,0},{2,3},{3,2},{4,5},{5,4},{6,7},{7,6},{8,9},{9,8},{10,11... | collective-permute-start | bytes 786440 | tf_op jit(solution)/shard_map/ppermute | solution.py:419
  40.7 10.5 %collective-permute-done.refs_1_ = bf16[128,2048]{1,0:T(8,128)(2,1)S(1)} collective-permute-done((bf16[128,2048]{1,0:T(8,128)(2,1)S(1)}, bf16[128,2048]{1,0:T(8,128)(2,1)S(1)}, u32[]{:S(2)}, u32[]{:S(2)}) %collective-permute-start) | collective-permute-done | bytes 524320 | tf_op jit(solution)/shard_map/ppermute | solution.py:419
  51.5 2.1 %collective-permute-start.3 = (bf16[128,1024]{1,0:T(8,128)(2,1)S(1)}, bf16[128,1024]{1,0:T(8,128)(2,1)S(1)}, u32[]{:S(2)}, u32[]{:S(2)}) collective-permute-start(bf16[128,1024]{1,0:T(8,128)(2,1)S(1)} %get-tuple-element.50), channel_id=1, source_target_pairs={{0,1},{1,0},{2,3},{3,2},{4,5},{5,4},{6,7},{7,6},{8,9},{9,8},{10,11... | collective-permute-start | bytes 786440 | tf_op jit(solution)/shard_map/ppermute | solution.py:419
  53.6 2.5 %collective-permute-done.7.refs_5_ = bf16[128,1024]{1,0:T(8,128)(2,1)S(1)} collective-permute-done((bf16[128,1024]{1,0:T(8,128)(2,1)S(1)}, bf16[128,1024]{1,0:T(8,128)(2,1)S(1)}, u32[]{:S(2)}, u32[]{:S(2)}) %collective-permute-start.7) | collective-permute-done | bytes 262176 | tf_op jit(solution)/shard_map/ppermute | solution.py:419
  56.1 1.6 collective-permute-done.6.refs_2_.refs_8_
  57.7 1.8 %items_0_0.1 = (bf16[128,2048]{1,0:T(8,128)(2,1)S(1)}, bf16[128,128]{1,0:T(8,128)(2,1)S(1)}) custom-call(f32[16384,128]{1,0:T(8,128)} %items.3, bf16[128,2048]{1,0:T(8,128)(2,1)S(1)} %get-tuple-element.51.refs_0_, bf16[128,2176]{1,0:T(8,128)(2,1)S(1)} %collective-permute-done.4.refs_1_.refs_5_.refs_7_, ...), custom_call_target="tpu_custom_call" | custom-call | flops 65536 | bytes 65536 | tf_op jit(solution)/shard_map/items_0_0/pallas_call | solution.py:402
  59.5 1.3 collective-permute-start.15
  60.8 2.2 %collective-permute-done.2.refs_2_ = bf16[128,1024]{1,0:T(8,128)(2,1)S(1)} collective-permute-done((bf16[128,1024]{1,0:T(8,128)(2,1)S(1)}, bf16[128,1024]{1,0:T(8,128)(2,1)S(1)}, u32[]{:S(2)}, u32[]{:S(2)}) %collective-permute-start.2) | collective-permute-done | bytes 262176 | tf_op jit(solution)/shard_map/ppermute | solution.py:419
  63.0 1.8 %items_0_1.1 = bf16[128,2048]{1,0:T(8,128)(2,1)S(1)} custom-call(f32[16384,128]{1,0:T(8,128)} %items.3, bf16[128,2048]{1,0:T(8,128)(2,1)S(1)} %get-tuple-element.45.refs_0_, bf16[128,2048]{1,0:T(8,128)(2,1)S(1)} %collective-permute-done.refs_1_, bf16[128,1024]{1,0:T(8,128)(2,1)S(1)} %collective-permute-done.2.refs_2_, ...), custom_call_target="tpu_custom_call" | custom-call | flops 65536 | bytes 65536 | tf_op jit(solution)/shard_map/items_0_1/pallas_call | solution.py:402
  64.8 2.0 %collective-permute-start.9 = (bf16[128,2048]{1,0:T(8,128)(2,1)S(1)}, bf16[128,2048]{1,0:T(8,128)(2,1)S(1)}, u32[]{:S(2)}, u32[]{:S(2)}) collective-permute-start(bf16[128,2048]{1,0:T(8,128)(2,1)S(1)} %items_0_1.1), channel_id=1, source_target_pairs={{0,5},{1,4},{2,7},{3,6},{4,9},{5,8},{6,11},{7,10},{8,13},{9,12},{1... | collective-permute-start | bytes 1572872 | tf_op jit(solution)/shard_map/ppermute | solution.py:429
  67.1 4.7 %collective-permute-done.14.refs_8_ = bf16[128,2048]{1,0:T(8,128)(2,1)S(1)} collective-permute-done((bf16[128,2048]{1,0:T(8,128)(2,1)S(1)}, bf16[128,2048]{1,0:T(8,128)(2,1)S(1)}, u32[]{:S(2)}, u32[]{:S(2)}) %collective-permute-start.14) | collective-permute-done | bytes 524320 | tf_op jit(solution)/shard_map/ppermute | solution.py:429
  71.8 2.6 %collective-permute-start.8 = (bf16[128,2048]{1,0:T(8,128)(2,1)S(1)}, bf16[128,2048]{1,0:T(8,128)(2,1)S(1)}, u32[]{:S(2)}, u32[]{:S(2)}) collective-permute-start(bf16[128,2048]{1,0:T(8,128)(2,1)S(1)} %items_0_1.1), channel_id=1, source_target_pairs={{0,4},{1,5},{2,6},{3,7},{4,8},{5,9},{6,10},{7,11},{8,12},{9,13},{1... | collective-permute-start | bytes 1572872 | tf_op jit(solution)/shard_map/ppermute | solution.py:429
  74.4 2.1 %collective-permute-done.15.refs_9_ = bf16[128,2048]{1,0:T(8,128)(2,1)S(1)} collective-permute-done((bf16[128,2048]{1,0:T(8,128)(2,1)S(1)}, bf16[128,2048]{1,0:T(8,128)(2,1)S(1)}, u32[]{:S(2)}, u32[]{:S(2)}) %collective-permute-start.15) | collective-permute-done | bytes 524320 | tf_op jit(solution)/shard_map/ppermute | solution.py:429
  76.5 2.1 %collective-permute-start.16 = (bf16[128,1024]{1,0:T(8,128)(2,1)S(1)}, bf16[128,1024]{1,0:T(8,128)(2,1)S(1)}, u32[]{:S(2)}, u32[]{:S(2)}) collective-permute-start(bf16[128,1024]{1,0:T(8,128)(2,1)S(1)} %slice.18), channel_id=1, source_target_pairs={{0,2},{1,3},{2,0},{3,1},{4,6},{5,7},{6,4},{7,5},{8,10},{9,11},{10,... | collective-permute-start | bytes 786440 | tf_op jit(solution)/shard_map/ppermute | solution.py:419
  78.6 4.5 %collective-permute-done.9.refs_8_ = bf16[128,2048]{1,0:T(8,128)(2,1)S(1)} collective-permute-done((bf16[128,2048]{1,0:T(8,128)(2,1)S(1)}, bf16[128,2048]{1,0:T(8,128)(2,1)S(1)}, u32[]{:S(2)}, u32[]{:S(2)}) %collective-permute-start.9) | collective-permute-done | bytes 524320 | tf_op jit(solution)/shard_map/ppermute | solution.py:429
  83.1 2.0 %collective-permute-start.17 = (bf16[128,1024]{1,0:T(8,128)(2,1)S(1)}, bf16[128,1024]{1,0:T(8,128)(2,1)S(1)}, u32[]{:S(2)}, u32[]{:S(2)}) collective-permute-start(bf16[128,1024]{1,0:T(8,128)(2,1)S(1)} %slice.19), channel_id=1, source_target_pairs={{0,1},{1,0},{2,3},{3,2},{4,5},{5,4},{6,7},{7,6},{8,9},{9,8},{10,11... | collective-permute-start | bytes 786440 | tf_op jit(solution)/shard_map/ppermute | solution.py:419
  85.1 2.7 %collective-permute-done.10.refs_9_ = bf16[128,2048]{1,0:T(8,128)(2,1)S(1)} collective-permute-done((bf16[128,2048]{1,0:T(8,128)(2,1)S(1)}, bf16[128,2048]{1,0:T(8,128)(2,1)S(1)}, u32[]{:S(2)}, u32[]{:S(2)}) %collective-permute-start.10) | collective-permute-done | bytes 524320 | tf_op jit(solution)/shard_map/ppermute | solution.py:429
  87.9 2.1 %collective-permute-start.11 = (bf16[128,1024]{1,0:T(8,128)(2,1)S(1)}, bf16[128,1024]{1,0:T(8,128)(2,1)S(1)}, u32[]{:S(2)}, u32[]{:S(2)}) collective-permute-start(bf16[128,1024]{1,0:T(8,128)(2,1)S(1)} %slice.16), channel_id=1, source_target_pairs={{0,2},{1,3},{2,0},{3,1},{4,6},{5,7},{6,4},{7,5},{8,10},{9,11},{10,... | collective-permute-start | bytes 786440 | tf_op jit(solution)/shard_map/ppermute | solution.py:419
  89.9 4.1 %collective-permute-done.13.refs_7_.items = bf16[128,2048]{1,0:T(8,128)(2,1)S(1)} collective-permute-done((bf16[128,2048]{1,0:T(8,128)(2,1)S(1)}, bf16[128,2048]{1,0:T(8,128)(2,1)S(1)}, u32[]{:S(2)}, u32[]{:S(2)}) %collective-permute-start.13) | collective-permute-done | bytes 524320 | tf_op jit(solution)/shard_map/ppermute | solution.py:429
  94.1 1.9 %users_0.1 = (f32[2048,128]{1,0:T(8,128)S(1)}, bf16[128,128]{1,0:T(8,128)(2,1)S(1)}) custom-call(s32[2,1]{1,0:T(2,128)S(1)} %copy.19.refs_3_.owner_ref, f32[2048,128]{1,0:T(8,128)S(1)} %copy-done.1, f32[128,2048]{1,0:T(8,128)S(1)} %get-tuple-element.42.grad, f32[128,128]{1,0:T(8,128)S(1)} %get-tuple-element.43.gram), custom_call_target="tpu_custom_call" | custom-call | flops 1048576 | bytes 65536 | tf_op jit(solution)/shard_map/users_0/pallas_call | solution.py:304
  96.0 11.5 %tiles_1_0.1 = (bf16[128,2176]{1,0:T(8,128)(2,1)S(1)}, bf16[128,2048]{1,0:T(8,128)(2,1)S(1)}, bf16[128,2048]{1,0:T(8,128)(2,1)S(1)}, bf16[128,2048]{1,0:T(8,128)...) custom-call(s32[2,1,1,64]{3,2,1,0:T(1,128)S(1)} %copy-done.5, s32[2,1,1,64]{3,2,1,0:T(1,128)S(1)} %copy-done.7, ...), custom_call_target="tpu_custom_call" | custom-call | flops 1048576 | bytes 65536 | tf_op jit(solution)/shard_map/tiles_1_0/pallas_call | solution.py:260
  107.6 3.0 %collective-permute-start.19 = (bf16[128,2048]{1,0:T(8,128)(2,1)S(1)}, bf16[128,2048]{1,0:T(8,128)(2,1)S(1)}, u32[]{:S(2)}, u32[]{:S(2)}) collective-permute-start(bf16[128,2048]{1,0:T(8,128)(2,1)S(1)} %get-tuple-element.67), channel_id=1, source_target_pairs={{0,2},{1,3},{2,0},{3,1},{4,6},{5,7},{6,4},{7,5},{8,10},{9,11},{10,... | collective-permute-start | bytes 1572872 | tf_op jit(solution)/shard_map/ppermute | solution.py:419
  110.6 11.8 %tiles_1_1.1 = (bf16[128,2048]{1,0:T(8,128)(2,1)S(1)}, bf16[128,2048]{1,0:T(8,128)(2,1)S(1)}, bf16[128,2048]{1,0:T(8,128)(2,1)S(1)}, bf16[128,2048]{1,0:T(8,128)...) custom-call(s32[2,1,1,64]{3,2,1,0:T(1,128)S(1)} %copy-done.5, s32[2,1,1,64]{3,2,1,0:T(1,128)S(1)} %copy-done.7, ...), custom_call_target="tpu_custom_call" | custom-call | flops 1048576 | bytes 65536 | tf_op jit(solution)/shard_map/tiles_1_1/pallas_call | solution.py:260
  122.4 1.0 collective-permute-start.24
  123.6 1.1 collective-permute-start.20
  124.7 9.6 %collective-permute-done.23.refs_1_ = bf16[128,2048]{1,0:T(8,128)(2,1)S(1)} collective-permute-done((bf16[128,2048]{1,0:T(8,128)(2,1)S(1)}, bf16[128,2048]{1,0:T(8,128)(2,1)S(1)}, u32[]{:S(2)}, u32[]{:S(2)}) %collective-permute-start.23) | collective-permute-done | bytes 524320 | tf_op jit(solution)/shard_map/ppermute | solution.py:419
  134.3 3.1 %collective-permute-done.24.refs_3_.refs_4_ = bf16[128,2048]{1,0:T(8,128)(2,1)S(1)} collective-permute-done((bf16[128,2048]{1,0:T(8,128)(2,1)S(1)}, bf16[128,2048]{1,0:T(8,128)(2,1)S(1)}, u32[]{:S(2)}, u32[]{:S(2)}) %collective-permute-start.24) | collective-permute-done | bytes 524320 | tf_op jit(solution)/shard_map/ppermute | solution.py:419
  137.5 2.0 %collective-permute-start.21 = (bf16[128,1024]{1,0:T(8,128)(2,1)S(1)}, bf16[128,1024]{1,0:T(8,128)(2,1)S(1)}, u32[]{:S(2)}, u32[]{:S(2)}) collective-permute-start(bf16[128,1024]{1,0:T(8,128)(2,1)S(1)} %get-tuple-element.69), channel_id=1, source_target_pairs={{0,1},{1,0},{2,3},{3,2},{4,5},{5,4},{6,7},{7,6},{8,9},{9,8},{10,11... | collective-permute-start | bytes 786440 | tf_op jit(solution)/shard_map/ppermute | solution.py:419
  139.5 1.0 collective-permute-start.26
  140.5 3.4 %collective-permute-done.21.refs_5_ = bf16[128,1024]{1,0:T(8,128)(2,1)S(1)} collective-permute-done((bf16[128,1024]{1,0:T(8,128)(2,1)S(1)}, bf16[128,1024]{1,0:T(8,128)(2,1)S(1)}, u32[]{:S(2)}, u32[]{:S(2)}) %collective-permute-start.21) | collective-permute-done | bytes 262176 | tf_op jit(solution)/shard_map/ppermute | solution.py:419
  143.9 0.6 items_1_0.1
  144.5 1.8 %collective-permute-done.25.refs_2_ = bf16[128,1024]{1,0:T(8,128)(2,1)S(1)} collective-permute-done((bf16[128,1024]{1,0:T(8,128)(2,1)S(1)}, bf16[128,1024]{1,0:T(8,128)(2,1)S(1)}, u32[]{:S(2)}, u32[]{:S(2)}) %collective-permute-start.25) | collective-permute-done | bytes 262176 | tf_op jit(solution)/shard_map/ppermute | solution.py:419
  146.7 0.6 items_1_1.1
  147.4 2.5 %users_1.1 = f32[2048,128]{1,0:T(8,128)} custom-call(s32[2,1]{1,0:T(2,128)S(1)} %copy.19.refs_3_.owner_ref, f32[2048,128]{1,0:T(8,128)S(1)} %get-tuple-element.44.refs_6_.users, f32[128,2048]{1,0:T(8,128)S(1)} %get-tuple-element.62.grad, f32[128,128]{1,0:T(8,128)S(1)} %get-tuple-element.63.gram), custom_call_target="tpu_custom_call" | custom-call | flops 1048576 | bytes 65536 | tf_op jit(solution)/shard_map/users_1/pallas_call | solution.py:304
  149.9 7.8 %collective-permute-done.27 = bf16[2048,128]{1,0:T(8,128)(2,1)S(1)} collective-permute-done((bf16[2048,128]{1,0:T(8,128)(2,1)S(1)}, bf16[2048,128]{1,0:T(8,128)(2,1)S(1)}, u32[]{:S(2)}, u32[]{:S(2)}) %collective-permute-start.27) | collective-permute-done | bytes 524320 | tf_op jit(solution)/shard_map/ppermute | solution.py:429
  157.8 5.6 %collective-permute-done.22 = bf16[2048,128]{1,0:T(8,128)(2,1)S(1)} collective-permute-done((bf16[2048,128]{1,0:T(8,128)(2,1)S(1)}, bf16[2048,128]{1,0:T(8,128)(2,1)S(1)}, u32[]{:S(2)}, u32[]{:S(2)}) %collective-permute-start.22) | collective-permute-done | bytes 524320 | tf_op jit(solution)/shard_map/ppermute | solution.py:429
  163.4 1.5 maximum_convert_fusion
  (45 shorter events, 2.0 us)
Async XLA Ops:
  2.1 1.2 copy-start
  3.3 0.9 copy-start.2
  4.2 0.7 copy-start.4
  4.9 0.7 copy-start.6
  14.9 21.7 %collective-permute-start.4 = (bf16[128,2176]{1,0:T(8,128)(2,1)S(1)}, bf16[128,2176]{1,0:T(8,128)(2,1)S(1)}, u32[]{:S(2)}, u32[]{:S(2)}) collective-permute-start(bf16[128,2176]{1,0:T(8,128)(2,1)S(1)} %get-tuple-element.52.refs_4_.refs_6_), channel_id=1, source_target_pairs={{0,1},{1,0},{2,3},{3,2},{4,5},{5,4},{6,7},{7,6},{8,9},{9,8},{10,11... | collective-permute-start | bytes 1671176 | tf_op jit(solution)/shard_map/ppermute | solution.py:419
  17.4 19.2 %collective-permute-start.5 = (bf16[128,2048]{1,0:T(8,128)(2,1)S(1)}, bf16[128,2048]{1,0:T(8,128)(2,1)S(1)}, u32[]{:S(2)}, u32[]{:S(2)}) collective-permute-start(bf16[128,2048]{1,0:T(8,128)(2,1)S(1)} %get-tuple-element.54), channel_id=1, source_target_pairs={{0,2},{1,3},{2,0},{3,1},{4,6},{5,7},{6,4},{7,5},{8,10},{9,11},{10,... | collective-permute-start | bytes 1572872 | tf_op jit(solution)/shard_map/ppermute | solution.py:419
  36.4 14.9 %collective-permute-start = (bf16[128,2048]{1,0:T(8,128)(2,1)S(1)}, bf16[128,2048]{1,0:T(8,128)(2,1)S(1)}, u32[]{:S(2)}, u32[]{:S(2)}) collective-permute-start(bf16[128,2048]{1,0:T(8,128)(2,1)S(1)} %get-tuple-element.46), channel_id=1, source_target_pairs={{0,1},{1,0},{2,3},{3,2},{4,5},{5,4},{6,7},{7,6},{8,9},{9,8},{10,11... | collective-permute-start | bytes 1572872 | tf_op jit(solution)/shard_map/ppermute | solution.py:419
  36.5 14.9 %collective-permute-start.1 = (bf16[128,2048]{1,0:T(8,128)(2,1)S(1)}, bf16[128,2048]{1,0:T(8,128)(2,1)S(1)}, u32[]{:S(2)}, u32[]{:S(2)}) collective-permute-start(bf16[128,2048]{1,0:T(8,128)(2,1)S(1)} %get-tuple-element.48), channel_id=1, source_target_pairs={{0,2},{1,3},{2,0},{3,1},{4,6},{5,7},{6,4},{7,5},{8,10},{9,11},{10,... | collective-permute-start | bytes 1572872 | tf_op jit(solution)/shard_map/ppermute | solution.py:419
  36.7 20.9 %collective-permute-start.6 = (bf16[128,1152]{1,0:T(8,128)(2,1)S(1)}, bf16[128,1152]{1,0:T(8,128)(2,1)S(1)}, u32[]{:S(2)}, u32[]{:S(2)}) collective-permute-start(bf16[128,1152]{1,0:T(8,128)(2,1)S(1)} %get-tuple-element.55), channel_id=1, source_target_pairs={{0,2},{1,3},{2,0},{3,1},{4,6},{5,7},{6,4},{7,5},{8,10},{9,11},{10,... | collective-permute-start | bytes 884744 | tf_op jit(solution)/shard_map/ppermute | solution.py:419
  38.8 17.3 %collective-permute-start.7 = (bf16[128,1024]{1,0:T(8,128)(2,1)S(1)}, bf16[128,1024]{1,0:T(8,128)(2,1)S(1)}, u32[]{:S(2)}, u32[]{:S(2)}) collective-permute-start(bf16[128,1024]{1,0:T(8,128)(2,1)S(1)} %get-tuple-element.56), channel_id=1, source_target_pairs={{0,1},{1,0},{2,3},{3,2},{4,5},{5,4},{6,7},{7,6},{8,9},{9,8},{10,11... | collective-permute-start | bytes 786440 | tf_op jit(solution)/shard_map/ppermute | solution.py:419
  51.5 11.5 %collective-permute-start.2 = (bf16[128,1024]{1,0:T(8,128)(2,1)S(1)}, bf16[128,1024]{1,0:T(8,128)(2,1)S(1)}, u32[]{:S(2)}, u32[]{:S(2)}) collective-permute-start(bf16[128,1024]{1,0:T(8,128)(2,1)S(1)} %get-tuple-element.49), channel_id=1, source_target_pairs={{0,2},{1,3},{2,0},{3,1},{4,6},{5,7},{6,4},{7,5},{8,10},{9,11},{10,... | collective-permute-start | bytes 786440 | tf_op jit(solution)/shard_map/ppermute | solution.py:419
  51.5 11.4 %collective-permute-start.3 = (bf16[128,1024]{1,0:T(8,128)(2,1)S(1)}, bf16[128,1024]{1,0:T(8,128)(2,1)S(1)}, u32[]{:S(2)}, u32[]{:S(2)}) collective-permute-start(bf16[128,1024]{1,0:T(8,128)(2,1)S(1)} %get-tuple-element.50), channel_id=1, source_target_pairs={{0,1},{1,0},{2,3},{3,2},{4,5},{5,4},{6,7},{7,6},{8,9},{9,8},{10,11... | collective-permute-start | bytes 786440 | tf_op jit(solution)/shard_map/ppermute | solution.py:419
  59.5 12.4 %collective-permute-start.14 = (bf16[128,2048]{1,0:T(8,128)(2,1)S(1)}, bf16[128,2048]{1,0:T(8,128)(2,1)S(1)}, u32[]{:S(2)}, u32[]{:S(2)}) collective-permute-start(bf16[128,2048]{1,0:T(8,128)(2,1)S(1)} %get-tuple-element.58), channel_id=1, source_target_pairs={{0,5},{1,4},{2,7},{3,6},{4,9},{5,8},{6,11},{7,10},{8,13},{9,12},{1... | collective-permute-start | bytes 1572872 | tf_op jit(solution)/shard_map/ppermute | solution.py:429
  59.5 17.0 %collective-permute-start.15 = (bf16[128,2048]{1,0:T(8,128)(2,1)S(1)}, bf16[128,2048]{1,0:T(8,128)(2,1)S(1)}, u32[]{:S(2)}, u32[]{:S(2)}) collective-permute-start(bf16[128,2048]{1,0:T(8,128)(2,1)S(1)} %get-tuple-element.58), channel_id=1, source_target_pairs={{0,6},{1,7},{2,4},{3,5},{4,10},{5,11},{6,8},{7,9},{8,14},{9,15},{1... | collective-permute-start | bytes 1572872 | tf_op jit(solution)/shard_map/ppermute | solution.py:429
  64.8 29.3 %copy-start.1 = (f32[2048,128]{1,0:T(8,128)S(1)}, f32[2048,128]{1,0:T(8,128)}, u32[]{:S(2)}) copy-start(f32[2048,128]{1,0:T(8,128)} %users.1) | copy-start | bytes 3145732
  64.8 31.2 %copy-start.3 = (s32[2,1,1,64,256]{4,3,2,1,0:T(8,128)S(1)}, s32[2,1,1,64,256]{4,3,2,1,0:T(8,128)}, u32[]{:S(2)}) copy-start(s32[2,1,1,64,256]{4,3,2,1,0:T(8,128)} %refs_5_.7) | copy-start | bytes 393220
  64.8 31.2 %copy-start.5 = (s32[2,1,1,64]{3,2,1,0:T(1,128)S(1)}, s32[2,1,1,64]{3,2,1,0:T(1,128)}, u32[]{:S(2)}) copy-start(s32[2,1,1,64]{3,2,1,0:T(1,128)} %refs_0_.7) | copy-start | bytes 1540
  64.8 31.2 %copy-start.7 = (s32[2,1,1,64]{3,2,1,0:T(1,128)S(1)}, s32[2,1,1,64]{3,2,1,0:T(1,128)}, u32[]{:S(2)}) copy-start(s32[2,1,1,64]{3,2,1,0:T(1,128)} %refs_1_.7) | copy-start | bytes 1540
  64.8 18.3 %collective-permute-start.9 = (bf16[128,2048]{1,0:T(8,128)(2,1)S(1)}, bf16[128,2048]{1,0:T(8,128)(2,1)S(1)}, u32[]{:S(2)}, u32[]{:S(2)}) collective-permute-start(bf16[128,2048]{1,0:T(8,128)(2,1)S(1)} %items_0_1.1), channel_id=1, source_target_pairs={{0,5},{1,4},{2,7},{3,6},{4,9},{5,8},{6,11},{7,10},{8,13},{9,12},{1... | collective-permute-start | bytes 1572872 | tf_op jit(solution)/shard_map/ppermute | solution.py:429
  66.8 21.0 %collective-permute-start.10 = (bf16[128,2048]{1,0:T(8,128)(2,1)S(1)}, bf16[128,2048]{1,0:T(8,128)(2,1)S(1)}, u32[]{:S(2)}, u32[]{:S(2)}) collective-permute-start(bf16[128,2048]{1,0:T(8,128)(2,1)S(1)} %items_0_1.1), channel_id=1, source_target_pairs={{0,6},{1,7},{2,4},{3,5},{4,10},{5,11},{6,8},{7,9},{8,14},{9,15},{1... | collective-permute-start | bytes 1572872 | tf_op jit(solution)/shard_map/ppermute | solution.py:429
  67.1 26.9 %collective-permute-start.13 = (bf16[128,2048]{1,0:T(8,128)(2,1)S(1)}, bf16[128,2048]{1,0:T(8,128)(2,1)S(1)}, u32[]{:S(2)}, u32[]{:S(2)}) collective-permute-start(bf16[128,2048]{1,0:T(8,128)(2,1)S(1)} %get-tuple-element.58), channel_id=1, source_target_pairs={{0,4},{1,5},{2,6},{3,7},{4,8},{5,9},{6,10},{7,11},{8,12},{9,13},{1... | collective-permute-start | bytes 1572872 | tf_op jit(solution)/shard_map/ppermute | solution.py:429
  71.8 38.7 %collective-permute-start.8 = (bf16[128,2048]{1,0:T(8,128)(2,1)S(1)}, bf16[128,2048]{1,0:T(8,128)(2,1)S(1)}, u32[]{:S(2)}, u32[]{:S(2)}) collective-permute-start(bf16[128,2048]{1,0:T(8,128)(2,1)S(1)} %items_0_1.1), channel_id=1, source_target_pairs={{0,4},{1,5},{2,6},{3,7},{4,8},{5,9},{6,10},{7,11},{8,12},{9,13},{1... | collective-permute-start | bytes 1572872 | tf_op jit(solution)/shard_map/ppermute | solution.py:429
  76.5 19.5 %collective-permute-start.16 = (bf16[128,1024]{1,0:T(8,128)(2,1)S(1)}, bf16[128,1024]{1,0:T(8,128)(2,1)S(1)}, u32[]{:S(2)}, u32[]{:S(2)}) collective-permute-start(bf16[128,1024]{1,0:T(8,128)(2,1)S(1)} %slice.18), channel_id=1, source_target_pairs={{0,2},{1,3},{2,0},{3,1},{4,6},{5,7},{6,4},{7,5},{8,10},{9,11},{10,... | collective-permute-start | bytes 786440 | tf_op jit(solution)/shard_map/ppermute | solution.py:419
  83.1 12.9 %collective-permute-start.17 = (bf16[128,1024]{1,0:T(8,128)(2,1)S(1)}, bf16[128,1024]{1,0:T(8,128)(2,1)S(1)}, u32[]{:S(2)}, u32[]{:S(2)}) collective-permute-start(bf16[128,1024]{1,0:T(8,128)(2,1)S(1)} %slice.19), channel_id=1, source_target_pairs={{0,1},{1,0},{2,3},{3,2},{4,5},{5,4},{6,7},{7,6},{8,9},{9,8},{10,11... | collective-permute-start | bytes 786440 | tf_op jit(solution)/shard_map/ppermute | solution.py:419
  87.9 22.7 %collective-permute-start.11 = (bf16[128,1024]{1,0:T(8,128)(2,1)S(1)}, bf16[128,1024]{1,0:T(8,128)(2,1)S(1)}, u32[]{:S(2)}, u32[]{:S(2)}) collective-permute-start(bf16[128,1024]{1,0:T(8,128)(2,1)S(1)} %slice.16), channel_id=1, source_target_pairs={{0,2},{1,3},{2,0},{3,1},{4,6},{5,7},{6,4},{7,5},{8,10},{9,11},{10,... | collective-permute-start | bytes 786440 | tf_op jit(solution)/shard_map/ppermute | solution.py:419
  94.0 16.6 %collective-permute-start.12 = (bf16[128,1024]{1,0:T(8,128)(2,1)S(1)}, bf16[128,1024]{1,0:T(8,128)(2,1)S(1)}, u32[]{:S(2)}, u32[]{:S(2)}) collective-permute-start(bf16[128,1024]{1,0:T(8,128)(2,1)S(1)} %slice.17), channel_id=1, source_target_pairs={{0,1},{1,0},{2,3},{3,2},{4,5},{5,4},{6,7},{7,6},{8,9},{9,8},{10,11... | collective-permute-start | bytes 786440 | tf_op jit(solution)/shard_map/ppermute | solution.py:419
  107.5 15.9 %collective-permute-start.18 = (bf16[128,2176]{1,0:T(8,128)(2,1)S(1)}, bf16[128,2176]{1,0:T(8,128)(2,1)S(1)}, u32[]{:S(2)}, u32[]{:S(2)}) collective-permute-start(bf16[128,2176]{1,0:T(8,128)(2,1)S(1)} %get-tuple-element.65.refs_4_.refs_6_), channel_id=1, source_target_pairs={{0,1},{1,0},{2,3},{3,2},{4,5},{5,4},{6,7},{7,6},{8,9},{9,8},{10,11... | collective-permute-start | bytes 1671176 | tf_op jit(solution)/shard_map/ppermute | solution.py:419
  107.6 15.9 %collective-permute-start.19 = (bf16[128,2048]{1,0:T(8,128)(2,1)S(1)}, bf16[128,2048]{1,0:T(8,128)(2,1)S(1)}, u32[]{:S(2)}, u32[]{:S(2)}) collective-permute-start(bf16[128,2048]{1,0:T(8,128)(2,1)S(1)} %get-tuple-element.67), channel_id=1, source_target_pairs={{0,2},{1,3},{2,0},{3,1},{4,6},{5,7},{6,4},{7,5},{8,10},{9,11},{10,... | collective-permute-start | bytes 1572872 | tf_op jit(solution)/shard_map/ppermute | solution.py:419
  122.4 11.9 %collective-permute-start.23 = (bf16[128,2048]{1,0:T(8,128)(2,1)S(1)}, bf16[128,2048]{1,0:T(8,128)(2,1)S(1)}, u32[]{:S(2)}, u32[]{:S(2)}) collective-permute-start(bf16[128,2048]{1,0:T(8,128)(2,1)S(1)} %get-tuple-element.72), channel_id=1, source_target_pairs={{0,1},{1,0},{2,3},{3,2},{4,5},{5,4},{6,7},{7,6},{8,9},{9,8},{10,11... | collective-permute-start | bytes 1572872 | tf_op jit(solution)/shard_map/ppermute | solution.py:419
  122.4 14.9 %collective-permute-start.24 = (bf16[128,2048]{1,0:T(8,128)(2,1)S(1)}, bf16[128,2048]{1,0:T(8,128)(2,1)S(1)}, u32[]{:S(2)}, u32[]{:S(2)}) collective-permute-start(bf16[128,2048]{1,0:T(8,128)(2,1)S(1)} %get-tuple-element.74), channel_id=1, source_target_pairs={{0,2},{1,3},{2,0},{3,1},{4,6},{5,7},{6,4},{7,5},{8,10},{9,11},{10,... | collective-permute-start | bytes 1572872 | tf_op jit(solution)/shard_map/ppermute | solution.py:419
  123.6 20.3 %collective-permute-start.20 = (bf16[128,1152]{1,0:T(8,128)(2,1)S(1)}, bf16[128,1152]{1,0:T(8,128)(2,1)S(1)}, u32[]{:S(2)}, u32[]{:S(2)}) collective-permute-start(bf16[128,1152]{1,0:T(8,128)(2,1)S(1)} %get-tuple-element.68), channel_id=1, source_target_pairs={{0,2},{1,3},{2,0},{3,1},{4,6},{5,7},{6,4},{7,5},{8,10},{9,11},{10,... | collective-permute-start | bytes 884744 | tf_op jit(solution)/shard_map/ppermute | solution.py:419
  137.5 6.4 %collective-permute-start.21 = (bf16[128,1024]{1,0:T(8,128)(2,1)S(1)}, bf16[128,1024]{1,0:T(8,128)(2,1)S(1)}, u32[]{:S(2)}, u32[]{:S(2)}) collective-permute-start(bf16[128,1024]{1,0:T(8,128)(2,1)S(1)} %get-tuple-element.69), channel_id=1, source_target_pairs={{0,1},{1,0},{2,3},{3,2},{4,5},{5,4},{6,7},{7,6},{8,9},{9,8},{10,11... | collective-permute-start | bytes 786440 | tf_op jit(solution)/shard_map/ppermute | solution.py:419
  139.5 6.8 %collective-permute-start.25 = (bf16[128,1024]{1,0:T(8,128)(2,1)S(1)}, bf16[128,1024]{1,0:T(8,128)(2,1)S(1)}, u32[]{:S(2)}, u32[]{:S(2)}) collective-permute-start(bf16[128,1024]{1,0:T(8,128)(2,1)S(1)} %get-tuple-element.75), channel_id=1, source_target_pairs={{0,2},{1,3},{2,0},{3,1},{4,6},{5,7},{6,4},{7,5},{8,10},{9,11},{10,... | collective-permute-start | bytes 786440 | tf_op jit(solution)/shard_map/ppermute | solution.py:419
  139.5 7.2 %collective-permute-start.26 = (bf16[128,1024]{1,0:T(8,128)(2,1)S(1)}, bf16[128,1024]{1,0:T(8,128)(2,1)S(1)}, u32[]{:S(2)}, u32[]{:S(2)}) collective-permute-start(bf16[128,1024]{1,0:T(8,128)(2,1)S(1)} %get-tuple-element.76), channel_id=1, source_target_pairs={{0,1},{1,0},{2,3},{3,2},{4,5},{5,4},{6,7},{7,6},{8,9},{9,8},{10,11... | collective-permute-start | bytes 786440 | tf_op jit(solution)/shard_map/ppermute | solution.py:419
  147.3 10.5 %collective-permute-start.27 = (bf16[2048,128]{1,0:T(8,128)(2,1)S(1)}, bf16[2048,128]{1,0:T(8,128)(2,1)S(1)}, u32[]{:S(2)}, u32[]{:S(2)}) collective-permute-start(bf16[2048,128]{1,0:T(8,128)(2,1)S(1)} %items_1_1.1), channel_id=1, source_target_pairs={{0,4},{1,5},{2,6},{3,7},{4,8},{5,9},{6,10},{7,11},{8,12},{9,13},{1... | collective-permute-start | bytes 1572872 | tf_op jit(solution)/shard_map/ppermute | solution.py:429
  147.4 16.0 %collective-permute-start.22 = (bf16[2048,128]{1,0:T(8,128)(2,1)S(1)}, bf16[2048,128]{1,0:T(8,128)(2,1)S(1)}, u32[]{:S(2)}, u32[]{:S(2)}) collective-permute-start(bf16[2048,128]{1,0:T(8,128)(2,1)S(1)} %get-tuple-element.70), channel_id=1, source_target_pairs={{0,4},{1,5},{2,6},{3,7},{4,8},{5,9},{6,10},{7,11},{8,12},{9,13},{1... | collective-permute-start | bytes 1572872 | tf_op jit(solution)/shard_map/ppermute | solution.py:429

commit v3 on v2

v3 whole, which is shorter than its diff:
```python
import functools

import jax
import jax.numpy as jnp
from jax import lax
from jax.experimental import pallas as pl
from jax.experimental.pallas import tpu as pltpu
from jax.sharding import PartitionSpec as P

SUB = 2
LEARN = 0.004
GRAM = 256.0
RIDGE = 1.0
CHUNKS = 2
START_MIB = 54
F32 = jnp.float32
BF16 = jnp.bfloat16
BIG = float(jnp.finfo(jnp.bfloat16).max)

ANY = pl.BlockSpec(memory_space=pl.ANY)
HBM = pl.BlockSpec(memory_space=pltpu.HBM)
VMEM = pl.BlockSpec(memory_space=pltpu.VMEM)


def params(mib):
    return pltpu.CompilerParams(vmem_limit_bytes=mib * 1024 * 1024)


def cost(flops, bytes_accessed):
    return pl.CostEstimate(flops=flops, bytes_accessed=bytes_accessed, transcendentals=0)


def over_rows(a, b):
    return lax.dot_general(a, b, (((1,), (1,)), ((), ())), preferred_element_type=F32)


def over_columns(a, b):
    return lax.dot_general(a, b, (((0,), (0,)), ((), ())), preferred_element_type=F32)


def ridge(rank):
    down = lax.broadcasted_iota(jnp.int32, (rank, rank), 0)
    across = lax.broadcasted_iota(jnp.int32, (rank, rank), 1)
    return jnp.where(down == across, RIDGE, 0.0)


def owned(gram, rows, owner):
    full = gram * (GRAM / rows) + ridge(gram.shape[0])
    return jnp.where(owner == lax.axis_index("grp"), full, 0.0).astype(BF16)


def without(members, bit):
    return [r for r in range(members) if not r & bit]


def tile_kernel(epoch, chunk, members, shard_tiles, tile, pieces, *refs):
    start_up = epoch == 0 and chunk == 0
    first = chunk == 0
    refs = list(refs)

    def take(n):
        out, refs[:n] = refs[:n], []
        return out

    row_hbm, col_hbm, count_hbm, owner_hbm, ratings, mask_hbm = take(6)
    users = take(1) if start_up else take(2)
    sources = take(pieces)
    grad_in = take(0 if first else 1)
    own_in = take(1 if first and epoch > 0 else 0)
    send_a, keep_a, send_b, keep_b, grad_user = take(5)
    if epoch == 0:
        items, old = take(2)
    if start_up:
        user_bf, user_t = take(2)
    else:
        user_bf, user_t = users
    (row_ref, col_ref, count_ref, owner_ref, mask, parts, held, error_0, error_1,
     slots, slot_row, slot_place, sem_tile, sem_item, sem_small) = take(15)
    if epoch == 0:
        items_f, = take(1)
    else:
        items, = take(1)
    if start_up:
        users_f, = take(1)
    errors = (error_0, error_1)

    me = lax.axis_index("grp")
    chunk_tiles = shard_tiles // CHUNKS
    rows = chunk_tiles * tile
    half = rows // 2
    bits_tile = chunk_tiles.bit_length() - 1
    bits_shard = shard_tiles.bit_length() - 1

    pairs = [(row_hbm, row_ref), (col_hbm, col_ref), (count_hbm, count_ref),
             (owner_hbm, owner_ref), (mask_hbm.at[epoch, 0, 0], mask)]
    if not first:
        pairs.append((grad_in[0], grad_user))
    if start_up:
        pairs.append((users[0], users_f))
    small = [
        pltpu.make_async_copy(src, dst, sem_small.at[i]) for i, (src, dst) in enumerate(pairs)
    ]
    for copy in small:
        copy.start()
    copies = []
    if epoch == 0:
        for r in range(members):
            start = pl.multiple_of((me ^ r) * (shard_tiles * tile) + chunk * rows, rows)
            copies.append(
                pltpu.make_async_copy(
                    sources[0].at[pl.ds(start, rows)], items_f.at[pl.ds(r * rows, rows)], sem_item.at[r]
                )
            )
    else:
        at = 0
        for i, source in enumerate(sources):
            width = source.shape[1]
            copies.append(
                pltpu.make_async_copy(source, items.at[:, pl.ds(at, width)], sem_item.at[i])
            )
            at += width
    for copy in copies:
        copy.start()
    for copy in small[:4]:
        copy.wait()

    count = count_ref[epoch, 0, 0]

    def pick(t, found):
        col = col_ref[epoch, 0, 0, t]
        slots[found] = t
        slot_row[found] = row_ref[epoch, 0, 0, t]
        slot_place[found] = ((col >> bits_shard) ^ me) * chunk_tiles + (col & (chunk_tiles - 1))
        here = ((col >> bits_tile) & (CHUNKS - 1)) == chunk
        return found + jnp.where(here & (t < count), 1, 0).astype(jnp.int32)

    total = lax.fori_loop(0, col_ref.shape[3], pick, jnp.int32(0), unroll=8)

    def fetch(i):
        return pltpu.make_async_copy(ratings.at[epoch, 0, 0, slots[i]], held.at[i], sem_tile.at[i])

    def begin(i, _):
        fetch(i).start()
        return 0

    lax.fori_loop(0, total, begin, 0)

    parts[...] = jnp.zeros_like(parts)
    if first:
        grad_user[...] = jnp.zeros_like(grad_user)
    for copy in small[4:]:
        copy.wait()

    def user_tile(j, _):
        spot = pl.ds(pl.multiple_of(j * tile, tile), tile)
        part = users_f[spot]
        user_bf[spot] = part.astype(BF16)
        user_t[:, spot] = part.T.astype(BF16)
        return 0

    if start_up:
        lax.fori_loop(0, users_f.shape[0] // tile, user_tile, 0, unroll=2)

    def item_tile(own, j, _):
        spot = pl.ds(pl.multiple_of(j * tile, tile), tile)
        turned = items_f[spot].T
        items[:, spot] = turned.astype(BF16)
        if own:
            old[:, spot] = turned
        return 0

    for r, copy in enumerate(copies):
        copy.wait()
        if epoch == 0:
            lax.fori_loop(
                r * chunk_tiles, (r + 1) * chunk_tiles, functools.partial(item_tile, r == 0), 0,
                unroll=2,
            )

    def spots(i):
        row = pl.multiple_of(slot_row[i] * tile, tile)
        place = pl.multiple_of(slot_place[i] * tile, tile)
        return pl.ds(row, tile), pl.ds(place, tile)

    def ready(j):
        for k in range(2):
            i = 2 * j + k

            @pl.when(i < total)
            def _():
                fetch(i).wait()

    def front(j):
        for k in range(2):
            i = jnp.minimum(2 * j + k, total - 1)
            row, place = spots(i)
            predicted = jnp.dot(user_bf[row], items[:, place], preferred_element_type=F32)
            error = (predicted - held[i].astype(F32)).astype(BF16)
            errors[k][j & 1] = jnp.clip(error, -BIG, BIG)

    def back(j):
        adds = []
        for k in range(2):
            valid = 2 * j + k < total
            i = jnp.minimum(2 * j + k, total - 1)
            row, place = spots(i)
            weight = mask[pl.ds(slots[i], 1), :].astype(F32)
            weight = jnp.where(valid, weight, 0.0)
            error = errors[k][j & 1]
            user_add = over_rows(items[:, place], error)
            item_add = jnp.dot(
                user_t[:, row] * weight.astype(BF16), error, preferred_element_type=F32
            )
            adds.append((row, place, jnp.where(weight > 0.5, user_add, 0.0), item_add))
        return adds

    def add(adds):
        for row, place, user_add, item_add in adds:
            grad_user[:, row] += user_add
            parts[:, place] += item_add

    twos = (total + 1) // 2

    @pl.when(total > 0)
    def _():
        ready(0)
        front(0)

    def step(j, _):
        ready(j + 1)
        adds = back(j)
        front(j + 1)
        add(adds)
        return 0

    lax.fori_loop(0, twos, step, 0)

    for bit, send, keep, start, width in (
        (1, send_a, keep_a, 0, half), (members // 2, send_b, keep_b, half, rows - half)
    ):
        for k, r in enumerate(without(members, bit)):
            keep[:, k * width:(k + 1) * width] = parts[:, pl.ds(r * rows + start, width)].astype(BF16)
            r = r | bit
            send[:, k * width:(k + 1) * width] = parts[:, pl.ds(r * rows + start, width)].astype(BF16)
    if start_up:
        own = jnp.dot(user_t[...], user_bf[...], preferred_element_type=F32)
        own = owned(own, users_f.shape[0], owner_ref[epoch, 0])
    elif first:
        own = own_in[0][...]
    if first:
        send_a[:, members // 2 * half:] = own


def tile_call(epoch, chunk, members, scalars, ratings, row_mask, users, sources, carried, own):
    tile = ratings.shape[-1]
    slots = ratings.shape[3]
    start_up = epoch == 0 and chunk == 0
    first = chunk == 0
    user_rows, rank = users[0].shape
    if epoch == 0:
        block_rows = sources[0].shape[0]
    else:
        block_rows = sum(s.shape[1] for s in sources) * CHUNKS
    shard_tiles = block_rows // members // tile
    rows = shard_tiles // CHUNKS * tile
    half = rows // 2
    sd = jax.ShapeDtypeStruct
    wide_a, wide_b = members // 2 * half, members // 2 * (rows - half)
    extra = rank if first else 0
    out_shape = [
        sd((rank, wide_a + extra), BF16), sd((rank, wide_a), BF16),
        sd((rank, wide_b), BF16), sd((rank, wide_b), BF16), sd((rank, user_rows), F32),
    ]
    if epoch == 0:
        out_shape += [sd((rank, members * rows), BF16), sd((rank, rows), F32)]
    if start_up:
        out_shape += [sd((user_rows, rank), BF16), sd((rank, user_rows), BF16)]
    in_specs = [HBM] * 6 + ([HBM] if start_up else [VMEM] * 2)
    in_specs += [HBM if epoch == 0 else ANY] * len(sources)
    operands = [*scalars, ratings, row_mask, *users, *sources]
    if not first:
        in_specs += [ANY]
        operands += [carried]
    elif epoch > 0:
        in_specs += [VMEM]
        operands += [own]
    scratch = [
        *[pltpu.SMEM(s.shape, jnp.int32) for s in scalars],
        pltpu.VMEM((slots, tile), jnp.int32),
        pltpu.VMEM((rank, members * rows), F32),
        pltpu.VMEM((slots, tile, tile), BF16),
        *[pltpu.VMEM((2, tile, tile), BF16)] * 2,
        *[pltpu.SMEM((slots + 1,), jnp.int32)] * 3,
        pltpu.SemaphoreType.DMA((slots,)),
        pltpu.SemaphoreType.DMA((max(members, len(sources)),)),
        pltpu.SemaphoreType.DMA((7,)),
    ]
    if epoch == 0:
        scratch.append(pltpu.VMEM((members * rows, rank), F32))
    else:
        scratch.append(pltpu.VMEM((rank, members * rows), BF16))
    if start_up:
        scratch.append(pltpu.VMEM((user_rows, rank), F32))
    return pl.pallas_call(
        functools.partial(tile_kernel, epoch, chunk, members, shard_tiles, tile, len(sources)),
        out_shape=out_shape,
        in_specs=in_specs,
        out_specs=[VMEM] * len(out_shape),
        scratch_shapes=scratch,
        compiler_params=params(START_MIB if start_up else 40),
        cost_estimate=cost(1 << 20, 1 << 16),
        name=f"tiles_{epoch}_{chunk}",
    )(*operands)


def user_kernel(epoch, block_rows, owner_ref, users, grad, *refs):
    outs = 4 if epoch + 1 < SUB else 1
    pieces, outs = refs[:-outs], refs[-outs:]
    gram = over_rows(pieces[0][...], pieces[0][...])
    for piece in pieces[1:]:
        gram += over_rows(piece[...], piece[...])
    full = gram * (GRAM / block_rows) + ridge(users.shape[1])
    pull = jnp.dot(users[...], full, precision=lax.Precision.HIGHEST, preferred_element_type=F32)
    new = users[...] - LEARN * (grad[...].T + pull)
    outs[0][...] = new
    if len(outs) > 1:
        plain = new.astype(BF16)
        turned = new.T.astype(BF16)
        outs[1][...] = plain
        outs[2][...] = turned
        own = jnp.dot(turned, plain, preferred_element_type=F32)
        outs[3][...] = owned(own, users.shape[0], owner_ref[epoch + 1, 0])


def user_call(epoch, block_rows, owner_list, users, grad, pieces):
    rows, rank = users.shape
    sd = jax.ShapeDtypeStruct
    out_shape = [sd(users.shape, F32)]
    if epoch + 1 < SUB:
        out_shape += [sd((rows, rank), BF16), sd((rank, rows), BF16), sd((rank, rank), BF16)]
    return pl.pallas_call(
        functools.partial(user_kernel, epoch, block_rows),
        out_shape=out_shape,
        in_specs=[pl.BlockSpec(memory_space=pltpu.SMEM)] + [VMEM] * (2 + len(pieces)),
        out_specs=[VMEM] * len(out_shape),
        compiler_params=params(40),
        cost_estimate=cost(1 << 20, 1 << 16),
        name=f"users_{epoch}",
    )(owner_list, users, grad, *pieces)


def summed(refs, names, r, width):
    total = None
    for ref, order in zip(refs, names):
        k = order.index(r)
        term = ref[:, k * width:(k + 1) * width].astype(F32)
        total = term if total is None else total + term
    return total


def mid_kernel(paths, grams, *refs):
    at = 0
    outs = refs[sum(len(names) for names, _, _ in paths) + grams:]
    gram_refs = refs[len(refs) - len(paths) - grams:len(refs) - len(paths)]
    for (names, going, width), out in zip(paths, outs):
        terms = refs[at:at + len(names)]
        at += len(names)
        for k, r in enumerate(going):
            out[:, k * width:(k + 1) * width] = summed(terms, names, r, width).astype(BF16)
    if grams:
        rank = outs[0].shape[0]
        total = gram_refs[0][:, gram_refs[0].shape[1] - rank:].astype(F32)
        for ref in gram_refs[1:]:
            total += ref[:, ref.shape[1] - rank:].astype(F32)
        outs[0][:, outs[0].shape[1] - rank:] = total.astype(BF16)


def mid_call(epoch, chunk, step, paths, grams):
    rank = paths[0][0][0][0].shape[0]
    specs, operands, out_shape = [], [], []
    for terms, going, width in paths:
        specs.append(([names for _, names in terms], going, width))
        operands += [array for array, _ in terms]
        extra = rank if grams and not out_shape else 0
        out_shape.append(jax.ShapeDtypeStruct((rank, len(going) * width + extra), BF16))
    operands += grams
    return pl.pallas_call(
        functools.partial(mid_kernel, specs, len(grams)),
        out_shape=out_shape,
        in_specs=[VMEM] * len(operands),
        out_specs=[VMEM] * len(out_shape),
        compiler_params=params(40),
        cost_estimate=cost(1 << 16, 1 << 16),
        name=f"mid_{epoch}_{chunk}_{step}",
    )(*operands)


def item_kernel(epoch, count, rows, width, grams, items, *refs):
    terms_a, terms_b = refs[:count], refs[count:2 * count]
    gram_refs = refs[2 * count:2 * count + grams]
    refs = refs[2 * count + grams:]
    out = refs[0]
    rank = gram_refs[0].shape[0]
    gram = gram_refs[0][:, gram_refs[0].shape[1] - rank:]
    for ref in gram_refs[1:]:
        gram = (gram.astype(F32) + ref[:, ref.shape[1] - rank:].astype(F32)).astype(BF16)
    if grams > 1:
        refs[1][...] = gram
    zero = [[0]] * count
    grad = jnp.concatenate(
        [summed(terms_a, zero, 0, width), summed(terms_b, zero, 0, rows - width)], axis=1
    )
    if epoch == 0:
        high = items[...].astype(BF16)
        low = (items[...] - high.astype(F32)).astype(BF16)
        pull = over_columns(gram, high) + over_columns(gram, low)
    else:
        pull = over_columns(gram, items[...])
    new = items[...].astype(F32) - LEARN * (grad + pull)
    out[...] = (new if epoch + 1 < SUB else new.T).astype(BF16)


def item_call(epoch, chunk, shard_rows, items, terms_a, terms_b, grams):
    rank = grams[0].shape[0]
    rows = shard_rows // CHUNKS
    last = epoch + 1 == SUB
    out_shape = [jax.ShapeDtypeStruct((rows, rank) if last else (rank, rows), BF16)]
    if len(grams) > 1:
        out_shape.append(jax.ShapeDtypeStruct((rank, rank), BF16))
    out = pl.pallas_call(
        functools.partial(
            item_kernel, epoch, len(terms_a), rows, rows // 2, len(grams)
        ),
        out_shape=out_shape,
        in_specs=[VMEM] * (1 + 2 * len(terms_a) + len(grams)),
        out_specs=[VMEM] * len(out_shape),
        compiler_params=params(40),
        cost_estimate=cost(1 << 16, 1 << 16),
        name=f"items_{epoch}_{chunk}",
    )(items, *terms_a, *terms_b, *grams)
    return out[0], out[-1]


def swapped(value, bit):
    length = lax.axis_size("grp")
    return lax.ppermute(value, "grp", [(i, i ^ bit) for i in range(length)])


def moved(value, bit):
    length, blocks = lax.axis_size("grp"), lax.axis_size("blk")
    pairs = [
        (b * length + i, (b + 1) % blocks * length + (i ^ bit))
        for b in range(blocks)
        for i in range(length)
    ]
    return lax.ppermute(value, ("blk", "grp"), pairs)


def scattered(epoch, chunk, out, members, width_a, width_b, after):
    send_a, keep_a, send_b, keep_b = out[:4]
    bits = [1 << i for i in range(members.bit_length() - 1)]
    orders = (bits, bits[::-1])
    widths = (width_a, width_b)
    sends = [send_a, send_b]
    names = [without(members, order[0]) for order in orders]
    terms = [[(keep_a, names[0])], [(keep_b, names[1])]]
    grams = [send_a] if chunk == 0 else []
    for step in range(len(bits)):
        for p in range(2):
            arrived = swapped(sends[p], orders[p][step])
            if step == 0:
                arrived = tied(arrived, after)
            terms[p].append((arrived, names[p]))
            if p == 0 and grams:
                grams.append(arrived)
        if step + 1 == len(bits):
            break
        paths = []
        for p in range(2):
            bit = orders[p][step + 1]
            paths.append((terms[p], [r for r in names[p] if r & bit], widths[p]))
            names[p] = [r for r in names[p] if not r & bit]
        sends = mid_call(epoch, chunk, step, paths, grams)
    return [a for a, _ in terms[0]], [a for a, _ in terms[1]], grams


def tied(value, *others):
    return lax.optimization_barrier((value, *others))[0]


def gather_start(shard):
    known = {0: moved(shard, 0)}
    bit = 1
    while bit < lax.axis_size("grp"):
        known[bit] = moved(shard, bit)
        bit *= 2
    return known


def gather_finish(known, after):
    length = lax.axis_size("grp")
    known = {r: [tied(piece, *after)] for r, piece in known.items()}

    def cut(r, lower):
        pieces = known[r]
        if len(pieces) == 1:
            half = pieces[0].shape[1] // 2
            return pieces[0][:, half:] if lower else pieces[0][:, :half]
        return pieces[1] if lower else pieces[0]

    for r in range(1, length):
        if r in known:
            continue
        low = r & -r
        high = 1 << (r.bit_length() - 1)
        known[r] = [swapped(cut(r ^ high, False), high), swapped(cut(r ^ low, True), low)]
    return [piece for r in range(length) for piece in known[r]]


def local(ratings, row_index, col_index, row_mask, counts, owner_list, user_factors, item_factors):
    members = lax.axis_size("grp")
    block_rows = item_factors.shape[0]
    shard_rows = block_rows // members
    rows = shard_rows // CHUNKS
    scalars = (row_index, col_index, counts, owner_list)
    full_users = user_factors
    users = [user_factors]
    own_gram = None
    known = []
    for epoch in range(SUB):
        grad_user = None
        outs, olds, pieces = [], [], []
        for c in range(CHUNKS):
            if epoch == 0:
                sources = [item_factors]
            else:
                sources = gather_finish(known[c], [] if c == 0 else [grad_user])
            out = tile_call(
                epoch, c, members, scalars, ratings, row_mask, users, sources, grad_user, own_gram
            )
            grad_user = out[4]
            outs.append(out)
            if epoch == 0:
                pieces.append(out[5])
                olds.append(out[6])
                if c == 0:
                    users = out[7:9]
            else:
                pieces += sources
                olds.append(sources[0])
        new_users = user_call(epoch, block_rows, owner_list, full_users, grad_user, pieces)
        full_users = new_users[0]
        shards = []
        grams = None
        for c in range(CHUNKS):
            terms_a, terms_b, found = scattered(
                epoch, c, outs[c], members, rows // 2, rows - rows // 2,
                outs[min(c + 1, CHUNKS - 1)][4],
            )
            if found:
                found[0] = tied(found[0], full_users)
            shard, gram = item_call(epoch, c, shard_rows, olds[c], terms_a, terms_b, found or grams)
            if found:
                grams = [gram]
            shards.append(shard)
        if epoch + 1 < SUB:
            users, own_gram = new_users[1:3], new_users[3]
            known = []
            for shard in shards:
                early = [piece for r, piece in known[-1].items() if r] if known else []
                known.append(gather_start(tied(shard, *early)))
    finals = [moved(shard, 0) for shard in shards]
    return full_users, jnp.concatenate(finals, axis=0).astype(F32)


def solution(mesh):
    in_specs = (
        P(None, "blk", "grp", None, None, None),
        P(None, "blk", "grp", None),
        P(None, "blk", "grp", None),
        P(None, "blk", "grp", None, None),
        P(None, "blk", "grp"),
        P(None, "blk"),
        P(("blk", "grp"), None),
        P("blk", None),
    )
    out_specs = (P(("blk", "grp"), None), P(("blk", "grp"), None))
    return jax.shard_map(local, mesh=mesh, in_specs=in_specs, out_specs=out_specs, check_vma=False)
```

time: 165 us -> 163 us (0.988)
  waiting for transfers between devices: 66.6 us -> 75.3 us
  starting transfers between devices: 37.4 us -> 30.7 us
  Pallas kernels: 53.4 us -> 49.2 us
    ppermute x20, waiting for transfers between devices: 35.1 us -> 62.1 us  [swapped(): return lax.ppermute(value, 'grp', [(i, i ^ bit) for i in range(length)])]
    ppermute x8, waiting for transfers between devices: 31.5 us -> 13.2 us  [moved(): return lax.ppermute(value, ('blk', 'grp'), pairs)]
    ppermute x20, starting transfers between devices: 31.1 us -> 22.1 us  [swapped(): return lax.ppermute(value, 'grp', [(i, i ^ bit) for i in range(length)])]
    pallas_call x4, Pallas kernels: 43.7 us -> 36.4 us  [tile_call(): pl.pallas_call(functools.partial(tile_kernel, epoch, chunk, members, shar...]
    pallas_call x2, Pallas kernels: 4.44 us -> 10 us  [user_call(): pl.pallas_call(functools.partial(user_kernel, epoch, block_rows), out_sha...]
    pallas_call x4, Pallas kernels: 4.72 us -> 2.26 us  [item_call(): pl.pallas_call(functools.partial(item_kernel, epoch, len(terms_a), rows,...]
    ppermute x8, starting transfers between devices: 6.31 us -> 8.56 us  [moved(): return lax.ppermute(value, ('blk', 'grp'), pairs)]
    unnamed x18 -> x30, local copies, waits for them, and re-layouts: 4.99 us -> 5.9 us
  transfers between devices with their start and end apart: 28 -> 28, of which waited for: 17 -> 9; matrix products, arithmetic and copies ran while one was open for 0% -> 0% of each run, Pallas kernels for 26% -> 22%
where the time goes in v3:
time: 163 us
  waiting for transfers between devices  75.3 us (46%)
  Pallas kernels  49.2 us (30%)
  starting transfers between devices  30.7 us (19%)
  local copies, waits for them, and re-layouts  5.97 us (4%)
    ppermute x20, waiting for transfers between devices, swapped(): return lax.ppermute(value, 'grp', [(i, i ^ bit) for i in range(length)])  62.1 us
    pallas_call x4, Pallas kernels, tile_call(): pl.pallas_call(functools.partial(tile_kernel, epoch, chunk, members, shar...  36.4 us
    ppermute x20, starting transfers between devices, swapped(): return lax.ppermute(value, 'grp', [(i, i ^ bit) for i in range(length)])  22.1 us
    ppermute x8, waiting for transfers between devices, moved(): return lax.ppermute(value, ('blk', 'grp'), pairs)  13.2 us
    pallas_call x2, Pallas kernels, user_call(): pl.pallas_call(functools.partial(user_kernel, epoch, block_rows), out_sha...  10 us
    ppermute x8, starting transfers between devices, moved(): return lax.ppermute(value, ('blk', 'grp'), pairs)  8.56 us
    unnamed x30, local copies, waits for them, and re-layouts  5.9 us
  transfers between devices with their start and end apart: 28, of which 9 were waited for; matrix products, arithmetic and copies ran while one was open for 0% of the time, Pallas kernels for 22%

profile of v3, /device:TPU:0, one launch (start us, length us, event | category | flops | bytes accessed | tf_op | source)
XLA Modules:
  0.0 163.5 jit_solution(3241506916147589290)
XLA Ops:
  0.6 1.3 copy.19.refs_3_.owner_ref
  1.9 1.3 copy.12.refs_2_
  3.2 13.8 %tiles_0_0.1 = (bf16[128,2176]{1,0:T(8,128)(2,1)}, bf16[128,2048]{1,0:T(8,128)(2,1)}, bf16[128,2048]{1,0:T(8,128)(2,1)}, bf16[128,2048]{1,0:T(8,128)(2,1)}, f32[...) custom-call(s32[2,1,1,64]{3,2,1,0:T(1,128)} %refs_0_.7, ...), custom_call_target="tpu_custom_call" | custom-call | flops 1048576 | bytes 65536 | tf_op jit(solution)/shard_map/tiles_0_0/pallas_call | solution.py:304
  17.0 1.0 collective-permute-start.4
  18.0 2.2 %collective-permute-start.5 = (bf16[128,2048]{1,0:T(8,128)(2,1)}, bf16[128,2048]{1,0:T(8,128)(2,1)S(1)}, u32[]{:S(2)}, u32[]{:S(2)}) collective-permute-start(bf16[128,2048]{1,0:T(8,128)(2,1)} %get-tuple-element.81), channel_id=1, source_target_pairs={{0,2},{1,3},{2,0},{3,1},{4,6},{5,7},{6,4},{7,5},{8,10},{9,11},{10,... | collective-permute-start | bytes 1572872 | tf_op jit(solution)/shard_map/ppermute | solution.py:446
  20.2 1.2 copy-done.7
  21.5 1.0 copy-done.8
  22.5 1.0 copy-done.9
  23.5 10.1 %tiles_0_1.1 = (bf16[128,2048]{1,0:T(8,128)(2,1)S(1)}, bf16[128,2048]{1,0:T(8,128)(2,1)S(1)}, bf16[128,2048]{1,0:T(8,128)(2,1)S(1)}, bf16[128,2048]{1,0:T(8,128)...) custom-call(s32[2,1,1,64]{3,2,1,0:T(1,128)S(1)} %copy-done.11, ...), custom_call_target="tpu_custom_call" | custom-call | flops 1048576 | bytes 65536 | tf_op jit(solution)/shard_map/tiles_0_1/pallas_call | solution.py:304
  33.7 0.1 mid_0_0_0.1
  33.9 0.9 collective-permute-start
  34.9 1.1 collective-permute-start.1
  36.0 2.0 %collective-permute-start.7 = (bf16[128,1024]{1,0:T(8,128)(2,1)S(1)}, bf16[128,1024]{1,0:T(8,128)(2,1)S(1)}, u32[]{:S(2)}, u32[]{:S(2)}) collective-permute-start(bf16[128,1024]{1,0:T(8,128)(2,1)S(1)} %get-tuple-element.84), channel_id=1, source_target_pairs={{0,1},{1,0},{2,3},{3,2},{4,5},{5,4},{6,7},{7,6},{8,9},{9,8},{10,11... | collective-permute-start | bytes 786440 | tf_op jit(solution)/shard_map/ppermute | solution.py:446
  38.0 4.7 %users_0.1 = (f32[2048,128]{1,0:T(8,128)S(1)}, bf16[2048,128]{1,0:T(8,128)(2,1)S(1)}, bf16[128,2048]{1,0:T(8,128)(2,1)S(1)}, bf16[128,128]{1,0:T(8,128)(2,1)S(1)}) custom-call(s32[2,1]{1,0:T(2,128)S(1)} %copy-done.10, f32[2048,128]{1,0:T(8,128)S(1)} %copy-done, f32[128,2048]{1,0:T(8,128)S(1)} %get-tuple-element.61.grad, bf16[128,8192]{1,0:T(8,128)(2,1)S(1)} %copy-done.5, ...), custom_call_target="tpu_custom_call" | custom-call | flops 1048576 | bytes 65536 | tf_op jit(solution)/shard_map/users_0/pallas_call | solution.py:341
  42.7 10.1 %collective-permute-done.7.refs_5_ = bf16[128,1024]{1,0:T(8,128)(2,1)S(1)} collective-permute-done((bf16[128,1024]{1,0:T(8,128)(2,1)S(1)}, bf16[128,1024]{1,0:T(8,128)(2,1)S(1)}, u32[]{:S(2)}, u32[]{:S(2)}) %collective-permute-start.7) | collective-permute-done | bytes 262176 | tf_op jit(solution)/shard_map/ppermute | solution.py:446
  52.8 0.6 items_0_0.1
  53.5 4.6 %collective-permute-start.9 = (bf16[128,2048]{1,0:T(8,128)(2,1)S(1)}, bf16[128,2048]{1,0:T(8,128)(2,1)S(1)}, u32[]{:S(2)}, u32[]{:S(2)}) collective-permute-start(bf16[128,2048]{1,0:T(8,128)(2,1)S(1)} %get-tuple-element.87), channel_id=1, source_target_pairs={{0,6},{1,7},{2,4},{3,5},{4,10},{5,11},{6,8},{7,9},{8,14},{9,15},{1... | collective-permute-start | bytes 1572872 | tf_op jit(solution)/shard_map/ppermute | solution.py:456
  58.1 0.1 mid_0_1_0.1
  58.3 0.6 collective-permute-start.2
  58.9 1.3 collective-permute-start.3
  60.2 16.8 %collective-permute-done.2.refs_2_ = bf16[128,1024]{1,0:T(8,128)(2,1)S(1)} collective-permute-done((bf16[128,1024]{1,0:T(8,128)(2,1)S(1)}, bf16[128,1024]{1,0:T(8,128)(2,1)S(1)}, u32[]{:S(2)}, u32[]{:S(2)}) %collective-permute-start.2) | collective-permute-done | bytes 262176 | tf_op jit(solution)/shard_map/ppermute | solution.py:446
  77.1 0.6 items_0_1.1
  77.7 1.5 collective-permute-start.15
  79.2 1.0 collective-permute-start.12
  80.3 1.2 collective-permute-start.13
  81.5 16.7 %collective-permute-done.12.refs_11_.refs_3_ = bf16[128,1024]{1,0:T(8,128)(2,1)S(1)} collective-permute-done((bf16[128,1024]{1,0:T(8,128)(2,1)S(1)}, bf16[128,1024]{1,0:T(8,128)(2,1)S(1)}, u32[]{:S(2)}, u32[]{:S(2)}) %collective-permute-start.12) | collective-permute-done | bytes 262176 | tf_op jit(solution)/shard_map/ppermute | solution.py:446
  98.2 5.8 %tiles_1_0.1 = (bf16[128,2176]{1,0:T(8,128)(2,1)S(1)}, bf16[128,2048]{1,0:T(8,128)(2,1)S(1)}, bf16[128,2048]{1,0:T(8,128)(2,1)S(1)}, bf16[128,2048]{1,0:T(8,128)(2,1)S(1)}, f32[128,2048]{1,0:T(8,128)S(1)}) custom-call(s32[2,1,1,64]{3,2,1,0:T(1,128)S(1)} %copy-done.11, s32[2,1,1,64]{3,2,1,0:T(1,128)S(1)} %copy-done.12, s32[2,1,1]{2,1,0:T(1,128)S(1)} %copy-done.13, ...), custom_call_target="tpu_custom_call" | custom-call | flops 1048576 | bytes 65536 | tf_op jit(solution)/shard_map/tiles_1_0/pallas_call | solution.py:304
  104.0 1.9 %collective-permute-start.16 = (bf16[128,1024]{1,0:T(8,128)(2,1)S(1)}, bf16[128,1024]{1,0:T(8,128)(2,1)S(1)}, u32[]{:S(2)}, u32[]{:S(2)}) collective-permute-start(bf16[128,1024]{1,0:T(8,128)(2,1)S(1)} %slice.14), channel_id=1, source_target_pairs={{0,2},{1,3},{2,0},{3,1},{4,6},{5,7},{6,4},{7,5},{8,10},{9,11},{10,... | collective-permute-start | bytes 786440 | tf_op jit(solution)/shard_map/ppermute | solution.py:446
  105.9 1.2 collective-permute-start.17
  107.2 0.8 collective-permute-start.18
  108.0 0.3 collective-permute-start.19
  108.4 5.0 %collective-permute-done.16.refs_11_.refs_8_ = bf16[128,1024]{1,0:T(8,128)(2,1)S(1)} collective-permute-done((bf16[128,1024]{1,0:T(8,128)(2,1)S(1)}, bf16[128,1024]{1,0:T(8,128)(2,1)S(1)}, u32[]{:S(2)}, u32[]{:S(2)}) %collective-permute-start.16) | collective-permute-done | bytes 262176 | tf_op jit(solution)/shard_map/ppermute | solution.py:446
  113.4 1.9 %collective-permute-done.17.refs_12_.refs_9_ = bf16[128,1024]{1,0:T(8,128)(2,1)S(1)} collective-permute-done((bf16[128,1024]{1,0:T(8,128)(2,1)S(1)}, bf16[128,1024]{1,0:T(8,128)(2,1)S(1)}, u32[]{:S(2)}, u32[]{:S(2)}) %collective-permute-start.17) | collective-permute-done | bytes 262176 | tf_op jit(solution)/shard_map/ppermute | solution.py:446
  115.2 6.7 %tiles_1_1.1 = (bf16[128,2048]{1,0:T(8,128)(2,1)S(1)}, bf16[128,2048]{1,0:T(8,128)(2,1)S(1)}, bf16[128,2048]{1,0:T(8,128)(2,1)S(1)}, bf16[128,2048]{1,0:T(8,128)(2,1)S(1)}, f32[128,2048]{1,0:T(8,128)S(1)}) custom-call(s32[2,1,1,64]{3,2,1,0:T(1,128)S(1)} %copy-done.11, s32[2,1,1,64]{3,2,1,0:T(1,128)S(1)} %copy-done.12, s32[2,1,1]{2,1,0:T(1,128)S(1)} %copy-done.13, ...), custom_call_target="tpu_custom_call" | custom-call | flops 1048576 | bytes 65536 | tf_op jit(solution)/shard_map/tiles_1_1/pallas_call | solution.py:304
  121.9 0.6 collective-permute-start.23
  122.5 1.2 collective-permute-start.24
  123.6 2.7 %collective-permute-done.18.refs_1_.refs_5_.refs_7_ = bf16[128,2176]{1,0:T(8,128)(2,1)S(1)} collective-permute-done((bf16[128,2176]{1,0:T(8,128)(2,1)S(1)}, bf16[128,2176]{1,0:T(8,128)(2,1)S(1)}, u32[]{:S(2)}, u32[]{:S(2)}) %collective-permute-start.18) | collective-permute-done | bytes 557088 | tf_op jit(solution)/shard_map/ppermute | solution.py:446
  126.5 2.1 %collective-permute-start.21 = (bf16[128,1024]{1,0:T(8,128)(2,1)S(1)}, bf16[128,1024]{1,0:T(8,128)(2,1)S(1)}, u32[]{:S(2)}, u32[]{:S(2)}) collective-permute-start(bf16[128,1024]{1,0:T(8,128)(2,1)S(1)} %get-tuple-element.102), channel_id=1, source_target_pairs={{0,1},{1,0},{2,3},{3,2},{4,5},{5,4},{6,7},{7,6},{8,9},{9,8},{10,11... | collective-permute-start | bytes 786440 | tf_op jit(solution)/shard_map/ppermute | solution.py:446
  128.6 8.9 %collective-permute-done.23.refs_1_ = bf16[128,2048]{1,0:T(8,128)(2,1)S(1)} collective-permute-done((bf16[128,2048]{1,0:T(8,128)(2,1)S(1)}, bf16[128,2048]{1,0:T(8,128)(2,1)S(1)}, u32[]{:S(2)}, u32[]{:S(2)}) %collective-permute-start.23) | collective-permute-done | bytes 524320 | tf_op jit(solution)/shard_map/ppermute | solution.py:446
  137.7 0.9 collective-permute-start.25
  138.6 1.4 collective-permute-start.26
  140.1 5.3 %users_1.1 = f32[2048,128]{1,0:T(8,128)} custom-call(s32[2,1]{1,0:T(2,128)S(1)} %copy-done.10, f32[2048,128]{1,0:T(8,128)S(1)} %get-tuple-element.64.users, f32[128,2048]{1,0:T(8,128)S(1)} %get-tuple-element.94.grad, bf16[128,2048]{1,0:T(8,128)(2,1)S(1)} %collective-permute-done.11.refs_8_.refs_0_.items, ...), custom_call_target="tpu_custom_call" | custom-call | flops 1048576 | bytes 65536 | tf_op jit(solution)/shard_map/users_1/pallas_call | solution.py:341
  145.4 0.6 items_1_0.1
  146.0 0.6 items_1_1.1
  146.6 2.3 %collective-permute-start.27 = (bf16[2048,128]{1,0:T(8,128)(2,1)S(1)}, bf16[2048,128]{1,0:T(8,128)(2,1)S(1)}, u32[]{:S(2)}, u32[]{:S(2)}) collective-permute-start(bf16[2048,128]{1,0:T(8,128)(2,1)S(1)} %items_1_1.1), channel_id=1, source_target_pairs={{0,4},{1,5},{2,6},{3,7},{4,8},{5,9},{6,10},{7,11},{8,12},{9,13},{1... | collective-permute-start | bytes 1572872 | tf_op jit(solution)/shard_map/ppermute | solution.py:456
  148.8 7.5 %collective-permute-done.22 = bf16[2048,128]{1,0:T(8,128)(2,1)S(1)} collective-permute-done((bf16[2048,128]{1,0:T(8,128)(2,1)S(1)}, bf16[2048,128]{1,0:T(8,128)(2,1)S(1)}, u32[]{:S(2)}, u32[]{:S(2)}) %collective-permute-start.22) | collective-permute-done | bytes 524320 | tf_op jit(solution)/shard_map/ppermute | solution.py:456
  156.4 5.6 %collective-permute-done.27 = bf16[2048,128]{1,0:T(8,128)(2,1)S(1)} collective-permute-done((bf16[2048,128]{1,0:T(8,128)(2,1)S(1)}, bf16[2048,128]{1,0:T(8,128)(2,1)S(1)}, u32[]{:S(2)}, u32[]{:S(2)}) %collective-permute-start.27) | collective-permute-done | bytes 524320 | tf_op jit(solution)/shard_map/ppermute | solution.py:456
  162.0 1.5 maximum_convert_fusion
  (57 shorter events, 0.7 us)
Async XLA Ops:
  3.2 17.0 %copy-start.2 = (s32[2,1,1,64,256]{4,3,2,1,0:T(8,128)S(1)}, s32[2,1,1,64,256]{4,3,2,1,0:T(8,128)}, u32[]{:S(2)}) copy-start(s32[2,1,1,64,256]{4,3,2,1,0:T(8,128)} %refs_5_.7) | copy-start | bytes 393220
  3.2 17.0 %copy-start.10 = (s32[2,1]{1,0:T(2,128)S(1)}, s32[2,1]{1,0:T(2,128)}, u32[]{:S(2)}) copy-start(s32[2,1]{1,0:T(2,128)} %copy.19.refs_3_.owner_ref) | copy-start | bytes 28
  3.2 17.0 %copy-start.11 = (s32[2,1,1,64]{3,2,1,0:T(1,128)S(1)}, s32[2,1,1,64]{3,2,1,0:T(1,128)}, u32[]{:S(2)}) copy-start(s32[2,1,1,64]{3,2,1,0:T(1,128)} %refs_0_.7) | copy-start | bytes 1540
  3.2 17.0 %copy-start.12 = (s32[2,1,1,64]{3,2,1,0:T(1,128)S(1)}, s32[2,1,1,64]{3,2,1,0:T(1,128)}, u32[]{:S(2)}) copy-start(s32[2,1,1,64]{3,2,1,0:T(1,128)} %refs_1_.7) | copy-start | bytes 1540
  3.2 17.0 %copy-start.13 = (s32[2,1,1]{2,1,0:T(1,128)S(1)}, s32[2,1,1]{2,1,0:T(1,128)}, u32[]{:S(2)}) copy-start(s32[2,1,1]{2,1,0:T(1,128)} %copy.12.refs_2_) | copy-start | bytes 28
  17.0 16.7 %collective-permute-start.4 = (bf16[128,2176]{1,0:T(8,128)(2,1)}, bf16[128,2176]{1,0:T(8,128)(2,1)S(1)}, u32[]{:S(2)}, u32[]{:S(2)}) collective-permute-start(bf16[128,2176]{1,0:T(8,128)(2,1)} %get-tuple-element.85.refs_4_.refs_6_), channel_id=1, source_target_pairs={{0,1},{1,0},{2,3},{3,2},{4,5},{5,4},{6,7},{7,6},{8,9},{9,8},{10,11... | collective-permute-start | bytes 1671176 | tf_op jit(solution)/shard_map/ppermute | solution.py:446
  18.0 15.6 %collective-permute-start.5 = (bf16[128,2048]{1,0:T(8,128)(2,1)}, bf16[128,2048]{1,0:T(8,128)(2,1)S(1)}, u32[]{:S(2)}, u32[]{:S(2)}) collective-permute-start(bf16[128,2048]{1,0:T(8,128)(2,1)} %get-tuple-element.81), channel_id=1, source_target_pairs={{0,2},{1,3},{2,0},{3,1},{4,6},{5,7},{6,4},{7,5},{8,10},{9,11},{10,... | collective-permute-start | bytes 1572872 | tf_op jit(solution)/shard_map/ppermute | solution.py:446
  20.2 1.2 copy-start.7
  21.4 1.0 copy-start.8
  22.5 1.0 copy-start.9
  23.5 10.2 %copy-start.1 = (bf16[128,2176]{1,0:T(8,128)(2,1)S(1)}, bf16[128,2176]{1,0:T(8,128)(2,1)}, u32[]{:S(2)}) copy-start(bf16[128,2176]{1,0:T(8,128)(2,1)} %get-tuple-element.85.refs_4_.refs_6_) | copy-start | bytes 1671172
  23.5 10.2 %copy-start.3 = (bf16[128,2048]{1,0:T(8,128)(2,1)S(1)}, bf16[128,2048]{1,0:T(8,128)(2,1)}, u32[]{:S(2)}) copy-start(bf16[128,2048]{1,0:T(8,128)(2,1)} %get-tuple-element.77.refs_0_) | copy-start | bytes 1572868
  23.5 10.2 %copy-start.4 = (bf16[128,2048]{1,0:T(8,128)(2,1)S(1)}, bf16[128,2048]{1,0:T(8,128)(2,1)}, u32[]{:S(2)}) copy-start(bf16[128,2048]{1,0:T(8,128)(2,1)} %get-tuple-element.80.refs_2_.refs_3_) | copy-start | bytes 1572868
  33.6 4.3 %copy-start = (f32[2048,128]{1,0:T(8,128)S(1)}, f32[2048,128]{1,0:T(8,128)}, u32[]{:S(2)}) copy-start(f32[2048,128]{1,0:T(8,128)} %users.1) | copy-start | bytes 3145732
  33.7 4.3 %copy-start.5 = (bf16[128,8192]{1,0:T(8,128)(2,1)S(1)}, bf16[128,8192]{1,0:T(8,128)(2,1)}, u32[]{:S(2)}) copy-start(bf16[128,8192]{1,0:T(8,128)(2,1)} %get-tuple-element.62.refs_0_) | copy-start | bytes 6291460
  33.9 19.0 %collective-permute-start.6 = (bf16[128,1152]{1,0:T(8,128)(2,1)S(1)}, bf16[128,1152]{1,0:T(8,128)(2,1)S(1)}, u32[]{:S(2)}, u32[]{:S(2)}) collective-permute-start(bf16[128,1152]{1,0:T(8,128)(2,1)S(1)} %get-tuple-element.83), channel_id=1, source_target_pairs={{0,2},{1,3},{2,0},{3,1},{4,6},{5,7},{6,4},{7,5},{8,10},{9,11},{10,... | collective-permute-start | bytes 884744 | tf_op jit(solution)/shard_map/ppermute | solution.py:446
  33.9 24.2 %collective-permute-start = (bf16[128,2048]{1,0:T(8,128)(2,1)S(1)}, bf16[128,2048]{1,0:T(8,128)(2,1)S(1)}, u32[]{:S(2)}, u32[]{:S(2)}) collective-permute-start(bf16[128,2048]{1,0:T(8,128)(2,1)S(1)} %get-tuple-element.69), channel_id=1, source_target_pairs={{0,1},{1,0},{2,3},{3,2},{4,5},{5,4},{6,7},{7,6},{8,9},{9,8},{10,11... | collective-permute-start | bytes 1572872 | tf_op jit(solution)/shard_map/ppermute | solution.py:446
  34.9 23.3 %collective-permute-start.1 = (bf16[128,2048]{1,0:T(8,128)(2,1)S(1)}, bf16[128,2048]{1,0:T(8,128)(2,1)S(1)}, u32[]{:S(2)}, u32[]{:S(2)}) collective-permute-start(bf16[128,2048]{1,0:T(8,128)(2,1)S(1)} %get-tuple-element.72), channel_id=1, source_target_pairs={{0,2},{1,3},{2,0},{3,1},{4,6},{5,7},{6,4},{7,5},{8,10},{9,11},{10,... | collective-permute-start | bytes 1572872 | tf_op jit(solution)/shard_map/ppermute | solution.py:446
  36.0 16.9 %collective-permute-start.7 = (bf16[128,1024]{1,0:T(8,128)(2,1)S(1)}, bf16[128,1024]{1,0:T(8,128)(2,1)S(1)}, u32[]{:S(2)}, u32[]{:S(2)}) collective-permute-start(bf16[128,1024]{1,0:T(8,128)(2,1)S(1)} %get-tuple-element.84), channel_id=1, source_target_pairs={{0,1},{1,0},{2,3},{3,2},{4,5},{5,4},{6,7},{7,6},{8,9},{9,8},{10,11... | collective-permute-start | bytes 786440 | tf_op jit(solution)/shard_map/ppermute | solution.py:446
  38.0 14.9 %copy-start.6 = (f32[128,2048]{1,0:T(8,128)S(1)}, f32[128,2048]{1,0:T(8,128)}, u32[]{:S(2)}) copy-start(f32[128,2048]{1,0:T(8,128)} %get-tuple-element.76.items) | copy-start | bytes 3145732
  53.4 24.2 %collective-permute-start.8 = (bf16[128,2048]{1,0:T(8,128)(2,1)S(1)}, bf16[128,2048]{1,0:T(8,128)(2,1)S(1)}, u32[]{:S(2)}, u32[]{:S(2)}) collective-permute-start(bf16[128,2048]{1,0:T(8,128)(2,1)S(1)} %get-tuple-element.87), channel_id=1, source_target_pairs={{0,5},{1,4},{2,7},{3,6},{4,9},{5,8},{6,11},{7,10},{8,13},{9,12},{1... | collective-permute-start | bytes 1572872 | tf_op jit(solution)/shard_map/ppermute | solution.py:456
  53.5 24.2 %collective-permute-start.9 = (bf16[128,2048]{1,0:T(8,128)(2,1)S(1)}, bf16[128,2048]{1,0:T(8,128)(2,1)S(1)}, u32[]{:S(2)}, u32[]{:S(2)}) collective-permute-start(bf16[128,2048]{1,0:T(8,128)(2,1)S(1)} %get-tuple-element.87), channel_id=1, source_target_pairs={{0,6},{1,7},{2,4},{3,5},{4,10},{5,11},{6,8},{7,9},{8,14},{9,15},{1... | collective-permute-start | bytes 1572872 | tf_op jit(solution)/shard_map/ppermute | solution.py:456
  58.3 18.8 %collective-permute-start.2 = (bf16[128,1024]{1,0:T(8,128)(2,1)S(1)}, bf16[128,1024]{1,0:T(8,128)(2,1)S(1)}, u32[]{:S(2)}, u32[]{:S(2)}) collective-permute-start(bf16[128,1024]{1,0:T(8,128)(2,1)S(1)} %get-tuple-element.74), channel_id=1, source_target_pairs={{0,2},{1,3},{2,0},{3,1},{4,6},{5,7},{6,4},{7,5},{8,10},{9,11},{10,... | collective-permute-start | bytes 786440 | tf_op jit(solution)/shard_map/ppermute | solution.py:446
  58.9 18.2 %collective-permute-start.3 = (bf16[128,1024]{1,0:T(8,128)(2,1)S(1)}, bf16[128,1024]{1,0:T(8,128)(2,1)S(1)}, u32[]{:S(2)}, u32[]{:S(2)}) collective-permute-start(bf16[128,1024]{1,0:T(8,128)(2,1)S(1)} %get-tuple-element.75), channel_id=1, source_target_pairs={{0,1},{1,0},{2,3},{3,2},{4,5},{5,4},{6,7},{7,6},{8,9},{9,8},{10,11... | collective-permute-start | bytes 786440 | tf_op jit(solution)/shard_map/ppermute | solution.py:446
  60.2 21.3 %collective-permute-start.11 = (bf16[128,2048]{1,0:T(8,128)(2,1)S(1)}, bf16[128,2048]{1,0:T(8,128)(2,1)S(1)}, u32[]{:S(2)}, u32[]{:S(2)}) collective-permute-start(bf16[128,2048]{1,0:T(8,128)(2,1)S(1)} %get-tuple-element.87), channel_id=1, source_target_pairs={{0,4},{1,5},{2,6},{3,7},{4,8},{5,9},{6,10},{7,11},{8,12},{9,13},{1... | collective-permute-start | bytes 1572872 | tf_op jit(solution)/shard_map/ppermute | solution.py:456
  77.6 26.4 %collective-permute-start.14 = (bf16[128,2048]{1,0:T(8,128)(2,1)S(1)}, bf16[128,2048]{1,0:T(8,128)(2,1)S(1)}, u32[]{:S(2)}, u32[]{:S(2)}) collective-permute-start(bf16[128,2048]{1,0:T(8,128)(2,1)S(1)} %items_0_1.1), channel_id=1, source_target_pairs={{0,5},{1,4},{2,7},{3,6},{4,9},{5,8},{6,11},{7,10},{8,13},{9,12},{1... | collective-permute-start | bytes 1572872 | tf_op jit(solution)/shard_map/ppermute | solution.py:456
  77.7 26.3 %collective-permute-start.15 = (bf16[128,2048]{1,0:T(8,128)(2,1)S(1)}, bf16[128,2048]{1,0:T(8,128)(2,1)S(1)}, u32[]{:S(2)}, u32[]{:S(2)}) collective-permute-start(bf16[128,2048]{1,0:T(8,128)(2,1)S(1)} %items_0_1.1), channel_id=1, source_target_pairs={{0,6},{1,7},{2,4},{3,5},{4,10},{5,11},{6,8},{7,9},{8,14},{9,15},{1... | collective-permute-start | bytes 1572872 | tf_op jit(solution)/shard_map/ppermute | solution.py:456
  79.2 19.0 %collective-permute-start.12 = (bf16[128,1024]{1,0:T(8,128)(2,1)S(1)}, bf16[128,1024]{1,0:T(8,128)(2,1)S(1)}, u32[]{:S(2)}, u32[]{:S(2)}) collective-permute-start(bf16[128,1024]{1,0:T(8,128)(2,1)S(1)} %slice.16), channel_id=1, source_target_pairs={{0,2},{1,3},{2,0},{3,1},{4,6},{5,7},{6,4},{7,5},{8,10},{9,11},{10,... | collective-permute-start | bytes 786440 | tf_op jit(solution)/shard_map/ppermute | solution.py:446
  80.3 17.9 %collective-permute-start.13 = (bf16[128,1024]{1,0:T(8,128)(2,1)S(1)}, bf16[128,1024]{1,0:T(8,128)(2,1)S(1)}, u32[]{:S(2)}, u32[]{:S(2)}) collective-permute-start(bf16[128,1024]{1,0:T(8,128)(2,1)S(1)} %slice.17), channel_id=1, source_target_pairs={{0,1},{1,0},{2,3},{3,2},{4,5},{5,4},{6,7},{7,6},{8,9},{9,8},{10,11... | collective-permute-start | bytes 786440 | tf_op jit(solution)/shard_map/ppermute | solution.py:446
  81.5 26.9 %collective-permute-start.10 = (bf16[128,2048]{1,0:T(8,128)(2,1)S(1)}, bf16[128,2048]{1,0:T(8,128)(2,1)S(1)}, u32[]{:S(2)}, u32[]{:S(2)}) collective-permute-start(bf16[128,2048]{1,0:T(8,128)(2,1)S(1)} %items_0_1.1), channel_id=1, source_target_pairs={{0,4},{1,5},{2,6},{3,7},{4,8},{5,9},{6,10},{7,11},{8,12},{9,13},{1... | collective-permute-start | bytes 1572872 | tf_op jit(solution)/shard_map/ppermute | solution.py:456
  104.0 9.3 %collective-permute-start.16 = (bf16[128,1024]{1,0:T(8,128)(2,1)S(1)}, bf16[128,1024]{1,0:T(8,128)(2,1)S(1)}, u32[]{:S(2)}, u32[]{:S(2)}) collective-permute-start(bf16[128,1024]{1,0:T(8,128)(2,1)S(1)} %slice.14), channel_id=1, source_target_pairs={{0,2},{1,3},{2,0},{3,1},{4,6},{5,7},{6,4},{7,5},{8,10},{9,11},{10,... | collective-permute-start | bytes 786440 | tf_op jit(solution)/shard_map/ppermute | solution.py:446
  105.9 9.3 %collective-permute-start.17 = (bf16[128,1024]{1,0:T(8,128)(2,1)S(1)}, bf16[128,1024]{1,0:T(8,128)(2,1)S(1)}, u32[]{:S(2)}, u32[]{:S(2)}) collective-permute-start(bf16[128,1024]{1,0:T(8,128)(2,1)S(1)} %slice.15), channel_id=1, source_target_pairs={{0,1},{1,0},{2,3},{3,2},{4,5},{5,4},{6,7},{7,6},{8,9},{9,8},{10,11... | collective-permute-start | bytes 786440 | tf_op jit(solution)/shard_map/ppermute | solution.py:446
  107.2 19.1 %collective-permute-start.18 = (bf16[128,2176]{1,0:T(8,128)(2,1)S(1)}, bf16[128,2176]{1,0:T(8,128)(2,1)S(1)}, u32[]{:S(2)}, u32[]{:S(2)}) collective-permute-start(bf16[128,2176]{1,0:T(8,128)(2,1)S(1)} %get-tuple-element.103.refs_4_.refs_6_), channel_id=1, source_target_pairs={{0,1},{1,0},{2,3},{3,2},{4,5},{5,4},{6,7},{7,6},{8,9},{9,8},{10,11... | collective-permute-start | bytes 1671176 | tf_op jit(solution)/shard_map/ppermute | solution.py:446
  108.0 15.6 %collective-permute-start.19 = (bf16[128,2048]{1,0:T(8,128)(2,1)S(1)}, bf16[128,2048]{1,0:T(8,128)(2,1)S(1)}, u32[]{:S(2)}, u32[]{:S(2)}) collective-permute-start(bf16[128,2048]{1,0:T(8,128)(2,1)S(1)} %get-tuple-element.99), channel_id=1, source_target_pairs={{0,2},{1,3},{2,0},{3,1},{4,6},{5,7},{6,4},{7,5},{8,10},{9,11},{10,... | collective-permute-start | bytes 1572872 | tf_op jit(solution)/shard_map/ppermute | solution.py:446
  121.9 15.6 %collective-permute-start.23 = (bf16[128,2048]{1,0:T(8,128)(2,1)S(1)}, bf16[128,2048]{1,0:T(8,128)(2,1)S(1)}, u32[]{:S(2)}, u32[]{:S(2)}) collective-permute-start(bf16[128,2048]{1,0:T(8,128)(2,1)S(1)} %get-tuple-element.106), channel_id=1, source_target_pairs={{0,1},{1,0},{2,3},{3,2},{4,5},{5,4},{6,7},{7,6},{8,9},{9,8},{10,11... | collective-permute-start | bytes 1572872 | tf_op jit(solution)/shard_map/ppermute | solution.py:446
  122.5 15.1 %collective-permute-start.24 = (bf16[128,2048]{1,0:T(8,128)(2,1)S(1)}, bf16[128,2048]{1,0:T(8,128)(2,1)S(1)}, u32[]{:S(2)}, u32[]{:S(2)}) collective-permute-start(bf16[128,2048]{1,0:T(8,128)(2,1)S(1)} %get-tuple-element.109), channel_id=1, source_target_pairs={{0,2},{1,3},{2,0},{3,1},{4,6},{5,7},{6,4},{7,5},{8,10},{9,11},{10,... | collective-permute-start | bytes 1572872 | tf_op jit(solution)/shard_map/ppermute | solution.py:446
  126.4 18.9 %collective-permute-start.20 = (bf16[128,1152]{1,0:T(8,128)(2,1)S(1)}, bf16[128,1152]{1,0:T(8,128)(2,1)S(1)}, u32[]{:S(2)}, u32[]{:S(2)}) collective-permute-start(bf16[128,1152]{1,0:T(8,128)(2,1)S(1)} %get-tuple-element.101), channel_id=1, source_target_pairs={{0,2},{1,3},{2,0},{3,1},{4,6},{5,7},{6,4},{7,5},{8,10},{9,11},{10,... | collective-permute-start | bytes 884744 | tf_op jit(solution)/shard_map/ppermute | solution.py:446
  126.5 18.8 %collective-permute-start.21 = (bf16[128,1024]{1,0:T(8,128)(2,1)S(1)}, bf16[128,1024]{1,0:T(8,128)(2,1)S(1)}, u32[]{:S(2)}, u32[]{:S(2)}) collective-permute-start(bf16[128,1024]{1,0:T(8,128)(2,1)S(1)} %get-tuple-element.102), channel_id=1, source_target_pairs={{0,1},{1,0},{2,3},{3,2},{4,5},{5,4},{6,7},{7,6},{8,9},{9,8},{10,11... | collective-permute-start | bytes 786440 | tf_op jit(solution)/shard_map/ppermute | solution.py:446
  137.7 8.3 %collective-permute-start.25 = (bf16[128,1024]{1,0:T(8,128)(2,1)S(1)}, bf16[128,1024]{1,0:T(8,128)(2,1)S(1)}, u32[]{:S(2)}, u32[]{:S(2)}) collective-permute-start(bf16[128,1024]{1,0:T(8,128)(2,1)S(1)} %get-tuple-element.111), channel_id=1, source_target_pairs={{0,2},{1,3},{2,0},{3,1},{4,6},{5,7},{6,4},{7,5},{8,10},{9,11},{10,... | collective-permute-start | bytes 786440 | tf_op jit(solution)/shard_map/ppermute | solution.py:446
  138.6 7.4 %collective-permute-start.26 = (bf16[128,1024]{1,0:T(8,128)(2,1)S(1)}, bf16[128,1024]{1,0:T(8,128)(2,1)S(1)}, u32[]{:S(2)}, u32[]{:S(2)}) collective-permute-start(bf16[128,1024]{1,0:T(8,128)(2,1)S(1)} %get-tuple-element.112), channel_id=1, source_target_pairs={{0,1},{1,0},{2,3},{3,2},{4,5},{5,4},{6,7},{7,6},{8,9},{9,8},{10,11... | collective-permute-start | bytes 786440 | tf_op jit(solution)/shard_map/ppermute | solution.py:446
  145.9 10.5 %collective-permute-start.22 = (bf16[2048,128]{1,0:T(8,128)(2,1)S(1)}, bf16[2048,128]{1,0:T(8,128)(2,1)S(1)}, u32[]{:S(2)}, u32[]{:S(2)}) collective-permute-start(bf16[2048,128]{1,0:T(8,128)(2,1)S(1)} %get-tuple-element.104), channel_id=1, source_target_pairs={{0,4},{1,5},{2,6},{3,7},{4,8},{5,9},{6,10},{7,11},{8,12},{9,13},{1... | collective-permute-start | bytes 1572872 | tf_op jit(solution)/shard_map/ppermute | solution.py:456
  146.6 15.4 %collective-permute-start.27 = (bf16[2048,128]{1,0:T(8,128)(2,1)S(1)}, bf16[2048,128]{1,0:T(8,128)(2,1)S(1)}, u32[]{:S(2)}, u32[]{:S(2)}) collective-permute-start(bf16[2048,128]{1,0:T(8,128)(2,1)S(1)} %items_1_1.1), channel_id=1, source_target_pairs={{0,4},{1,5},{2,6},{3,7},{4,8},{5,9},{6,10},{7,11},{8,12},{9,13},{1... | collective-permute-start | bytes 1572872 | tf_op jit(solution)/shard_map/ppermute | solution.py:456

commit v4 on v3

--- a/solution.py
+++ b/solution.py
@@ -12,7 +12,6 @@
 GRAM = 256.0
 RIDGE = 1.0
 CHUNKS = 2
-START_MIB = 54
 F32 = jnp.float32
 BF16 = jnp.bfloat16
 BIG = float(jnp.finfo(jnp.bfloat16).max)
@@ -62,7 +61,7 @@
         out, refs[:n] = refs[:n], []
         return out
 
-    row_hbm, col_hbm, count_hbm, owner_hbm, ratings, mask_hbm = take(6)
+    row_hbm, col_hbm, plan_hbm, ratings, mask_hbm = take(5)
     users = take(1) if start_up else take(2)
     sources = take(pieces)
     grad_in = take(0 if first else 1)
@@ -74,8 +73,8 @@
         user_bf, user_t = take(2)
     else:
         user_bf, user_t = users
-    (row_ref, col_ref, count_ref, owner_ref, mask, parts, held, error_0, error_1,
-     slots, slot_row, slot_place, sem_tile, sem_item, sem_small) = take(15)
+    (row_ref, col_ref, plan_ref, mask, parts, held, error_0, error_1,
+     slots, slot_row, slot_place, sem_tile, sem_item, sem_small) = take(14)
     if epoch == 0:
         items_f, = take(1)
     else:
@@ -91,8 +90,8 @@
     bits_tile = chunk_tiles.bit_length() - 1
     bits_shard = shard_tiles.bit_length() - 1
 
-    pairs = [(row_hbm, row_ref), (col_hbm, col_ref), (count_hbm, count_ref),
-             (owner_hbm, owner_ref), (mask_hbm.at[epoch, 0, 0], mask)]
+    pairs = [(row_hbm, row_ref), (col_hbm, col_ref), (plan_hbm, plan_ref),
+             (mask_hbm.at[epoch, 0, 0], mask)]
     if not first:
         pairs.append((grad_in[0], grad_user))
     if start_up:
@@ -121,10 +120,10 @@
             at += width
     for copy in copies:
         copy.start()
-    for copy in small[:4]:
+    for copy in small[:3]:
         copy.wait()
 
-    count = count_ref[epoch, 0, 0]
+    count = plan_ref[0, epoch]
 
     def pick(t, found):
         col = col_ref[epoch, 0, 0, t]
@@ -148,7 +147,7 @@
     parts[...] = jnp.zeros_like(parts)
     if first:
         grad_user[...] = jnp.zeros_like(grad_user)
-    for copy in small[4:]:
+    for copy in small[3:]:
         copy.wait()
 
     def user_tile(j, _):
@@ -244,7 +243,7 @@
             send[:, k * width:(k + 1) * width] = parts[:, pl.ds(r * rows + start, width)].astype(BF16)
     if start_up:
         own = jnp.dot(user_t[...], user_bf[...], preferred_element_type=F32)
-        own = owned(own, users_f.shape[0], owner_ref[epoch, 0])
+        own = owned(own, users_f.shape[0], plan_ref[1, epoch])
     elif first:
         own = own_in[0][...]
     if first:
@@ -275,7 +274,7 @@
         out_shape += [sd((rank, members * rows), BF16), sd((rank, rows), F32)]
     if start_up:
         out_shape += [sd((user_rows, rank), BF16), sd((rank, user_rows), BF16)]
-    in_specs = [HBM] * 6 + ([HBM] if start_up else [VMEM] * 2)
+    in_specs = [HBM] * 5 + ([HBM] if start_up else [VMEM] * 2)
     in_specs += [HBM if epoch == 0 else ANY] * len(sources)
     operands = [*scalars, ratings, row_mask, *users, *sources]
     if not first:
@@ -293,7 +292,7 @@
         *[pltpu.SMEM((slots + 1,), jnp.int32)] * 3,
         pltpu.SemaphoreType.DMA((slots,)),
         pltpu.SemaphoreType.DMA((max(members, len(sources)),)),
-        pltpu.SemaphoreType.DMA((7,)),
+        pltpu.SemaphoreType.DMA((6,)),
     ]
     if epoch == 0:
         scratch.append(pltpu.VMEM((members * rows, rank), F32))
@@ -307,13 +306,13 @@
         in_specs=in_specs,
         out_specs=[VMEM] * len(out_shape),
         scratch_shapes=scratch,
-        compiler_params=params(START_MIB if start_up else 40),
+        compiler_params=params(40),
         cost_estimate=cost(1 << 20, 1 << 16),
         name=f"tiles_{epoch}_{chunk}",
     )(*operands)
 
 
-def user_kernel(epoch, block_rows, owner_ref, users, grad, *refs):
+def user_kernel(epoch, block_rows, plan_ref, users, grad, *refs):
     outs = 4 if epoch + 1 < SUB else 1
     pieces, outs = refs[:-outs], refs[-outs:]
     gram = over_rows(pieces[0][...], pieces[0][...])
@@ -329,10 +328,10 @@
         outs[1][...] = plain
         outs[2][...] = turned
         own = jnp.dot(turned, plain, preferred_element_type=F32)
-        outs[3][...] = owned(own, users.shape[0], owner_ref[epoch + 1, 0])
-
-
-def user_call(epoch, block_rows, owner_list, users, grad, pieces):
+        outs[3][...] = owned(own, users.shape[0], plan_ref[1, epoch + 1])
+
+
+def user_call(epoch, block_rows, plan, users, grad, pieces):
     rows, rank = users.shape
     sd = jax.ShapeDtypeStruct
     out_shape = [sd(users.shape, F32)]
@@ -346,7 +345,7 @@
         compiler_params=params(40),
         cost_estimate=cost(1 << 20, 1 << 16),
         name=f"users_{epoch}",
-    )(owner_list, users, grad, *pieces)
+    )(plan, users, grad, *pieces)
 
 
 def summed(refs, names, r, width):
@@ -522,11 +521,18 @@
     block_rows = item_factors.shape[0]
     shard_rows = block_rows // members
     rows = shard_rows // CHUNKS
-    scalars = (row_index, col_index, counts, owner_list)
+    plan = jnp.stack([counts[:, 0, 0], owner_list[:, 0]])
+    row_index, col_index, plan_hbm, row_mask, first_users, ratings, item_factors = (
+        pltpu.with_memory_space_constraint(array, pltpu.HBM)
+        for array in (
+            row_index, col_index, plan, row_mask, user_factors, ratings, item_factors
+        )
+    )
+    scalars = (row_index, col_index, plan_hbm)
     full_users = user_factors
-    users = [user_factors]
+    users = [first_users]
     own_gram = None
-    known = []
+    gathers = []
     for epoch in range(SUB):
         grad_user = None
         outs, olds, pieces = [], [], []
@@ -534,7 +540,8 @@
             if epoch == 0:
                 sources = [item_factors]
             else:
-                sources = gather_finish(known[c], [] if c == 0 else [grad_user])
+                known, sources = gathers[c]
+                sources = sources or gather_finish(known, [grad_user])
             out = tile_call(
                 epoch, c, members, scalars, ratings, row_mask, users, sources, grad_user, own_gram
             )
@@ -548,8 +555,10 @@
             else:
                 pieces += sources
                 olds.append(sources[0])
-        new_users = user_call(epoch, block_rows, owner_list, full_users, grad_user, pieces)
-        full_users = new_users[0]
+        last = epoch + 1 == SUB
+        if not last:
+            new_users = user_call(epoch, block_rows, plan, full_users, grad_user, pieces)
+            full_users = new_users[0]
         shards = []
         grams = None
         for c in range(CHUNKS):
@@ -557,18 +566,25 @@
                 epoch, c, outs[c], members, rows // 2, rows - rows // 2,
                 outs[min(c + 1, CHUNKS - 1)][4],
             )
-            if found:
+            if found and not last:
                 found[0] = tied(found[0], full_users)
             shard, gram = item_call(epoch, c, shard_rows, olds[c], terms_a, terms_b, found or grams)
             if found:
                 grams = [gram]
             shards.append(shard)
-        if epoch + 1 < SUB:
+        if last:
+            grad_user = tied(grad_user, *shards)
+            full_users = user_call(epoch, block_rows, plan, full_users, grad_user, pieces)[0]
+        else:
             users, own_gram = new_users[1:3], new_users[3]
-            known = []
+            gathers = []
             for shard in shards:
-                early = [piece for r, piece in known[-1].items() if r] if known else []
-                known.append(gather_start(tied(shard, *early)))
+                known = gather_start(tied(shard, *early) if gathers else shard)
+                if gathers:
+                    gathers.append((known, None))
+                else:
+                    gathers.append((known, gather_finish(known, [])))
+                early = [piece for r, piece in enumerate(gathers[0][1]) if r > 2]
     finals = [moved(shard, 0) for shard in shards]
     return full_users, jnp.concatenate(finals, axis=0).astype(F32)
 

time: 163 us -> 146 us (0.90); the launches traced: 163 us -> 144 us
  waiting for transfers between devices: 75.3 us -> 62.7 us
  local copies, waits for them, and re-layouts: 5.97 us -> 0.09 us
  Pallas kernels: 49.2 us -> 45 us
    ppermute x20, waiting for transfers between devices: 62.1 us -> 41.9 us  [swapped(): return lax.ppermute(value, 'grp', [(i, i ^ bit) for i in range(length)])]
    ppermute x8, waiting for transfers between devices: 13.2 us -> 20.8 us  [moved(): return lax.ppermute(value, ('blk', 'grp'), pairs)]
    unnamed x30 -> x6, local copies, waits for them, and re-layouts: 5.9 us -> 0.02 us
    pallas_call x4, Pallas kernels: 36.4 us -> 32.1 us  [tile_call(): pl.pallas_call(functools.partial(tile_kernel, epoch, chunk, members, shar...]
  transfers between devices with their start and end apart: 28 -> 28, of which waited for: 9 -> 20; matrix products, arithmetic and copies ran while one was open for 0% -> 0% of each run, Pallas kernels for 22% -> 23%
where the time goes in v4:
time: 146 us; the launch traced here: 144 us
  waiting for transfers between devices  62.7 us (43%)
  Pallas kernels  45 us (31%)
  starting transfers between devices  32.3 us (22%)
  other arithmetic  2.7 us (2%)
    ppermute x20, waiting for transfers between devices, swapped(): return lax.ppermute(value, 'grp', [(i, i ^ bit) for i in range(length)])  41.9 us
    pallas_call x4, Pallas kernels, tile_call(): pl.pallas_call(functools.partial(tile_kernel, epoch, chunk, members, shar...  32.1 us
    ppermute x20, starting transfers between devices, swapped(): return lax.ppermute(value, 'grp', [(i, i ^ bit) for i in range(length)])  23.7 us
    ppermute x8, waiting for transfers between devices, moved(): return lax.ppermute(value, ('blk', 'grp'), pairs)  20.8 us
    pallas_call x2, Pallas kernels, user_call(): pl.pallas_call(functools.partial(user_kernel, epoch, block_rows), out_sha...  10.1 us
    ppermute x8, starting transfers between devices, moved(): return lax.ppermute(value, ('blk', 'grp'), pairs)  8.65 us
  transfers between devices with their start and end apart: 28, of which 20 were waited for; matrix products, arithmetic and copies ran while one was open for 0% of the time, Pallas kernels for 23%

profile of v4, /device:TPU:0, one launch (start us, length us, event | category | flops | bytes accessed | tf_op | source)
XLA Modules:
  0.0 143.6 jit_solution(5407400602796121682)
XLA Ops:
  0.6 1.2 pad_add_fusion.refs_2_.plan_ref
  1.9 11.5 %tiles_0_0.1 = (bf16[128,2176]{1,0:T(8,128)(2,1)S(1)}, bf16[128,2048]{1,0:T(8,128)(2,1)S(1)}, bf16[128,2048]{1,0:T(8,128)(2,1)S(1)}, bf16[128,2048]{1,0:T(8,128)...) custom-call(s32[2,1,1,64]{3,2,1,0:T(1,128)} %refs_0_.7, ...), custom_call_target="tpu_custom_call" | custom-call | flops 1048576 | bytes 65536 | tf_op jit(solution)/shard_map/tiles_0_0/pallas_call | solution.py:303
  13.5 3.0 %collective-permute-start.5 = (bf16[128,2048]{1,0:T(8,128)(2,1)S(1)}, bf16[128,2048]{1,0:T(8,128)(2,1)S(1)}, u32[]{:S(2)}, u32[]{:S(2)}) collective-permute-start(bf16[128,2048]{1,0:T(8,128)(2,1)S(1)} %get-tuple-element.81), channel_id=1, source_target_pairs={{0,2},{1,3},{2,0},{3,1},{4,6},{5,7},{6,4},{7,5},{8,10},{9,11},{10,... | collective-permute-start | bytes 1572872 | tf_op jit(solution)/shard_map/ppermute | solution.py:445
  16.5 9.5 %tiles_0_1.1 = (bf16[128,2048]{1,0:T(8,128)(2,1)S(1)}, bf16[128,2048]{1,0:T(8,128)(2,1)S(1)}, bf16[128,2048]{1,0:T(8,128)(2,1)S(1)}, bf16[128,2048]{1,0:T(8,128)...) custom-call(s32[2,1,1,64]{3,2,1,0:T(1,128)} %refs_0_.7, ...), custom_call_target="tpu_custom_call" | custom-call | flops 1048576 | bytes 65536 | tf_op jit(solution)/shard_map/tiles_0_1/pallas_call | solution.py:303
  26.1 1.7 %collective-permute-done.5.refs_3_.refs_4_ = bf16[128,2048]{1,0:T(8,128)(2,1)S(1)} collective-permute-done((bf16[128,2048]{1,0:T(8,128)(2,1)S(1)}, bf16[128,2048]{1,0:T(8,128)(2,1)S(1)}, u32[]{:S(2)}, u32[]{:S(2)}) %collective-permute-start.5) | collective-permute-done | bytes 524320 | tf_op jit(solution)/shard_map/ppermute | solution.py:445
  28.3 0.9 collective-permute-start.7
  29.2 1.1 collective-permute-start
  30.3 1.8 %collective-permute-start.1 = (bf16[128,2048]{1,0:T(8,128)(2,1)S(1)}, bf16[128,2048]{1,0:T(8,128)(2,1)S(1)}, u32[]{:S(2)}, u32[]{:S(2)}) collective-permute-start(bf16[128,2048]{1,0:T(8,128)(2,1)S(1)} %get-tuple-element.72), channel_id=1, source_target_pairs={{0,2},{1,3},{2,0},{3,1},{4,6},{5,7},{6,4},{7,5},{8,10},{9,11},{10,... | collective-permute-start | bytes 1572872 | tf_op jit(solution)/shard_map/ppermute | solution.py:445
  32.1 4.8 %users_0.1 = (f32[2048,128]{1,0:T(8,128)S(1)}, bf16[2048,128]{1,0:T(8,128)(2,1)S(1)}, bf16[128,2048]{1,0:T(8,128)(2,1)S(1)}, bf16[128,128]{1,0:T(8,128)(2,1)S(1)}) custom-call(s32[2,2]{1,0:T(2,128)S(1)} %copy-done.1, f32[2048,128]{1,0:T(8,128)S(1)} %copy-done, f32[128,2048]{1,0:T(8,128)S(1)} %get-tuple-element.61.grad, ...), custom_call_target="tpu_custom_call" | custom-call | flops 1048576 | bytes 65536 | tf_op jit(solution)/shard_map/users_0/pallas_call | solution.py:340
  36.9 0.7 collective-permute-done.7.refs_5_
  38.0 0.6 items_0_0.1
  38.6 4.2 %collective-permute-start.10 = (bf16[128,2048]{1,0:T(8,128)(2,1)S(1)}, bf16[128,2048]{1,0:T(8,128)(2,1)S(1)}, u32[]{:S(2)}, u32[]{:S(2)}) collective-permute-start(bf16[128,2048]{1,0:T(8,128)(2,1)S(1)} %get-tuple-element.87), channel_id=1, source_target_pairs={{0,6},{1,7},{2,4},{3,5},{4,10},{5,11},{6,8},{7,9},{8,14},{9,15},{1... | collective-permute-start | bytes 1572872 | tf_op jit(solution)/shard_map/ppermute | solution.py:455
  42.8 9.5 %collective-permute-done.refs_1_ = bf16[128,2048]{1,0:T(8,128)(2,1)S(1)} collective-permute-done((bf16[128,2048]{1,0:T(8,128)(2,1)S(1)}, bf16[128,2048]{1,0:T(8,128)(2,1)S(1)}, u32[]{:S(2)}, u32[]{:S(2)}) %collective-permute-start) | collective-permute-done | bytes 524320 | tf_op jit(solution)/shard_map/ppermute | solution.py:445
  52.5 1.7 %collective-permute-start.2 = (bf16[128,1024]{1,0:T(8,128)(2,1)S(1)}, bf16[128,1024]{1,0:T(8,128)(2,1)S(1)}, u32[]{:S(2)}, u32[]{:S(2)}) collective-permute-start(bf16[128,1024]{1,0:T(8,128)(2,1)S(1)} %get-tuple-element.74), channel_id=1, source_target_pairs={{0,2},{1,3},{2,0},{3,1},{4,6},{5,7},{6,4},{7,5},{8,10},{9,11},{10,... | collective-permute-start | bytes 786440 | tf_op jit(solution)/shard_map/ppermute | solution.py:445
  54.2 1.7 %collective-permute-start.3 = (bf16[128,1024]{1,0:T(8,128)(2,1)S(1)}, bf16[128,1024]{1,0:T(8,128)(2,1)S(1)}, u32[]{:S(2)}, u32[]{:S(2)}) collective-permute-start(bf16[128,1024]{1,0:T(8,128)(2,1)S(1)} %get-tuple-element.75), channel_id=1, source_target_pairs={{0,1},{1,0},{2,3},{3,2},{4,5},{5,4},{6,7},{7,6},{8,9},{9,8},{10,11... | collective-permute-start | bytes 786440 | tf_op jit(solution)/shard_map/ppermute | solution.py:445
  56.0 3.9 %collective-permute-done.8.refs_8_.refs_1_ = bf16[128,2048]{1,0:T(8,128)(2,1)S(1)} collective-permute-done((bf16[128,2048]{1,0:T(8,128)(2,1)S(1)}, bf16[128,2048]{1,0:T(8,128)(2,1)S(1)}, u32[]{:S(2)}, u32[]{:S(2)}) %collective-permute-start.8) | collective-permute-done | bytes 524320 | tf_op jit(solution)/shard_map/ppermute | solution.py:455
  59.8 1.9 %collective-permute-start.9 = (bf16[128,1024]{1,0:T(8,128)(2,1)S(1)}, bf16[128,1024]{1,0:T(8,128)(2,1)S(1)}, u32[]{:S(2)}, u32[]{:S(2)}) collective-permute-start(bf16[128,1024]{1,0:T(8,128)(2,1)S(1)} %slice.16), channel_id=1, source_target_pairs={{0,2},{1,3},{2,0},{3,1},{4,6},{5,7},{6,4},{7,5},{8,10},{9,11},{10,... | collective-permute-start | bytes 786440 | tf_op jit(solution)/shard_map/ppermute | solution.py:445
  62.2 1.8 %collective-permute-start.13 = (bf16[128,2048]{1,0:T(8,128)(2,1)S(1)}, bf16[128,2048]{1,0:T(8,128)(2,1)S(1)}, u32[]{:S(2)}, u32[]{:S(2)}) collective-permute-start(bf16[128,2048]{1,0:T(8,128)(2,1)S(1)} %get-tuple-element.87), channel_id=1, source_target_pairs={{0,4},{1,5},{2,6},{3,7},{4,8},{5,9},{6,10},{7,11},{8,12},{9,13},{1... | collective-permute-start | bytes 1572872 | tf_op jit(solution)/shard_map/ppermute | solution.py:455
  63.9 0.6 items_0_1.1
  64.5 4.7 %collective-permute-done.9.refs_10_.refs_3_ = bf16[128,1024]{1,0:T(8,128)(2,1)S(1)} collective-permute-done((bf16[128,1024]{1,0:T(8,128)(2,1)S(1)}, bf16[128,1024]{1,0:T(8,128)(2,1)S(1)}, u32[]{:S(2)}, u32[]{:S(2)}) %collective-permute-start.9) | collective-permute-done | bytes 262176 | tf_op jit(solution)/shard_map/ppermute | solution.py:445
  69.2 1.4 collective-permute-done.11.refs_11_.refs_4_
  71.1 1.8 %collective-permute-start.15 = (bf16[128,2048]{1,0:T(8,128)(2,1)S(1)}, bf16[128,2048]{1,0:T(8,128)(2,1)S(1)}, u32[]{:S(2)}, u32[]{:S(2)}) collective-permute-start(bf16[128,2048]{1,0:T(8,128)(2,1)S(1)} %items_0_1.1), channel_id=1, source_target_pairs={{0,6},{1,7},{2,4},{3,5},{4,10},{5,11},{6,8},{7,9},{8,14},{9,15},{1... | collective-permute-start | bytes 1572872 | tf_op jit(solution)/shard_map/ppermute | solution.py:455
  73.2 5.9 %tiles_1_0.1 = (bf16[128,2176]{1,0:T(8,128)(2,1)S(1)}, bf16[128,2048]{1,0:T(8,128)(2,1)S(1)}, bf16[128,2048]{1,0:T(8,128)(2,1)S(1)}, bf16[128,2048]{1,0:T(8,128)(2,1)S(1)}, f32[128,2048]{1,0:T(8,128)S(1)}) custom-call(s32[2,1,1,64]{3,2,1,0:T(1,128)} %refs_0_.7, s32[2,1,1,64]{3,2,1,0:T(1,128)} %refs_1_.7, s32[2,2]{1,0:T(2,128)} %pad_add_fusion.refs_2_.plan_ref, ...), custom_call_target="tpu_custom_call" | custom-call | flops 1048576 | bytes 65536 | tf_op jit(solution)/shard_map/tiles_1_0/pallas_call | solution.py:303
  79.1 4.2 %collective-permute-done.14.refs_8_.refs_6_ = bf16[128,2048]{1,0:T(8,128)(2,1)S(1)} collective-permute-done((bf16[128,2048]{1,0:T(8,128)(2,1)S(1)}, bf16[128,2048]{1,0:T(8,128)(2,1)S(1)}, u32[]{:S(2)}, u32[]{:S(2)}) %collective-permute-start.14) | collective-permute-done | bytes 524320 | tf_op jit(solution)/shard_map/ppermute | solution.py:455
  83.4 4.0 %collective-permute-done.15.refs_9_.refs_7_ = bf16[128,2048]{1,0:T(8,128)(2,1)S(1)} collective-permute-done((bf16[128,2048]{1,0:T(8,128)(2,1)S(1)}, bf16[128,2048]{1,0:T(8,128)(2,1)S(1)}, u32[]{:S(2)}, u32[]{:S(2)}) %collective-permute-start.15) | collective-permute-done | bytes 524320 | tf_op jit(solution)/shard_map/ppermute | solution.py:455
  87.4 1.2 collective-permute-start.16
  88.6 1.2 collective-permute-start.17
  89.8 0.9 collective-permute-start.18
  90.7 0.9 collective-permute-start.19
  91.6 1.1 collective-permute-done.12.refs_7_.items.refs_5_
  92.7 4.0 %collective-permute-done.16.refs_10_.refs_8_ = bf16[128,1024]{1,0:T(8,128)(2,1)S(1)} collective-permute-done((bf16[128,1024]{1,0:T(8,128)(2,1)S(1)}, bf16[128,1024]{1,0:T(8,128)(2,1)S(1)}, u32[]{:S(2)}, u32[]{:S(2)}) %collective-permute-start.16) | collective-permute-done | bytes 262176 | tf_op jit(solution)/shard_map/ppermute | solution.py:445
  96.7 1.3 collective-permute-done.17.refs_11_.refs_9_
  98.0 5.1 %tiles_1_1.1 = (bf16[128,2048]{1,0:T(8,128)(2,1)S(1)}, bf16[128,2048]{1,0:T(8,128)(2,1)S(1)}, bf16[128,2048]{1,0:T(8,128)(2,1)S(1)}, bf16[128,2048]{1,0:T(8,128)(2,1)S(1)}, f32[128,2048]{1,0:T(8,128)S(1)}) custom-call(s32[2,1,1,64]{3,2,1,0:T(1,128)} %refs_0_.7, s32[2,1,1,64]{3,2,1,0:T(1,128)} %refs_1_.7, s32[2,2]{1,0:T(2,128)} %pad_add_fusion.refs_2_.plan_ref, ...), custom_call_target="tpu_custom_call" | custom-call | flops 1048576 | bytes 65536 | tf_op jit(solution)/shard_map/tiles_1_1/pallas_call | solution.py:303
  103.1 3.5 %collective-permute-start.22 = (bf16[128,2048]{1,0:T(8,128)(2,1)S(1)}, bf16[128,2048]{1,0:T(8,128)(2,1)S(1)}, u32[]{:S(2)}, u32[]{:S(2)}) collective-permute-start(bf16[128,2048]{1,0:T(8,128)(2,1)S(1)} %get-tuple-element.105), channel_id=1, source_target_pairs={{0,1},{1,0},{2,3},{3,2},{4,5},{5,4},{6,7},{7,6},{8,9},{9,8},{10,11... | collective-permute-start | bytes 1572872 | tf_op jit(solution)/shard_map/ppermute | solution.py:445
  106.6 3.3 %collective-permute-done.18.refs_1_.refs_5_.refs_7_ = bf16[128,2176]{1,0:T(8,128)(2,1)S(1)} collective-permute-done((bf16[128,2176]{1,0:T(8,128)(2,1)S(1)}, bf16[128,2176]{1,0:T(8,128)(2,1)S(1)}, u32[]{:S(2)}, u32[]{:S(2)}) %collective-permute-start.18) | collective-permute-done | bytes 557088 | tf_op jit(solution)/shard_map/ppermute | solution.py:445
  110.0 0.9 collective-permute-start.20
  111.0 0.6 collective-permute-start.21
  111.5 9.6 %collective-permute-done.22.refs_1_ = bf16[128,2048]{1,0:T(8,128)(2,1)S(1)} collective-permute-done((bf16[128,2048]{1,0:T(8,128)(2,1)S(1)}, bf16[128,2048]{1,0:T(8,128)(2,1)S(1)}, u32[]{:S(2)}, u32[]{:S(2)}) %collective-permute-start.22) | collective-permute-done | bytes 524320 | tf_op jit(solution)/shard_map/ppermute | solution.py:445
  121.6 0.6 collective-permute-start.24
  122.2 0.9 collective-permute-start.25
  123.1 2.4 %collective-permute-done.21.refs_5_ = bf16[128,1024]{1,0:T(8,128)(2,1)S(1)} collective-permute-done((bf16[128,1024]{1,0:T(8,128)(2,1)S(1)}, bf16[128,1024]{1,0:T(8,128)(2,1)S(1)}, u32[]{:S(2)}, u32[]{:S(2)}) %collective-permute-start.21) | collective-permute-done | bytes 262176 | tf_op jit(solution)/shard_map/ppermute | solution.py:445
  125.5 0.6 items_1_0.1
  126.1 2.1 %collective-permute-done.24.refs_2_ = bf16[128,1024]{1,0:T(8,128)(2,1)S(1)} collective-permute-done((bf16[128,1024]{1,0:T(8,128)(2,1)S(1)}, bf16[128,1024]{1,0:T(8,128)(2,1)S(1)}, u32[]{:S(2)}, u32[]{:S(2)}) %collective-permute-start.24) | collective-permute-done | bytes 262176 | tf_op jit(solution)/shard_map/ppermute | solution.py:445
  128.6 0.5 items_1_1.1
  129.2 5.3 %users_1.1 = f32[2048,128]{1,0:T(8,128)} custom-call(s32[2,2]{1,0:T(2,128)S(1)} %copy-done.2, f32[2048,128]{1,0:T(8,128)S(1)} %get-tuple-element.64.users, f32[128,2048]{1,0:T(8,128)S(1)} %get-tuple-element.113.grad, bf16[128,2048]{1,0:T(8,128)(2,1)S(1)} %collective-permute-done.13.refs_7_.items.refs_0_, ...), custom_call_target="tpu_custom_call" | custom-call | flops 1048576 | bytes 65536 | tf_op jit(solution)/shard_map/users_1/pallas_call | solution.py:340
  134.5 2.0 %collective-permute-done.26 = bf16[2048,128]{1,0:T(8,128)(2,1)S(1)} collective-permute-done((bf16[2048,128]{1,0:T(8,128)(2,1)S(1)}, bf16[2048,128]{1,0:T(8,128)(2,1)S(1)}, u32[]{:S(2)}, u32[]{:S(2)}) %collective-permute-start.26) | collective-permute-done | bytes 524320 | tf_op jit(solution)/shard_map/ppermute | solution.py:455
  136.5 5.6 %collective-permute-done.27 = bf16[2048,128]{1,0:T(8,128)(2,1)S(1)} collective-permute-done((bf16[2048,128]{1,0:T(8,128)(2,1)S(1)}, bf16[2048,128]{1,0:T(8,128)(2,1)S(1)}, u32[]{:S(2)}, u32[]{:S(2)}) %collective-permute-start.27) | collective-permute-done | bytes 524320 | tf_op jit(solution)/shard_map/ppermute | solution.py:455
  142.1 1.5 %maximum_convert_fusion = f32[4096,128]{1,0:T(8,128)} fusion(bf16[2048,128]{1,0:T(8,128)(2,1)S(1)} %collective-permute-done.27, bf16[2048,128]{1,0:T(8,128)(2,1)S(1)} %collective-permute-done.26), kind=kLoop, calls=%fused_computation | loop fusion | flops 2097152 | bytes 3145728 | tf_op jit(solution)/shard_map/convert_element_type | solution.py:589
  (34 shorter events, 3.5 us)
Async XLA Ops:
  13.4 14.4 %collective-permute-start.4 = (bf16[128,2176]{1,0:T(8,128)(2,1)S(1)}, bf16[128,2176]{1,0:T(8,128)(2,1)S(1)}, u32[]{:S(2)}, u32[]{:S(2)}) collective-permute-start(bf16[128,2176]{1,0:T(8,128)(2,1)S(1)} %get-tuple-element.85.refs_4_.refs_6_), channel_id=1, source_target_pairs={{0,1},{1,0},{2,3},{3,2},{4,5},{5,4},{6,7},{7,6},{8,9},{9,8},{10,11... | collective-permute-start | bytes 1671176 | tf_op jit(solution)/shard_map/ppermute | solution.py:445
  13.5 14.3 %collective-permute-start.5 = (bf16[128,2048]{1,0:T(8,128)(2,1)S(1)}, bf16[128,2048]{1,0:T(8,128)(2,1)S(1)}, u32[]{:S(2)}, u32[]{:S(2)}) collective-permute-start(bf16[128,2048]{1,0:T(8,128)(2,1)S(1)} %get-tuple-element.81), channel_id=1, source_target_pairs={{0,2},{1,3},{2,0},{3,1},{4,6},{5,7},{6,4},{7,5},{8,10},{9,11},{10,... | collective-permute-start | bytes 1572872 | tf_op jit(solution)/shard_map/ppermute | solution.py:445
  26.1 6.0 %copy-start = (f32[2048,128]{1,0:T(8,128)S(1)}, f32[2048,128]{1,0:T(8,128)}, u32[]{:S(2)}) copy-start(f32[2048,128]{1,0:T(8,128)} %users.1) | copy-start | bytes 3145732
  26.1 6.0 %copy-start.1 = (s32[2,2]{1,0:T(2,128)S(1)}, s32[2,2]{1,0:T(2,128)}, u32[]{:S(2)}) copy-start(s32[2,2]{1,0:T(2,128)} %pad_add_fusion.refs_2_.plan_ref) | copy-start | bytes 52
  28.0 10.0 %collective-permute-start.6 = (bf16[128,1152]{1,0:T(8,128)(2,1)S(1)}, bf16[128,1152]{1,0:T(8,128)(2,1)S(1)}, u32[]{:S(2)}, u32[]{:S(2)}) collective-permute-start(bf16[128,1152]{1,0:T(8,128)(2,1)S(1)} %get-tuple-element.83), channel_id=1, source_target_pairs={{0,2},{1,3},{2,0},{3,1},{4,6},{5,7},{6,4},{7,5},{8,10},{9,11},{10,... | collective-permute-start | bytes 884744 | tf_op jit(solution)/shard_map/ppermute | solution.py:445
  28.3 9.2 %collective-permute-start.7 = (bf16[128,1024]{1,0:T(8,128)(2,1)S(1)}, bf16[128,1024]{1,0:T(8,128)(2,1)S(1)}, u32[]{:S(2)}, u32[]{:S(2)}) collective-permute-start(bf16[128,1024]{1,0:T(8,128)(2,1)S(1)} %get-tuple-element.84), channel_id=1, source_target_pairs={{0,1},{1,0},{2,3},{3,2},{4,5},{5,4},{6,7},{7,6},{8,9},{9,8},{10,11... | collective-permute-start | bytes 786440 | tf_op jit(solution)/shard_map/ppermute | solution.py:445
  29.2 23.1 %collective-permute-start = (bf16[128,2048]{1,0:T(8,128)(2,1)S(1)}, bf16[128,2048]{1,0:T(8,128)(2,1)S(1)}, u32[]{:S(2)}, u32[]{:S(2)}) collective-permute-start(bf16[128,2048]{1,0:T(8,128)(2,1)S(1)} %get-tuple-element.69), channel_id=1, source_target_pairs={{0,1},{1,0},{2,3},{3,2},{4,5},{5,4},{6,7},{7,6},{8,9},{9,8},{10,11... | collective-permute-start | bytes 1572872 | tf_op jit(solution)/shard_map/ppermute | solution.py:445
  30.3 22.0 %collective-permute-start.1 = (bf16[128,2048]{1,0:T(8,128)(2,1)S(1)}, bf16[128,2048]{1,0:T(8,128)(2,1)S(1)}, u32[]{:S(2)}, u32[]{:S(2)}) collective-permute-start(bf16[128,2048]{1,0:T(8,128)(2,1)S(1)} %get-tuple-element.72), channel_id=1, source_target_pairs={{0,2},{1,3},{2,0},{3,1},{4,6},{5,7},{6,4},{7,5},{8,10},{9,11},{10,... | collective-permute-start | bytes 1572872 | tf_op jit(solution)/shard_map/ppermute | solution.py:445
  38.6 21.3 %collective-permute-start.8 = (bf16[128,2048]{1,0:T(8,128)(2,1)S(1)}, bf16[128,2048]{1,0:T(8,128)(2,1)S(1)}, u32[]{:S(2)}, u32[]{:S(2)}) collective-permute-start(bf16[128,2048]{1,0:T(8,128)(2,1)S(1)} %get-tuple-element.87), channel_id=1, source_target_pairs={{0,5},{1,4},{2,7},{3,6},{4,9},{5,8},{6,11},{7,10},{8,13},{9,12},{1... | collective-permute-start | bytes 1572872 | tf_op jit(solution)/shard_map/ppermute | solution.py:455
  38.6 23.1 %collective-permute-start.10 = (bf16[128,2048]{1,0:T(8,128)(2,1)S(1)}, bf16[128,2048]{1,0:T(8,128)(2,1)S(1)}, u32[]{:S(2)}, u32[]{:S(2)}) collective-permute-start(bf16[128,2048]{1,0:T(8,128)(2,1)S(1)} %get-tuple-element.87), channel_id=1, source_target_pairs={{0,6},{1,7},{2,4},{3,5},{4,10},{5,11},{6,8},{7,9},{8,14},{9,15},{1... | collective-permute-start | bytes 1572872 | tf_op jit(solution)/shard_map/ppermute | solution.py:455
  52.5 11.4 %collective-permute-start.2 = (bf16[128,1024]{1,0:T(8,128)(2,1)S(1)}, bf16[128,1024]{1,0:T(8,128)(2,1)S(1)}, u32[]{:S(2)}, u32[]{:S(2)}) collective-permute-start(bf16[128,1024]{1,0:T(8,128)(2,1)S(1)} %get-tuple-element.74), channel_id=1, source_target_pairs={{0,2},{1,3},{2,0},{3,1},{4,6},{5,7},{6,4},{7,5},{8,10},{9,11},{10,... | collective-permute-start | bytes 786440 | tf_op jit(solution)/shard_map/ppermute | solution.py:445
  54.2 9.7 %collective-permute-start.3 = (bf16[128,1024]{1,0:T(8,128)(2,1)S(1)}, bf16[128,1024]{1,0:T(8,128)(2,1)S(1)}, u32[]{:S(2)}, u32[]{:S(2)}) collective-permute-start(bf16[128,1024]{1,0:T(8,128)(2,1)S(1)} %get-tuple-element.75), channel_id=1, source_target_pairs={{0,1},{1,0},{2,3},{3,2},{4,5},{5,4},{6,7},{7,6},{8,9},{9,8},{10,11... | collective-permute-start | bytes 786440 | tf_op jit(solution)/shard_map/ppermute | solution.py:445
  59.8 9.4 %collective-permute-start.9 = (bf16[128,1024]{1,0:T(8,128)(2,1)S(1)}, bf16[128,1024]{1,0:T(8,128)(2,1)S(1)}, u32[]{:S(2)}, u32[]{:S(2)}) collective-permute-start(bf16[128,1024]{1,0:T(8,128)(2,1)S(1)} %slice.16), channel_id=1, source_target_pairs={{0,2},{1,3},{2,0},{3,1},{4,6},{5,7},{6,4},{7,5},{8,10},{9,11},{10,... | collective-permute-start | bytes 786440 | tf_op jit(solution)/shard_map/ppermute | solution.py:445
  61.8 8.9 %collective-permute-start.11 = (bf16[128,1024]{1,0:T(8,128)(2,1)S(1)}, bf16[128,1024]{1,0:T(8,128)(2,1)S(1)}, u32[]{:S(2)}, u32[]{:S(2)}) collective-permute-start(bf16[128,1024]{1,0:T(8,128)(2,1)S(1)} %slice.17), channel_id=1, source_target_pairs={{0,1},{1,0},{2,3},{3,2},{4,5},{5,4},{6,7},{7,6},{8,9},{9,8},{10,11... | collective-permute-start | bytes 786440 | tf_op jit(solution)/shard_map/ppermute | solution.py:445
  62.2 11.0 %collective-permute-start.13 = (bf16[128,2048]{1,0:T(8,128)(2,1)S(1)}, bf16[128,2048]{1,0:T(8,128)(2,1)S(1)}, u32[]{:S(2)}, u32[]{:S(2)}) collective-permute-start(bf16[128,2048]{1,0:T(8,128)(2,1)S(1)} %get-tuple-element.87), channel_id=1, source_target_pairs={{0,4},{1,5},{2,6},{3,7},{4,8},{5,9},{6,10},{7,11},{8,12},{9,13},{1... | collective-permute-start | bytes 1572872 | tf_op jit(solution)/shard_map/ppermute | solution.py:455
  70.7 12.7 %collective-permute-start.14 = (bf16[128,2048]{1,0:T(8,128)(2,1)S(1)}, bf16[128,2048]{1,0:T(8,128)(2,1)S(1)}, u32[]{:S(2)}, u32[]{:S(2)}) collective-permute-start(bf16[128,2048]{1,0:T(8,128)(2,1)S(1)} %items_0_1.1), channel_id=1, source_target_pairs={{0,5},{1,4},{2,7},{3,6},{4,9},{5,8},{6,11},{7,10},{8,13},{9,12},{1... | collective-permute-start | bytes 1572872 | tf_op jit(solution)/shard_map/ppermute | solution.py:455
  71.1 16.3 %collective-permute-start.15 = (bf16[128,2048]{1,0:T(8,128)(2,1)S(1)}, bf16[128,2048]{1,0:T(8,128)(2,1)S(1)}, u32[]{:S(2)}, u32[]{:S(2)}) collective-permute-start(bf16[128,2048]{1,0:T(8,128)(2,1)S(1)} %items_0_1.1), channel_id=1, source_target_pairs={{0,6},{1,7},{2,4},{3,5},{4,10},{5,11},{6,8},{7,9},{8,14},{9,15},{1... | collective-permute-start | bytes 1572872 | tf_op jit(solution)/shard_map/ppermute | solution.py:455
  72.8 19.9 %collective-permute-start.12 = (bf16[128,2048]{1,0:T(8,128)(2,1)S(1)}, bf16[128,2048]{1,0:T(8,128)(2,1)S(1)}, u32[]{:S(2)}, u32[]{:S(2)}) collective-permute-start(bf16[128,2048]{1,0:T(8,128)(2,1)S(1)} %items_0_1.1), channel_id=1, source_target_pairs={{0,4},{1,5},{2,6},{3,7},{4,8},{5,9},{6,10},{7,11},{8,12},{9,13},{1... | collective-permute-start | bytes 1572872 | tf_op jit(solution)/shard_map/ppermute | solution.py:455
  87.4 9.3 %collective-permute-start.16 = (bf16[128,1024]{1,0:T(8,128)(2,1)S(1)}, bf16[128,1024]{1,0:T(8,128)(2,1)S(1)}, u32[]{:S(2)}, u32[]{:S(2)}) collective-permute-start(bf16[128,1024]{1,0:T(8,128)(2,1)S(1)} %slice.14), channel_id=1, source_target_pairs={{0,2},{1,3},{2,0},{3,1},{4,6},{5,7},{6,4},{7,5},{8,10},{9,11},{10,... | collective-permute-start | bytes 786440 | tf_op jit(solution)/shard_map/ppermute | solution.py:445
  88.6 9.3 %collective-permute-start.17 = (bf16[128,1024]{1,0:T(8,128)(2,1)S(1)}, bf16[128,1024]{1,0:T(8,128)(2,1)S(1)}, u32[]{:S(2)}, u32[]{:S(2)}) collective-permute-start(bf16[128,1024]{1,0:T(8,128)(2,1)S(1)} %slice.15), channel_id=1, source_target_pairs={{0,1},{1,0},{2,3},{3,2},{4,5},{5,4},{6,7},{7,6},{8,9},{9,8},{10,11... | collective-permute-start | bytes 786440 | tf_op jit(solution)/shard_map/ppermute | solution.py:445
  89.8 20.1 %collective-permute-start.18 = (bf16[128,2176]{1,0:T(8,128)(2,1)S(1)}, bf16[128,2176]{1,0:T(8,128)(2,1)S(1)}, u32[]{:S(2)}, u32[]{:S(2)}) collective-permute-start(bf16[128,2176]{1,0:T(8,128)(2,1)S(1)} %get-tuple-element.96.refs_4_.refs_6_), channel_id=1, source_target_pairs={{0,1},{1,0},{2,3},{3,2},{4,5},{5,4},{6,7},{7,6},{8,9},{9,8},{10,11... | collective-permute-start | bytes 1671176 | tf_op jit(solution)/shard_map/ppermute | solution.py:445
  90.7 19.2 %collective-permute-start.19 = (bf16[128,2048]{1,0:T(8,128)(2,1)S(1)}, bf16[128,2048]{1,0:T(8,128)(2,1)S(1)}, u32[]{:S(2)}, u32[]{:S(2)}) collective-permute-start(bf16[128,2048]{1,0:T(8,128)(2,1)S(1)} %get-tuple-element.99), channel_id=1, source_target_pairs={{0,2},{1,3},{2,0},{3,1},{4,6},{5,7},{6,4},{7,5},{8,10},{9,11},{10,... | collective-permute-start | bytes 1572872 | tf_op jit(solution)/shard_map/ppermute | solution.py:445
  103.1 18.1 %collective-permute-start.22 = (bf16[128,2048]{1,0:T(8,128)(2,1)S(1)}, bf16[128,2048]{1,0:T(8,128)(2,1)S(1)}, u32[]{:S(2)}, u32[]{:S(2)}) collective-permute-start(bf16[128,2048]{1,0:T(8,128)(2,1)S(1)} %get-tuple-element.105), channel_id=1, source_target_pairs={{0,1},{1,0},{2,3},{3,2},{4,5},{5,4},{6,7},{7,6},{8,9},{9,8},{10,11... | collective-permute-start | bytes 1572872 | tf_op jit(solution)/shard_map/ppermute | solution.py:445
  106.6 14.9 %collective-permute-start.23 = (bf16[128,2048]{1,0:T(8,128)(2,1)S(1)}, bf16[128,2048]{1,0:T(8,128)(2,1)S(1)}, u32[]{:S(2)}, u32[]{:S(2)}) collective-permute-start(bf16[128,2048]{1,0:T(8,128)(2,1)S(1)} %get-tuple-element.108), channel_id=1, source_target_pairs={{0,2},{1,3},{2,0},{3,1},{4,6},{5,7},{6,4},{7,5},{8,10},{9,11},{10,... | collective-permute-start | bytes 1572872 | tf_op jit(solution)/shard_map/ppermute | solution.py:445
  110.0 15.4 %collective-permute-start.20 = (bf16[128,1152]{1,0:T(8,128)(2,1)S(1)}, bf16[128,1152]{1,0:T(8,128)(2,1)S(1)}, u32[]{:S(2)}, u32[]{:S(2)}) collective-permute-start(bf16[128,1152]{1,0:T(8,128)(2,1)S(1)} %get-tuple-element.101), channel_id=1, source_target_pairs={{0,2},{1,3},{2,0},{3,1},{4,6},{5,7},{6,4},{7,5},{8,10},{9,11},{10,... | collective-permute-start | bytes 884744 | tf_op jit(solution)/shard_map/ppermute | solution.py:445
  111.0 14.5 %collective-permute-start.21 = (bf16[128,1024]{1,0:T(8,128)(2,1)S(1)}, bf16[128,1024]{1,0:T(8,128)(2,1)S(1)}, u32[]{:S(2)}, u32[]{:S(2)}) collective-permute-start(bf16[128,1024]{1,0:T(8,128)(2,1)S(1)} %get-tuple-element.102), channel_id=1, source_target_pairs={{0,1},{1,0},{2,3},{3,2},{4,5},{5,4},{6,7},{7,6},{8,9},{9,8},{10,11... | collective-permute-start | bytes 786440 | tf_op jit(solution)/shard_map/ppermute | solution.py:445
  121.6 6.6 %collective-permute-start.24 = (bf16[128,1024]{1,0:T(8,128)(2,1)S(1)}, bf16[128,1024]{1,0:T(8,128)(2,1)S(1)}, u32[]{:S(2)}, u32[]{:S(2)}) collective-permute-start(bf16[128,1024]{1,0:T(8,128)(2,1)S(1)} %get-tuple-element.110), channel_id=1, source_target_pairs={{0,2},{1,3},{2,0},{3,1},{4,6},{5,7},{6,4},{7,5},{8,10},{9,11},{10,... | collective-permute-start | bytes 786440 | tf_op jit(solution)/shard_map/ppermute | solution.py:445
  122.2 6.4 %collective-permute-start.25 = (bf16[128,1024]{1,0:T(8,128)(2,1)S(1)}, bf16[128,1024]{1,0:T(8,128)(2,1)S(1)}, u32[]{:S(2)}, u32[]{:S(2)}) collective-permute-start(bf16[128,1024]{1,0:T(8,128)(2,1)S(1)} %get-tuple-element.111), channel_id=1, source_target_pairs={{0,1},{1,0},{2,3},{3,2},{4,5},{5,4},{6,7},{7,6},{8,9},{9,8},{10,11... | collective-permute-start | bytes 786440 | tf_op jit(solution)/shard_map/ppermute | solution.py:445
  126.0 3.1 %copy-start.2 = (s32[2,2]{1,0:T(2,128)S(1)}, s32[2,2]{1,0:T(2,128)}, u32[]{:S(2)}) copy-start(s32[2,2]{1,0:T(2,128)} %pad_add_fusion.refs_2_.plan_ref) | copy-start | bytes 52
  126.0 10.5 %collective-permute-start.26 = (bf16[2048,128]{1,0:T(8,128)(2,1)S(1)}, bf16[2048,128]{1,0:T(8,128)(2,1)S(1)}, u32[]{:S(2)}, u32[]{:S(2)}) collective-permute-start(bf16[2048,128]{1,0:T(8,128)(2,1)S(1)} %get-tuple-element.103), channel_id=1, source_target_pairs={{0,4},{1,5},{2,6},{3,7},{4,8},{5,9},{6,10},{7,11},{8,12},{9,13},{1... | collective-permute-start | bytes 1572872 | tf_op jit(solution)/shard_map/ppermute | solution.py:455
  129.1 13.0 %collective-permute-start.27 = (bf16[2048,128]{1,0:T(8,128)(2,1)S(1)}, bf16[2048,128]{1,0:T(8,128)(2,1)S(1)}, u32[]{:S(2)}, u32[]{:S(2)}) collective-permute-start(bf16[2048,128]{1,0:T(8,128)(2,1)S(1)} %items_1_1.1), channel_id=1, source_target_pairs={{0,4},{1,5},{2,6},{3,7},{4,8},{5,9},{6,10},{7,11},{8,12},{9,13},{1... | collective-permute-start | bytes 1572872 | tf_op jit(solution)/shard_map/ppermute | solution.py:455

commit v5 on v4

--- a/solution.py
+++ b/solution.py
@@ -12,6 +12,7 @@
 GRAM = 256.0
 RIDGE = 1.0
 CHUNKS = 2
+WIDE = 4
 F32 = jnp.float32
 BF16 = jnp.bfloat16
 BIG = float(jnp.finfo(jnp.bfloat16).max)
@@ -61,7 +62,7 @@
         out, refs[:n] = refs[:n], []
         return out
 
-    row_hbm, col_hbm, plan_hbm, ratings, mask_hbm = take(5)
+    row_hbm, col_hbm, count_hbm, owner_hbm, ratings, mask_hbm = take(6)
     users = take(1) if start_up else take(2)
     sources = take(pieces)
     grad_in = take(0 if first else 1)
@@ -73,15 +74,15 @@
         user_bf, user_t = take(2)
     else:
         user_bf, user_t = users
-    (row_ref, col_ref, plan_ref, mask, parts, held, error_0, error_1,
-     slots, slot_row, slot_place, sem_tile, sem_item, sem_small) = take(14)
+    (row_ref, col_ref, count_ref, owner_ref, mask, parts, held, slots, slot_row, slot_place,
+     sem_tile, sem_item, sem_small) = take(13)
+    errors = take(WIDE)
     if epoch == 0:
         items_f, = take(1)
     else:
         items, = take(1)
     if start_up:
         users_f, = take(1)
-    errors = (error_0, error_1)
 
     me = lax.axis_index("grp")
     chunk_tiles = shard_tiles // CHUNKS
@@ -90,8 +91,8 @@
     bits_tile = chunk_tiles.bit_length() - 1
     bits_shard = shard_tiles.bit_length() - 1
 
-    pairs = [(row_hbm, row_ref), (col_hbm, col_ref), (plan_hbm, plan_ref),
-             (mask_hbm.at[epoch, 0, 0], mask)]
+    pairs = [(row_hbm, row_ref), (col_hbm, col_ref), (count_hbm, count_ref),
+             (owner_hbm, owner_ref), (mask_hbm.at[epoch, 0, 0], mask)]
     if not first:
         pairs.append((grad_in[0], grad_user))
     if start_up:
@@ -120,10 +121,10 @@
             at += width
     for copy in copies:
         copy.start()
-    for copy in small[:3]:
+    for copy in small[:4]:
         copy.wait()
 
-    count = plan_ref[0, epoch]
+    count = count_ref[0, epoch]
 
     def pick(t, found):
         col = col_ref[epoch, 0, 0, t]
@@ -147,14 +148,14 @@
     parts[...] = jnp.zeros_like(parts)
     if first:
         grad_user[...] = jnp.zeros_like(grad_user)
-    for copy in small[3:]:
+    for copy in small[4:]:
         copy.wait()
 
     def user_tile(j, _):
         spot = pl.ds(pl.multiple_of(j * tile, tile), tile)
-        part = users_f[spot]
-        user_bf[spot] = part.astype(BF16)
-        user_t[:, spot] = part.T.astype(BF16)
+        part = users_f[spot].astype(BF16)
+        user_bf[spot] = part
+        user_t[:, spot] = part.T
         return 0
 
     if start_up:
@@ -162,10 +163,9 @@
 
     def item_tile(own, j, _):
         spot = pl.ds(pl.multiple_of(j * tile, tile), tile)
-        turned = items_f[spot].T
-        items[:, spot] = turned.astype(BF16)
+        items[:, spot] = items_f[spot].astype(BF16).T
         if own:
-            old[:, spot] = turned
+            old[:, spot] = items_f[spot].T
         return 0
 
     for r, copy in enumerate(copies):
@@ -182,16 +182,16 @@
         return pl.ds(row, tile), pl.ds(place, tile)
 
     def ready(j):
-        for k in range(2):
-            i = 2 * j + k
+        for k in range(WIDE):
+            i = WIDE * j + k
 
             @pl.when(i < total)
             def _():
                 fetch(i).wait()
 
     def front(j):
-        for k in range(2):
-            i = jnp.minimum(2 * j + k, total - 1)
+        for k in range(WIDE):
+            i = jnp.minimum(WIDE * j + k, total - 1)
             row, place = spots(i)
             predicted = jnp.dot(user_bf[row], items[:, place], preferred_element_type=F32)
             error = (predicted - held[i].astype(F32)).astype(BF16)
@@ -199,9 +199,9 @@
 
     def back(j):
         adds = []
-        for k in range(2):
-            valid = 2 * j + k < total
-            i = jnp.minimum(2 * j + k, total - 1)
+        for k in range(WIDE):
+            valid = WIDE * j + k < total
+            i = jnp.minimum(WIDE * j + k, total - 1)
             row, place = spots(i)
             weight = mask[pl.ds(slots[i], 1), :].astype(F32)
             weight = jnp.where(valid, weight, 0.0)
@@ -218,7 +218,7 @@
             grad_user[:, row] += user_add
             parts[:, place] += item_add
 
-    twos = (total + 1) // 2
+    groups = (total + WIDE - 1) // WIDE
 
     @pl.when(total > 0)
     def _():
@@ -232,7 +232,7 @@
         add(adds)
         return 0
 
-    lax.fori_loop(0, twos, step, 0)
+    lax.fori_loop(0, groups, step, 0)
 
     for bit, send, keep, start, width in (
         (1, send_a, keep_a, 0, half), (members // 2, send_b, keep_b, half, rows - half)
@@ -243,7 +243,7 @@
             send[:, k * width:(k + 1) * width] = parts[:, pl.ds(r * rows + start, width)].astype(BF16)
     if start_up:
         own = jnp.dot(user_t[...], user_bf[...], preferred_element_type=F32)
-        own = owned(own, users_f.shape[0], plan_ref[1, epoch])
+        own = owned(own, users_f.shape[0], owner_ref[0, epoch])
     elif first:
         own = own_in[0][...]
     if first:
@@ -274,7 +274,7 @@
         out_shape += [sd((rank, members * rows), BF16), sd((rank, rows), F32)]
     if start_up:
         out_shape += [sd((user_rows, rank), BF16), sd((rank, user_rows), BF16)]
-    in_specs = [HBM] * 5 + ([HBM] if start_up else [VMEM] * 2)
+    in_specs = [HBM] * 6 + ([HBM] if start_up else [VMEM] * 2)
     in_specs += [HBM if epoch == 0 else ANY] * len(sources)
     operands = [*scalars, ratings, row_mask, *users, *sources]
     if not first:
@@ -288,11 +288,11 @@
         pltpu.VMEM((slots, tile), jnp.int32),
         pltpu.VMEM((rank, members * rows), F32),
         pltpu.VMEM((slots, tile, tile), BF16),
-        *[pltpu.VMEM((2, tile, tile), BF16)] * 2,
         *[pltpu.SMEM((slots + 1,), jnp.int32)] * 3,
         pltpu.SemaphoreType.DMA((slots,)),
         pltpu.SemaphoreType.DMA((max(members, len(sources)),)),
-        pltpu.SemaphoreType.DMA((6,)),
+        pltpu.SemaphoreType.DMA((7,)),
+        *[pltpu.VMEM((2, tile, tile), BF16)] * WIDE,
     ]
     if epoch == 0:
         scratch.append(pltpu.VMEM((members * rows, rank), F32))
@@ -312,7 +312,7 @@
     )(*operands)
 
 
-def user_kernel(epoch, block_rows, plan_ref, users, grad, *refs):
+def user_kernel(epoch, block_rows, owner_ref, users, grad, *refs):
     outs = 4 if epoch + 1 < SUB else 1
     pieces, outs = refs[:-outs], refs[-outs:]
     gram = over_rows(pieces[0][...], pieces[0][...])
@@ -328,10 +328,10 @@
         outs[1][...] = plain
         outs[2][...] = turned
         own = jnp.dot(turned, plain, preferred_element_type=F32)
-        outs[3][...] = owned(own, users.shape[0], plan_ref[1, epoch + 1])
-
-
-def user_call(epoch, block_rows, plan, users, grad, pieces):
+        outs[3][...] = owned(own, users.shape[0], owner_ref[0, epoch + 1])
+
+
+def user_call(epoch, block_rows, owners, users, grad, pieces):
     rows, rank = users.shape
     sd = jax.ShapeDtypeStruct
     out_shape = [sd(users.shape, F32)]
@@ -345,7 +345,7 @@
         compiler_params=params(40),
         cost_estimate=cost(1 << 20, 1 << 16),
         name=f"users_{epoch}",
-    )(plan, users, grad, *pieces)
+    )(owners, users, grad, *pieces)
 
 
 def summed(refs, names, r, width):
@@ -455,24 +455,27 @@
     return lax.ppermute(value, ("blk", "grp"), pairs)
 
 
-def scattered(epoch, chunk, out, members, width_a, width_b, after):
-    send_a, keep_a, send_b, keep_b = out[:4]
+def orders_of(members):
     bits = [1 << i for i in range(members.bit_length() - 1)]
-    orders = (bits, bits[::-1])
-    widths = (width_a, width_b)
-    sends = [send_a, send_b]
+    return bits, bits[::-1]
+
+
+def exchanged(out, members):
+    return [swapped(send, order[0]) for send, order in zip((out[0], out[2]), orders_of(members))]
+
+
+def scattered(epoch, chunk, out, arrived, members, widths):
+    send_a, keep_a, _, keep_b = out[:4]
+    orders = orders_of(members)
     names = [without(members, order[0]) for order in orders]
     terms = [[(keep_a, names[0])], [(keep_b, names[1])]]
     grams = [send_a] if chunk == 0 else []
-    for step in range(len(bits)):
+    for step in range(len(orders[0])):
         for p in range(2):
-            arrived = swapped(sends[p], orders[p][step])
-            if step == 0:
-                arrived = tied(arrived, after)
-            terms[p].append((arrived, names[p]))
-            if p == 0 and grams:
-                grams.append(arrived)
-        if step + 1 == len(bits):
+            terms[p].append((arrived[p], names[p]))
+        if grams:
+            grams.append(arrived[0])
+        if step + 1 == len(orders[0]):
             break
         paths = []
         for p in range(2):
@@ -480,6 +483,7 @@
             paths.append((terms[p], [r for r in names[p] if r & bit], widths[p]))
             names[p] = [r for r in names[p] if not r & bit]
         sends = mid_call(epoch, chunk, step, paths, grams)
+        arrived = [swapped(sends[p], orders[p][step + 1]) for p in range(2)]
     return [a for a, _ in terms[0]], [a for a, _ in terms[1]], grams
 
 
@@ -521,14 +525,15 @@
     block_rows = item_factors.shape[0]
     shard_rows = block_rows // members
     rows = shard_rows // CHUNKS
-    plan = jnp.stack([counts[:, 0, 0], owner_list[:, 0]])
-    row_index, col_index, plan_hbm, row_mask, first_users, ratings, item_factors = (
+    owners = owner_list.reshape(1, -1)
+    row_index, col_index, counts, owner_hbm, row_mask, first_users, ratings, item_factors = (
         pltpu.with_memory_space_constraint(array, pltpu.HBM)
         for array in (
-            row_index, col_index, plan, row_mask, user_factors, ratings, item_factors
+            row_index, col_index, counts.reshape(1, -1), owners, row_mask, user_factors, ratings,
+            item_factors,
         )
     )
-    scalars = (row_index, col_index, plan_hbm)
+    scalars = (row_index, col_index, counts, owner_hbm)
     full_users = user_factors
     users = [first_users]
     own_gram = None
@@ -557,24 +562,27 @@
                 olds.append(sources[0])
         last = epoch + 1 == SUB
         if not last:
-            new_users = user_call(epoch, block_rows, plan, full_users, grad_user, pieces)
+            new_users = user_call(epoch, block_rows, owners, full_users, grad_user, pieces)
             full_users = new_users[0]
         shards = []
         grams = None
+        firsts = [exchanged(out, members) for out in outs]
         for c in range(CHUNKS):
+            following = min(c + 1, CHUNKS - 1)
+            arrived = [tied(array, outs[following][4]) for array in firsts[c]]
             terms_a, terms_b, found = scattered(
-                epoch, c, outs[c], members, rows // 2, rows - rows // 2,
-                outs[min(c + 1, CHUNKS - 1)][4],
+                epoch, c, outs[c], arrived, members, (rows // 2, rows - rows // 2)
             )
-            if found and not last:
-                found[0] = tied(found[0], full_users)
-            shard, gram = item_call(epoch, c, shard_rows, olds[c], terms_a, terms_b, found or grams)
+            old = olds[c]
+            if not last:
+                old = tied(old, full_users, *firsts[following])
+            shard, gram = item_call(epoch, c, shard_rows, old, terms_a, terms_b, found or grams)
             if found:
                 grams = [gram]
             shards.append(shard)
         if last:
             grad_user = tied(grad_user, *shards)
-            full_users = user_call(epoch, block_rows, plan, full_users, grad_user, pieces)[0]
+            full_users = user_call(epoch, block_rows, owners, full_users, grad_user, pieces)[0]
         else:
             users, own_gram = new_users[1:3], new_users[3]
             gathers = []

time: 146 us -> 147 us (level)
  waiting for transfers between devices: 62.7 us -> 67.4 us
  Pallas kernels: 45 us -> 41.4 us
  starting transfers between devices: 32.3 us -> 34.5 us
    ppermute x8, waiting for transfers between devices: 20.8 us -> 29.3 us  [moved(): return lax.ppermute(value, ('blk', 'grp'), pairs)]
    ppermute x20, waiting for transfers between devices: 41.9 us -> 38.1 us  [swapped(): return lax.ppermute(value, 'grp', [(i, i ^ bit) for i in range(length)])]
    ppermute x20, starting transfers between devices: 23.7 us -> 27.4 us  [swapped(): return lax.ppermute(value, 'grp', [(i, i ^ bit) for i in range(length)])]
    pallas_call x4, Pallas kernels: 32.1 us -> 28.6 us  [tile_call(): pl.pallas_call(functools.partial(tile_kernel, epoch, chunk, members, shar...]
    ppermute x8, starting transfers between devices: 8.65 us -> 7.18 us  [moved(): return lax.ppermute(value, ('blk', 'grp'), pairs)]
  transfers between devices with their start and end apart: 28 -> 28, of which waited for: 20 -> 22; matrix products, arithmetic and copies ran while one was open for 0% -> 0% of each run, Pallas kernels for 23% -> 21%
where the time goes in v5:
time: 147 us; the launch traced here: 146 us
  waiting for transfers between devices  67.4 us (46%)
  Pallas kernels  41.4 us (28%)
  starting transfers between devices  34.5 us (23%)
    ppermute x20, waiting for transfers between devices, swapped(): return lax.ppermute(value, 'grp', [(i, i ^ bit) for i in range(length)])  38.1 us
    ppermute x8, waiting for transfers between devices, moved(): return lax.ppermute(value, ('blk', 'grp'), pairs)  29.3 us
    pallas_call x4, Pallas kernels, tile_call(): pl.pallas_call(functools.partial(tile_kernel, epoch, chunk, members, shar...  28.6 us
    ppermute x20, starting transfers between devices, swapped(): return lax.ppermute(value, 'grp', [(i, i ^ bit) for i in range(length)])  27.4 us
    pallas_call x2, Pallas kernels, user_call(): pl.pallas_call(functools.partial(user_kernel, epoch, block_rows), out_sha...  10.1 us
    ppermute x8, starting transfers between devices, moved(): return lax.ppermute(value, ('blk', 'grp'), pairs)  7.18 us
  transfers between devices with their start and end apart: 28, of which 22 were waited for; matrix products, arithmetic and copies ran while one was open for 0% of the time, Pallas kernels for 21%

profile of v5, /device:TPU:0, one launch (start us, length us, event | category | flops | bytes accessed | tf_op | source)
XLA Modules:
  0.0 145.8 jit_solution(5460143562942039504)
XLA Ops:
  0.6 9.6 %tiles_0_0.1 = (bf16[128,2176]{1,0:T(8,128)(2,1)S(1)}, bf16[128,2048]{1,0:T(8,128)(2,1)S(1)}, bf16[128,2048]{1,0:T(8,128)(2,1)S(1)}, bf16[128,2048]{1,0:T(8,128)...) custom-call(s32[2,1,1,64]{3,2,1,0:T(1,128)} %refs_0_.7, ...), custom_call_target="tpu_custom_call" | custom-call | flops 1048576 | bytes 65536 | tf_op jit(solution)/shard_map/tiles_0_0/pallas_call | solution.py:303
  10.6 2.7 %collective-permute-start.5 = (bf16[128,2048]{1,0:T(8,128)(2,1)S(1)}, bf16[128,2048]{1,0:T(8,128)(2,1)S(1)}, u32[]{:S(2)}, u32[]{:S(2)}) collective-permute-start(bf16[128,2048]{1,0:T(8,128)(2,1)S(1)} %get-tuple-element.84), channel_id=1, source_target_pairs={{0,2},{1,3},{2,0},{3,1},{4,6},{5,7},{6,4},{7,5},{8,10},{9,11},{10,... | collective-permute-start | bytes 1572872 | tf_op jit(solution)/shard_map/ppermute | solution.py:445
  13.3 8.3 %tiles_0_1.1 = (bf16[128,2048]{1,0:T(8,128)(2,1)S(1)}, bf16[128,2048]{1,0:T(8,128)(2,1)S(1)}, bf16[128,2048]{1,0:T(8,128)(2,1)S(1)}, bf16[128,2048]{1,0:T(8,128)...) custom-call(s32[2,1,1,64]{3,2,1,0:T(1,128)} %refs_0_.7, ...), custom_call_target="tpu_custom_call" | custom-call | flops 1048576 | bytes 65536 | tf_op jit(solution)/shard_map/tiles_0_1/pallas_call | solution.py:303
  22.0 1.5 %collective-permute-start.1 = (bf16[128,2048]{1,0:T(8,128)(2,1)S(1)}, bf16[128,2048]{1,0:T(8,128)(2,1)S(1)}, u32[]{:S(2)}, u32[]{:S(2)}) collective-permute-start(bf16[128,2048]{1,0:T(8,128)(2,1)S(1)} %get-tuple-element.70), channel_id=1, source_target_pairs={{0,2},{1,3},{2,0},{3,1},{4,6},{5,7},{6,4},{7,5},{8,10},{9,11},{10,... | collective-permute-start | bytes 1572872 | tf_op jit(solution)/shard_map/ppermute | solution.py:445
  23.5 2.4 %collective-permute-done.5.refs_3_.refs_4_ = bf16[128,2048]{1,0:T(8,128)(2,1)S(1)} collective-permute-done((bf16[128,2048]{1,0:T(8,128)(2,1)S(1)}, bf16[128,2048]{1,0:T(8,128)(2,1)S(1)}, u32[]{:S(2)}, u32[]{:S(2)}) %collective-permute-start.5) | collective-permute-done | bytes 524320 | tf_op jit(solution)/shard_map/ppermute | solution.py:445
  25.9 3.0 %collective-permute-start.6 = (bf16[128,1152]{1,0:T(8,128)(2,1)S(1)}, bf16[128,1152]{1,0:T(8,128)(2,1)S(1)}, u32[]{:S(2)}, u32[]{:S(2)}) collective-permute-start(bf16[128,1152]{1,0:T(8,128)(2,1)S(1)} %get-tuple-element.86), channel_id=1, source_target_pairs={{0,2},{1,3},{2,0},{3,1},{4,6},{5,7},{6,4},{7,5},{8,10},{9,11},{10,... | collective-permute-start | bytes 884744 | tf_op jit(solution)/shard_map/ppermute | solution.py:445
  29.0 1.4 collective-permute-start.7
  30.3 4.8 %users_0.1 = (f32[2048,128]{1,0:T(8,128)S(1)}, bf16[2048,128]{1,0:T(8,128)(2,1)S(1)}, bf16[128,2048]{1,0:T(8,128)(2,1)S(1)}, bf16[128,128]{1,0:T(8,128)(2,1)S(1)}) custom-call(s32[1,2]{1,0:T(1,128)S(1)} %bitcast.6, f32[2048,128]{1,0:T(8,128)S(1)} %copy-done, f32[128,2048]{1,0:T(8,128)S(1)} %get-tuple-element.62.grad, ...), custom_call_target="tpu_custom_call" | custom-call | flops 1048576 | bytes 65536 | tf_op jit(solution)/shard_map/users_0/pallas_call | solution.py:340
  35.1 1.4 collective-permute-done.refs_1_
  36.5 0.6 collective-permute-done.1.refs_3_.refs_4_
  37.0 4.6 %collective-permute-done.7.refs_5_ = bf16[128,1024]{1,0:T(8,128)(2,1)S(1)} collective-permute-done((bf16[128,1024]{1,0:T(8,128)(2,1)S(1)}, bf16[128,1024]{1,0:T(8,128)(2,1)S(1)}, u32[]{:S(2)}, u32[]{:S(2)}) %collective-permute-start.7) | collective-permute-done | bytes 262176 | tf_op jit(solution)/shard_map/ppermute | solution.py:445
  41.6 1.7 %collective-permute-done.6.refs_2_.refs_8_ = bf16[128,1152]{1,0:T(8,128)(2,1)S(1)} collective-permute-done((bf16[128,1152]{1,0:T(8,128)(2,1)S(1)}, bf16[128,1152]{1,0:T(8,128)(2,1)S(1)}, u32[]{:S(2)}, u32[]{:S(2)}) %collective-permute-start.6) | collective-permute-done | bytes 294944 | tf_op jit(solution)/shard_map/ppermute | solution.py:445
  43.4 0.6 items_0_0.1
  44.2 4.5 %collective-permute-start.10 = (bf16[128,2048]{1,0:T(8,128)(2,1)S(1)}, bf16[128,2048]{1,0:T(8,128)(2,1)S(1)}, u32[]{:S(2)}, u32[]{:S(2)}) collective-permute-start(bf16[128,2048]{1,0:T(8,128)(2,1)S(1)} %get-tuple-element.89), channel_id=1, source_target_pairs={{0,6},{1,7},{2,4},{3,5},{4,10},{5,11},{6,8},{7,9},{8,14},{9,15},{1... | collective-permute-start | bytes 1572872 | tf_op jit(solution)/shard_map/ppermute | solution.py:455
  49.5 9.4 %collective-permute-done.8.refs_9_.refs_1_ = bf16[128,2048]{1,0:T(8,128)(2,1)S(1)} collective-permute-done((bf16[128,2048]{1,0:T(8,128)(2,1)S(1)}, bf16[128,2048]{1,0:T(8,128)(2,1)S(1)}, u32[]{:S(2)}, u32[]{:S(2)}) %collective-permute-start.8) | collective-permute-done | bytes 524320 | tf_op jit(solution)/shard_map/ppermute | solution.py:455
  58.9 2.6 %collective-permute-start.9 = (bf16[128,1024]{1,0:T(8,128)(2,1)S(1)}, bf16[128,1024]{1,0:T(8,128)(2,1)S(1)}, u32[]{:S(2)}, u32[]{:S(2)}) collective-permute-start(bf16[128,1024]{1,0:T(8,128)(2,1)S(1)} %slice.16), channel_id=1, source_target_pairs={{0,2},{1,3},{2,0},{3,1},{4,6},{5,7},{6,4},{7,5},{8,10},{9,11},{10,... | collective-permute-start | bytes 786440 | tf_op jit(solution)/shard_map/ppermute | solution.py:445
  61.5 1.8 %collective-permute-done.10.refs_10_.refs_2_ = bf16[128,2048]{1,0:T(8,128)(2,1)S(1)} collective-permute-done((bf16[128,2048]{1,0:T(8,128)(2,1)S(1)}, bf16[128,2048]{1,0:T(8,128)(2,1)S(1)}, u32[]{:S(2)}, u32[]{:S(2)}) %collective-permute-start.10) | collective-permute-done | bytes 524320 | tf_op jit(solution)/shard_map/ppermute | solution.py:455
  63.4 0.4 collective-permute-start.11
  63.8 0.8 collective-permute-start.13
  64.6 5.5 %collective-permute-done.2.refs_2_ = bf16[128,1024]{1,0:T(8,128)(2,1)S(1)} collective-permute-done((bf16[128,1024]{1,0:T(8,128)(2,1)S(1)}, bf16[128,1024]{1,0:T(8,128)(2,1)S(1)}, u32[]{:S(2)}, u32[]{:S(2)}) %collective-permute-start.2) | collective-permute-done | bytes 262176 | tf_op jit(solution)/shard_map/ppermute | solution.py:445
  70.1 0.6 items_0_1.1
  70.7 2.2 %collective-permute-done.9.refs_11_.refs_3_ = bf16[128,1024]{1,0:T(8,128)(2,1)S(1)} collective-permute-done((bf16[128,1024]{1,0:T(8,128)(2,1)S(1)}, bf16[128,1024]{1,0:T(8,128)(2,1)S(1)}, u32[]{:S(2)}, u32[]{:S(2)}) %collective-permute-start.9) | collective-permute-done | bytes 262176 | tf_op jit(solution)/shard_map/ppermute | solution.py:445
  72.9 1.6 %collective-permute-start.15 = (bf16[128,2048]{1,0:T(8,128)(2,1)S(1)}, bf16[128,2048]{1,0:T(8,128)(2,1)S(1)}, u32[]{:S(2)}, u32[]{:S(2)}) collective-permute-start(bf16[128,2048]{1,0:T(8,128)(2,1)S(1)} %items_0_1.1), channel_id=1, source_target_pairs={{0,6},{1,7},{2,4},{3,5},{4,10},{5,11},{6,8},{7,9},{8,14},{9,15},{1... | collective-permute-start | bytes 1572872 | tf_op jit(solution)/shard_map/ppermute | solution.py:455
  74.6 5.1 %tiles_1_0.1 = (bf16[128,2176]{1,0:T(8,128)(2,1)S(1)}, bf16[128,2048]{1,0:T(8,128)(2,1)S(1)}, bf16[128,2048]{1,0:T(8,128)(2,1)S(1)}, bf16[128,2048]{1,0:T(8,128)(2,1)S(1)}, f32[128,2048]{1,0:T(8,128)S(1)}) custom-call(s32[2,1,1,64]{3,2,1,0:T(1,128)} %refs_0_.7, s32[2,1,1,64]{3,2,1,0:T(1,128)} %refs_1_.7, s32[1,2]{1,0:T(1,128)} %bitcast.10, s32[1,2]{1,0:T(1,128)} %bitcast.4, ...), custom_call_target="tpu_custom_call" | custom-call | flops 1048576 | bytes 65536 | tf_op jit(solution)/shard_map/tiles_1_0/pallas_call | solution.py:303
  79.7 5.6 %collective-permute-done.14.refs_9_.refs_6_ = bf16[128,2048]{1,0:T(8,128)(2,1)S(1)} collective-permute-done((bf16[128,2048]{1,0:T(8,128)(2,1)S(1)}, bf16[128,2048]{1,0:T(8,128)(2,1)S(1)}, u32[]{:S(2)}, u32[]{:S(2)}) %collective-permute-start.14) | collective-permute-done | bytes 524320 | tf_op jit(solution)/shard_map/ppermute | solution.py:455
  85.2 4.3 %collective-permute-done.15.refs_10_.refs_7_ = bf16[128,2048]{1,0:T(8,128)(2,1)S(1)} collective-permute-done((bf16[128,2048]{1,0:T(8,128)(2,1)S(1)}, bf16[128,2048]{1,0:T(8,128)(2,1)S(1)}, u32[]{:S(2)}, u32[]{:S(2)}) %collective-permute-start.15) | collective-permute-done | bytes 524320 | tf_op jit(solution)/shard_map/ppermute | solution.py:455
  89.6 0.7 collective-permute-start.16
  90.4 1.7 %collective-permute-start.17 = (bf16[128,1024]{1,0:T(8,128)(2,1)S(1)}, bf16[128,1024]{1,0:T(8,128)(2,1)S(1)}, u32[]{:S(2)}, u32[]{:S(2)}) collective-permute-start(bf16[128,1024]{1,0:T(8,128)(2,1)S(1)} %slice.15), channel_id=1, source_target_pairs={{0,1},{1,0},{2,3},{3,2},{4,5},{5,4},{6,7},{7,6},{8,9},{9,8},{10,11... | collective-permute-start | bytes 786440 | tf_op jit(solution)/shard_map/ppermute | solution.py:445
  92.4 1.4 collective-permute-start.19
  93.8 0.6 collective-permute-done.12.refs_8_.items.refs_5_
  94.4 4.5 %collective-permute-done.16.refs_11_.refs_8_ = bf16[128,1024]{1,0:T(8,128)(2,1)S(1)} collective-permute-done((bf16[128,1024]{1,0:T(8,128)(2,1)S(1)}, bf16[128,1024]{1,0:T(8,128)(2,1)S(1)}, u32[]{:S(2)}, u32[]{:S(2)}) %collective-permute-start.16) | collective-permute-done | bytes 262176 | tf_op jit(solution)/shard_map/ppermute | solution.py:445
  98.9 0.7 collective-permute-done.17.refs_12_.refs_9_
  99.7 5.6 %tiles_1_1.1 = (bf16[128,2048]{1,0:T(8,128)(2,1)S(1)}, bf16[128,2048]{1,0:T(8,128)(2,1)S(1)}, bf16[128,2048]{1,0:T(8,128)(2,1)S(1)}, bf16[128,2048]{1,0:T(8,128)(2,1)S(1)}, f32[128,2048]{1,0:T(8,128)S(1)}) custom-call(s32[2,1,1,64]{3,2,1,0:T(1,128)} %refs_0_.7, s32[2,1,1,64]{3,2,1,0:T(1,128)} %refs_1_.7, s32[1,2]{1,0:T(1,128)} %bitcast.11, s32[1,2]{1,0:T(1,128)} %bitcast.5, ...), custom_call_target="tpu_custom_call" | custom-call | flops 1048576 | bytes 65536 | tf_op jit(solution)/shard_map/tiles_1_1/pallas_call | solution.py:303
  105.3 4.9 %collective-permute-start.22 = (bf16[128,2048]{1,0:T(8,128)(2,1)S(1)}, bf16[128,2048]{1,0:T(8,128)(2,1)S(1)}, u32[]{:S(2)}, u32[]{:S(2)}) collective-permute-start(bf16[128,2048]{1,0:T(8,128)(2,1)S(1)} %get-tuple-element.107), channel_id=1, source_target_pairs={{0,1},{1,0},{2,3},{3,2},{4,5},{5,4},{6,7},{7,6},{8,9},{9,8},{10,11... | collective-permute-start | bytes 1572872 | tf_op jit(solution)/shard_map/ppermute | solution.py:445
  110.2 1.4 collective-permute-done.18.refs_1_.refs_5_.refs_7_
  111.7 1.4 collective-permute-start.20
  113.2 1.7 %collective-permute-start.21 = (bf16[128,1024]{1,0:T(8,128)(2,1)S(1)}, bf16[128,1024]{1,0:T(8,128)(2,1)S(1)}, u32[]{:S(2)}, u32[]{:S(2)}) collective-permute-start(bf16[128,1024]{1,0:T(8,128)(2,1)S(1)} %get-tuple-element.104), channel_id=1, source_target_pairs={{0,1},{1,0},{2,3},{3,2},{4,5},{5,4},{6,7},{7,6},{8,9},{9,8},{10,11... | collective-permute-start | bytes 786440 | tf_op jit(solution)/shard_map/ppermute | solution.py:445
  114.9 8.2 %collective-permute-done.22.refs_1_ = bf16[128,2048]{1,0:T(8,128)(2,1)S(1)} collective-permute-done((bf16[128,2048]{1,0:T(8,128)(2,1)S(1)}, bf16[128,2048]{1,0:T(8,128)(2,1)S(1)}, u32[]{:S(2)}, u32[]{:S(2)}) %collective-permute-start.22) | collective-permute-done | bytes 524320 | tf_op jit(solution)/shard_map/ppermute | solution.py:445
  123.1 0.9 collective-permute-done.23.refs_3_.refs_4_
  124.4 1.7 %collective-permute-start.25 = (bf16[128,1024]{1,0:T(8,128)(2,1)S(1)}, bf16[128,1024]{1,0:T(8,128)(2,1)S(1)}, u32[]{:S(2)}, u32[]{:S(2)}) collective-permute-start(bf16[128,1024]{1,0:T(8,128)(2,1)S(1)} %get-tuple-element.113), channel_id=1, source_target_pairs={{0,1},{1,0},{2,3},{3,2},{4,5},{5,4},{6,7},{7,6},{8,9},{9,8},{10,11... | collective-permute-start | bytes 786440 | tf_op jit(solution)/shard_map/ppermute | solution.py:445
  126.1 1.5 %collective-permute-done.21.refs_5_ = bf16[128,1024]{1,0:T(8,128)(2,1)S(1)} collective-permute-done((bf16[128,1024]{1,0:T(8,128)(2,1)S(1)}, bf16[128,1024]{1,0:T(8,128)(2,1)S(1)}, u32[]{:S(2)}, u32[]{:S(2)}) %collective-permute-start.21) | collective-permute-done | bytes 262176 | tf_op jit(solution)/shard_map/ppermute | solution.py:445
  127.7 0.6 items_1_0.1
  128.3 2.3 %collective-permute-done.24.refs_2_ = bf16[128,1024]{1,0:T(8,128)(2,1)S(1)} collective-permute-done((bf16[128,1024]{1,0:T(8,128)(2,1)S(1)}, bf16[128,1024]{1,0:T(8,128)(2,1)S(1)}, u32[]{:S(2)}, u32[]{:S(2)}) %collective-permute-start.24) | collective-permute-done | bytes 262176 | tf_op jit(solution)/shard_map/ppermute | solution.py:445
  130.8 0.6 items_1_1.1
  131.4 5.3 %users_1.1 = f32[2048,128]{1,0:T(8,128)} custom-call(s32[1,2]{1,0:T(1,128)S(1)} %bitcast.7, f32[2048,128]{1,0:T(8,128)S(1)} %get-tuple-element.65.users, f32[128,2048]{1,0:T(8,128)S(1)} %get-tuple-element.115.grad, bf16[128,2048]{1,0:T(8,128)(2,1)S(1)} %collective-permute-done.13.refs_8_.items.refs_0_, ...), custom_call_target="tpu_custom_call" | custom-call | flops 1048576 | bytes 65536 | tf_op jit(solution)/shard_map/users_1/pallas_call | solution.py:340
  136.7 2.0 %collective-permute-done.26 = bf16[2048,128]{1,0:T(8,128)(2,1)S(1)} collective-permute-done((bf16[2048,128]{1,0:T(8,128)(2,1)S(1)}, bf16[2048,128]{1,0:T(8,128)(2,1)S(1)}, u32[]{:S(2)}, u32[]{:S(2)}) %collective-permute-start.26) | collective-permute-done | bytes 524320 | tf_op jit(solution)/shard_map/ppermute | solution.py:455
  138.7 5.6 %collective-permute-done.27 = bf16[2048,128]{1,0:T(8,128)(2,1)S(1)} collective-permute-done((bf16[2048,128]{1,0:T(8,128)(2,1)S(1)}, bf16[2048,128]{1,0:T(8,128)(2,1)S(1)}, u32[]{:S(2)}, u32[]{:S(2)}) %collective-permute-start.27) | collective-permute-done | bytes 524320 | tf_op jit(solution)/shard_map/ppermute | solution.py:455
  144.3 1.5 maximum_convert_fusion
  (33 shorter events, 3.2 us)
Async XLA Ops:
  10.2 15.6 %collective-permute-start.4 = (bf16[128,2176]{1,0:T(8,128)(2,1)S(1)}, bf16[128,2176]{1,0:T(8,128)(2,1)S(1)}, u32[]{:S(2)}, u32[]{:S(2)}) collective-permute-start(bf16[128,2176]{1,0:T(8,128)(2,1)S(1)} %get-tuple-element.81.refs_4_.refs_6_), channel_id=1, source_target_pairs={{0,1},{1,0},{2,3},{3,2},{4,5},{5,4},{6,7},{7,6},{8,9},{9,8},{10,11... | collective-permute-start | bytes 1671176 | tf_op jit(solution)/shard_map/ppermute | solution.py:445
  10.6 15.2 %collective-permute-start.5 = (bf16[128,2048]{1,0:T(8,128)(2,1)S(1)}, bf16[128,2048]{1,0:T(8,128)(2,1)S(1)}, u32[]{:S(2)}, u32[]{:S(2)}) collective-permute-start(bf16[128,2048]{1,0:T(8,128)(2,1)S(1)} %get-tuple-element.84), channel_id=1, source_target_pairs={{0,2},{1,3},{2,0},{3,1},{4,6},{5,7},{6,4},{7,5},{8,10},{9,11},{10,... | collective-permute-start | bytes 1572872 | tf_op jit(solution)/shard_map/ppermute | solution.py:445
  21.6 8.7 %copy-start = (f32[2048,128]{1,0:T(8,128)S(1)}, f32[2048,128]{1,0:T(8,128)}, u32[]{:S(2)}) copy-start(f32[2048,128]{1,0:T(8,128)} %users.1) | copy-start | bytes 3145732
  21.6 8.7 %copy-start.1 = (s32[2,1]{0,1:T(1,128)S(1)}, s32[2,1]{0,1:T(1,128)}, u32[]{:S(2)}) copy-start(s32[2,1]{0,1:T(1,128)} %param.13) | copy-start | bytes 28
  21.6 14.8 %collective-permute-start = (bf16[128,2048]{1,0:T(8,128)(2,1)S(1)}, bf16[128,2048]{1,0:T(8,128)(2,1)S(1)}, u32[]{:S(2)}, u32[]{:S(2)}) collective-permute-start(bf16[128,2048]{1,0:T(8,128)(2,1)S(1)} %get-tuple-element.69), channel_id=1, source_target_pairs={{0,1},{1,0},{2,3},{3,2},{4,5},{5,4},{6,7},{7,6},{8,9},{9,8},{10,11... | collective-permute-start | bytes 1572872 | tf_op jit(solution)/shard_map/ppermute | solution.py:445
  22.0 15.1 %collective-permute-start.1 = (bf16[128,2048]{1,0:T(8,128)(2,1)S(1)}, bf16[128,2048]{1,0:T(8,128)(2,1)S(1)}, u32[]{:S(2)}, u32[]{:S(2)}) collective-permute-start(bf16[128,2048]{1,0:T(8,128)(2,1)S(1)} %get-tuple-element.70), channel_id=1, source_target_pairs={{0,2},{1,3},{2,0},{3,1},{4,6},{5,7},{6,4},{7,5},{8,10},{9,11},{10,... | collective-permute-start | bytes 1572872 | tf_op jit(solution)/shard_map/ppermute | solution.py:445
  25.9 17.4 %collective-permute-start.6 = (bf16[128,1152]{1,0:T(8,128)(2,1)S(1)}, bf16[128,1152]{1,0:T(8,128)(2,1)S(1)}, u32[]{:S(2)}, u32[]{:S(2)}) collective-permute-start(bf16[128,1152]{1,0:T(8,128)(2,1)S(1)} %get-tuple-element.86), channel_id=1, source_target_pairs={{0,2},{1,3},{2,0},{3,1},{4,6},{5,7},{6,4},{7,5},{8,10},{9,11},{10,... | collective-permute-start | bytes 884744 | tf_op jit(solution)/shard_map/ppermute | solution.py:445
  29.0 12.7 %collective-permute-start.7 = (bf16[128,1024]{1,0:T(8,128)(2,1)S(1)}, bf16[128,1024]{1,0:T(8,128)(2,1)S(1)}, u32[]{:S(2)}, u32[]{:S(2)}) collective-permute-start(bf16[128,1024]{1,0:T(8,128)(2,1)S(1)} %get-tuple-element.87), channel_id=1, source_target_pairs={{0,1},{1,0},{2,3},{3,2},{4,5},{5,4},{6,7},{7,6},{8,9},{9,8},{10,11... | collective-permute-start | bytes 786440 | tf_op jit(solution)/shard_map/ppermute | solution.py:445
  44.0 14.9 %collective-permute-start.8 = (bf16[128,2048]{1,0:T(8,128)(2,1)S(1)}, bf16[128,2048]{1,0:T(8,128)(2,1)S(1)}, u32[]{:S(2)}, u32[]{:S(2)}) collective-permute-start(bf16[128,2048]{1,0:T(8,128)(2,1)S(1)} %get-tuple-element.89), channel_id=1, source_target_pairs={{0,5},{1,4},{2,7},{3,6},{4,9},{5,8},{6,11},{7,10},{8,13},{9,12},{1... | collective-permute-start | bytes 1572872 | tf_op jit(solution)/shard_map/ppermute | solution.py:455
  44.2 19.2 %collective-permute-start.10 = (bf16[128,2048]{1,0:T(8,128)(2,1)S(1)}, bf16[128,2048]{1,0:T(8,128)(2,1)S(1)}, u32[]{:S(2)}, u32[]{:S(2)}) collective-permute-start(bf16[128,2048]{1,0:T(8,128)(2,1)S(1)} %get-tuple-element.89), channel_id=1, source_target_pairs={{0,6},{1,7},{2,4},{3,5},{4,10},{5,11},{6,8},{7,9},{8,14},{9,15},{1... | collective-permute-start | bytes 1572872 | tf_op jit(solution)/shard_map/ppermute | solution.py:455
  48.8 21.4 %collective-permute-start.2 = (bf16[128,1024]{1,0:T(8,128)(2,1)S(1)}, bf16[128,1024]{1,0:T(8,128)(2,1)S(1)}, u32[]{:S(2)}, u32[]{:S(2)}) collective-permute-start(bf16[128,1024]{1,0:T(8,128)(2,1)S(1)} %get-tuple-element.76), channel_id=1, source_target_pairs={{0,2},{1,3},{2,0},{3,1},{4,6},{5,7},{6,4},{7,5},{8,10},{9,11},{10,... | collective-permute-start | bytes 786440 | tf_op jit(solution)/shard_map/ppermute | solution.py:445
  49.1 21.0 %collective-permute-start.3 = (bf16[128,1024]{1,0:T(8,128)(2,1)S(1)}, bf16[128,1024]{1,0:T(8,128)(2,1)S(1)}, u32[]{:S(2)}, u32[]{:S(2)}) collective-permute-start(bf16[128,1024]{1,0:T(8,128)(2,1)S(1)} %get-tuple-element.77), channel_id=1, source_target_pairs={{0,1},{1,0},{2,3},{3,2},{4,5},{5,4},{6,7},{7,6},{8,9},{9,8},{10,11... | collective-permute-start | bytes 786440 | tf_op jit(solution)/shard_map/ppermute | solution.py:445
  58.9 14.0 %collective-permute-start.9 = (bf16[128,1024]{1,0:T(8,128)(2,1)S(1)}, bf16[128,1024]{1,0:T(8,128)(2,1)S(1)}, u32[]{:S(2)}, u32[]{:S(2)}) collective-permute-start(bf16[128,1024]{1,0:T(8,128)(2,1)S(1)} %slice.16), channel_id=1, source_target_pairs={{0,2},{1,3},{2,0},{3,1},{4,6},{5,7},{6,4},{7,5},{8,10},{9,11},{10,... | collective-permute-start | bytes 786440 | tf_op jit(solution)/shard_map/ppermute | solution.py:445
  63.4 9.5 %collective-permute-start.11 = (bf16[128,1024]{1,0:T(8,128)(2,1)S(1)}, bf16[128,1024]{1,0:T(8,128)(2,1)S(1)}, u32[]{:S(2)}, u32[]{:S(2)}) collective-permute-start(bf16[128,1024]{1,0:T(8,128)(2,1)S(1)} %slice.17), channel_id=1, source_target_pairs={{0,1},{1,0},{2,3},{3,2},{4,5},{5,4},{6,7},{7,6},{8,9},{9,8},{10,11... | collective-permute-start | bytes 786440 | tf_op jit(solution)/shard_map/ppermute | solution.py:445
  63.8 10.7 %collective-permute-start.13 = (bf16[128,2048]{1,0:T(8,128)(2,1)S(1)}, bf16[128,2048]{1,0:T(8,128)(2,1)S(1)}, u32[]{:S(2)}, u32[]{:S(2)}) collective-permute-start(bf16[128,2048]{1,0:T(8,128)(2,1)S(1)} %get-tuple-element.89), channel_id=1, source_target_pairs={{0,4},{1,5},{2,6},{3,7},{4,8},{5,9},{6,10},{7,11},{8,12},{9,13},{1... | collective-permute-start | bytes 1572872 | tf_op jit(solution)/shard_map/ppermute | solution.py:455
  72.9 12.3 %collective-permute-start.14 = (bf16[128,2048]{1,0:T(8,128)(2,1)S(1)}, bf16[128,2048]{1,0:T(8,128)(2,1)S(1)}, u32[]{:S(2)}, u32[]{:S(2)}) collective-permute-start(bf16[128,2048]{1,0:T(8,128)(2,1)S(1)} %items_0_1.1), channel_id=1, source_target_pairs={{0,5},{1,4},{2,7},{3,6},{4,9},{5,8},{6,11},{7,10},{8,13},{9,12},{1... | collective-permute-start | bytes 1572872 | tf_op jit(solution)/shard_map/ppermute | solution.py:455
  72.9 16.7 %collective-permute-start.15 = (bf16[128,2048]{1,0:T(8,128)(2,1)S(1)}, bf16[128,2048]{1,0:T(8,128)(2,1)S(1)}, u32[]{:S(2)}, u32[]{:S(2)}) collective-permute-start(bf16[128,2048]{1,0:T(8,128)(2,1)S(1)} %items_0_1.1), channel_id=1, source_target_pairs={{0,6},{1,7},{2,4},{3,5},{4,10},{5,11},{6,8},{7,9},{8,14},{9,15},{1... | collective-permute-start | bytes 1572872 | tf_op jit(solution)/shard_map/ppermute | solution.py:455
  74.6 19.8 %collective-permute-start.12 = (bf16[128,2048]{1,0:T(8,128)(2,1)S(1)}, bf16[128,2048]{1,0:T(8,128)(2,1)S(1)}, u32[]{:S(2)}, u32[]{:S(2)}) collective-permute-start(bf16[128,2048]{1,0:T(8,128)(2,1)S(1)} %items_0_1.1), channel_id=1, source_target_pairs={{0,4},{1,5},{2,6},{3,7},{4,8},{5,9},{6,10},{7,11},{8,12},{9,13},{1... | collective-permute-start | bytes 1572872 | tf_op jit(solution)/shard_map/ppermute | solution.py:455
  89.6 9.3 %collective-permute-start.16 = (bf16[128,1024]{1,0:T(8,128)(2,1)S(1)}, bf16[128,1024]{1,0:T(8,128)(2,1)S(1)}, u32[]{:S(2)}, u32[]{:S(2)}) collective-permute-start(bf16[128,1024]{1,0:T(8,128)(2,1)S(1)} %slice.14), channel_id=1, source_target_pairs={{0,2},{1,3},{2,0},{3,1},{4,6},{5,7},{6,4},{7,5},{8,10},{9,11},{10,... | collective-permute-start | bytes 786440 | tf_op jit(solution)/shard_map/ppermute | solution.py:445
  90.4 9.3 %collective-permute-start.17 = (bf16[128,1024]{1,0:T(8,128)(2,1)S(1)}, bf16[128,1024]{1,0:T(8,128)(2,1)S(1)}, u32[]{:S(2)}, u32[]{:S(2)}) collective-permute-start(bf16[128,1024]{1,0:T(8,128)(2,1)S(1)} %slice.15), channel_id=1, source_target_pairs={{0,1},{1,0},{2,3},{3,2},{4,5},{5,4},{6,7},{7,6},{8,9},{9,8},{10,11... | collective-permute-start | bytes 786440 | tf_op jit(solution)/shard_map/ppermute | solution.py:445
  92.1 19.5 %collective-permute-start.18 = (bf16[128,2176]{1,0:T(8,128)(2,1)S(1)}, bf16[128,2176]{1,0:T(8,128)(2,1)S(1)}, u32[]{:S(2)}, u32[]{:S(2)}) collective-permute-start(bf16[128,2176]{1,0:T(8,128)(2,1)S(1)} %get-tuple-element.98.refs_4_.refs_6_), channel_id=1, source_target_pairs={{0,1},{1,0},{2,3},{3,2},{4,5},{5,4},{6,7},{7,6},{8,9},{9,8},{10,11... | collective-permute-start | bytes 1671176 | tf_op jit(solution)/shard_map/ppermute | solution.py:445
  92.4 19.2 %collective-permute-start.19 = (bf16[128,2048]{1,0:T(8,128)(2,1)S(1)}, bf16[128,2048]{1,0:T(8,128)(2,1)S(1)}, u32[]{:S(2)}, u32[]{:S(2)}) collective-permute-start(bf16[128,2048]{1,0:T(8,128)(2,1)S(1)} %get-tuple-element.101), channel_id=1, source_target_pairs={{0,2},{1,3},{2,0},{3,1},{4,6},{5,7},{6,4},{7,5},{8,10},{9,11},{10,... | collective-permute-start | bytes 1572872 | tf_op jit(solution)/shard_map/ppermute | solution.py:445
  105.3 17.8 %collective-permute-start.22 = (bf16[128,2048]{1,0:T(8,128)(2,1)S(1)}, bf16[128,2048]{1,0:T(8,128)(2,1)S(1)}, u32[]{:S(2)}, u32[]{:S(2)}) collective-permute-start(bf16[128,2048]{1,0:T(8,128)(2,1)S(1)} %get-tuple-element.107), channel_id=1, source_target_pairs={{0,1},{1,0},{2,3},{3,2},{4,5},{5,4},{6,7},{7,6},{8,9},{9,8},{10,11... | collective-permute-start | bytes 1572872 | tf_op jit(solution)/shard_map/ppermute | solution.py:445
  110.2 13.8 %collective-permute-start.23 = (bf16[128,2048]{1,0:T(8,128)(2,1)S(1)}, bf16[128,2048]{1,0:T(8,128)(2,1)S(1)}, u32[]{:S(2)}, u32[]{:S(2)}) collective-permute-start(bf16[128,2048]{1,0:T(8,128)(2,1)S(1)} %get-tuple-element.110), channel_id=1, source_target_pairs={{0,2},{1,3},{2,0},{3,1},{4,6},{5,7},{6,4},{7,5},{8,10},{9,11},{10,... | collective-permute-start | bytes 1572872 | tf_op jit(solution)/shard_map/ppermute | solution.py:445
  111.7 15.9 %collective-permute-start.20 = (bf16[128,1152]{1,0:T(8,128)(2,1)S(1)}, bf16[128,1152]{1,0:T(8,128)(2,1)S(1)}, u32[]{:S(2)}, u32[]{:S(2)}) collective-permute-start(bf16[128,1152]{1,0:T(8,128)(2,1)S(1)} %get-tuple-element.103), channel_id=1, source_target_pairs={{0,2},{1,3},{2,0},{3,1},{4,6},{5,7},{6,4},{7,5},{8,10},{9,11},{10,... | collective-permute-start | bytes 884744 | tf_op jit(solution)/shard_map/ppermute | solution.py:445
  113.2 14.5 %collective-permute-start.21 = (bf16[128,1024]{1,0:T(8,128)(2,1)S(1)}, bf16[128,1024]{1,0:T(8,128)(2,1)S(1)}, u32[]{:S(2)}, u32[]{:S(2)}) collective-permute-start(bf16[128,1024]{1,0:T(8,128)(2,1)S(1)} %get-tuple-element.104), channel_id=1, source_target_pairs={{0,1},{1,0},{2,3},{3,2},{4,5},{5,4},{6,7},{7,6},{8,9},{9,8},{10,11... | collective-permute-start | bytes 786440 | tf_op jit(solution)/shard_map/ppermute | solution.py:445
  124.1 6.4 %collective-permute-start.24 = (bf16[128,1024]{1,0:T(8,128)(2,1)S(1)}, bf16[128,1024]{1,0:T(8,128)(2,1)S(1)}, u32[]{:S(2)}, u32[]{:S(2)}) collective-permute-start(bf16[128,1024]{1,0:T(8,128)(2,1)S(1)} %get-tuple-element.112), channel_id=1, source_target_pairs={{0,2},{1,3},{2,0},{3,1},{4,6},{5,7},{6,4},{7,5},{8,10},{9,11},{10,... | collective-permute-start | bytes 786440 | tf_op jit(solution)/shard_map/ppermute | solution.py:445
  124.4 6.4 %collective-permute-start.25 = (bf16[128,1024]{1,0:T(8,128)(2,1)S(1)}, bf16[128,1024]{1,0:T(8,128)(2,1)S(1)}, u32[]{:S(2)}, u32[]{:S(2)}) collective-permute-start(bf16[128,1024]{1,0:T(8,128)(2,1)S(1)} %get-tuple-element.113), channel_id=1, source_target_pairs={{0,1},{1,0},{2,3},{3,2},{4,5},{5,4},{6,7},{7,6},{8,9},{9,8},{10,11... | collective-permute-start | bytes 786440 | tf_op jit(solution)/shard_map/ppermute | solution.py:445
  128.2 3.2 %copy-start.2 = (s32[2,1]{0,1:T(1,128)S(1)}, s32[2,1]{0,1:T(1,128)}, u32[]{:S(2)}) copy-start(s32[2,1]{0,1:T(1,128)} %param.13) | copy-start | bytes 28
  128.2 10.5 %collective-permute-start.26 = (bf16[2048,128]{1,0:T(8,128)(2,1)S(1)}, bf16[2048,128]{1,0:T(8,128)(2,1)S(1)}, u32[]{:S(2)}, u32[]{:S(2)}) collective-permute-start(bf16[2048,128]{1,0:T(8,128)(2,1)S(1)} %get-tuple-element.105), channel_id=1, source_target_pairs={{0,4},{1,5},{2,6},{3,7},{4,8},{5,9},{6,10},{7,11},{8,12},{9,13},{1... | collective-permute-start | bytes 1572872 | tf_op jit(solution)/shard_map/ppermute | solution.py:455
  131.3 13.0 %collective-permute-start.27 = (bf16[2048,128]{1,0:T(8,128)(2,1)S(1)}, bf16[2048,128]{1,0:T(8,128)(2,1)S(1)}, u32[]{:S(2)}, u32[]{:S(2)}) collective-permute-start(bf16[2048,128]{1,0:T(8,128)(2,1)S(1)} %items_1_1.1), channel_id=1, source_target_pairs={{0,4},{1,5},{2,6},{3,7},{4,8},{5,9},{6,10},{7,11},{8,12},{9,13},{1... | collective-permute-start | bytes 1572872 | tf_op jit(solution)/shard_map/ppermute | solution.py:455

commit v6 on v5

--- a/solution.py
+++ b/solution.py
@@ -26,8 +26,9 @@
     return pltpu.CompilerParams(vmem_limit_bytes=mib * 1024 * 1024)
 
 
-def cost(flops, bytes_accessed):
-    return pl.CostEstimate(flops=flops, bytes_accessed=bytes_accessed, transcendentals=0)
+def declared(name):
+    flops = {"tiles": 16e9, "users": 10e9, "items": 1.2e9, "mid": 0.2e9}[name.split("_")[0]]
+    return pl.CostEstimate(flops=int(flops), bytes_accessed=1 << 16, transcendentals=0)
 
 
 def over_rows(a, b):
@@ -53,7 +54,19 @@
     return [r for r in range(members) if not r & bit]
 
 
-def tile_kernel(epoch, chunk, members, shard_tiles, tile, pieces, *refs):
+def chunk_columns(members, rows, direct):
+    half = rows // 2
+    found = []
+    alone = []
+    for bit, start, width in ((1, 0, half), (members // 2, half, rows - half)):
+        names = [r for r in without(members, bit) if r or not direct]
+        found.append([(r | bit, start, width) for r in names])
+        found.append([(r, start, width) for r in names])
+        alone.append([(bit, start, width)])
+    return found + [*alone, [(0, 0, rows)]] if direct else found
+
+
+def tile_kernel(epoch, chunk, direct, members, shard_tiles, tile, pieces, *refs):
     start_up = epoch == 0 and chunk == 0
     first = chunk == 0
     refs = list(refs)
@@ -64,10 +77,11 @@
 
     row_hbm, col_hbm, count_hbm, owner_hbm, ratings, mask_hbm = take(6)
     users = take(1) if start_up else take(2)
-    sources = take(pieces)
+    sources = take(len(pieces))
     grad_in = take(0 if first else 1)
     own_in = take(1 if first and epoch > 0 else 0)
-    send_a, keep_a, send_b, keep_b, grad_user = take(5)
+    outs = take(7 if direct else 4)
+    grad_user, = take(1)
     if epoch == 0:
         items, old = take(2)
     if start_up:
@@ -112,13 +126,16 @@
                 )
             )
     else:
-        at = 0
-        for i, source in enumerate(sources):
-            width = source.shape[1]
-            copies.append(
-                pltpu.make_async_copy(source, items.at[:, pl.ds(at, width)], sem_item.at[i])
-            )
-            at += width
+        for source, columns in zip(sources, pieces):
+            at = 0
+            for r, start, width in columns:
+                copies.append(
+                    pltpu.make_async_copy(
+                        source.at[:, pl.ds(at, width)], items.at[:, pl.ds(r * rows + start, width)],
+                        sem_item.at[len(copies)],
+                    )
+                )
+                at += width
     for copy in copies:
         copy.start()
     for copy in small[:4]:
@@ -234,42 +251,40 @@
 
     lax.fori_loop(0, groups, step, 0)
 
-    for bit, send, keep, start, width in (
-        (1, send_a, keep_a, 0, half), (members // 2, send_b, keep_b, half, rows - half)
-    ):
-        for k, r in enumerate(without(members, bit)):
-            keep[:, k * width:(k + 1) * width] = parts[:, pl.ds(r * rows + start, width)].astype(BF16)
-            r = r | bit
-            send[:, k * width:(k + 1) * width] = parts[:, pl.ds(r * rows + start, width)].astype(BF16)
+    for out, columns in zip(outs, chunk_columns(members, rows, direct)):
+        at = 0
+        for r, start, width in columns:
+            out[:, at:at + width] = parts[:, pl.ds(r * rows + start, width)].astype(BF16)
+            at += width
     if start_up:
         own = jnp.dot(user_t[...], user_bf[...], preferred_element_type=F32)
         own = owned(own, users_f.shape[0], owner_ref[0, epoch])
     elif first:
         own = own_in[0][...]
     if first:
-        send_a[:, members // 2 * half:] = own
-
-
-def tile_call(epoch, chunk, members, scalars, ratings, row_mask, users, sources, carried, own):
+        outs[0][:, members // 2 * half:] = own
+
+
+def tile_call(
+    epoch, chunk, direct, members, scalars, ratings, row_mask, users, sources, carried, own
+):
     tile = ratings.shape[-1]
     slots = ratings.shape[3]
     start_up = epoch == 0 and chunk == 0
     first = chunk == 0
     user_rows, rank = users[0].shape
+    pieces = [columns for _, columns in sources]
+    sources = [array for array, _ in sources]
     if epoch == 0:
         block_rows = sources[0].shape[0]
     else:
         block_rows = sum(s.shape[1] for s in sources) * CHUNKS
     shard_tiles = block_rows // members // tile
     rows = shard_tiles // CHUNKS * tile
-    half = rows // 2
     sd = jax.ShapeDtypeStruct
-    wide_a, wide_b = members // 2 * half, members // 2 * (rows - half)
-    extra = rank if first else 0
-    out_shape = [
-        sd((rank, wide_a + extra), BF16), sd((rank, wide_a), BF16),
-        sd((rank, wide_b), BF16), sd((rank, wide_b), BF16), sd((rank, user_rows), F32),
-    ]
+    widths = [sum(w for _, _, w in columns) for columns in chunk_columns(members, rows, direct)]
+    widths[0] += rank if first else 0
+    out_shape = [sd((rank, width), BF16) for width in widths] + [sd((rank, user_rows), F32)]
     if epoch == 0:
         out_shape += [sd((rank, members * rows), BF16), sd((rank, rows), F32)]
     if start_up:
@@ -290,7 +305,7 @@
         pltpu.VMEM((slots, tile, tile), BF16),
         *[pltpu.SMEM((slots + 1,), jnp.int32)] * 3,
         pltpu.SemaphoreType.DMA((slots,)),
-        pltpu.SemaphoreType.DMA((max(members, len(sources)),)),
+        pltpu.SemaphoreType.DMA((2 * members,)),
         pltpu.SemaphoreType.DMA((7,)),
         *[pltpu.VMEM((2, tile, tile), BF16)] * WIDE,
     ]
@@ -301,13 +316,15 @@
     if start_up:
         scratch.append(pltpu.VMEM((user_rows, rank), F32))
     return pl.pallas_call(
-        functools.partial(tile_kernel, epoch, chunk, members, shard_tiles, tile, len(sources)),
+        functools.partial(
+            tile_kernel, epoch, chunk, direct, members, shard_tiles, tile, pieces
+        ),
         out_shape=out_shape,
         in_specs=in_specs,
         out_specs=[VMEM] * len(out_shape),
         scratch_shapes=scratch,
         compiler_params=params(40),
-        cost_estimate=cost(1 << 20, 1 << 16),
+        cost_estimate=declared(f"tiles_{epoch}_{chunk}"),
         name=f"tiles_{epoch}_{chunk}",
     )(*operands)
 
@@ -343,7 +360,7 @@
         in_specs=[pl.BlockSpec(memory_space=pltpu.SMEM)] + [VMEM] * (2 + len(pieces)),
         out_specs=[VMEM] * len(out_shape),
         compiler_params=params(40),
-        cost_estimate=cost(1 << 20, 1 << 16),
+        cost_estimate=declared(f"users_{epoch}"),
         name=f"users_{epoch}",
     )(owners, users, grad, *pieces)
 
@@ -389,7 +406,7 @@
         in_specs=[VMEM] * len(operands),
         out_specs=[VMEM] * len(out_shape),
         compiler_params=params(40),
-        cost_estimate=cost(1 << 16, 1 << 16),
+        cost_estimate=declared(f"mid_{epoch}_{chunk}_{step}"),
         name=f"mid_{epoch}_{chunk}_{step}",
     )(*operands)
 
@@ -416,16 +433,28 @@
     else:
         pull = over_columns(gram, items[...])
     new = items[...].astype(F32) - LEARN * (grad + pull)
-    out[...] = (new if epoch + 1 < SUB else new.T).astype(BF16)
+    if epoch + 1 < SUB:
+        new = new.astype(BF16)
+        out[...] = new
+        refs[-2][...] = new[:, :width]
+        refs[-1][...] = new[:, width:]
+    else:
+        out[:rows] = new.T.astype(BF16)
+        if grams > 1:
+            out[rows:] = gram
 
 
 def item_call(epoch, chunk, shard_rows, items, terms_a, terms_b, grams):
     rank = grams[0].shape[0]
     rows = shard_rows // CHUNKS
     last = epoch + 1 == SUB
-    out_shape = [jax.ShapeDtypeStruct((rows, rank) if last else (rank, rows), BF16)]
+    tall = rows + (rank if len(grams) > 1 else 0)
+    out_shape = [jax.ShapeDtypeStruct((tall, rank) if last else (rank, rows), BF16)]
     if len(grams) > 1:
         out_shape.append(jax.ShapeDtypeStruct((rank, rank), BF16))
+    if not last:
+        out_shape += [jax.ShapeDtypeStruct((rank, rows // 2), BF16)]
+        out_shape += [jax.ShapeDtypeStruct((rank, rows - rows // 2), BF16)]
     out = pl.pallas_call(
         functools.partial(
             item_kernel, epoch, len(terms_a), rows, rows // 2, len(grams)
@@ -434,10 +463,11 @@
         in_specs=[VMEM] * (1 + 2 * len(terms_a) + len(grams)),
         out_specs=[VMEM] * len(out_shape),
         compiler_params=params(40),
-        cost_estimate=cost(1 << 16, 1 << 16),
+        cost_estimate=declared(f"items_{epoch}_{chunk}"),
         name=f"items_{epoch}_{chunk}",
     )(items, *terms_a, *terms_b, *grams)
-    return out[0], out[-1]
+    gram = out[1] if len(grams) > 1 else None
+    return out[0] if last else (out[0], *out[-2:]), gram
 
 
 def swapped(value, bit):
@@ -470,6 +500,7 @@
     names = [without(members, order[0]) for order in orders]
     terms = [[(keep_a, names[0])], [(keep_b, names[1])]]
     grams = [send_a] if chunk == 0 else []
+    sends = []
     for step in range(len(orders[0])):
         for p in range(2):
             terms[p].append((arrived[p], names[p]))
@@ -484,40 +515,103 @@
             names[p] = [r for r in names[p] if not r & bit]
         sends = mid_call(epoch, chunk, step, paths, grams)
         arrived = [swapped(sends[p], orders[p][step + 1]) for p in range(2)]
-    return [a for a, _ in terms[0]], [a for a, _ in terms[1]], grams
+    return [a for a, _ in terms[0]], [a for a, _ in terms[1]], grams, sends
+
+
+def scattered_direct(epoch, chunk, out, arrived, members, widths):
+    _, keep_a, _, keep_b = out[:4]
+    orders = orders_of(members)
+    names = [[r for r in without(members, order[0]) if r] for order in orders]
+    terms = [[(keep_a, names[0])], [(keep_b, names[1])]]
+    ended = [[moved(out[4 + p], orders[p][0])] for p in range(2)]
+    own = moved(out[6], 0)
+    arrived = [tied(array, own) for array in arrived]
+    sends = []
+    for step in range(len(orders[0]) - 1):
+        paths, kinds = [], []
+        for p in range(2):
+            terms[p].append((arrived[p], names[p]))
+            bit = orders[p][step + 1]
+            paths.append((terms[p], [bit], widths[p]))
+            kinds.append((p, True))
+            going = [r for r in names[p] if r & bit and r != bit]
+            names[p] = [r for r in names[p] if not r & bit]
+            if going:
+                paths.append((terms[p], going, widths[p]))
+                kinds.append((p, False))
+        sends = mid_call(epoch, chunk, step, paths, [])
+        arrived = [None, None]
+        for (p, alone), send in zip(kinds, sends):
+            bit = orders[p][step + 1]
+            if alone:
+                ended[p].append(moved(send, bit))
+            else:
+                arrived[p] = swapped(send, bit)
+    return own, ended[0], ended[1], sends
+
+
+def final_kernel(rows, width, others, count, *refs):
+    done, refs = refs[:others], refs[others:]
+    items, own = refs[:2]
+    sides = refs[2:2 + count], refs[2 + count:2 + 2 * count]
+    out = refs[2 + 2 * count]
+    for c, ref in enumerate(done):
+        out[c * rows:(c + 1) * rows] = ref[:rows].astype(F32)
+    gram = done[0][rows:]
+    totals = []
+    for side, start, size in zip(sides, (0, width), (width, rows - width)):
+        total = own[:, start:start + size].astype(F32)
+        for ref in side:
+            total += ref[...].astype(F32)
+        totals.append(total)
+    grad = jnp.concatenate(totals, axis=1)
+    new = items[...].astype(F32) - LEARN * (grad + over_columns(gram, items[...]))
+    out[others * rows:] = new.T
+
+
+def final_call(done, items, own, side_a, side_b):
+    rank, rows = items.shape
+    operands = [*done, items, own, *side_a, *side_b]
+    return pl.pallas_call(
+        functools.partial(final_kernel, rows, rows // 2, len(done), len(side_a)),
+        out_shape=jax.ShapeDtypeStruct(((len(done) + 1) * rows, rank), F32),
+        in_specs=[VMEM] * len(operands),
+        out_specs=VMEM,
+        compiler_params=params(40),
+        cost_estimate=declared("items_final"),
+        name="items_final",
+    )(*operands)
 
 
 def tied(value, *others):
     return lax.optimization_barrier((value, *others))[0]
 
 
-def gather_start(shard):
-    known = {0: moved(shard, 0)}
-    bit = 1
-    while bit < lax.axis_size("grp"):
-        known[bit] = moved(shard, bit)
-        bit *= 2
-    return known
-
-
-def gather_finish(known, after):
+def gathered(shard, upper, lower, after):
     length = lax.axis_size("grp")
-    known = {r: [tied(piece, *after)] for r, piece in known.items()}
-
-    def cut(r, lower):
+    rows, half = shard.shape[1], upper.shape[1]
+    known = {0: [moved(tied(shard, *after), 0)]}
+    for bit in orders_of(length)[0]:
+        known[bit] = [moved(shard, bit)]
+    near = [known[bit][0] for bit in orders_of(length)[0]]
+
+    def cut(r, p):
         pieces = known[r]
-        if len(pieces) == 1:
-            half = pieces[0].shape[1] // 2
-            return pieces[0][:, half:] if lower else pieces[0][:, :half]
-        return pieces[1] if lower else pieces[0]
+        if len(pieces) == 2:
+            return pieces[p]
+        return pieces[0][:, half:] if p else pieces[0][:, :half]
 
     for r in range(1, length):
-        if r in known:
-            continue
-        low = r & -r
-        high = 1 << (r.bit_length() - 1)
-        known[r] = [swapped(cut(r ^ high, False), high), swapped(cut(r ^ low, True), low)]
-    return [piece for r in range(length) for piece in known[r]]
+        if r not in known:
+            low, high = r & -r, 1 << (r.bit_length() - 1)
+            sent = [cut(r ^ high, 0), cut(r ^ low, 1)]
+            sent = [tied(piece, *after) for piece in sent]
+            known[r] = [swapped(sent[0], high), swapped(sent[1], low)]
+    found = []
+    for r, pieces in known.items():
+        spots = [(0, rows)] if len(pieces) == 1 else [(0, half), (half, rows - half)]
+        found += [(piece, [(r, *spot)]) for piece, spot in zip(pieces, spots)]
+    return found, near
 
 
 def local(ratings, row_index, col_index, row_mask, counts, owner_list, user_factors, item_factors):
@@ -543,14 +637,17 @@
         outs, olds, pieces = [], [], []
         for c in range(CHUNKS):
             if epoch == 0:
-                sources = [item_factors]
+                sources = [(item_factors, None)]
             else:
-                known, sources = gathers[c]
-                sources = sources or gather_finish(known, [grad_user])
+                sources = gathers[c]
+                if epoch + 1 == SUB and c + 1 == CHUNKS:
+                    kept = moved(tied(sources[0][0], grad_user), 0)
+            direct = epoch + 1 == SUB and c + 1 == CHUNKS
             out = tile_call(
-                epoch, c, members, scalars, ratings, row_mask, users, sources, grad_user, own_gram
+                epoch, c, direct, members, scalars, ratings, row_mask, users, sources, grad_user,
+                own_gram,
             )
-            grad_user = out[4]
+            grad_user = out[7 if direct else 4]
             outs.append(out)
             if epoch == 0:
                 pieces.append(out[5])
@@ -558,43 +655,53 @@
                 if c == 0:
                     users = out[7:9]
             else:
-                pieces += sources
-                olds.append(sources[0])
+                pieces += [array for array, _ in sources]
+                olds.append(sources[0][0])
         last = epoch + 1 == SUB
         if not last:
             new_users = user_call(epoch, block_rows, owners, full_users, grad_user, pieces)
             full_users = new_users[0]
         shards = []
         grams = None
-        firsts = [exchanged(out, members) for out in outs]
+        reduced = []
+        ahead = None
         for c in range(CHUNKS):
-            following = min(c + 1, CHUNKS - 1)
-            arrived = [tied(array, outs[following][4]) for array in firsts[c]]
-            terms_a, terms_b, found = scattered(
-                epoch, c, outs[c], arrived, members, (rows // 2, rows - rows // 2)
+            arrived = ahead if ahead else exchanged(outs[c], members)
+            arrived = [tied(array, grad_user if last else outs[-1][4]) for array in arrived]
+            if last:
+                if c == 0:
+                    ahead = exchanged(outs[1], members)
+                    arrived = [tied(array, kept, *ahead) for array in arrived]
+                else:
+                    arrived = [tied(array, grad_user) for array in ahead]
+            reduce = scattered_direct if last and c + 1 == CHUNKS else scattered
+            reduced.append(
+                reduce(epoch, c, outs[c], arrived, members, (rows // 2, rows - rows // 2))
             )
+        for c in range(CHUNKS - 1 if last else CHUNKS):
+            terms_a, terms_b, found, sent = reduced[c]
             old = olds[c]
             if not last:
-                old = tied(old, full_users, *firsts[following])
+                old = tied(old, *reduced[min(c + 1, CHUNKS - 1)][3])
+                old = tied(old, full_users)
             shard, gram = item_call(epoch, c, shard_rows, old, terms_a, terms_b, found or grams)
             if found:
                 grams = [gram]
             shards.append(shard)
         if last:
-            grad_user = tied(grad_user, *shards)
+            done = [moved(shard, 0) for shard in shards]
+            own, side_a, side_b, sent = reduced[-1]
+            grad_user = tied(grad_user, *sent)
+            item_final = final_call(done, kept, own, side_a, side_b)
             full_users = user_call(epoch, block_rows, owners, full_users, grad_user, pieces)[0]
         else:
             users, own_gram = new_users[1:3], new_users[3]
-            gathers = []
-            for shard in shards:
-                known = gather_start(tied(shard, *early) if gathers else shard)
-                if gathers:
-                    gathers.append((known, None))
-                else:
-                    gathers.append((known, gather_finish(known, [])))
-                early = [piece for r, piece in enumerate(gathers[0][1]) if r > 2]
-    finals = [moved(shard, 0) for shard in shards]
-    return full_users, jnp.concatenate(finals, axis=0).astype(F32)
+            gathers = [gathered(*shard, [shards[-1][0]]) for shard in shards]
+            near = gathers[-1][1]
+            gathers = [found for found, _ in gathers]
+            (array, columns), *rest = gathers[0]
+            gathers[0] = [(tied(array, *near), columns), *rest]
+    return full_users, item_final
 
 
 def solution(mesh):

time: 147 us -> 137 us (0.932)
  waiting for transfers between devices: 67.4 us -> 40 us
  starting transfers between devices: 34.5 us -> 53.6 us
    ppermute x8 -> x13, starting transfers between devices: 7.18 us -> 25.2 us  [moved(): return lax.ppermute(value, ('blk', 'grp'), pairs)]
    ppermute x20 -> x18, waiting for transfers between devices: 38.1 us -> 22.5 us  [swapped(): return lax.ppermute(value, 'grp', [(i, i ^ bit) for i in range(length)])]
    ppermute x8 -> x13, waiting for transfers between devices: 29.3 us -> 17.4 us  [moved(): return lax.ppermute(value, ('blk', 'grp'), pairs)]
    pallas_call x4 -> x3, Pallas kernels: 2.26 us -> 3.65 us  [item_call(): pl.pallas_call(functools.partial(item_kernel, epoch, len(terms_a), rows,...]
    ppermute x20 -> x18, starting transfers between devices: 27.4 us -> 28.4 us  [swapped(): return lax.ppermute(value, 'grp', [(i, i ^ bit) for i in range(length)])]
    pallas_call x4 -> x5, Pallas kernels: 28.6 us -> 28.4 us  [the longest x4 26.5 us: tile_call(): pl.pallas_call(functools.partial(tile_kernel, epoch, chunk, direct, membe...]
  transfers between devices with their start and end apart: 28 -> 31, of which waited for: 22 -> 15; matrix products, arithmetic and copies ran while one was open for 0% -> 0% of each run, Pallas kernels for 21% -> 24%
where the time goes in v6:
time: 137 us
  starting transfers between devices  53.6 us (39%)
  Pallas kernels  42.6 us (31%)
  waiting for transfers between devices  40 us (29%)
    ppermute x18, starting transfers between devices, swapped(): return lax.ppermute(value, 'grp', [(i, i ^ bit) for i in range(length)])  28.4 us
    pallas_call x4, Pallas kernels, tile_call(): pl.pallas_call(functools.partial(tile_kernel, epoch, chunk, direct, membe...  26.5 us
    ppermute x13, starting transfers between devices, moved(): return lax.ppermute(value, ('blk', 'grp'), pairs)  25.2 us
    ppermute x18, waiting for transfers between devices, swapped(): return lax.ppermute(value, 'grp', [(i, i ^ bit) for i in range(length)])  22.5 us
    ppermute x13, waiting for transfers between devices, moved(): return lax.ppermute(value, ('blk', 'grp'), pairs)  17.4 us
    pallas_call x2, Pallas kernels, user_call(): pl.pallas_call(functools.partial(user_kernel, epoch, block_rows), out_sha...  10.1 us
    pallas_call x3, Pallas kernels, item_call(): pl.pallas_call(functools.partial(item_kernel, epoch, len(terms_a), rows,...  3.65 us
  transfers between devices with their start and end apart: 31, of which 15 were waited for; matrix products, arithmetic and copies ran while one was open for 0% of the time, Pallas kernels for 24%

profile of v6, /device:TPU:0, one launch (start us, length us, event | category | flops | bytes accessed | tf_op | source)
XLA Modules:
  0.0 137.1 jit_solution(1039240247272058795)
XLA Ops:
  0.6 8.0 %tiles_0_0.1 = (bf16[128,2176]{1,0:T(8,128)(2,1)S(1)}, bf16[128,2048]{1,0:T(8,128)(2,1)S(1)}, bf16[128,2048]{1,0:T(8,128)(2,1)S(1)}, bf16[128,2048]{1,0:T(8,128)...) custom-call(s32[2,1,1,64]{3,2,1,0:T(1,128)} %refs_0_.7, ...), custom_call_target="tpu_custom_call" | custom-call | flops 16000000000 | bytes 65536 | tf_op jit(solution)/shard_map/tiles_0_0/pallas_call | solution.py:318
  8.7 3.0 %collective-permute-start.4 = (bf16[128,2176]{1,0:T(8,128)(2,1)S(1)}, bf16[128,2176]{1,0:T(8,128)(2,1)S(1)}, u32[]{:S(2)}, u32[]{:S(2)}) collective-permute-start(bf16[128,2176]{1,0:T(8,128)(2,1)S(1)} %get-tuple-element.96.refs_4_.refs_6_), channel_id=1, source_target_pairs={{0,1},{1,0},{2,3},{3,2},{4,5},{5,4},{6,7},{7,6},{8,9},{9,8},{10,11... | collective-permute-start | bytes 1671176 | tf_op jit(solution)/shard_map/ppermute | solution.py:475
  11.7 2.0 %collective-permute-start.5 = (bf16[128,2048]{1,0:T(8,128)(2,1)S(1)}, bf16[128,2048]{1,0:T(8,128)(2,1)S(1)}, u32[]{:S(2)}, u32[]{:S(2)}) collective-permute-start(bf16[128,2048]{1,0:T(8,128)(2,1)S(1)} %get-tuple-element.99), channel_id=1, source_target_pairs={{0,2},{1,3},{2,0},{3,1},{4,6},{5,7},{6,4},{7,5},{8,10},{9,11},{10,... | collective-permute-start | bytes 1572872 | tf_op jit(solution)/shard_map/ppermute | solution.py:475
  13.7 6.1 %tiles_0_1.1 = (bf16[128,2048]{1,0:T(8,128)(2,1)S(1)}, bf16[128,2048]{1,0:T(8,128)(2,1)S(1)}, bf16[128,2048]{1,0:T(8,128)(2,1)S(1)}, bf16[128,2048]{1,0:T(8,128)...) custom-call(s32[2,1,1,64]{3,2,1,0:T(1,128)} %refs_0_.7, ...), custom_call_target="tpu_custom_call" | custom-call | flops 16000000000 | bytes 65536 | tf_op jit(solution)/shard_map/tiles_0_1/pallas_call | solution.py:318
  19.9 1.7 %collective-permute-start.1 = (bf16[128,2048]{1,0:T(8,128)(2,1)S(1)}, bf16[128,2048]{1,0:T(8,128)(2,1)S(1)}, u32[]{:S(2)}, u32[]{:S(2)}) collective-permute-start(bf16[128,2048]{1,0:T(8,128)(2,1)S(1)} %get-tuple-element.86), channel_id=1, source_target_pairs={{0,2},{1,3},{2,0},{3,1},{4,6},{5,7},{6,4},{7,5},{8,10},{9,11},{10,... | collective-permute-start | bytes 1572872 | tf_op jit(solution)/shard_map/ppermute | solution.py:475
  21.7 4.7 %collective-permute-done.5.refs_3_.refs_4_ = bf16[128,2048]{1,0:T(8,128)(2,1)S(1)} collective-permute-done((bf16[128,2048]{1,0:T(8,128)(2,1)S(1)}, bf16[128,2048]{1,0:T(8,128)(2,1)S(1)}, u32[]{:S(2)}, u32[]{:S(2)}) %collective-permute-start.5) | collective-permute-done | bytes 524320 | tf_op jit(solution)/shard_map/ppermute | solution.py:475
  26.4 2.3 %collective-permute-start.6 = (bf16[128,1152]{1,0:T(8,128)(2,1)S(1)}, bf16[128,1152]{1,0:T(8,128)(2,1)S(1)}, u32[]{:S(2)}, u32[]{:S(2)}) collective-permute-start(bf16[128,1152]{1,0:T(8,128)(2,1)S(1)} %get-tuple-element.101), channel_id=1, source_target_pairs={{0,2},{1,3},{2,0},{3,1},{4,6},{5,7},{6,4},{7,5},{8,10},{9,11},{10,... | collective-permute-start | bytes 884744 | tf_op jit(solution)/shard_map/ppermute | solution.py:475
  28.8 0.7 collective-permute-start.7
  29.4 4.8 %users_0.1 = (f32[2048,128]{1,0:T(8,128)S(1)}, bf16[2048,128]{1,0:T(8,128)(2,1)S(1)}, bf16[128,2048]{1,0:T(8,128)(2,1)S(1)}, bf16[128,128]{1,0:T(8,128)(2,1)S(1)}) custom-call(s32[1,2]{1,0:T(1,128)S(1)} %bitcast.6, f32[2048,128]{1,0:T(8,128)S(1)} %copy-done, f32[128,2048]{1,0:T(8,128)S(1)} %get-tuple-element.75.grad, ...), custom_call_target="tpu_custom_call" | custom-call | flops 10000000000 | bytes 65536 | tf_op jit(solution)/shard_map/users_0/pallas_call | solution.py:357
  34.2 1.5 %collective-permute-done.refs_1_ = bf16[128,2048]{1,0:T(8,128)(2,1)S(1)} collective-permute-done((bf16[128,2048]{1,0:T(8,128)(2,1)S(1)}, bf16[128,2048]{1,0:T(8,128)(2,1)S(1)}, u32[]{:S(2)}, u32[]{:S(2)}) %collective-permute-start) | collective-permute-done | bytes 524320 | tf_op jit(solution)/shard_map/ppermute | solution.py:475
  35.7 1.8 %collective-permute-done.1.refs_3_.refs_4_ = bf16[128,2048]{1,0:T(8,128)(2,1)S(1)} collective-permute-done((bf16[128,2048]{1,0:T(8,128)(2,1)S(1)}, bf16[128,2048]{1,0:T(8,128)(2,1)S(1)}, u32[]{:S(2)}, u32[]{:S(2)}) %collective-permute-start.1) | collective-permute-done | bytes 524320 | tf_op jit(solution)/shard_map/ppermute | solution.py:475
  37.7 2.3 %collective-permute-start.2 = (bf16[128,1024]{1,0:T(8,128)(2,1)S(1)}, bf16[128,1024]{1,0:T(8,128)(2,1)S(1)}, u32[]{:S(2)}, u32[]{:S(2)}) collective-permute-start(bf16[128,1024]{1,0:T(8,128)(2,1)S(1)} %get-tuple-element.88), channel_id=1, source_target_pairs={{0,2},{1,3},{2,0},{3,1},{4,6},{5,7},{6,4},{7,5},{8,10},{9,11},{10,... | collective-permute-start | bytes 786440 | tf_op jit(solution)/shard_map/ppermute | solution.py:475
  40.0 0.7 collective-permute-start.3
  40.6 0.7 collective-permute-done.7.refs_5_
  41.3 2.5 %collective-permute-done.6.refs_2_.refs_8_ = bf16[128,1152]{1,0:T(8,128)(2,1)S(1)} collective-permute-done((bf16[128,1152]{1,0:T(8,128)(2,1)S(1)}, bf16[128,1152]{1,0:T(8,128)(2,1)S(1)}, u32[]{:S(2)}, u32[]{:S(2)}) %collective-permute-start.6) | collective-permute-done | bytes 294944 | tf_op jit(solution)/shard_map/ppermute | solution.py:475
  43.9 1.3 items_0_0.1
  45.5 2.8 %collective-permute-start.15 = (bf16[128,2048]{1,0:T(8,128)(2,1)S(1)}, bf16[128,2048]{1,0:T(8,128)(2,1)S(1)}, u32[]{:S(2)}, u32[]{:S(2)}) collective-permute-start(bf16[128,2048]{1,0:T(8,128)(2,1)S(1)} %get-tuple-element.109), channel_id=1, source_target_pairs={{0,6},{1,7},{2,4},{3,5},{4,10},{5,11},{6,8},{7,9},{8,14},{9,15},{1... | collective-permute-start | bytes 1572872 | tf_op jit(solution)/shard_map/ppermute | solution.py:485
  48.3 1.2 collective-permute-done.2.refs_2_
  49.5 1.3 items_0_1.1
  50.8 1.0 collective-permute-start.9
  51.8 7.7 %collective-permute-start.10 = (bf16[128,2048]{1,0:T(8,128)(2,1)S(1)}, bf16[128,2048]{1,0:T(8,128)(2,1)S(1)}, u32[]{:S(2)}, u32[]{:S(2)}) collective-permute-start(bf16[128,2048]{1,0:T(8,128)(2,1)S(1)} %get-tuple-element.105), channel_id=1, source_target_pairs={{0,6},{1,7},{2,4},{3,5},{4,10},{5,11},{6,8},{7,9},{8,14},{9,15},{1... | collective-permute-start | bytes 1572872 | tf_op jit(solution)/shard_map/ppermute | solution.py:485
  59.5 0.9 collective-permute-start.13
  60.4 2.0 %collective-permute-done.15.refs_10_.refs_2_ = bf16[128,2048]{1,0:T(8,128)(2,1)S(1)} collective-permute-done((bf16[128,2048]{1,0:T(8,128)(2,1)S(1)}, bf16[128,2048]{1,0:T(8,128)(2,1)S(1)}, u32[]{:S(2)}, u32[]{:S(2)}) %collective-permute-start.15) | collective-permute-done | bytes 524320 | tf_op jit(solution)/shard_map/ppermute | solution.py:485
  62.5 2.1 %collective-permute-start.17 = (bf16[128,1024]{1,0:T(8,128)(2,1)S(1)}, bf16[128,1024]{1,0:T(8,128)(2,1)S(1)}, u32[]{:S(2)}, u32[]{:S(2)}) collective-permute-start(bf16[128,1024]{1,0:T(8,128)(2,1)S(1)} %slice.19), channel_id=1, source_target_pairs={{0,1},{1,0},{2,3},{3,2},{4,5},{5,4},{6,7},{7,6},{8,9},{9,8},{10,11... | collective-permute-start | bytes 786440 | tf_op jit(solution)/shard_map/ppermute | solution.py:475
  64.5 7.9 %collective-permute-done.9.refs_9_.refs_6_ = bf16[128,2048]{1,0:T(8,128)(2,1)S(1)} collective-permute-done((bf16[128,2048]{1,0:T(8,128)(2,1)S(1)}, bf16[128,2048]{1,0:T(8,128)(2,1)S(1)}, u32[]{:S(2)}, u32[]{:S(2)}) %collective-permute-start.9) | collective-permute-done | bytes 524320 | tf_op jit(solution)/shard_map/ppermute | solution.py:485
  72.4 1.7 %collective-permute-start.8 = (bf16[128,2048]{1,0:T(8,128)(2,1)S(1)}, bf16[128,2048]{1,0:T(8,128)(2,1)S(1)}, u32[]{:S(2)}, u32[]{:S(2)}) collective-permute-start(bf16[128,2048]{1,0:T(8,128)(2,1)S(1)} %get-tuple-element.105), channel_id=1, source_target_pairs={{0,4},{1,5},{2,6},{3,7},{4,8},{5,9},{6,10},{7,11},{8,12},{9,13},{1... | collective-permute-start | bytes 1572872 | tf_op jit(solution)/shard_map/ppermute | solution.py:485
  74.7 1.3 collective-permute-start.11
  75.9 1.6 %collective-permute-done.13.refs_8_.refs_0_.items = bf16[128,2048]{1,0:T(8,128)(2,1)S(1)} collective-permute-done((bf16[128,2048]{1,0:T(8,128)(2,1)S(1)}, bf16[128,2048]{1,0:T(8,128)(2,1)S(1)}, u32[]{:S(2)}, u32[]{:S(2)}) %collective-permute-start.13) | collective-permute-done | bytes 524320 | tf_op jit(solution)/shard_map/ppermute | solution.py:485
  77.5 2.1 %collective-permute-start.12 = (bf16[128,1024]{1,0:T(8,128)(2,1)S(1)}, bf16[128,1024]{1,0:T(8,128)(2,1)S(1)}, u32[]{:S(2)}, u32[]{:S(2)}) collective-permute-start(bf16[128,1024]{1,0:T(8,128)(2,1)S(1)} %slice.17), channel_id=1, source_target_pairs={{0,1},{1,0},{2,3},{3,2},{4,5},{5,4},{6,7},{7,6},{8,9},{9,8},{10,11... | collective-permute-start | bytes 786440 | tf_op jit(solution)/shard_map/ppermute | solution.py:475
  79.7 7.2 %tiles_1_0.1 = (bf16[128,2176]{1,0:T(8,128)(2,1)S(1)}, bf16[128,2048]{1,0:T(8,128)(2,1)S(1)}, bf16[128,2048]{1,0:T(8,128)(2,1)S(1)}, bf16[128,2048]{1,0:T(8,128)(2,1)S(1)}, f32[128,2048]{1,0:T(8,128)S(1)}) custom-call(s32[2,1,1,64]{3,2,1,0:T(1,128)} %refs_0_.7, s32[2,1,1,64]{3,2,1,0:T(1,128)} %refs_1_.7, s32[1,2]{1,0:T(1,128)} %bitcast.10, s32[1,2]{1,0:T(1,128)} %bitcast.4, ...), custom_call_target="tpu_custom_call" | custom-call | flops 16000000000 | bytes 65536 | tf_op jit(solution)/shard_map/tiles_1_0/pallas_call | solution.py:318
  87.1 1.8 %collective-permute-start.23 = (bf16[128,2048]{1,0:T(8,128)(2,1)S(1)}, bf16[128,2048]{1,0:T(8,128)(2,1)S(1)}, u32[]{:S(2)}, u32[]{:S(2)}) collective-permute-start(bf16[128,2048]{1,0:T(8,128)(2,1)S(1)} %get-tuple-element.134), channel_id=1, source_target_pairs={{0,2},{1,3},{2,0},{3,1},{4,6},{5,7},{6,4},{7,5},{8,10},{9,11},{10,... | collective-permute-start | bytes 1572872 | tf_op jit(solution)/shard_map/ppermute | solution.py:475
  88.9 5.1 %tiles_1_1.1 = (bf16[128,1024]{1,0:T(8,128)(2,1)S(1)}, bf16[128,1024]{1,0:T(8,128)(2,1)S(1)}, bf16[128,1024]{1,0:T(8,128)(2,1)S(1)}, bf16[128,1024]{1,0:T(8,128)...) custom-call(s32[2,1,1,64]{3,2,1,0:T(1,128)} %refs_0_.7, ...), custom_call_target="tpu_custom_call" | custom-call | flops 16000000000 | bytes 65536 | tf_op jit(solution)/shard_map/tiles_1_1/pallas_call | solution.py:318
  94.0 4.0 %collective-permute-start.18 = (bf16[128,1024]{1,0:T(8,128)(2,1)S(1)}, bf16[128,1024]{1,0:T(8,128)(2,1)S(1)}, u32[]{:S(2)}, u32[]{:S(2)}) collective-permute-start(bf16[128,1024]{1,0:T(8,128)(2,1)S(1)} %get-tuple-element.117), channel_id=1, source_target_pairs={{0,1},{1,0},{2,3},{3,2},{4,5},{5,4},{6,7},{7,6},{8,9},{9,8},{10,11... | collective-permute-start | bytes 786440 | tf_op jit(solution)/shard_map/ppermute | solution.py:475
  98.0 1.5 %collective-permute-done.23.refs_3_.refs_4_ = bf16[128,2048]{1,0:T(8,128)(2,1)S(1)} collective-permute-done((bf16[128,2048]{1,0:T(8,128)(2,1)S(1)}, bf16[128,2048]{1,0:T(8,128)(2,1)S(1)}, u32[]{:S(2)}, u32[]{:S(2)}) %collective-permute-start.23) | collective-permute-done | bytes 524320 | tf_op jit(solution)/shard_map/ppermute | solution.py:475
  99.5 3.8 %collective-permute-start.19 = (bf16[128,2048]{1,0:T(8,128)(2,1)S(1)}, bf16[128,2048]{1,0:T(8,128)(2,1)S(1)}, u32[]{:S(2)}, u32[]{:S(2)}) collective-permute-start(bf16[128,2048]{1,0:T(8,128)(2,1)S(1)} %get-tuple-element.119), channel_id=1, source_target_pairs={{0,4},{1,5},{2,6},{3,7},{4,8},{5,9},{6,10},{7,11},{8,12},{9,13},{1... | collective-permute-start | bytes 1572872 | tf_op jit(solution)/shard_map/ppermute | solution.py:485
  103.3 1.0 collective-permute-done.18.refs_1_
  104.3 2.3 %collective-permute-done.20.refs_3_ = bf16[128,1024]{1,0:T(8,128)(2,1)S(1)} collective-permute-done((bf16[128,1024]{1,0:T(8,128)(2,1)S(1)}, bf16[128,1024]{1,0:T(8,128)(2,1)S(1)}, u32[]{:S(2)}, u32[]{:S(2)}) %collective-permute-start.20) | collective-permute-done | bytes 262176 | tf_op jit(solution)/shard_map/ppermute | solution.py:475
  106.7 1.0 collective-permute-start.24
  107.8 3.1 %collective-permute-start.25 = (bf16[128,1024]{1,0:T(8,128)(2,1)S(1)}, bf16[128,1024]{1,0:T(8,128)(2,1)S(1)}, u32[]{:S(2)}, u32[]{:S(2)}) collective-permute-start(bf16[128,1024]{1,0:T(8,128)(2,1)S(1)} %get-tuple-element.138), channel_id=1, source_target_pairs={{0,1},{1,0},{2,3},{3,2},{4,5},{5,4},{6,7},{7,6},{8,9},{9,8},{10,11... | collective-permute-start | bytes 786440 | tf_op jit(solution)/shard_map/ppermute | solution.py:475
  110.9 3.1 %collective-permute-start.29 = (bf16[128,1024]{1,0:T(8,128)(2,1)S(1)}, bf16[128,1024]{1,0:T(8,128)(2,1)S(1)}, u32[]{:S(2)}, u32[]{:S(2)}) collective-permute-start(bf16[128,1024]{1,0:T(8,128)(2,1)S(1)} %get-tuple-element.141), channel_id=1, source_target_pairs={{0,6},{1,7},{2,4},{3,5},{4,10},{5,11},{6,8},{7,9},{8,14},{9,15},{1... | collective-permute-start | bytes 786440 | tf_op jit(solution)/shard_map/ppermute | solution.py:485
  114.1 1.0 collective-permute-start.28
  115.1 5.3 %collective-permute-done.25.refs_5_ = bf16[128,1024]{1,0:T(8,128)(2,1)S(1)} collective-permute-done((bf16[128,1024]{1,0:T(8,128)(2,1)S(1)}, bf16[128,1024]{1,0:T(8,128)(2,1)S(1)}, u32[]{:S(2)}, u32[]{:S(2)}) %collective-permute-start.25) | collective-permute-done | bytes 262176 | tf_op jit(solution)/shard_map/ppermute | solution.py:475
  120.4 0.8 collective-permute-start.30
  121.2 1.1 items_1_0.1
  122.3 2.0 %collective-permute-start.26 = (bf16[2176,128]{1,0:T(8,128)(2,1)S(1)}, bf16[2176,128]{1,0:T(8,128)(2,1)S(1)}, u32[]{:S(2)}, u32[]{:S(2)}) collective-permute-start(bf16[2176,128]{1,0:T(8,128)(2,1)S(1)} %get-tuple-element.139), channel_id=1, source_target_pairs={{0,4},{1,5},{2,6},{3,7},{4,8},{5,9},{6,10},{7,11},{8,12},{9,13},{1... | collective-permute-start | bytes 1671176 | tf_op jit(solution)/shard_map/ppermute | solution.py:485
  124.4 5.3 %users_1.1 = f32[2048,128]{1,0:T(8,128)} custom-call(s32[1,2]{1,0:T(1,128)S(1)} %bitcast.7, f32[2048,128]{1,0:T(8,128)S(1)} %get-tuple-element.78.users, f32[128,2048]{1,0:T(8,128)S(1)} %get-tuple-element.127.grad, bf16[128,2048]{1,0:T(8,128)(2,1)S(1)} %collective-permute-done.13.refs_8_.refs_0_.items, ...), custom_call_target="tpu_custom_call" | custom-call | flops 10000000000 | bytes 65536 | tf_op jit(solution)/shard_map/users_1/pallas_call | solution.py:357
  129.7 5.5 %collective-permute-done.26.refs_0_ = bf16[2176,128]{1,0:T(8,128)(2,1)S(1)} collective-permute-done((bf16[2176,128]{1,0:T(8,128)(2,1)S(1)}, bf16[2176,128]{1,0:T(8,128)(2,1)S(1)}, u32[]{:S(2)}, u32[]{:S(2)}) %collective-permute-start.26) | collective-permute-done | bytes 557088 | tf_op jit(solution)/shard_map/ppermute | solution.py:485
  135.2 1.9 %items_final.1 = f32[4096,128]{1,0:T(8,128)} custom-call(bf16[2176,128]{1,0:T(8,128)(2,1)S(1)} %collective-permute-done.26.refs_0_, bf16[128,2048]{1,0:T(8,128)(2,1)S(1)} %collective-permute-done.22.refs_1_, bf16[128,2048]{1,0:T(8,128)(2,1)S(1)} %collective-permute-done.19.refs_2_, bf16[128,1024]{1,0:T(8,128)(2,1)S(1)} %collective-permute-done.27.refs_3_, ...), custom_call_target="tpu_custom_call" | custom-call | flops 1200000000 | bytes 65536 | tf_op jit(solution)/shard_map/items_final/pallas_call | solution.py:575
  (38 shorter events, 1.8 us)
Async XLA Ops:
  8.7 17.7 %collective-permute-start.4 = (bf16[128,2176]{1,0:T(8,128)(2,1)S(1)}, bf16[128,2176]{1,0:T(8,128)(2,1)S(1)}, u32[]{:S(2)}, u32[]{:S(2)}) collective-permute-start(bf16[128,2176]{1,0:T(8,128)(2,1)S(1)} %get-tuple-element.96.refs_4_.refs_6_), channel_id=1, source_target_pairs={{0,1},{1,0},{2,3},{3,2},{4,5},{5,4},{6,7},{7,6},{8,9},{9,8},{10,11... | collective-permute-start | bytes 1671176 | tf_op jit(solution)/shard_map/ppermute | solution.py:475
  11.7 14.6 %collective-permute-start.5 = (bf16[128,2048]{1,0:T(8,128)(2,1)S(1)}, bf16[128,2048]{1,0:T(8,128)(2,1)S(1)}, u32[]{:S(2)}, u32[]{:S(2)}) collective-permute-start(bf16[128,2048]{1,0:T(8,128)(2,1)S(1)} %get-tuple-element.99), channel_id=1, source_target_pairs={{0,2},{1,3},{2,0},{3,1},{4,6},{5,7},{6,4},{7,5},{8,10},{9,11},{10,... | collective-permute-start | bytes 1572872 | tf_op jit(solution)/shard_map/ppermute | solution.py:475
  19.8 9.6 %copy-start = (f32[2048,128]{1,0:T(8,128)S(1)}, f32[2048,128]{1,0:T(8,128)}, u32[]{:S(2)}) copy-start(f32[2048,128]{1,0:T(8,128)} %users.1) | copy-start | bytes 3145732
  19.8 9.6 %copy-start.1 = (s32[2,1]{0,1:T(1,128)S(1)}, s32[2,1]{0,1:T(1,128)}, u32[]{:S(2)}) copy-start(s32[2,1]{0,1:T(1,128)} %param.13) | copy-start | bytes 28
  19.8 15.9 %collective-permute-start = (bf16[128,2048]{1,0:T(8,128)(2,1)S(1)}, bf16[128,2048]{1,0:T(8,128)(2,1)S(1)}, u32[]{:S(2)}, u32[]{:S(2)}) collective-permute-start(bf16[128,2048]{1,0:T(8,128)(2,1)S(1)} %get-tuple-element.83), channel_id=1, source_target_pairs={{0,1},{1,0},{2,3},{3,2},{4,5},{5,4},{6,7},{7,6},{8,9},{9,8},{10,11... | collective-permute-start | bytes 1572872 | tf_op jit(solution)/shard_map/ppermute | solution.py:475
  19.9 17.6 %collective-permute-start.1 = (bf16[128,2048]{1,0:T(8,128)(2,1)S(1)}, bf16[128,2048]{1,0:T(8,128)(2,1)S(1)}, u32[]{:S(2)}, u32[]{:S(2)}) collective-permute-start(bf16[128,2048]{1,0:T(8,128)(2,1)S(1)} %get-tuple-element.86), channel_id=1, source_target_pairs={{0,2},{1,3},{2,0},{3,1},{4,6},{5,7},{6,4},{7,5},{8,10},{9,11},{10,... | collective-permute-start | bytes 1572872 | tf_op jit(solution)/shard_map/ppermute | solution.py:475
  26.4 17.4 %collective-permute-start.6 = (bf16[128,1152]{1,0:T(8,128)(2,1)S(1)}, bf16[128,1152]{1,0:T(8,128)(2,1)S(1)}, u32[]{:S(2)}, u32[]{:S(2)}) collective-permute-start(bf16[128,1152]{1,0:T(8,128)(2,1)S(1)} %get-tuple-element.101), channel_id=1, source_target_pairs={{0,2},{1,3},{2,0},{3,1},{4,6},{5,7},{6,4},{7,5},{8,10},{9,11},{10,... | collective-permute-start | bytes 884744 | tf_op jit(solution)/shard_map/ppermute | solution.py:475
  28.8 12.6 %collective-permute-start.7 = (bf16[128,1024]{1,0:T(8,128)(2,1)S(1)}, bf16[128,1024]{1,0:T(8,128)(2,1)S(1)}, u32[]{:S(2)}, u32[]{:S(2)}) collective-permute-start(bf16[128,1024]{1,0:T(8,128)(2,1)S(1)} %get-tuple-element.102), channel_id=1, source_target_pairs={{0,1},{1,0},{2,3},{3,2},{4,5},{5,4},{6,7},{7,6},{8,9},{9,8},{10,11... | collective-permute-start | bytes 786440 | tf_op jit(solution)/shard_map/ppermute | solution.py:475
  37.7 11.8 %collective-permute-start.2 = (bf16[128,1024]{1,0:T(8,128)(2,1)S(1)}, bf16[128,1024]{1,0:T(8,128)(2,1)S(1)}, u32[]{:S(2)}, u32[]{:S(2)}) collective-permute-start(bf16[128,1024]{1,0:T(8,128)(2,1)S(1)} %get-tuple-element.88), channel_id=1, source_target_pairs={{0,2},{1,3},{2,0},{3,1},{4,6},{5,7},{6,4},{7,5},{8,10},{9,11},{10,... | collective-permute-start | bytes 786440 | tf_op jit(solution)/shard_map/ppermute | solution.py:475
  40.0 9.5 %collective-permute-start.3 = (bf16[128,1024]{1,0:T(8,128)(2,1)S(1)}, bf16[128,1024]{1,0:T(8,128)(2,1)S(1)}, u32[]{:S(2)}, u32[]{:S(2)}) collective-permute-start(bf16[128,1024]{1,0:T(8,128)(2,1)S(1)} %get-tuple-element.89), channel_id=1, source_target_pairs={{0,1},{1,0},{2,3},{3,2},{4,5},{5,4},{6,7},{7,6},{8,9},{9,8},{10,11... | collective-permute-start | bytes 786440 | tf_op jit(solution)/shard_map/ppermute | solution.py:475
  45.1 15.2 %collective-permute-start.14 = (bf16[128,2048]{1,0:T(8,128)(2,1)S(1)}, bf16[128,2048]{1,0:T(8,128)(2,1)S(1)}, u32[]{:S(2)}, u32[]{:S(2)}) collective-permute-start(bf16[128,2048]{1,0:T(8,128)(2,1)S(1)} %get-tuple-element.109), channel_id=1, source_target_pairs={{0,5},{1,4},{2,7},{3,6},{4,9},{5,8},{6,11},{7,10},{8,13},{9,12},{1... | collective-permute-start | bytes 1572872 | tf_op jit(solution)/shard_map/ppermute | solution.py:485
  45.5 17.0 %collective-permute-start.15 = (bf16[128,2048]{1,0:T(8,128)(2,1)S(1)}, bf16[128,2048]{1,0:T(8,128)(2,1)S(1)}, u32[]{:S(2)}, u32[]{:S(2)}) collective-permute-start(bf16[128,2048]{1,0:T(8,128)(2,1)S(1)} %get-tuple-element.109), channel_id=1, source_target_pairs={{0,6},{1,7},{2,4},{3,5},{4,10},{5,11},{6,8},{7,9},{8,14},{9,15},{1... | collective-permute-start | bytes 1572872 | tf_op jit(solution)/shard_map/ppermute | solution.py:485
  50.8 21.7 %collective-permute-start.9 = (bf16[128,2048]{1,0:T(8,128)(2,1)S(1)}, bf16[128,2048]{1,0:T(8,128)(2,1)S(1)}, u32[]{:S(2)}, u32[]{:S(2)}) collective-permute-start(bf16[128,2048]{1,0:T(8,128)(2,1)S(1)} %get-tuple-element.105), channel_id=1, source_target_pairs={{0,5},{1,4},{2,7},{3,6},{4,9},{5,8},{6,11},{7,10},{8,13},{9,12},{1... | collective-permute-start | bytes 1572872 | tf_op jit(solution)/shard_map/ppermute | solution.py:485
  51.8 22.8 %collective-permute-start.10 = (bf16[128,2048]{1,0:T(8,128)(2,1)S(1)}, bf16[128,2048]{1,0:T(8,128)(2,1)S(1)}, u32[]{:S(2)}, u32[]{:S(2)}) collective-permute-start(bf16[128,2048]{1,0:T(8,128)(2,1)S(1)} %get-tuple-element.105), channel_id=1, source_target_pairs={{0,6},{1,7},{2,4},{3,5},{4,10},{5,11},{6,8},{7,9},{8,14},{9,15},{1... | collective-permute-start | bytes 1572872 | tf_op jit(solution)/shard_map/ppermute | solution.py:485
  59.5 18.1 %collective-permute-start.13 = (bf16[128,2048]{1,0:T(8,128)(2,1)S(1)}, bf16[128,2048]{1,0:T(8,128)(2,1)S(1)}, u32[]{:S(2)}, u32[]{:S(2)}) collective-permute-start(bf16[128,2048]{1,0:T(8,128)(2,1)S(1)} %get-tuple-element.109), channel_id=1, source_target_pairs={{0,4},{1,5},{2,6},{3,7},{4,8},{5,9},{6,10},{7,11},{8,12},{9,13},{1... | collective-permute-start | bytes 1572872 | tf_op jit(solution)/shard_map/ppermute | solution.py:485
  60.4 19.3 %collective-permute-start.16 = (bf16[128,1024]{1,0:T(8,128)(2,1)S(1)}, bf16[128,1024]{1,0:T(8,128)(2,1)S(1)}, u32[]{:S(2)}, u32[]{:S(2)}) collective-permute-start(bf16[128,1024]{1,0:T(8,128)(2,1)S(1)} %slice.18), channel_id=1, source_target_pairs={{0,2},{1,3},{2,0},{3,1},{4,6},{5,7},{6,4},{7,5},{8,10},{9,11},{10,... | collective-permute-start | bytes 786440 | tf_op jit(solution)/shard_map/ppermute | solution.py:475
  62.5 17.2 %collective-permute-start.17 = (bf16[128,1024]{1,0:T(8,128)(2,1)S(1)}, bf16[128,1024]{1,0:T(8,128)(2,1)S(1)}, u32[]{:S(2)}, u32[]{:S(2)}) collective-permute-start(bf16[128,1024]{1,0:T(8,128)(2,1)S(1)} %slice.19), channel_id=1, source_target_pairs={{0,1},{1,0},{2,3},{3,2},{4,5},{5,4},{6,7},{7,6},{8,9},{9,8},{10,11... | collective-permute-start | bytes 786440 | tf_op jit(solution)/shard_map/ppermute | solution.py:475
  72.4 14.6 %collective-permute-start.8 = (bf16[128,2048]{1,0:T(8,128)(2,1)S(1)}, bf16[128,2048]{1,0:T(8,128)(2,1)S(1)}, u32[]{:S(2)}, u32[]{:S(2)}) collective-permute-start(bf16[128,2048]{1,0:T(8,128)(2,1)S(1)} %get-tuple-element.105), channel_id=1, source_target_pairs={{0,4},{1,5},{2,6},{3,7},{4,8},{5,9},{6,10},{7,11},{8,12},{9,13},{1... | collective-permute-start | bytes 1572872 | tf_op jit(solution)/shard_map/ppermute | solution.py:485
  74.7 14.2 %collective-permute-start.11 = (bf16[128,1024]{1,0:T(8,128)(2,1)S(1)}, bf16[128,1024]{1,0:T(8,128)(2,1)S(1)}, u32[]{:S(2)}, u32[]{:S(2)}) collective-permute-start(bf16[128,1024]{1,0:T(8,128)(2,1)S(1)} %slice.16), channel_id=1, source_target_pairs={{0,2},{1,3},{2,0},{3,1},{4,6},{5,7},{6,4},{7,5},{8,10},{9,11},{10,... | collective-permute-start | bytes 786440 | tf_op jit(solution)/shard_map/ppermute | solution.py:475
  77.5 11.4 %collective-permute-start.12 = (bf16[128,1024]{1,0:T(8,128)(2,1)S(1)}, bf16[128,1024]{1,0:T(8,128)(2,1)S(1)}, u32[]{:S(2)}, u32[]{:S(2)}) collective-permute-start(bf16[128,1024]{1,0:T(8,128)(2,1)S(1)} %slice.17), channel_id=1, source_target_pairs={{0,1},{1,0},{2,3},{3,2},{4,5},{5,4},{6,7},{7,6},{8,9},{9,8},{10,11... | collective-permute-start | bytes 786440 | tf_op jit(solution)/shard_map/ppermute | solution.py:475
  86.9 19.7 %collective-permute-start.21 = (bf16[128,2176]{1,0:T(8,128)(2,1)S(1)}, bf16[128,2176]{1,0:T(8,128)(2,1)S(1)}, u32[]{:S(2)}, u32[]{:S(2)}) collective-permute-start(bf16[128,2176]{1,0:T(8,128)(2,1)S(1)} %get-tuple-element.129.refs_4_.refs_6_), channel_id=1, source_target_pairs={{0,1},{1,0},{2,3},{3,2},{4,5},{5,4},{6,7},{7,6},{8,9},{9,8},{10,11... | collective-permute-start | bytes 1671176 | tf_op jit(solution)/shard_map/ppermute | solution.py:475
  87.0 19.6 %collective-permute-start.22 = (bf16[128,2048]{1,0:T(8,128)(2,1)S(1)}, bf16[128,2048]{1,0:T(8,128)(2,1)S(1)}, u32[]{:S(2)}, u32[]{:S(2)}) collective-permute-start(bf16[128,2048]{1,0:T(8,128)(2,1)S(1)} %collective-permute-done.8.refs_8_.refs_5_), channel_id=1, source_target_pairs={{0,4},{1,5},{2,6},{3,7},{4,8},{5,9},{6,10},{7,11},{8,12},{9,13},{1... | collective-permute-start | bytes 1572872 | tf_op jit(solution)/shard_map/ppermute | solution.py:485
  87.1 12.5 %collective-permute-start.23 = (bf16[128,2048]{1,0:T(8,128)(2,1)S(1)}, bf16[128,2048]{1,0:T(8,128)(2,1)S(1)}, u32[]{:S(2)}, u32[]{:S(2)}) collective-permute-start(bf16[128,2048]{1,0:T(8,128)(2,1)S(1)} %get-tuple-element.134), channel_id=1, source_target_pairs={{0,2},{1,3},{2,0},{3,1},{4,6},{5,7},{6,4},{7,5},{8,10},{9,11},{10,... | collective-permute-start | bytes 1572872 | tf_op jit(solution)/shard_map/ppermute | solution.py:475
  94.0 10.3 %collective-permute-start.18 = (bf16[128,1024]{1,0:T(8,128)(2,1)S(1)}, bf16[128,1024]{1,0:T(8,128)(2,1)S(1)}, u32[]{:S(2)}, u32[]{:S(2)}) collective-permute-start(bf16[128,1024]{1,0:T(8,128)(2,1)S(1)} %get-tuple-element.117), channel_id=1, source_target_pairs={{0,1},{1,0},{2,3},{3,2},{4,5},{5,4},{6,7},{7,6},{8,9},{9,8},{10,11... | collective-permute-start | bytes 786440 | tf_op jit(solution)/shard_map/ppermute | solution.py:475
  98.0 8.6 %collective-permute-start.20 = (bf16[128,1024]{1,0:T(8,128)(2,1)S(1)}, bf16[128,1024]{1,0:T(8,128)(2,1)S(1)}, u32[]{:S(2)}, u32[]{:S(2)}) collective-permute-start(bf16[128,1024]{1,0:T(8,128)(2,1)S(1)} %get-tuple-element.122), channel_id=1, source_target_pairs={{0,2},{1,3},{2,0},{3,1},{4,6},{5,7},{6,4},{7,5},{8,10},{9,11},{10,... | collective-permute-start | bytes 786440 | tf_op jit(solution)/shard_map/ppermute | solution.py:475
  99.5 14.4 %collective-permute-start.19 = (bf16[128,2048]{1,0:T(8,128)(2,1)S(1)}, bf16[128,2048]{1,0:T(8,128)(2,1)S(1)}, u32[]{:S(2)}, u32[]{:S(2)}) collective-permute-start(bf16[128,2048]{1,0:T(8,128)(2,1)S(1)} %get-tuple-element.119), channel_id=1, source_target_pairs={{0,4},{1,5},{2,6},{3,7},{4,8},{5,9},{6,10},{7,11},{8,12},{9,13},{1... | collective-permute-start | bytes 1572872 | tf_op jit(solution)/shard_map/ppermute | solution.py:485
  106.7 14.5 %collective-permute-start.24 = (bf16[128,1152]{1,0:T(8,128)(2,1)S(1)}, bf16[128,1152]{1,0:T(8,128)(2,1)S(1)}, u32[]{:S(2)}, u32[]{:S(2)}) collective-permute-start(bf16[128,1152]{1,0:T(8,128)(2,1)S(1)} %get-tuple-element.137), channel_id=1, source_target_pairs={{0,2},{1,3},{2,0},{3,1},{4,6},{5,7},{6,4},{7,5},{8,10},{9,11},{10,... | collective-permute-start | bytes 884744 | tf_op jit(solution)/shard_map/ppermute | solution.py:475
  107.8 12.7 %collective-permute-start.25 = (bf16[128,1024]{1,0:T(8,128)(2,1)S(1)}, bf16[128,1024]{1,0:T(8,128)(2,1)S(1)}, u32[]{:S(2)}, u32[]{:S(2)}) collective-permute-start(bf16[128,1024]{1,0:T(8,128)(2,1)S(1)} %get-tuple-element.138), channel_id=1, source_target_pairs={{0,1},{1,0},{2,3},{3,2},{4,5},{5,4},{6,7},{7,6},{8,9},{9,8},{10,11... | collective-permute-start | bytes 786440 | tf_op jit(solution)/shard_map/ppermute | solution.py:475
  110.9 18.8 %collective-permute-start.27 = (bf16[128,1024]{1,0:T(8,128)(2,1)S(1)}, bf16[128,1024]{1,0:T(8,128)(2,1)S(1)}, u32[]{:S(2)}, u32[]{:S(2)}) collective-permute-start(bf16[128,1024]{1,0:T(8,128)(2,1)S(1)} %get-tuple-element.140), channel_id=1, source_target_pairs={{0,5},{1,4},{2,7},{3,6},{4,9},{5,8},{6,11},{7,10},{8,13},{9,12},{1... | collective-permute-start | bytes 786440 | tf_op jit(solution)/shard_map/ppermute | solution.py:485
  110.9 18.8 %collective-permute-start.29 = (bf16[128,1024]{1,0:T(8,128)(2,1)S(1)}, bf16[128,1024]{1,0:T(8,128)(2,1)S(1)}, u32[]{:S(2)}, u32[]{:S(2)}) collective-permute-start(bf16[128,1024]{1,0:T(8,128)(2,1)S(1)} %get-tuple-element.141), channel_id=1, source_target_pairs={{0,6},{1,7},{2,4},{3,5},{4,10},{5,11},{6,8},{7,9},{8,14},{9,15},{1... | collective-permute-start | bytes 786440 | tf_op jit(solution)/shard_map/ppermute | solution.py:485
  114.1 15.6 %collective-permute-start.28 = (bf16[128,1024]{1,0:T(8,128)(2,1)S(1)}, bf16[128,1024]{1,0:T(8,128)(2,1)S(1)}, u32[]{:S(2)}, u32[]{:S(2)}) collective-permute-start(bf16[128,1024]{1,0:T(8,128)(2,1)S(1)} %get-tuple-element.125), channel_id=1, source_target_pairs={{0,6},{1,7},{2,4},{3,5},{4,10},{5,11},{6,8},{7,9},{8,14},{9,15},{1... | collective-permute-start | bytes 786440 | tf_op jit(solution)/shard_map/ppermute | solution.py:485
  115.1 9.3 %copy-start.2 = (s32[2,1]{0,1:T(1,128)S(1)}, s32[2,1]{0,1:T(1,128)}, u32[]{:S(2)}) copy-start(s32[2,1]{0,1:T(1,128)} %param.13) | copy-start | bytes 28
  120.4 9.3 %collective-permute-start.30 = (bf16[128,1024]{1,0:T(8,128)(2,1)S(1)}, bf16[128,1024]{1,0:T(8,128)(2,1)S(1)}, u32[]{:S(2)}, u32[]{:S(2)}) collective-permute-start(bf16[128,1024]{1,0:T(8,128)(2,1)S(1)} %get-tuple-element.126), channel_id=1, source_target_pairs={{0,5},{1,4},{2,7},{3,6},{4,9},{5,8},{6,11},{7,10},{8,13},{9,12},{1... | collective-permute-start | bytes 786440 | tf_op jit(solution)/shard_map/ppermute | solution.py:485
  122.3 12.8 %collective-permute-start.26 = (bf16[2176,128]{1,0:T(8,128)(2,1)S(1)}, bf16[2176,128]{1,0:T(8,128)(2,1)S(1)}, u32[]{:S(2)}, u32[]{:S(2)}) collective-permute-start(bf16[2176,128]{1,0:T(8,128)(2,1)S(1)} %get-tuple-element.139), channel_id=1, source_target_pairs={{0,4},{1,5},{2,6},{3,7},{4,8},{5,9},{6,10},{7,11},{8,12},{9,13},{1... | collective-permute-start | bytes 1671176 | tf_op jit(solution)/shard_map/ppermute | solution.py:485

commit v7 on v6

--- a/solution.py
+++ b/solution.py
@@ -27,7 +27,8 @@
 
 
 def declared(name):
-    flops = {"tiles": 16e9, "users": 10e9, "items": 1.2e9, "mid": 0.2e9}[name.split("_")[0]]
+    costs = {"tiles": 16e9, "users": 10e9, "items": 1.2e9, "mid": 0.2e9, "mid_1_1_0": 1e9}
+    flops = costs.get(name, costs[name.split("_")[0]])
     return pl.CostEstimate(flops=int(flops), bytes_accessed=1 << 16, transcendentals=0)
 
 
@@ -554,9 +555,15 @@
     done, refs = refs[:others], refs[others:]
     items, own = refs[:2]
     sides = refs[2:2 + count], refs[2 + count:2 + 2 * count]
-    out = refs[2 + 2 * count]
+    out, held, sem = refs[2 + 2 * count:]
+
+    def leave(c):
+        spot = pl.ds(c * rows, rows)
+        return pltpu.make_async_copy(held.at[spot], out.at[spot], sem.at[c])
+
     for c, ref in enumerate(done):
-        out[c * rows:(c + 1) * rows] = ref[:rows].astype(F32)
+        held[c * rows:(c + 1) * rows] = ref[:rows].astype(F32)
+        leave(c).start()
     gram = done[0][rows:]
     totals = []
     for side, start, size in zip(sides, (0, width), (width, rows - width)):
@@ -566,7 +573,10 @@
         totals.append(total)
     grad = jnp.concatenate(totals, axis=1)
     new = items[...].astype(F32) - LEARN * (grad + over_columns(gram, items[...]))
-    out[others * rows:] = new.T
+    held[others * rows:] = new.T
+    leave(others).start()
+    for c in range(others + 1):
+        leave(c).wait()
 
 
 def final_call(done, items, own, side_a, side_b):
@@ -574,9 +584,12 @@
     operands = [*done, items, own, *side_a, *side_b]
     return pl.pallas_call(
         functools.partial(final_kernel, rows, rows // 2, len(done), len(side_a)),
-        out_shape=jax.ShapeDtypeStruct(((len(done) + 1) * rows, rank), F32),
+        out_shape=jax.ShapeDtypeStruct((CHUNKS * rows, rank), F32),
         in_specs=[VMEM] * len(operands),
-        out_specs=VMEM,
+        out_specs=HBM,
+        scratch_shapes=[
+            pltpu.VMEM((CHUNKS * rows, rank), F32), pltpu.SemaphoreType.DMA((CHUNKS,))
+        ],
         compiler_params=params(40),
         cost_estimate=declared("items_final"),
         name="items_final",
@@ -671,7 +684,7 @@
             if last:
                 if c == 0:
                     ahead = exchanged(outs[1], members)
-                    arrived = [tied(array, kept, *ahead) for array in arrived]
+                    arrived = [tied(array, kept) for array in arrived]
                 else:
                     arrived = [tied(array, grad_user) for array in ahead]
             reduce = scattered_direct if last and c + 1 == CHUNKS else scattered

time: 137 us -> 138 us (level)
  starting transfers between devices: 53.6 us -> 39.5 us
  waiting for transfers between devices: 40 us -> 49.9 us
  Pallas kernels: 42.6 us -> 47.2 us
    ppermute x13, starting transfers between devices: 25.2 us -> 15.8 us  [moved(): return lax.ppermute(value, ('blk', 'grp'), pairs)]
    ppermute x13, waiting for transfers between devices: 17.4 us -> 24.7 us  [moved(): return lax.ppermute(value, ('blk', 'grp'), pairs)]
    pallas_call x4, Pallas kernels: 26.5 us -> 31.3 us  [tile_call(): pl.pallas_call(functools.partial(tile_kernel, epoch, chunk, direct, membe...]
    ppermute x18, starting transfers between devices: 28.4 us -> 23.7 us  [swapped(): return lax.ppermute(value, 'grp', [(i, i ^ bit) for i in range(length)])]
    ppermute x18, waiting for transfers between devices: 22.5 us -> 25.2 us  [swapped(): return lax.ppermute(value, 'grp', [(i, i ^ bit) for i in range(length)])]
  transfers between devices with their start and end apart: 31 -> 31, of which waited for: 15 -> 16; matrix products, arithmetic and copies ran while one was open for 0% -> 0% of each run, Pallas kernels for 24% -> 26%
where the time goes in v7:
time: 138 us
  waiting for transfers between devices  49.9 us (36%)
  Pallas kernels  47.2 us (34%)
  starting transfers between devices  39.5 us (29%)
    pallas_call x4, Pallas kernels, tile_call(): pl.pallas_call(functools.partial(tile_kernel, epoch, chunk, direct, membe...  31.3 us
    ppermute x18, waiting for transfers between devices, swapped(): return lax.ppermute(value, 'grp', [(i, i ^ bit) for i in range(length)])  25.2 us
    ppermute x13, waiting for transfers between devices, moved(): return lax.ppermute(value, ('blk', 'grp'), pairs)  24.7 us
    ppermute x18, starting transfers between devices, swapped(): return lax.ppermute(value, 'grp', [(i, i ^ bit) for i in range(length)])  23.7 us
    ppermute x13, starting transfers between devices, moved(): return lax.ppermute(value, ('blk', 'grp'), pairs)  15.8 us
    pallas_call x2, Pallas kernels, user_call(): pl.pallas_call(functools.partial(user_kernel, epoch, block_rows), out_sha...  10.1 us
    pallas_call x3, Pallas kernels, item_call(): pl.pallas_call(functools.partial(item_kernel, epoch, len(terms_a), rows,...  3.66 us
  transfers between devices with their start and end apart: 31, of which 16 were waited for; matrix products, arithmetic and copies ran while one was open for 0% of the time, Pallas kernels for 26%

profile of v7, /device:TPU:0, one launch (start us, length us, event | category | flops | bytes accessed | tf_op | source)
XLA Modules:
  0.0 137.6 jit_solution(2202738334124734984)
XLA Ops:
  0.6 9.6 %tiles_0_0.1 = (bf16[128,2176]{1,0:T(8,128)(2,1)S(1)}, bf16[128,2048]{1,0:T(8,128)(2,1)S(1)}, bf16[128,2048]{1,0:T(8,128)(2,1)S(1)}, bf16[128,2048]{1,0:T(8,128)...) custom-call(s32[2,1,1,64]{3,2,1,0:T(1,128)} %refs_0_.7, ...), custom_call_target="tpu_custom_call" | custom-call | flops 16000000000 | bytes 65536 | tf_op jit(solution)/shard_map/tiles_0_0/pallas_call | solution.py:319
  10.2 3.6 %collective-permute-start.4 = (bf16[128,2176]{1,0:T(8,128)(2,1)S(1)}, bf16[128,2176]{1,0:T(8,128)(2,1)S(1)}, u32[]{:S(2)}, u32[]{:S(2)}) collective-permute-start(bf16[128,2176]{1,0:T(8,128)(2,1)S(1)} %get-tuple-element.96.refs_4_.refs_6_), channel_id=1, source_target_pairs={{0,1},{1,0},{2,3},{3,2},{4,5},{5,4},{6,7},{7,6},{8,9},{9,8},{10,11... | collective-permute-start | bytes 1671176 | tf_op jit(solution)/shard_map/ppermute | solution.py:476
  13.8 1.0 collective-permute-start.5
  14.8 9.4 %tiles_0_1.1 = (bf16[128,2048]{1,0:T(8,128)(2,1)S(1)}, bf16[128,2048]{1,0:T(8,128)(2,1)S(1)}, bf16[128,2048]{1,0:T(8,128)(2,1)S(1)}, bf16[128,2048]{1,0:T(8,128)...) custom-call(s32[2,1,1,64]{3,2,1,0:T(1,128)} %refs_0_.7, ...), custom_call_target="tpu_custom_call" | custom-call | flops 16000000000 | bytes 65536 | tf_op jit(solution)/shard_map/tiles_0_1/pallas_call | solution.py:319
  24.3 1.2 collective-permute-start.1
  25.4 1.9 %collective-permute-done.5.refs_3_.refs_4_ = bf16[128,2048]{1,0:T(8,128)(2,1)S(1)} collective-permute-done((bf16[128,2048]{1,0:T(8,128)(2,1)S(1)}, bf16[128,2048]{1,0:T(8,128)(2,1)S(1)}, u32[]{:S(2)}, u32[]{:S(2)}) %collective-permute-start.5) | collective-permute-done | bytes 524320 | tf_op jit(solution)/shard_map/ppermute | solution.py:476
  27.5 1.8 %collective-permute-start.6 = (bf16[128,1152]{1,0:T(8,128)(2,1)S(1)}, bf16[128,1152]{1,0:T(8,128)(2,1)S(1)}, u32[]{:S(2)}, u32[]{:S(2)}) collective-permute-start(bf16[128,1152]{1,0:T(8,128)(2,1)S(1)} %get-tuple-element.101), channel_id=1, source_target_pairs={{0,2},{1,3},{2,0},{3,1},{4,6},{5,7},{6,4},{7,5},{8,10},{9,11},{10,... | collective-permute-start | bytes 884744 | tf_op jit(solution)/shard_map/ppermute | solution.py:476
  29.3 1.2 collective-permute-start.7
  30.5 4.8 %users_0.1 = (f32[2048,128]{1,0:T(8,128)S(1)}, bf16[2048,128]{1,0:T(8,128)(2,1)S(1)}, bf16[128,2048]{1,0:T(8,128)(2,1)S(1)}, bf16[128,128]{1,0:T(8,128)(2,1)S(1)}) custom-call(s32[1,2]{1,0:T(1,128)S(1)} %bitcast.6, f32[2048,128]{1,0:T(8,128)S(1)} %copy-done, f32[128,2048]{1,0:T(8,128)S(1)} %get-tuple-element.75.grad, ...), custom_call_target="tpu_custom_call" | custom-call | flops 10000000000 | bytes 65536 | tf_op jit(solution)/shard_map/users_0/pallas_call | solution.py:358
  35.3 3.6 %collective-permute-done.refs_1_ = bf16[128,2048]{1,0:T(8,128)(2,1)S(1)} collective-permute-done((bf16[128,2048]{1,0:T(8,128)(2,1)S(1)}, bf16[128,2048]{1,0:T(8,128)(2,1)S(1)}, u32[]{:S(2)}, u32[]{:S(2)}) %collective-permute-start) | collective-permute-done | bytes 524320 | tf_op jit(solution)/shard_map/ppermute | solution.py:476
  38.9 0.3 collective-permute-done.1.refs_3_.refs_4_
  39.3 1.2 collective-permute-start.2
  40.5 1.2 collective-permute-start.3
  41.8 1.7 %collective-permute-done.7.refs_5_ = bf16[128,1024]{1,0:T(8,128)(2,1)S(1)} collective-permute-done((bf16[128,1024]{1,0:T(8,128)(2,1)S(1)}, bf16[128,1024]{1,0:T(8,128)(2,1)S(1)}, u32[]{:S(2)}, u32[]{:S(2)}) %collective-permute-start.7) | collective-permute-done | bytes 262176 | tf_op jit(solution)/shard_map/ppermute | solution.py:476
  43.4 2.1 %collective-permute-done.6.refs_2_.refs_8_ = bf16[128,1152]{1,0:T(8,128)(2,1)S(1)} collective-permute-done((bf16[128,1152]{1,0:T(8,128)(2,1)S(1)}, bf16[128,1152]{1,0:T(8,128)(2,1)S(1)}, u32[]{:S(2)}, u32[]{:S(2)}) %collective-permute-start.6) | collective-permute-done | bytes 294944 | tf_op jit(solution)/shard_map/ppermute | solution.py:476
  45.5 1.3 items_0_0.1
  46.8 2.1 %collective-permute-start.15 = (bf16[128,2048]{1,0:T(8,128)(2,1)S(1)}, bf16[128,2048]{1,0:T(8,128)(2,1)S(1)}, u32[]{:S(2)}, u32[]{:S(2)}) collective-permute-start(bf16[128,2048]{1,0:T(8,128)(2,1)S(1)} %get-tuple-element.109), channel_id=1, source_target_pairs={{0,6},{1,7},{2,4},{3,5},{4,10},{5,11},{6,8},{7,9},{8,14},{9,15},{1... | collective-permute-start | bytes 1572872 | tf_op jit(solution)/shard_map/ppermute | solution.py:486
  48.9 1.3 items_0_1.1
  50.2 0.8 collective-permute-start.9
  51.0 3.3 %collective-permute-start.10 = (bf16[128,2048]{1,0:T(8,128)(2,1)S(1)}, bf16[128,2048]{1,0:T(8,128)(2,1)S(1)}, u32[]{:S(2)}, u32[]{:S(2)}) collective-permute-start(bf16[128,2048]{1,0:T(8,128)(2,1)S(1)} %get-tuple-element.105), channel_id=1, source_target_pairs={{0,6},{1,7},{2,4},{3,5},{4,10},{5,11},{6,8},{7,9},{8,14},{9,15},{1... | collective-permute-start | bytes 1572872 | tf_op jit(solution)/shard_map/ppermute | solution.py:486
  54.2 4.9 %collective-permute-done.14.refs_9_.refs_1_ = bf16[128,2048]{1,0:T(8,128)(2,1)S(1)} collective-permute-done((bf16[128,2048]{1,0:T(8,128)(2,1)S(1)}, bf16[128,2048]{1,0:T(8,128)(2,1)S(1)}, u32[]{:S(2)}, u32[]{:S(2)}) %collective-permute-start.14) | collective-permute-done | bytes 524320 | tf_op jit(solution)/shard_map/ppermute | solution.py:486
  59.1 1.2 collective-permute-start.16
  60.3 3.5 %collective-permute-done.15.refs_10_.refs_2_ = bf16[128,2048]{1,0:T(8,128)(2,1)S(1)} collective-permute-done((bf16[128,2048]{1,0:T(8,128)(2,1)S(1)}, bf16[128,2048]{1,0:T(8,128)(2,1)S(1)}, u32[]{:S(2)}, u32[]{:S(2)}) %collective-permute-start.15) | collective-permute-done | bytes 524320 | tf_op jit(solution)/shard_map/ppermute | solution.py:486
  63.8 1.3 collective-permute-start.17
  65.1 7.2 %collective-permute-done.9.refs_9_.refs_6_ = bf16[128,2048]{1,0:T(8,128)(2,1)S(1)} collective-permute-done((bf16[128,2048]{1,0:T(8,128)(2,1)S(1)}, bf16[128,2048]{1,0:T(8,128)(2,1)S(1)}, u32[]{:S(2)}, u32[]{:S(2)}) %collective-permute-start.9) | collective-permute-done | bytes 524320 | tf_op jit(solution)/shard_map/ppermute | solution.py:486
  72.3 2.3 %collective-permute-start.8 = (bf16[128,2048]{1,0:T(8,128)(2,1)S(1)}, bf16[128,2048]{1,0:T(8,128)(2,1)S(1)}, u32[]{:S(2)}, u32[]{:S(2)}) collective-permute-start(bf16[128,2048]{1,0:T(8,128)(2,1)S(1)} %get-tuple-element.105), channel_id=1, source_target_pairs={{0,4},{1,5},{2,6},{3,7},{4,8},{5,9},{6,10},{7,11},{8,12},{9,13},{1... | collective-permute-start | bytes 1572872 | tf_op jit(solution)/shard_map/ppermute | solution.py:486
  74.7 0.6 collective-permute-done.10.refs_10_.refs_7_
  75.3 2.2 %collective-permute-start.11 = (bf16[128,1024]{1,0:T(8,128)(2,1)S(1)}, bf16[128,1024]{1,0:T(8,128)(2,1)S(1)}, u32[]{:S(2)}, u32[]{:S(2)}) collective-permute-start(bf16[128,1024]{1,0:T(8,128)(2,1)S(1)} %slice.16), channel_id=1, source_target_pairs={{0,2},{1,3},{2,0},{3,1},{4,6},{5,7},{6,4},{7,5},{8,10},{9,11},{10,... | collective-permute-start | bytes 786440 | tf_op jit(solution)/shard_map/ppermute | solution.py:476
  77.4 3.1 %collective-permute-done.13.refs_8_.refs_0_.items = bf16[128,2048]{1,0:T(8,128)(2,1)S(1)} collective-permute-done((bf16[128,2048]{1,0:T(8,128)(2,1)S(1)}, bf16[128,2048]{1,0:T(8,128)(2,1)S(1)}, u32[]{:S(2)}, u32[]{:S(2)}) %collective-permute-start.13) | collective-permute-done | bytes 524320 | tf_op jit(solution)/shard_map/ppermute | solution.py:486
  80.6 0.8 collective-permute-start.12
  81.3 6.2 %tiles_1_0.1 = (bf16[128,2176]{1,0:T(8,128)(2,1)S(1)}, bf16[128,2048]{1,0:T(8,128)(2,1)S(1)}, bf16[128,2048]{1,0:T(8,128)(2,1)S(1)}, bf16[128,2048]{1,0:T(8,128)(2,1)S(1)}, f32[128,2048]{1,0:T(8,128)S(1)}) custom-call(s32[2,1,1,64]{3,2,1,0:T(1,128)} %refs_0_.7, s32[2,1,1,64]{3,2,1,0:T(1,128)} %refs_1_.7, s32[1,2]{1,0:T(1,128)} %bitcast.10, s32[1,2]{1,0:T(1,128)} %bitcast.4, ...), custom_call_target="tpu_custom_call" | custom-call | flops 16000000000 | bytes 65536 | tf_op jit(solution)/shard_map/tiles_1_0/pallas_call | solution.py:319
  87.5 1.4 collective-permute-start.21
  89.0 6.2 %tiles_1_1.1 = (bf16[128,1024]{1,0:T(8,128)(2,1)S(1)}, bf16[128,1024]{1,0:T(8,128)(2,1)S(1)}, bf16[128,1024]{1,0:T(8,128)(2,1)S(1)}, bf16[128,1024]{1,0:T(8,128)...) custom-call(s32[2,1,1,64]{3,2,1,0:T(1,128)} %refs_0_.7, ...), custom_call_target="tpu_custom_call" | custom-call | flops 16000000000 | bytes 65536 | tf_op jit(solution)/shard_map/tiles_1_1/pallas_call | solution.py:319
  95.2 2.5 %collective-permute-start.19 = (bf16[128,2048]{1,0:T(8,128)(2,1)S(1)}, bf16[128,2048]{1,0:T(8,128)(2,1)S(1)}, u32[]{:S(2)}, u32[]{:S(2)}) collective-permute-start(bf16[128,2048]{1,0:T(8,128)(2,1)S(1)} %get-tuple-element.119), channel_id=1, source_target_pairs={{0,4},{1,5},{2,6},{3,7},{4,8},{5,9},{6,10},{7,11},{8,12},{9,13},{1... | collective-permute-start | bytes 1572872 | tf_op jit(solution)/shard_map/ppermute | solution.py:486
  97.6 2.2 %collective-permute-start.18 = (bf16[128,1024]{1,0:T(8,128)(2,1)S(1)}, bf16[128,1024]{1,0:T(8,128)(2,1)S(1)}, u32[]{:S(2)}, u32[]{:S(2)}) collective-permute-start(bf16[128,1024]{1,0:T(8,128)(2,1)S(1)} %get-tuple-element.117), channel_id=1, source_target_pairs={{0,1},{1,0},{2,3},{3,2},{4,5},{5,4},{6,7},{7,6},{8,9},{9,8},{10,11... | collective-permute-start | bytes 786440 | tf_op jit(solution)/shard_map/ppermute | solution.py:476
  99.8 3.2 %collective-permute-done.23.refs_3_.refs_4_ = bf16[128,2048]{1,0:T(8,128)(2,1)S(1)} collective-permute-done((bf16[128,2048]{1,0:T(8,128)(2,1)S(1)}, bf16[128,2048]{1,0:T(8,128)(2,1)S(1)}, u32[]{:S(2)}, u32[]{:S(2)}) %collective-permute-start.23) | collective-permute-done | bytes 524320 | tf_op jit(solution)/shard_map/ppermute | solution.py:476
  103.2 2.1 %collective-permute-start.24 = (bf16[128,1152]{1,0:T(8,128)(2,1)S(1)}, bf16[128,1152]{1,0:T(8,128)(2,1)S(1)}, u32[]{:S(2)}, u32[]{:S(2)}) collective-permute-start(bf16[128,1152]{1,0:T(8,128)(2,1)S(1)} %get-tuple-element.137), channel_id=1, source_target_pairs={{0,2},{1,3},{2,0},{3,1},{4,6},{5,7},{6,4},{7,5},{8,10},{9,11},{10,... | collective-permute-start | bytes 884744 | tf_op jit(solution)/shard_map/ppermute | solution.py:476
  105.3 1.3 collective-permute-start.25
  106.6 0.2 collective-permute-done.18.refs_1_
  106.8 1.8 %collective-permute-start.27 = (bf16[128,1024]{1,0:T(8,128)(2,1)S(1)}, bf16[128,1024]{1,0:T(8,128)(2,1)S(1)}, u32[]{:S(2)}, u32[]{:S(2)}) collective-permute-start(bf16[128,1024]{1,0:T(8,128)(2,1)S(1)} %get-tuple-element.140), channel_id=1, source_target_pairs={{0,5},{1,4},{2,7},{3,6},{4,9},{5,8},{6,11},{7,10},{8,13},{9,12},{1... | collective-permute-start | bytes 786440 | tf_op jit(solution)/shard_map/ppermute | solution.py:486
  108.6 3.6 %collective-permute-done.20.refs_3_ = bf16[128,1024]{1,0:T(8,128)(2,1)S(1)} collective-permute-done((bf16[128,1024]{1,0:T(8,128)(2,1)S(1)}, bf16[128,1024]{1,0:T(8,128)(2,1)S(1)}, u32[]{:S(2)}, u32[]{:S(2)}) %collective-permute-start.20) | collective-permute-done | bytes 262176 | tf_op jit(solution)/shard_map/ppermute | solution.py:476
  112.3 3.0 %collective-permute-start.28 = (bf16[128,1024]{1,0:T(8,128)(2,1)S(1)}, bf16[128,1024]{1,0:T(8,128)(2,1)S(1)}, u32[]{:S(2)}, u32[]{:S(2)}) collective-permute-start(bf16[128,1024]{1,0:T(8,128)(2,1)S(1)} %get-tuple-element.125), channel_id=1, source_target_pairs={{0,6},{1,7},{2,4},{3,5},{4,10},{5,11},{6,8},{7,9},{8,14},{9,15},{1... | collective-permute-start | bytes 786440 | tf_op jit(solution)/shard_map/ppermute | solution.py:486
  115.3 1.1 collective-permute-done.25.refs_5_
  116.5 7.5 %collective-permute-done.24.refs_2_.refs_8_ = bf16[128,1152]{1,0:T(8,128)(2,1)S(1)} collective-permute-done((bf16[128,1152]{1,0:T(8,128)(2,1)S(1)}, bf16[128,1152]{1,0:T(8,128)(2,1)S(1)}, u32[]{:S(2)}, u32[]{:S(2)}) %collective-permute-start.24) | collective-permute-done | bytes 294944 | tf_op jit(solution)/shard_map/ppermute | solution.py:476
  123.9 1.1 items_1_0.1
  125.0 5.3 %users_1.1 = f32[2048,128]{1,0:T(8,128)} custom-call(s32[1,2]{1,0:T(1,128)S(1)} %bitcast.7, f32[2048,128]{1,0:T(8,128)S(1)} %get-tuple-element.78.users, f32[128,2048]{1,0:T(8,128)S(1)} %get-tuple-element.127.grad, bf16[128,2048]{1,0:T(8,128)(2,1)S(1)} %collective-permute-done.13.refs_8_.refs_0_.items, ...), custom_call_target="tpu_custom_call" | custom-call | flops 10000000000 | bytes 65536 | tf_op jit(solution)/shard_map/users_1/pallas_call | solution.py:358
  130.4 5.4 %collective-permute-done.26.refs_0_ = bf16[2176,128]{1,0:T(8,128)(2,1)S(1)} collective-permute-done((bf16[2176,128]{1,0:T(8,128)(2,1)S(1)}, bf16[2176,128]{1,0:T(8,128)(2,1)S(1)}, u32[]{:S(2)}, u32[]{:S(2)}) %collective-permute-start.26) | collective-permute-done | bytes 557088 | tf_op jit(solution)/shard_map/ppermute | solution.py:486
  135.8 1.7 %items_final.1 = f32[4096,128]{1,0:T(8,128)} custom-call(bf16[2176,128]{1,0:T(8,128)(2,1)S(1)} %collective-permute-done.26.refs_0_, bf16[128,2048]{1,0:T(8,128)(2,1)S(1)} %collective-permute-done.22.refs_1_, bf16[128,2048]{1,0:T(8,128)(2,1)S(1)} %collective-permute-done.19.refs_2_, bf16[128,1024]{1,0:T(8,128)(2,1)S(1)} %collective-permute-done.27.refs_3_, ...), custom_call_target="tpu_custom_call" | custom-call | flops 1200000000 | bytes 65536 | tf_op jit(solution)/shard_map/items_final/pallas_call | solution.py:585
  (38 shorter events, 0.9 us)
Async XLA Ops:
  10.2 17.2 %collective-permute-start.4 = (bf16[128,2176]{1,0:T(8,128)(2,1)S(1)}, bf16[128,2176]{1,0:T(8,128)(2,1)S(1)}, u32[]{:S(2)}, u32[]{:S(2)}) collective-permute-start(bf16[128,2176]{1,0:T(8,128)(2,1)S(1)} %get-tuple-element.96.refs_4_.refs_6_), channel_id=1, source_target_pairs={{0,1},{1,0},{2,3},{3,2},{4,5},{5,4},{6,7},{7,6},{8,9},{9,8},{10,11... | collective-permute-start | bytes 1671176 | tf_op jit(solution)/shard_map/ppermute | solution.py:476
  13.8 13.6 %collective-permute-start.5 = (bf16[128,2048]{1,0:T(8,128)(2,1)S(1)}, bf16[128,2048]{1,0:T(8,128)(2,1)S(1)}, u32[]{:S(2)}, u32[]{:S(2)}) collective-permute-start(bf16[128,2048]{1,0:T(8,128)(2,1)S(1)} %get-tuple-element.99), channel_id=1, source_target_pairs={{0,2},{1,3},{2,0},{3,1},{4,6},{5,7},{6,4},{7,5},{8,10},{9,11},{10,... | collective-permute-start | bytes 1572872 | tf_op jit(solution)/shard_map/ppermute | solution.py:476
  24.2 6.4 %copy-start = (f32[2048,128]{1,0:T(8,128)S(1)}, f32[2048,128]{1,0:T(8,128)}, u32[]{:S(2)}) copy-start(f32[2048,128]{1,0:T(8,128)} %users.1) | copy-start | bytes 3145732
  24.2 6.4 %copy-start.1 = (s32[2,1]{0,1:T(1,128)S(1)}, s32[2,1]{0,1:T(1,128)}, u32[]{:S(2)}) copy-start(s32[2,1]{0,1:T(1,128)} %param.13) | copy-start | bytes 28
  24.2 14.7 %collective-permute-start = (bf16[128,2048]{1,0:T(8,128)(2,1)S(1)}, bf16[128,2048]{1,0:T(8,128)(2,1)S(1)}, u32[]{:S(2)}, u32[]{:S(2)}) collective-permute-start(bf16[128,2048]{1,0:T(8,128)(2,1)S(1)} %get-tuple-element.83), channel_id=1, source_target_pairs={{0,1},{1,0},{2,3},{3,2},{4,5},{5,4},{6,7},{7,6},{8,9},{9,8},{10,11... | collective-permute-start | bytes 1572872 | tf_op jit(solution)/shard_map/ppermute | solution.py:476
  24.3 14.9 %collective-permute-start.1 = (bf16[128,2048]{1,0:T(8,128)(2,1)S(1)}, bf16[128,2048]{1,0:T(8,128)(2,1)S(1)}, u32[]{:S(2)}, u32[]{:S(2)}) collective-permute-start(bf16[128,2048]{1,0:T(8,128)(2,1)S(1)} %get-tuple-element.86), channel_id=1, source_target_pairs={{0,2},{1,3},{2,0},{3,1},{4,6},{5,7},{6,4},{7,5},{8,10},{9,11},{10,... | collective-permute-start | bytes 1572872 | tf_op jit(solution)/shard_map/ppermute | solution.py:476
  27.5 18.0 %collective-permute-start.6 = (bf16[128,1152]{1,0:T(8,128)(2,1)S(1)}, bf16[128,1152]{1,0:T(8,128)(2,1)S(1)}, u32[]{:S(2)}, u32[]{:S(2)}) collective-permute-start(bf16[128,1152]{1,0:T(8,128)(2,1)S(1)} %get-tuple-element.101), channel_id=1, source_target_pairs={{0,2},{1,3},{2,0},{3,1},{4,6},{5,7},{6,4},{7,5},{8,10},{9,11},{10,... | collective-permute-start | bytes 884744 | tf_op jit(solution)/shard_map/ppermute | solution.py:476
  29.3 14.2 %collective-permute-start.7 = (bf16[128,1024]{1,0:T(8,128)(2,1)S(1)}, bf16[128,1024]{1,0:T(8,128)(2,1)S(1)}, u32[]{:S(2)}, u32[]{:S(2)}) collective-permute-start(bf16[128,1024]{1,0:T(8,128)(2,1)S(1)} %get-tuple-element.102), channel_id=1, source_target_pairs={{0,1},{1,0},{2,3},{3,2},{4,5},{5,4},{6,7},{7,6},{8,9},{9,8},{10,11... | collective-permute-start | bytes 786440 | tf_op jit(solution)/shard_map/ppermute | solution.py:476
  39.3 9.6 %collective-permute-start.2 = (bf16[128,1024]{1,0:T(8,128)(2,1)S(1)}, bf16[128,1024]{1,0:T(8,128)(2,1)S(1)}, u32[]{:S(2)}, u32[]{:S(2)}) collective-permute-start(bf16[128,1024]{1,0:T(8,128)(2,1)S(1)} %get-tuple-element.88), channel_id=1, source_target_pairs={{0,2},{1,3},{2,0},{3,1},{4,6},{5,7},{6,4},{7,5},{8,10},{9,11},{10,... | collective-permute-start | bytes 786440 | tf_op jit(solution)/shard_map/ppermute | solution.py:476
  40.5 8.4 %collective-permute-start.3 = (bf16[128,1024]{1,0:T(8,128)(2,1)S(1)}, bf16[128,1024]{1,0:T(8,128)(2,1)S(1)}, u32[]{:S(2)}, u32[]{:S(2)}) collective-permute-start(bf16[128,1024]{1,0:T(8,128)(2,1)S(1)} %get-tuple-element.89), channel_id=1, source_target_pairs={{0,1},{1,0},{2,3},{3,2},{4,5},{5,4},{6,7},{7,6},{8,9},{9,8},{10,11... | collective-permute-start | bytes 786440 | tf_op jit(solution)/shard_map/ppermute | solution.py:476
  46.8 12.3 %collective-permute-start.14 = (bf16[128,2048]{1,0:T(8,128)(2,1)S(1)}, bf16[128,2048]{1,0:T(8,128)(2,1)S(1)}, u32[]{:S(2)}, u32[]{:S(2)}) collective-permute-start(bf16[128,2048]{1,0:T(8,128)(2,1)S(1)} %get-tuple-element.109), channel_id=1, source_target_pairs={{0,5},{1,4},{2,7},{3,6},{4,9},{5,8},{6,11},{7,10},{8,13},{9,12},{1... | collective-permute-start | bytes 1572872 | tf_op jit(solution)/shard_map/ppermute | solution.py:486
  46.8 17.0 %collective-permute-start.15 = (bf16[128,2048]{1,0:T(8,128)(2,1)S(1)}, bf16[128,2048]{1,0:T(8,128)(2,1)S(1)}, u32[]{:S(2)}, u32[]{:S(2)}) collective-permute-start(bf16[128,2048]{1,0:T(8,128)(2,1)S(1)} %get-tuple-element.109), channel_id=1, source_target_pairs={{0,6},{1,7},{2,4},{3,5},{4,10},{5,11},{6,8},{7,9},{8,14},{9,15},{1... | collective-permute-start | bytes 1572872 | tf_op jit(solution)/shard_map/ppermute | solution.py:486
  50.2 22.1 %collective-permute-start.9 = (bf16[128,2048]{1,0:T(8,128)(2,1)S(1)}, bf16[128,2048]{1,0:T(8,128)(2,1)S(1)}, u32[]{:S(2)}, u32[]{:S(2)}) collective-permute-start(bf16[128,2048]{1,0:T(8,128)(2,1)S(1)} %get-tuple-element.105), channel_id=1, source_target_pairs={{0,5},{1,4},{2,7},{3,6},{4,9},{5,8},{6,11},{7,10},{8,13},{9,12},{1... | collective-permute-start | bytes 1572872 | tf_op jit(solution)/shard_map/ppermute | solution.py:486
  51.0 24.3 %collective-permute-start.10 = (bf16[128,2048]{1,0:T(8,128)(2,1)S(1)}, bf16[128,2048]{1,0:T(8,128)(2,1)S(1)}, u32[]{:S(2)}, u32[]{:S(2)}) collective-permute-start(bf16[128,2048]{1,0:T(8,128)(2,1)S(1)} %get-tuple-element.105), channel_id=1, source_target_pairs={{0,6},{1,7},{2,4},{3,5},{4,10},{5,11},{6,8},{7,9},{8,14},{9,15},{1... | collective-permute-start | bytes 1572872 | tf_op jit(solution)/shard_map/ppermute | solution.py:486
  54.2 26.3 %collective-permute-start.13 = (bf16[128,2048]{1,0:T(8,128)(2,1)S(1)}, bf16[128,2048]{1,0:T(8,128)(2,1)S(1)}, u32[]{:S(2)}, u32[]{:S(2)}) collective-permute-start(bf16[128,2048]{1,0:T(8,128)(2,1)S(1)} %get-tuple-element.109), channel_id=1, source_target_pairs={{0,4},{1,5},{2,6},{3,7},{4,8},{5,9},{6,10},{7,11},{8,12},{9,13},{1... | collective-permute-start | bytes 1572872 | tf_op jit(solution)/shard_map/ppermute | solution.py:486
  59.1 22.2 %collective-permute-start.16 = (bf16[128,1024]{1,0:T(8,128)(2,1)S(1)}, bf16[128,1024]{1,0:T(8,128)(2,1)S(1)}, u32[]{:S(2)}, u32[]{:S(2)}) collective-permute-start(bf16[128,1024]{1,0:T(8,128)(2,1)S(1)} %slice.18), channel_id=1, source_target_pairs={{0,2},{1,3},{2,0},{3,1},{4,6},{5,7},{6,4},{7,5},{8,10},{9,11},{10,... | collective-permute-start | bytes 786440 | tf_op jit(solution)/shard_map/ppermute | solution.py:476
  63.8 17.5 %collective-permute-start.17 = (bf16[128,1024]{1,0:T(8,128)(2,1)S(1)}, bf16[128,1024]{1,0:T(8,128)(2,1)S(1)}, u32[]{:S(2)}, u32[]{:S(2)}) collective-permute-start(bf16[128,1024]{1,0:T(8,128)(2,1)S(1)} %slice.19), channel_id=1, source_target_pairs={{0,1},{1,0},{2,3},{3,2},{4,5},{5,4},{6,7},{7,6},{8,9},{9,8},{10,11... | collective-permute-start | bytes 786440 | tf_op jit(solution)/shard_map/ppermute | solution.py:476
  72.3 16.5 %collective-permute-start.8 = (bf16[128,2048]{1,0:T(8,128)(2,1)S(1)}, bf16[128,2048]{1,0:T(8,128)(2,1)S(1)}, u32[]{:S(2)}, u32[]{:S(2)}) collective-permute-start(bf16[128,2048]{1,0:T(8,128)(2,1)S(1)} %get-tuple-element.105), channel_id=1, source_target_pairs={{0,4},{1,5},{2,6},{3,7},{4,8},{5,9},{6,10},{7,11},{8,12},{9,13},{1... | collective-permute-start | bytes 1572872 | tf_op jit(solution)/shard_map/ppermute | solution.py:486
  75.3 13.7 %collective-permute-start.11 = (bf16[128,1024]{1,0:T(8,128)(2,1)S(1)}, bf16[128,1024]{1,0:T(8,128)(2,1)S(1)}, u32[]{:S(2)}, u32[]{:S(2)}) collective-permute-start(bf16[128,1024]{1,0:T(8,128)(2,1)S(1)} %slice.16), channel_id=1, source_target_pairs={{0,2},{1,3},{2,0},{3,1},{4,6},{5,7},{6,4},{7,5},{8,10},{9,11},{10,... | collective-permute-start | bytes 786440 | tf_op jit(solution)/shard_map/ppermute | solution.py:476
  80.6 8.4 %collective-permute-start.12 = (bf16[128,1024]{1,0:T(8,128)(2,1)S(1)}, bf16[128,1024]{1,0:T(8,128)(2,1)S(1)}, u32[]{:S(2)}, u32[]{:S(2)}) collective-permute-start(bf16[128,1024]{1,0:T(8,128)(2,1)S(1)} %slice.17), channel_id=1, source_target_pairs={{0,1},{1,0},{2,3},{3,2},{4,5},{5,4},{6,7},{7,6},{8,9},{9,8},{10,11... | collective-permute-start | bytes 786440 | tf_op jit(solution)/shard_map/ppermute | solution.py:476
  87.5 15.6 %collective-permute-start.21 = (bf16[128,2176]{1,0:T(8,128)(2,1)S(1)}, bf16[128,2176]{1,0:T(8,128)(2,1)S(1)}, u32[]{:S(2)}, u32[]{:S(2)}) collective-permute-start(bf16[128,2176]{1,0:T(8,128)(2,1)S(1)} %get-tuple-element.129.refs_4_.refs_6_), channel_id=1, source_target_pairs={{0,1},{1,0},{2,3},{3,2},{4,5},{5,4},{6,7},{7,6},{8,9},{9,8},{10,11... | collective-permute-start | bytes 1671176 | tf_op jit(solution)/shard_map/ppermute | solution.py:476
  88.8 14.2 %collective-permute-start.22 = (bf16[128,2048]{1,0:T(8,128)(2,1)S(1)}, bf16[128,2048]{1,0:T(8,128)(2,1)S(1)}, u32[]{:S(2)}, u32[]{:S(2)}) collective-permute-start(bf16[128,2048]{1,0:T(8,128)(2,1)S(1)} %collective-permute-done.8.refs_8_.refs_5_), channel_id=1, source_target_pairs={{0,4},{1,5},{2,6},{3,7},{4,8},{5,9},{6,10},{7,11},{8,12},{9,13},{1... | collective-permute-start | bytes 1572872 | tf_op jit(solution)/shard_map/ppermute | solution.py:486
  88.8 14.2 %collective-permute-start.23 = (bf16[128,2048]{1,0:T(8,128)(2,1)S(1)}, bf16[128,2048]{1,0:T(8,128)(2,1)S(1)}, u32[]{:S(2)}, u32[]{:S(2)}) collective-permute-start(bf16[128,2048]{1,0:T(8,128)(2,1)S(1)} %get-tuple-element.134), channel_id=1, source_target_pairs={{0,2},{1,3},{2,0},{3,1},{4,6},{5,7},{6,4},{7,5},{8,10},{9,11},{10,... | collective-permute-start | bytes 1572872 | tf_op jit(solution)/shard_map/ppermute | solution.py:476
  95.2 17.1 %collective-permute-start.19 = (bf16[128,2048]{1,0:T(8,128)(2,1)S(1)}, bf16[128,2048]{1,0:T(8,128)(2,1)S(1)}, u32[]{:S(2)}, u32[]{:S(2)}) collective-permute-start(bf16[128,2048]{1,0:T(8,128)(2,1)S(1)} %get-tuple-element.119), channel_id=1, source_target_pairs={{0,4},{1,5},{2,6},{3,7},{4,8},{5,9},{6,10},{7,11},{8,12},{9,13},{1... | collective-permute-start | bytes 1572872 | tf_op jit(solution)/shard_map/ppermute | solution.py:486
  97.6 9.2 %collective-permute-start.18 = (bf16[128,1024]{1,0:T(8,128)(2,1)S(1)}, bf16[128,1024]{1,0:T(8,128)(2,1)S(1)}, u32[]{:S(2)}, u32[]{:S(2)}) collective-permute-start(bf16[128,1024]{1,0:T(8,128)(2,1)S(1)} %get-tuple-element.117), channel_id=1, source_target_pairs={{0,1},{1,0},{2,3},{3,2},{4,5},{5,4},{6,7},{7,6},{8,9},{9,8},{10,11... | collective-permute-start | bytes 786440 | tf_op jit(solution)/shard_map/ppermute | solution.py:476
  103.0 9.2 %collective-permute-start.20 = (bf16[128,1024]{1,0:T(8,128)(2,1)S(1)}, bf16[128,1024]{1,0:T(8,128)(2,1)S(1)}, u32[]{:S(2)}, u32[]{:S(2)}) collective-permute-start(bf16[128,1024]{1,0:T(8,128)(2,1)S(1)} %get-tuple-element.122), channel_id=1, source_target_pairs={{0,2},{1,3},{2,0},{3,1},{4,6},{5,7},{6,4},{7,5},{8,10},{9,11},{10,... | collective-permute-start | bytes 786440 | tf_op jit(solution)/shard_map/ppermute | solution.py:476
  103.2 20.7 %collective-permute-start.24 = (bf16[128,1152]{1,0:T(8,128)(2,1)S(1)}, bf16[128,1152]{1,0:T(8,128)(2,1)S(1)}, u32[]{:S(2)}, u32[]{:S(2)}) collective-permute-start(bf16[128,1152]{1,0:T(8,128)(2,1)S(1)} %get-tuple-element.137), channel_id=1, source_target_pairs={{0,2},{1,3},{2,0},{3,1},{4,6},{5,7},{6,4},{7,5},{8,10},{9,11},{10,... | collective-permute-start | bytes 884744 | tf_op jit(solution)/shard_map/ppermute | solution.py:476
  105.3 11.2 %collective-permute-start.25 = (bf16[128,1024]{1,0:T(8,128)(2,1)S(1)}, bf16[128,1024]{1,0:T(8,128)(2,1)S(1)}, u32[]{:S(2)}, u32[]{:S(2)}) collective-permute-start(bf16[128,1024]{1,0:T(8,128)(2,1)S(1)} %get-tuple-element.138), channel_id=1, source_target_pairs={{0,1},{1,0},{2,3},{3,2},{4,5},{5,4},{6,7},{7,6},{8,9},{9,8},{10,11... | collective-permute-start | bytes 786440 | tf_op jit(solution)/shard_map/ppermute | solution.py:476
  106.8 23.5 %collective-permute-start.27 = (bf16[128,1024]{1,0:T(8,128)(2,1)S(1)}, bf16[128,1024]{1,0:T(8,128)(2,1)S(1)}, u32[]{:S(2)}, u32[]{:S(2)}) collective-permute-start(bf16[128,1024]{1,0:T(8,128)(2,1)S(1)} %get-tuple-element.140), channel_id=1, source_target_pairs={{0,5},{1,4},{2,7},{3,6},{4,9},{5,8},{6,11},{7,10},{8,13},{9,12},{1... | collective-permute-start | bytes 786440 | tf_op jit(solution)/shard_map/ppermute | solution.py:486
  112.2 18.1 %collective-permute-start.29 = (bf16[128,1024]{1,0:T(8,128)(2,1)S(1)}, bf16[128,1024]{1,0:T(8,128)(2,1)S(1)}, u32[]{:S(2)}, u32[]{:S(2)}) collective-permute-start(bf16[128,1024]{1,0:T(8,128)(2,1)S(1)} %get-tuple-element.141), channel_id=1, source_target_pairs={{0,6},{1,7},{2,4},{3,5},{4,10},{5,11},{6,8},{7,9},{8,14},{9,15},{1... | collective-permute-start | bytes 786440 | tf_op jit(solution)/shard_map/ppermute | solution.py:486
  112.3 18.0 %collective-permute-start.28 = (bf16[128,1024]{1,0:T(8,128)(2,1)S(1)}, bf16[128,1024]{1,0:T(8,128)(2,1)S(1)}, u32[]{:S(2)}, u32[]{:S(2)}) collective-permute-start(bf16[128,1024]{1,0:T(8,128)(2,1)S(1)} %get-tuple-element.125), channel_id=1, source_target_pairs={{0,6},{1,7},{2,4},{3,5},{4,10},{5,11},{6,8},{7,9},{8,14},{9,15},{1... | collective-permute-start | bytes 786440 | tf_op jit(solution)/shard_map/ppermute | solution.py:486
  115.3 9.7 %copy-start.2 = (s32[2,1]{0,1:T(1,128)S(1)}, s32[2,1]{0,1:T(1,128)}, u32[]{:S(2)}) copy-start(s32[2,1]{0,1:T(1,128)} %param.13) | copy-start | bytes 28
  116.5 13.9 %collective-permute-start.30 = (bf16[128,1024]{1,0:T(8,128)(2,1)S(1)}, bf16[128,1024]{1,0:T(8,128)(2,1)S(1)}, u32[]{:S(2)}, u32[]{:S(2)}) collective-permute-start(bf16[128,1024]{1,0:T(8,128)(2,1)S(1)} %get-tuple-element.126), channel_id=1, source_target_pairs={{0,5},{1,4},{2,7},{3,6},{4,9},{5,8},{6,11},{7,10},{8,13},{9,12},{1... | collective-permute-start | bytes 786440 | tf_op jit(solution)/shard_map/ppermute | solution.py:486
  125.0 10.8 %collective-permute-start.26 = (bf16[2176,128]{1,0:T(8,128)(2,1)S(1)}, bf16[2176,128]{1,0:T(8,128)(2,1)S(1)}, u32[]{:S(2)}, u32[]{:S(2)}) collective-permute-start(bf16[2176,128]{1,0:T(8,128)(2,1)S(1)} %get-tuple-element.139), channel_id=1, source_target_pairs={{0,4},{1,5},{2,6},{3,7},{4,8},{5,9},{6,10},{7,11},{8,12},{9,13},{1... | collective-permute-start | bytes 1671176 | tf_op jit(solution)/shard_map/ppermute | solution.py:486

commit v8 on v7

--- a/solution.py
+++ b/solution.py
@@ -435,10 +435,7 @@
         pull = over_columns(gram, items[...])
     new = items[...].astype(F32) - LEARN * (grad + pull)
     if epoch + 1 < SUB:
-        new = new.astype(BF16)
-        out[...] = new
-        refs[-2][...] = new[:, :width]
-        refs[-1][...] = new[:, width:]
+        out[...] = new.astype(BF16)
     else:
         out[:rows] = new.T.astype(BF16)
         if grams > 1:
@@ -453,9 +450,6 @@
     out_shape = [jax.ShapeDtypeStruct((tall, rank) if last else (rank, rows), BF16)]
     if len(grams) > 1:
         out_shape.append(jax.ShapeDtypeStruct((rank, rank), BF16))
-    if not last:
-        out_shape += [jax.ShapeDtypeStruct((rank, rows // 2), BF16)]
-        out_shape += [jax.ShapeDtypeStruct((rank, rows - rows // 2), BF16)]
     out = pl.pallas_call(
         functools.partial(
             item_kernel, epoch, len(terms_a), rows, rows // 2, len(grams)
@@ -468,7 +462,7 @@
         name=f"items_{epoch}_{chunk}",
     )(items, *terms_a, *terms_b, *grams)
     gram = out[1] if len(grams) > 1 else None
-    return out[0] if last else (out[0], *out[-2:]), gram
+    return out[0], gram
 
 
 def swapped(value, bit):
@@ -600,9 +594,9 @@
     return lax.optimization_barrier((value, *others))[0]
 
 
-def gathered(shard, upper, lower, after):
+def gathered(shard, after):
     length = lax.axis_size("grp")
-    rows, half = shard.shape[1], upper.shape[1]
+    rows, half = shard.shape[1], shard.shape[1] // 2
     known = {0: [moved(tied(shard, *after), 0)]}
     for bit in orders_of(length)[0]:
         known[bit] = [moved(shard, bit)]
@@ -653,8 +647,6 @@
                 sources = [(item_factors, None)]
             else:
                 sources = gathers[c]
-                if epoch + 1 == SUB and c + 1 == CHUNKS:
-                    kept = moved(tied(sources[0][0], grad_user), 0)
             direct = epoch + 1 == SUB and c + 1 == CHUNKS
             out = tile_call(
                 epoch, c, direct, members, scalars, ratings, row_mask, users, sources, grad_user,
@@ -671,6 +663,8 @@
                 pieces += [array for array, _ in sources]
                 olds.append(sources[0][0])
         last = epoch + 1 == SUB
+        if last:
+            kept = moved(tied(olds[-1], grad_user), 0)
         if not last:
             new_users = user_call(epoch, block_rows, owners, full_users, grad_user, pieces)
             full_users = new_users[0]
@@ -709,7 +703,7 @@
             full_users = user_call(epoch, block_rows, owners, full_users, grad_user, pieces)[0]
         else:
             users, own_gram = new_users[1:3], new_users[3]
-            gathers = [gathered(*shard, [shards[-1][0]]) for shard in shards]
+            gathers = [gathered(shard, [shards[-1]]) for shard in shards]
             near = gathers[-1][1]
             gathers = [found for found, _ in gathers]
             (array, columns), *rest = gathers[0]

time: 138 us -> 134 us (0.971)
  starting transfers between devices: 39.5 us -> 26.4 us
  waiting for transfers between devices: 49.9 us -> 57.2 us
  Pallas kernels: 47.2 us -> 49 us
    ppermute x13, waiting for transfers between devices: 24.7 us -> 37.2 us  [moved(): return lax.ppermute(value, ('blk', 'grp'), pairs)]
    ppermute x18, starting transfers between devices: 23.7 us -> 15.9 us  [swapped(): return lax.ppermute(value, 'grp', [(i, i ^ bit) for i in range(length)])]
    ppermute x13, starting transfers between devices: 15.8 us -> 10.5 us  [moved(): return lax.ppermute(value, ('blk', 'grp'), pairs)]
    ppermute x18, waiting for transfers between devices: 25.2 us -> 20.1 us  [swapped(): return lax.ppermute(value, 'grp', [(i, i ^ bit) for i in range(length)])]
    pallas_call x4, Pallas kernels: 31.3 us -> 34.5 us  [tile_call(): pl.pallas_call(functools.partial(tile_kernel, epoch, chunk, direct, membe...]
    pallas_call x3, Pallas kernels: 3.66 us -> 2.25 us  [item_call(): pl.pallas_call(functools.partial(item_kernel, epoch, len(terms_a), rows,...]
  transfers between devices with their start and end apart: 31 -> 31, of which waited for: 16 -> 17; matrix products, arithmetic and copies ran while one was open for 0% -> 0% of each run, Pallas kernels for 26% -> 27%
where the time goes in v8:
time: 134 us
  waiting for transfers between devices  57.2 us (43%)
  Pallas kernels  49 us (37%)
  starting transfers between devices  26.4 us (20%)
    ppermute x13, waiting for transfers between devices, moved(): return lax.ppermute(value, ('blk', 'grp'), pairs)  37.2 us
    pallas_call x4, Pallas kernels, tile_call(): pl.pallas_call(functools.partial(tile_kernel, epoch, chunk, direct, membe...  34.5 us
    ppermute x18, waiting for transfers between devices, swapped(): return lax.ppermute(value, 'grp', [(i, i ^ bit) for i in range(length)])  20.1 us
    ppermute x18, starting transfers between devices, swapped(): return lax.ppermute(value, 'grp', [(i, i ^ bit) for i in range(length)])  15.9 us
    ppermute x13, starting transfers between devices, moved(): return lax.ppermute(value, ('blk', 'grp'), pairs)  10.5 us
    pallas_call x2, Pallas kernels, user_call(): pl.pallas_call(functools.partial(user_kernel, epoch, block_rows), out_sha...  10.1 us
  transfers between devices with their start and end apart: 31, of which 17 were waited for; matrix products, arithmetic and copies ran while one was open for 0% of the time, Pallas kernels for 27%

profile of v8, /device:TPU:0, one launch (start us, length us, event | category | flops | bytes accessed | tf_op | source)
XLA Modules:
  0.0 133.7 jit_solution(8586322957790742029)
XLA Ops:
  0.6 10.6 %tiles_0_0.1 = (bf16[128,2176]{1,0:T(8,128)(2,1)S(1)}, bf16[128,2048]{1,0:T(8,128)(2,1)S(1)}, bf16[128,2048]{1,0:T(8,128)(2,1)S(1)}, bf16[128,2048]{1,0:T(8,128)...) custom-call(s32[2,1,1,64]{3,2,1,0:T(1,128)} %refs_0_.7, ...), custom_call_target="tpu_custom_call" | custom-call | flops 16000000000 | bytes 65536 | tf_op jit(solution)/shard_map/tiles_0_0/pallas_call | solution.py:319
  11.3 0.4 collective-permute-start.4
  11.7 1.7 %collective-permute-start.5 = (bf16[128,2048]{1,0:T(8,128)(2,1)S(1)}, bf16[128,2048]{1,0:T(8,128)(2,1)S(1)}, u32[]{:S(2)}, u32[]{:S(2)}) collective-permute-start(bf16[128,2048]{1,0:T(8,128)(2,1)S(1)} %get-tuple-element.98), channel_id=1, source_target_pairs={{0,2},{1,3},{2,0},{3,1},{4,6},{5,7},{6,4},{7,5},{8,10},{9,11},{10,... | collective-permute-start | bytes 1572872 | tf_op jit(solution)/shard_map/ppermute | solution.py:470
  13.4 8.3 %tiles_0_1.1 = (bf16[128,2048]{1,0:T(8,128)(2,1)S(1)}, bf16[128,2048]{1,0:T(8,128)(2,1)S(1)}, bf16[128,2048]{1,0:T(8,128)(2,1)S(1)}, bf16[128,2048]{1,0:T(8,128)...) custom-call(s32[2,1,1,64]{3,2,1,0:T(1,128)} %refs_0_.7, ...), custom_call_target="tpu_custom_call" | custom-call | flops 16000000000 | bytes 65536 | tf_op jit(solution)/shard_map/tiles_0_1/pallas_call | solution.py:319
  21.8 0.4 collective-permute-start.1
  22.1 3.5 %collective-permute-done.5.refs_3_.refs_4_ = bf16[128,2048]{1,0:T(8,128)(2,1)S(1)} collective-permute-done((bf16[128,2048]{1,0:T(8,128)(2,1)S(1)}, bf16[128,2048]{1,0:T(8,128)(2,1)S(1)}, u32[]{:S(2)}, u32[]{:S(2)}) %collective-permute-start.5) | collective-permute-done | bytes 524320 | tf_op jit(solution)/shard_map/ppermute | solution.py:470
  25.7 1.1 collective-permute-done.4.refs_1_.refs_5_.refs_7_
  26.8 0.1 mid_0_0_0.1
  26.9 1.4 %collective-permute-start.6 = (bf16[128,1152]{1,0:T(8,128)(2,1)S(1)}, bf16[128,1152]{1,0:T(8,128)(2,1)S(1)}, u32[]{:S(2)}, u32[]{:S(2)}) collective-permute-start(bf16[128,1152]{1,0:T(8,128)(2,1)S(1)} %get-tuple-element.100), channel_id=1, source_target_pairs={{0,2},{1,3},{2,0},{3,1},{4,6},{5,7},{6,4},{7,5},{8,10},{9,11},{10,... | collective-permute-start | bytes 884744 | tf_op jit(solution)/shard_map/ppermute | solution.py:470
  28.4 0.6 collective-permute-start.7
  29.0 4.8 %users_0.1 = (f32[2048,128]{1,0:T(8,128)S(1)}, bf16[2048,128]{1,0:T(8,128)(2,1)S(1)}, bf16[128,2048]{1,0:T(8,128)(2,1)S(1)}, bf16[128,128]{1,0:T(8,128)(2,1)S(1)}) custom-call(s32[1,2]{1,0:T(1,128)S(1)} %bitcast.6, f32[2048,128]{1,0:T(8,128)S(1)} %copy-done, f32[128,2048]{1,0:T(8,128)S(1)} %get-tuple-element.74.grad, ...), custom_call_target="tpu_custom_call" | custom-call | flops 10000000000 | bytes 65536 | tf_op jit(solution)/shard_map/users_0/pallas_call | solution.py:358
  33.7 4.3 %collective-permute-done.refs_1_ = bf16[128,2048]{1,0:T(8,128)(2,1)S(1)} collective-permute-done((bf16[128,2048]{1,0:T(8,128)(2,1)S(1)}, bf16[128,2048]{1,0:T(8,128)(2,1)S(1)}, u32[]{:S(2)}, u32[]{:S(2)}) %collective-permute-start) | collective-permute-done | bytes 524320 | tf_op jit(solution)/shard_map/ppermute | solution.py:470
  38.1 1.4 %collective-permute-start.2 = (bf16[128,1024]{1,0:T(8,128)(2,1)S(1)}, bf16[128,1024]{1,0:T(8,128)(2,1)S(1)}, u32[]{:S(2)}, u32[]{:S(2)}) collective-permute-start(bf16[128,1024]{1,0:T(8,128)(2,1)S(1)} %get-tuple-element.87), channel_id=1, source_target_pairs={{0,2},{1,3},{2,0},{3,1},{4,6},{5,7},{6,4},{7,5},{8,10},{9,11},{10,... | collective-permute-start | bytes 786440 | tf_op jit(solution)/shard_map/ppermute | solution.py:470
  39.6 0.6 collective-permute-start.3
  40.2 3.4 %collective-permute-done.7.refs_5_ = bf16[128,1024]{1,0:T(8,128)(2,1)S(1)} collective-permute-done((bf16[128,1024]{1,0:T(8,128)(2,1)S(1)}, bf16[128,1024]{1,0:T(8,128)(2,1)S(1)}, u32[]{:S(2)}, u32[]{:S(2)}) %collective-permute-start.7) | collective-permute-done | bytes 262176 | tf_op jit(solution)/shard_map/ppermute | solution.py:470
  43.6 0.6 items_0_0.1
  44.2 1.6 %collective-permute-start.14 = (bf16[128,2048]{1,0:T(8,128)(2,1)S(1)}, bf16[128,2048]{1,0:T(8,128)(2,1)S(1)}, u32[]{:S(2)}, u32[]{:S(2)}) collective-permute-start(bf16[128,2048]{1,0:T(8,128)(2,1)S(1)} %get-tuple-element.107), channel_id=1, source_target_pairs={{0,5},{1,4},{2,7},{3,6},{4,9},{5,8},{6,11},{7,10},{8,13},{9,12},{1... | collective-permute-start | bytes 1572872 | tf_op jit(solution)/shard_map/ppermute | solution.py:480
  45.8 2.7 %collective-permute-start.15 = (bf16[128,2048]{1,0:T(8,128)(2,1)S(1)}, bf16[128,2048]{1,0:T(8,128)(2,1)S(1)}, u32[]{:S(2)}, u32[]{:S(2)}) collective-permute-start(bf16[128,2048]{1,0:T(8,128)(2,1)S(1)} %get-tuple-element.107), channel_id=1, source_target_pairs={{0,6},{1,7},{2,4},{3,5},{4,10},{5,11},{6,8},{7,9},{8,14},{9,15},{1... | collective-permute-start | bytes 1572872 | tf_op jit(solution)/shard_map/ppermute | solution.py:480
  48.5 0.2 collective-permute-done.2.refs_2_
  48.6 0.6 collective-permute-done.3.refs_5_
  49.2 0.6 items_0_1.1
  49.8 1.6 %collective-permute-start.9 = (bf16[128,2048]{1,0:T(8,128)(2,1)S(1)}, bf16[128,2048]{1,0:T(8,128)(2,1)S(1)}, u32[]{:S(2)}, u32[]{:S(2)}) collective-permute-start(bf16[128,2048]{1,0:T(8,128)(2,1)S(1)} %items_0_1.1), channel_id=1, source_target_pairs={{0,5},{1,4},{2,7},{3,6},{4,9},{5,8},{6,11},{7,10},{8,13},{9,12},{1... | collective-permute-start | bytes 1572872 | tf_op jit(solution)/shard_map/ppermute | solution.py:480
  51.4 1.8 %collective-permute-start.10 = (bf16[128,2048]{1,0:T(8,128)(2,1)S(1)}, bf16[128,2048]{1,0:T(8,128)(2,1)S(1)}, u32[]{:S(2)}, u32[]{:S(2)}) collective-permute-start(bf16[128,2048]{1,0:T(8,128)(2,1)S(1)} %items_0_1.1), channel_id=1, source_target_pairs={{0,6},{1,7},{2,4},{3,5},{4,10},{5,11},{6,8},{7,9},{8,14},{9,15},{1... | collective-permute-start | bytes 1572872 | tf_op jit(solution)/shard_map/ppermute | solution.py:480
  53.2 5.2 %collective-permute-done.14.refs_9_.refs_1_ = bf16[128,2048]{1,0:T(8,128)(2,1)S(1)} collective-permute-done((bf16[128,2048]{1,0:T(8,128)(2,1)S(1)}, bf16[128,2048]{1,0:T(8,128)(2,1)S(1)}, u32[]{:S(2)}, u32[]{:S(2)}) %collective-permute-start.14) | collective-permute-done | bytes 524320 | tf_op jit(solution)/shard_map/ppermute | solution.py:480
  58.4 1.5 %collective-permute-start.16 = (bf16[128,1024]{1,0:T(8,128)(2,1)S(1)}, bf16[128,1024]{1,0:T(8,128)(2,1)S(1)}, u32[]{:S(2)}, u32[]{:S(2)}) collective-permute-start(bf16[128,1024]{1,0:T(8,128)(2,1)S(1)} %slice.18), channel_id=1, source_target_pairs={{0,2},{1,3},{2,0},{3,1},{4,6},{5,7},{6,4},{7,5},{8,10},{9,11},{10,... | collective-permute-start | bytes 786440 | tf_op jit(solution)/shard_map/ppermute | solution.py:470
  59.9 1.7 %collective-permute-done.15.refs_10_.refs_2_ = bf16[128,2048]{1,0:T(8,128)(2,1)S(1)} collective-permute-done((bf16[128,2048]{1,0:T(8,128)(2,1)S(1)}, bf16[128,2048]{1,0:T(8,128)(2,1)S(1)}, u32[]{:S(2)}, u32[]{:S(2)}) %collective-permute-start.15) | collective-permute-done | bytes 524320 | tf_op jit(solution)/shard_map/ppermute | solution.py:480
  61.7 1.8 %collective-permute-start.17 = (bf16[128,1024]{1,0:T(8,128)(2,1)S(1)}, bf16[128,1024]{1,0:T(8,128)(2,1)S(1)}, u32[]{:S(2)}, u32[]{:S(2)}) collective-permute-start(bf16[128,1024]{1,0:T(8,128)(2,1)S(1)} %slice.19), channel_id=1, source_target_pairs={{0,1},{1,0},{2,3},{3,2},{4,5},{5,4},{6,7},{7,6},{8,9},{9,8},{10,11... | collective-permute-start | bytes 786440 | tf_op jit(solution)/shard_map/ppermute | solution.py:470
  63.5 8.9 %collective-permute-done.9.refs_9_.refs_6_ = bf16[128,2048]{1,0:T(8,128)(2,1)S(1)} collective-permute-done((bf16[128,2048]{1,0:T(8,128)(2,1)S(1)}, bf16[128,2048]{1,0:T(8,128)(2,1)S(1)}, u32[]{:S(2)}, u32[]{:S(2)}) %collective-permute-start.9) | collective-permute-done | bytes 524320 | tf_op jit(solution)/shard_map/ppermute | solution.py:480
  72.4 2.3 %collective-permute-start.8 = (bf16[128,2048]{1,0:T(8,128)(2,1)S(1)}, bf16[128,2048]{1,0:T(8,128)(2,1)S(1)}, u32[]{:S(2)}, u32[]{:S(2)}) collective-permute-start(bf16[128,2048]{1,0:T(8,128)(2,1)S(1)} %items_0_1.1), channel_id=1, source_target_pairs={{0,4},{1,5},{2,6},{3,7},{4,8},{5,9},{6,10},{7,11},{8,12},{9,13},{1... | collective-permute-start | bytes 1572872 | tf_op jit(solution)/shard_map/ppermute | solution.py:480
  74.8 0.8 collective-permute-start.11
  75.6 3.2 %collective-permute-done.13.refs_8_.refs_0_.items = bf16[128,2048]{1,0:T(8,128)(2,1)S(1)} collective-permute-done((bf16[128,2048]{1,0:T(8,128)(2,1)S(1)}, bf16[128,2048]{1,0:T(8,128)(2,1)S(1)}, u32[]{:S(2)}, u32[]{:S(2)}) %collective-permute-start.13) | collective-permute-done | bytes 524320 | tf_op jit(solution)/shard_map/ppermute | solution.py:480
  78.9 8.3 %tiles_1_0.1 = (bf16[128,2176]{1,0:T(8,128)(2,1)S(1)}, bf16[128,2048]{1,0:T(8,128)(2,1)S(1)}, bf16[128,2048]{1,0:T(8,128)(2,1)S(1)}, bf16[128,2048]{1,0:T(8,128)(2,1)S(1)}, f32[128,2048]{1,0:T(8,128)S(1)}) custom-call(s32[2,1,1,64]{3,2,1,0:T(1,128)} %refs_0_.7, s32[2,1,1,64]{3,2,1,0:T(1,128)} %refs_1_.7, s32[1,2]{1,0:T(1,128)} %bitcast.10, s32[1,2]{1,0:T(1,128)} %bitcast.4, ...), custom_call_target="tpu_custom_call" | custom-call | flops 16000000000 | bytes 65536 | tf_op jit(solution)/shard_map/tiles_1_0/pallas_call | solution.py:319
  87.2 1.7 %collective-permute-start.23 = (bf16[128,2048]{1,0:T(8,128)(2,1)S(1)}, bf16[128,2048]{1,0:T(8,128)(2,1)S(1)}, u32[]{:S(2)}, u32[]{:S(2)}) collective-permute-start(bf16[128,2048]{1,0:T(8,128)(2,1)S(1)} %get-tuple-element.132), channel_id=1, source_target_pairs={{0,2},{1,3},{2,0},{3,1},{4,6},{5,7},{6,4},{7,5},{8,10},{9,11},{10,... | collective-permute-start | bytes 1572872 | tf_op jit(solution)/shard_map/ppermute | solution.py:470
  89.0 7.3 %tiles_1_1.1 = (bf16[128,1024]{1,0:T(8,128)(2,1)S(1)}, bf16[128,1024]{1,0:T(8,128)(2,1)S(1)}, bf16[128,1024]{1,0:T(8,128)(2,1)S(1)}, bf16[128,1024]{1,0:T(8,128)...) custom-call(s32[2,1,1,64]{3,2,1,0:T(1,128)} %refs_0_.7, ...), custom_call_target="tpu_custom_call" | custom-call | flops 16000000000 | bytes 65536 | tf_op jit(solution)/shard_map/tiles_1_1/pallas_call | solution.py:319
  96.4 1.6 %collective-permute-start.18 = (bf16[128,1024]{1,0:T(8,128)(2,1)S(1)}, bf16[128,1024]{1,0:T(8,128)(2,1)S(1)}, u32[]{:S(2)}, u32[]{:S(2)}) collective-permute-start(bf16[128,1024]{1,0:T(8,128)(2,1)S(1)} %get-tuple-element.115), channel_id=1, source_target_pairs={{0,1},{1,0},{2,3},{3,2},{4,5},{5,4},{6,7},{7,6},{8,9},{9,8},{10,11... | collective-permute-start | bytes 786440 | tf_op jit(solution)/shard_map/ppermute | solution.py:470
  98.0 1.9 %collective-permute-done.23.refs_3_.refs_4_ = bf16[128,2048]{1,0:T(8,128)(2,1)S(1)} collective-permute-done((bf16[128,2048]{1,0:T(8,128)(2,1)S(1)}, bf16[128,2048]{1,0:T(8,128)(2,1)S(1)}, u32[]{:S(2)}, u32[]{:S(2)}) %collective-permute-start.23) | collective-permute-done | bytes 524320 | tf_op jit(solution)/shard_map/ppermute | solution.py:470
  99.9 0.3 collective-permute-start.20
  100.1 6.5 %collective-permute-done.22.refs_1_ = bf16[128,2048]{1,0:T(8,128)(2,1)S(1)} collective-permute-done((bf16[128,2048]{1,0:T(8,128)(2,1)S(1)}, bf16[128,2048]{1,0:T(8,128)(2,1)S(1)}, u32[]{:S(2)}, u32[]{:S(2)}) %collective-permute-start.22) | collective-permute-done | bytes 524320 | tf_op jit(solution)/shard_map/ppermute | solution.py:480
  106.8 1.5 %collective-permute-start.24 = (bf16[128,1152]{1,0:T(8,128)(2,1)S(1)}, bf16[128,1152]{1,0:T(8,128)(2,1)S(1)}, u32[]{:S(2)}, u32[]{:S(2)}) collective-permute-start(bf16[128,1152]{1,0:T(8,128)(2,1)S(1)} %get-tuple-element.135), channel_id=1, source_target_pairs={{0,2},{1,3},{2,0},{3,1},{4,6},{5,7},{6,4},{7,5},{8,10},{9,11},{10,... | collective-permute-start | bytes 884744 | tf_op jit(solution)/shard_map/ppermute | solution.py:470
  108.4 0.2 collective-permute-start.29
  108.6 3.7 %collective-permute-done.19.refs_2_ = bf16[128,2048]{1,0:T(8,128)(2,1)S(1)} collective-permute-done((bf16[128,2048]{1,0:T(8,128)(2,1)S(1)}, bf16[128,2048]{1,0:T(8,128)(2,1)S(1)}, u32[]{:S(2)}, u32[]{:S(2)}) %collective-permute-start.19) | collective-permute-done | bytes 524320 | tf_op jit(solution)/shard_map/ppermute | solution.py:480
  112.5 5.0 %collective-permute-done.25.refs_5_ = bf16[128,1024]{1,0:T(8,128)(2,1)S(1)} collective-permute-done((bf16[128,1024]{1,0:T(8,128)(2,1)S(1)}, bf16[128,1024]{1,0:T(8,128)(2,1)S(1)}, u32[]{:S(2)}, u32[]{:S(2)}) %collective-permute-start.25) | collective-permute-done | bytes 262176 | tf_op jit(solution)/shard_map/ppermute | solution.py:470
  117.5 1.1 items_1_0.1
  118.6 0.2 collective-permute-start.26
  118.8 5.3 %users_1.1 = f32[2048,128]{1,0:T(8,128)} custom-call(s32[1,2]{1,0:T(1,128)S(1)} %bitcast.7, f32[2048,128]{1,0:T(8,128)S(1)} %get-tuple-element.77.users, f32[128,2048]{1,0:T(8,128)S(1)} %get-tuple-element.125.grad, bf16[128,2048]{1,0:T(8,128)(2,1)S(1)} %collective-permute-done.13.refs_8_.refs_0_.items, ...), custom_call_target="tpu_custom_call" | custom-call | flops 10000000000 | bytes 65536 | tf_op jit(solution)/shard_map/users_1/pallas_call | solution.py:358
  124.2 1.8 %collective-permute-done.30.refs_6_ = bf16[128,1024]{1,0:T(8,128)(2,1)S(1)} collective-permute-done((bf16[128,1024]{1,0:T(8,128)(2,1)S(1)}, bf16[128,1024]{1,0:T(8,128)(2,1)S(1)}, u32[]{:S(2)}, u32[]{:S(2)}) %collective-permute-start.30) | collective-permute-done | bytes 262176 | tf_op jit(solution)/shard_map/ppermute | solution.py:480
  126.0 5.9 %collective-permute-done.26.refs_0_ = bf16[2176,128]{1,0:T(8,128)(2,1)S(1)} collective-permute-done((bf16[2176,128]{1,0:T(8,128)(2,1)S(1)}, bf16[2176,128]{1,0:T(8,128)(2,1)S(1)}, u32[]{:S(2)}, u32[]{:S(2)}) %collective-permute-start.26) | collective-permute-done | bytes 557088 | tf_op jit(solution)/shard_map/ppermute | solution.py:480
  131.9 1.7 %items_final.1 = f32[4096,128]{1,0:T(8,128)} custom-call(bf16[2176,128]{1,0:T(8,128)(2,1)S(1)} %collective-permute-done.26.refs_0_, bf16[128,2048]{1,0:T(8,128)(2,1)S(1)} %collective-permute-done.22.refs_1_, bf16[128,2048]{1,0:T(8,128)(2,1)S(1)} %collective-permute-done.19.refs_2_, bf16[128,1024]{1,0:T(8,128)(2,1)S(1)} %collective-permute-done.27.refs_3_, ...), custom_call_target="tpu_custom_call" | custom-call | flops 1200000000 | bytes 65536 | tf_op jit(solution)/shard_map/items_final/pallas_call | solution.py:579
  (38 shorter events, 0.9 us)
Async XLA Ops:
  11.3 15.5 %collective-permute-start.4 = (bf16[128,2176]{1,0:T(8,128)(2,1)S(1)}, bf16[128,2176]{1,0:T(8,128)(2,1)S(1)}, u32[]{:S(2)}, u32[]{:S(2)}) collective-permute-start(bf16[128,2176]{1,0:T(8,128)(2,1)S(1)} %get-tuple-element.95.refs_4_.refs_6_), channel_id=1, source_target_pairs={{0,1},{1,0},{2,3},{3,2},{4,5},{5,4},{6,7},{7,6},{8,9},{9,8},{10,11... | collective-permute-start | bytes 1671176 | tf_op jit(solution)/shard_map/ppermute | solution.py:470
  11.7 14.0 %collective-permute-start.5 = (bf16[128,2048]{1,0:T(8,128)(2,1)S(1)}, bf16[128,2048]{1,0:T(8,128)(2,1)S(1)}, u32[]{:S(2)}, u32[]{:S(2)}) collective-permute-start(bf16[128,2048]{1,0:T(8,128)(2,1)S(1)} %get-tuple-element.98), channel_id=1, source_target_pairs={{0,2},{1,3},{2,0},{3,1},{4,6},{5,7},{6,4},{7,5},{8,10},{9,11},{10,... | collective-permute-start | bytes 1572872 | tf_op jit(solution)/shard_map/ppermute | solution.py:470
  21.7 7.3 %copy-start = (f32[2048,128]{1,0:T(8,128)S(1)}, f32[2048,128]{1,0:T(8,128)}, u32[]{:S(2)}) copy-start(f32[2048,128]{1,0:T(8,128)} %users.1) | copy-start | bytes 3145732
  21.7 7.3 %copy-start.1 = (s32[2,1]{0,1:T(1,128)S(1)}, s32[2,1]{0,1:T(1,128)}, u32[]{:S(2)}) copy-start(s32[2,1]{0,1:T(1,128)} %param.13) | copy-start | bytes 28
  21.7 16.3 %collective-permute-start = (bf16[128,2048]{1,0:T(8,128)(2,1)S(1)}, bf16[128,2048]{1,0:T(8,128)(2,1)S(1)}, u32[]{:S(2)}, u32[]{:S(2)}) collective-permute-start(bf16[128,2048]{1,0:T(8,128)(2,1)S(1)} %get-tuple-element.82), channel_id=1, source_target_pairs={{0,1},{1,0},{2,3},{3,2},{4,5},{5,4},{6,7},{7,6},{8,9},{9,8},{10,11... | collective-permute-start | bytes 1572872 | tf_op jit(solution)/shard_map/ppermute | solution.py:470
  21.8 16.3 %collective-permute-start.1 = (bf16[128,2048]{1,0:T(8,128)(2,1)S(1)}, bf16[128,2048]{1,0:T(8,128)(2,1)S(1)}, u32[]{:S(2)}, u32[]{:S(2)}) collective-permute-start(bf16[128,2048]{1,0:T(8,128)(2,1)S(1)} %get-tuple-element.85), channel_id=1, source_target_pairs={{0,2},{1,3},{2,0},{3,1},{4,6},{5,7},{6,4},{7,5},{8,10},{9,11},{10,... | collective-permute-start | bytes 1572872 | tf_op jit(solution)/shard_map/ppermute | solution.py:470
  26.9 16.7 %collective-permute-start.6 = (bf16[128,1152]{1,0:T(8,128)(2,1)S(1)}, bf16[128,1152]{1,0:T(8,128)(2,1)S(1)}, u32[]{:S(2)}, u32[]{:S(2)}) collective-permute-start(bf16[128,1152]{1,0:T(8,128)(2,1)S(1)} %get-tuple-element.100), channel_id=1, source_target_pairs={{0,2},{1,3},{2,0},{3,1},{4,6},{5,7},{6,4},{7,5},{8,10},{9,11},{10,... | collective-permute-start | bytes 884744 | tf_op jit(solution)/shard_map/ppermute | solution.py:470
  28.4 15.3 %collective-permute-start.7 = (bf16[128,1024]{1,0:T(8,128)(2,1)S(1)}, bf16[128,1024]{1,0:T(8,128)(2,1)S(1)}, u32[]{:S(2)}, u32[]{:S(2)}) collective-permute-start(bf16[128,1024]{1,0:T(8,128)(2,1)S(1)} %get-tuple-element.101), channel_id=1, source_target_pairs={{0,1},{1,0},{2,3},{3,2},{4,5},{5,4},{6,7},{7,6},{8,9},{9,8},{10,11... | collective-permute-start | bytes 786440 | tf_op jit(solution)/shard_map/ppermute | solution.py:470
  38.1 10.5 %collective-permute-start.2 = (bf16[128,1024]{1,0:T(8,128)(2,1)S(1)}, bf16[128,1024]{1,0:T(8,128)(2,1)S(1)}, u32[]{:S(2)}, u32[]{:S(2)}) collective-permute-start(bf16[128,1024]{1,0:T(8,128)(2,1)S(1)} %get-tuple-element.87), channel_id=1, source_target_pairs={{0,2},{1,3},{2,0},{3,1},{4,6},{5,7},{6,4},{7,5},{8,10},{9,11},{10,... | collective-permute-start | bytes 786440 | tf_op jit(solution)/shard_map/ppermute | solution.py:470
  39.6 9.7 %collective-permute-start.3 = (bf16[128,1024]{1,0:T(8,128)(2,1)S(1)}, bf16[128,1024]{1,0:T(8,128)(2,1)S(1)}, u32[]{:S(2)}, u32[]{:S(2)}) collective-permute-start(bf16[128,1024]{1,0:T(8,128)(2,1)S(1)} %get-tuple-element.88), channel_id=1, source_target_pairs={{0,1},{1,0},{2,3},{3,2},{4,5},{5,4},{6,7},{7,6},{8,9},{9,8},{10,11... | collective-permute-start | bytes 786440 | tf_op jit(solution)/shard_map/ppermute | solution.py:470
  44.2 14.2 %collective-permute-start.14 = (bf16[128,2048]{1,0:T(8,128)(2,1)S(1)}, bf16[128,2048]{1,0:T(8,128)(2,1)S(1)}, u32[]{:S(2)}, u32[]{:S(2)}) collective-permute-start(bf16[128,2048]{1,0:T(8,128)(2,1)S(1)} %get-tuple-element.107), channel_id=1, source_target_pairs={{0,5},{1,4},{2,7},{3,6},{4,9},{5,8},{6,11},{7,10},{8,13},{9,12},{1... | collective-permute-start | bytes 1572872 | tf_op jit(solution)/shard_map/ppermute | solution.py:480
  45.8 15.8 %collective-permute-start.15 = (bf16[128,2048]{1,0:T(8,128)(2,1)S(1)}, bf16[128,2048]{1,0:T(8,128)(2,1)S(1)}, u32[]{:S(2)}, u32[]{:S(2)}) collective-permute-start(bf16[128,2048]{1,0:T(8,128)(2,1)S(1)} %get-tuple-element.107), channel_id=1, source_target_pairs={{0,6},{1,7},{2,4},{3,5},{4,10},{5,11},{6,8},{7,9},{8,14},{9,15},{1... | collective-permute-start | bytes 1572872 | tf_op jit(solution)/shard_map/ppermute | solution.py:480
  49.8 22.6 %collective-permute-start.9 = (bf16[128,2048]{1,0:T(8,128)(2,1)S(1)}, bf16[128,2048]{1,0:T(8,128)(2,1)S(1)}, u32[]{:S(2)}, u32[]{:S(2)}) collective-permute-start(bf16[128,2048]{1,0:T(8,128)(2,1)S(1)} %items_0_1.1), channel_id=1, source_target_pairs={{0,5},{1,4},{2,7},{3,6},{4,9},{5,8},{6,11},{7,10},{8,13},{9,12},{1... | collective-permute-start | bytes 1572872 | tf_op jit(solution)/shard_map/ppermute | solution.py:480
  51.4 23.4 %collective-permute-start.10 = (bf16[128,2048]{1,0:T(8,128)(2,1)S(1)}, bf16[128,2048]{1,0:T(8,128)(2,1)S(1)}, u32[]{:S(2)}, u32[]{:S(2)}) collective-permute-start(bf16[128,2048]{1,0:T(8,128)(2,1)S(1)} %items_0_1.1), channel_id=1, source_target_pairs={{0,6},{1,7},{2,4},{3,5},{4,10},{5,11},{6,8},{7,9},{8,14},{9,15},{1... | collective-permute-start | bytes 1572872 | tf_op jit(solution)/shard_map/ppermute | solution.py:480
  53.2 25.6 %collective-permute-start.13 = (bf16[128,2048]{1,0:T(8,128)(2,1)S(1)}, bf16[128,2048]{1,0:T(8,128)(2,1)S(1)}, u32[]{:S(2)}, u32[]{:S(2)}) collective-permute-start(bf16[128,2048]{1,0:T(8,128)(2,1)S(1)} %get-tuple-element.107), channel_id=1, source_target_pairs={{0,4},{1,5},{2,6},{3,7},{4,8},{5,9},{6,10},{7,11},{8,12},{9,13},{1... | collective-permute-start | bytes 1572872 | tf_op jit(solution)/shard_map/ppermute | solution.py:480
  58.4 20.4 %collective-permute-start.16 = (bf16[128,1024]{1,0:T(8,128)(2,1)S(1)}, bf16[128,1024]{1,0:T(8,128)(2,1)S(1)}, u32[]{:S(2)}, u32[]{:S(2)}) collective-permute-start(bf16[128,1024]{1,0:T(8,128)(2,1)S(1)} %slice.18), channel_id=1, source_target_pairs={{0,2},{1,3},{2,0},{3,1},{4,6},{5,7},{6,4},{7,5},{8,10},{9,11},{10,... | collective-permute-start | bytes 786440 | tf_op jit(solution)/shard_map/ppermute | solution.py:470
  61.7 17.2 %collective-permute-start.17 = (bf16[128,1024]{1,0:T(8,128)(2,1)S(1)}, bf16[128,1024]{1,0:T(8,128)(2,1)S(1)}, u32[]{:S(2)}, u32[]{:S(2)}) collective-permute-start(bf16[128,1024]{1,0:T(8,128)(2,1)S(1)} %slice.19), channel_id=1, source_target_pairs={{0,1},{1,0},{2,3},{3,2},{4,5},{5,4},{6,7},{7,6},{8,9},{9,8},{10,11... | collective-permute-start | bytes 786440 | tf_op jit(solution)/shard_map/ppermute | solution.py:470
  72.4 16.5 %collective-permute-start.8 = (bf16[128,2048]{1,0:T(8,128)(2,1)S(1)}, bf16[128,2048]{1,0:T(8,128)(2,1)S(1)}, u32[]{:S(2)}, u32[]{:S(2)}) collective-permute-start(bf16[128,2048]{1,0:T(8,128)(2,1)S(1)} %items_0_1.1), channel_id=1, source_target_pairs={{0,4},{1,5},{2,6},{3,7},{4,8},{5,9},{6,10},{7,11},{8,12},{9,13},{1... | collective-permute-start | bytes 1572872 | tf_op jit(solution)/shard_map/ppermute | solution.py:480
  74.8 14.1 %collective-permute-start.11 = (bf16[128,1024]{1,0:T(8,128)(2,1)S(1)}, bf16[128,1024]{1,0:T(8,128)(2,1)S(1)}, u32[]{:S(2)}, u32[]{:S(2)}) collective-permute-start(bf16[128,1024]{1,0:T(8,128)(2,1)S(1)} %slice.16), channel_id=1, source_target_pairs={{0,2},{1,3},{2,0},{3,1},{4,6},{5,7},{6,4},{7,5},{8,10},{9,11},{10,... | collective-permute-start | bytes 786440 | tf_op jit(solution)/shard_map/ppermute | solution.py:470
  78.8 10.1 %collective-permute-start.12 = (bf16[128,1024]{1,0:T(8,128)(2,1)S(1)}, bf16[128,1024]{1,0:T(8,128)(2,1)S(1)}, u32[]{:S(2)}, u32[]{:S(2)}) collective-permute-start(bf16[128,1024]{1,0:T(8,128)(2,1)S(1)} %slice.17), channel_id=1, source_target_pairs={{0,1},{1,0},{2,3},{3,2},{4,5},{5,4},{6,7},{7,6},{8,9},{9,8},{10,11... | collective-permute-start | bytes 786440 | tf_op jit(solution)/shard_map/ppermute | solution.py:470
  87.2 19.5 %collective-permute-start.21 = (bf16[128,2176]{1,0:T(8,128)(2,1)S(1)}, bf16[128,2176]{1,0:T(8,128)(2,1)S(1)}, u32[]{:S(2)}, u32[]{:S(2)}) collective-permute-start(bf16[128,2176]{1,0:T(8,128)(2,1)S(1)} %get-tuple-element.127.refs_4_.refs_6_), channel_id=1, source_target_pairs={{0,1},{1,0},{2,3},{3,2},{4,5},{5,4},{6,7},{7,6},{8,9},{9,8},{10,11... | collective-permute-start | bytes 1671176 | tf_op jit(solution)/shard_map/ppermute | solution.py:470
  87.2 12.6 %collective-permute-start.23 = (bf16[128,2048]{1,0:T(8,128)(2,1)S(1)}, bf16[128,2048]{1,0:T(8,128)(2,1)S(1)}, u32[]{:S(2)}, u32[]{:S(2)}) collective-permute-start(bf16[128,2048]{1,0:T(8,128)(2,1)S(1)} %get-tuple-element.132), channel_id=1, source_target_pairs={{0,2},{1,3},{2,0},{3,1},{4,6},{5,7},{6,4},{7,5},{8,10},{9,11},{10,... | collective-permute-start | bytes 1572872 | tf_op jit(solution)/shard_map/ppermute | solution.py:470
  96.2 10.5 %collective-permute-start.22 = (bf16[128,2048]{1,0:T(8,128)(2,1)S(1)}, bf16[128,2048]{1,0:T(8,128)(2,1)S(1)}, u32[]{:S(2)}, u32[]{:S(2)}) collective-permute-start(bf16[128,2048]{1,0:T(8,128)(2,1)S(1)} %collective-permute-done.8.refs_8_.refs_5_), channel_id=1, source_target_pairs={{0,4},{1,5},{2,6},{3,7},{4,8},{5,9},{6,10},{7,11},{8,12},{9,13},{1... | collective-permute-start | bytes 1572872 | tf_op jit(solution)/shard_map/ppermute | solution.py:480
  96.3 16.0 %collective-permute-start.19 = (bf16[128,2048]{1,0:T(8,128)(2,1)S(1)}, bf16[128,2048]{1,0:T(8,128)(2,1)S(1)}, u32[]{:S(2)}, u32[]{:S(2)}) collective-permute-start(bf16[128,2048]{1,0:T(8,128)(2,1)S(1)} %get-tuple-element.117), channel_id=1, source_target_pairs={{0,4},{1,5},{2,6},{3,7},{4,8},{5,9},{6,10},{7,11},{8,12},{9,13},{1... | collective-permute-start | bytes 1572872 | tf_op jit(solution)/shard_map/ppermute | solution.py:480
  96.4 12.0 %collective-permute-start.18 = (bf16[128,1024]{1,0:T(8,128)(2,1)S(1)}, bf16[128,1024]{1,0:T(8,128)(2,1)S(1)}, u32[]{:S(2)}, u32[]{:S(2)}) collective-permute-start(bf16[128,1024]{1,0:T(8,128)(2,1)S(1)} %get-tuple-element.115), channel_id=1, source_target_pairs={{0,1},{1,0},{2,3},{3,2},{4,5},{5,4},{6,7},{7,6},{8,9},{9,8},{10,11... | collective-permute-start | bytes 786440 | tf_op jit(solution)/shard_map/ppermute | solution.py:470
  99.9 8.5 %collective-permute-start.20 = (bf16[128,1024]{1,0:T(8,128)(2,1)S(1)}, bf16[128,1024]{1,0:T(8,128)(2,1)S(1)}, u32[]{:S(2)}, u32[]{:S(2)}) collective-permute-start(bf16[128,1024]{1,0:T(8,128)(2,1)S(1)} %get-tuple-element.120), channel_id=1, source_target_pairs={{0,2},{1,3},{2,0},{3,1},{4,6},{5,7},{6,4},{7,5},{8,10},{9,11},{10,... | collective-permute-start | bytes 786440 | tf_op jit(solution)/shard_map/ppermute | solution.py:470
  106.8 10.7 %collective-permute-start.24 = (bf16[128,1152]{1,0:T(8,128)(2,1)S(1)}, bf16[128,1152]{1,0:T(8,128)(2,1)S(1)}, u32[]{:S(2)}, u32[]{:S(2)}) collective-permute-start(bf16[128,1152]{1,0:T(8,128)(2,1)S(1)} %get-tuple-element.135), channel_id=1, source_target_pairs={{0,2},{1,3},{2,0},{3,1},{4,6},{5,7},{6,4},{7,5},{8,10},{9,11},{10,... | collective-permute-start | bytes 884744 | tf_op jit(solution)/shard_map/ppermute | solution.py:470
  108.3 9.2 %collective-permute-start.25 = (bf16[128,1024]{1,0:T(8,128)(2,1)S(1)}, bf16[128,1024]{1,0:T(8,128)(2,1)S(1)}, u32[]{:S(2)}, u32[]{:S(2)}) collective-permute-start(bf16[128,1024]{1,0:T(8,128)(2,1)S(1)} %get-tuple-element.136), channel_id=1, source_target_pairs={{0,1},{1,0},{2,3},{3,2},{4,5},{5,4},{6,7},{7,6},{8,9},{9,8},{10,11... | collective-permute-start | bytes 786440 | tf_op jit(solution)/shard_map/ppermute | solution.py:470
  108.3 15.8 %collective-permute-start.27 = (bf16[128,1024]{1,0:T(8,128)(2,1)S(1)}, bf16[128,1024]{1,0:T(8,128)(2,1)S(1)}, u32[]{:S(2)}, u32[]{:S(2)}) collective-permute-start(bf16[128,1024]{1,0:T(8,128)(2,1)S(1)} %get-tuple-element.138), channel_id=1, source_target_pairs={{0,5},{1,4},{2,7},{3,6},{4,9},{5,8},{6,11},{7,10},{8,13},{9,12},{1... | collective-permute-start | bytes 786440 | tf_op jit(solution)/shard_map/ppermute | solution.py:480
  108.4 15.8 %collective-permute-start.29 = (bf16[128,1024]{1,0:T(8,128)(2,1)S(1)}, bf16[128,1024]{1,0:T(8,128)(2,1)S(1)}, u32[]{:S(2)}, u32[]{:S(2)}) collective-permute-start(bf16[128,1024]{1,0:T(8,128)(2,1)S(1)} %get-tuple-element.139), channel_id=1, source_target_pairs={{0,6},{1,7},{2,4},{3,5},{4,10},{5,11},{6,8},{7,9},{8,14},{9,15},{1... | collective-permute-start | bytes 786440 | tf_op jit(solution)/shard_map/ppermute | solution.py:480
  112.4 11.7 %collective-permute-start.28 = (bf16[128,1024]{1,0:T(8,128)(2,1)S(1)}, bf16[128,1024]{1,0:T(8,128)(2,1)S(1)}, u32[]{:S(2)}, u32[]{:S(2)}) collective-permute-start(bf16[128,1024]{1,0:T(8,128)(2,1)S(1)} %get-tuple-element.123), channel_id=1, source_target_pairs={{0,6},{1,7},{2,4},{3,5},{4,10},{5,11},{6,8},{7,9},{8,14},{9,15},{1... | collective-permute-start | bytes 786440 | tf_op jit(solution)/shard_map/ppermute | solution.py:480
  112.5 6.3 %copy-start.2 = (s32[2,1]{0,1:T(1,128)S(1)}, s32[2,1]{0,1:T(1,128)}, u32[]{:S(2)}) copy-start(s32[2,1]{0,1:T(1,128)} %param.13) | copy-start | bytes 28
  117.5 8.5 %collective-permute-start.30 = (bf16[128,1024]{1,0:T(8,128)(2,1)S(1)}, bf16[128,1024]{1,0:T(8,128)(2,1)S(1)}, u32[]{:S(2)}, u32[]{:S(2)}) collective-permute-start(bf16[128,1024]{1,0:T(8,128)(2,1)S(1)} %get-tuple-element.124), channel_id=1, source_target_pairs={{0,5},{1,4},{2,7},{3,6},{4,9},{5,8},{6,11},{7,10},{8,13},{9,12},{1... | collective-permute-start | bytes 786440 | tf_op jit(solution)/shard_map/ppermute | solution.py:480
  118.6 13.3 %collective-permute-start.26 = (bf16[2176,128]{1,0:T(8,128)(2,1)S(1)}, bf16[2176,128]{1,0:T(8,128)(2,1)S(1)}, u32[]{:S(2)}, u32[]{:S(2)}) collective-permute-start(bf16[2176,128]{1,0:T(8,128)(2,1)S(1)} %get-tuple-element.137), channel_id=1, source_target_pairs={{0,4},{1,5},{2,6},{3,7},{4,8},{5,9},{6,10},{7,11},{8,12},{9,13},{1... | collective-permute-start | bytes 1671176 | tf_op jit(solution)/shard_map/ppermute | solution.py:480

commit v9 on v8

--- a/solution.py
+++ b/solution.py
@@ -470,10 +470,10 @@
     return lax.ppermute(value, "grp", [(i, i ^ bit) for i in range(length)])
 
 
-def moved(value, bit):
+def moved(value, bit, by=1):
     length, blocks = lax.axis_size("grp"), lax.axis_size("blk")
     pairs = [
-        (b * length + i, (b + 1) % blocks * length + (i ^ bit))
+        (b * length + i, (b + by) % blocks * length + (i ^ bit))
         for b in range(blocks)
         for i in range(length)
     ]
@@ -663,8 +663,6 @@
                 pieces += [array for array, _ in sources]
                 olds.append(sources[0][0])
         last = epoch + 1 == SUB
-        if last:
-            kept = moved(tied(olds[-1], grad_user), 0)
         if not last:
             new_users = user_call(epoch, block_rows, owners, full_users, grad_user, pieces)
             full_users = new_users[0]
@@ -705,6 +703,7 @@
             users, own_gram = new_users[1:3], new_users[3]
             gathers = [gathered(shard, [shards[-1]]) for shard in shards]
             near = gathers[-1][1]
+            kept = moved(tied(shards[-1], *near), 0, 2)
             gathers = [found for found, _ in gathers]
             (array, columns), *rest = gathers[0]
             gathers[0] = [(tied(array, *near), columns), *rest]

time: 134 us -> 147 us (1.097)
  starting transfers between devices: 26.4 us -> 39.8 us
  Pallas kernels: 49 us -> 46.9 us
    ppermute x18, waiting for transfers between devices: 20.1 us -> 30.6 us  [swapped(): return lax.ppermute(value, 'grp', [(i, i ^ bit) for i in range(length)])]
    ppermute x13, waiting for transfers between devices: 37.2 us -> 28 us  [moved(): return lax.ppermute(value, ('blk', 'grp'), pairs)]
    ppermute x13, starting transfers between devices: 10.5 us -> 19.7 us  [moved(): return lax.ppermute(value, ('blk', 'grp'), pairs)]
    ppermute x18, starting transfers between devices: 15.9 us -> 20.1 us  [swapped(): return lax.ppermute(value, 'grp', [(i, i ^ bit) for i in range(length)])]
    pallas_call x4, Pallas kernels: 34.5 us -> 32.3 us  [tile_call(): pl.pallas_call(functools.partial(tile_kernel, epoch, chunk, direct, membe...]
  transfers between devices with their start and end apart: 31 -> 31, of which waited for: 17 -> 15; matrix products, arithmetic and copies ran while one was open for 0% -> 0% of each run, Pallas kernels for 27% -> 24%
where the time goes in v9:
time: 147 us; the launch traced here: 146 us
  waiting for transfers between devices  58.6 us (40%)
  Pallas kernels  46.9 us (32%)
  starting transfers between devices  39.8 us (27%)
    pallas_call x4, Pallas kernels, tile_call(): pl.pallas_call(functools.partial(tile_kernel, epoch, chunk, direct, membe...  32.3 us
    ppermute x18, waiting for transfers between devices, swapped(): return lax.ppermute(value, 'grp', [(i, i ^ bit) for i in range(length)])  30.6 us
    ppermute x13, waiting for transfers between devices, moved(): return lax.ppermute(value, ('blk', 'grp'), pairs)  28 us
    ppermute x18, starting transfers between devices, swapped(): return lax.ppermute(value, 'grp', [(i, i ^ bit) for i in range(length)])  20.1 us
    ppermute x13, starting transfers between devices, moved(): return lax.ppermute(value, ('blk', 'grp'), pairs)  19.7 us
    pallas_call x2, Pallas kernels, user_call(): pl.pallas_call(functools.partial(user_kernel, epoch, block_rows), out_sha...  10.1 us
  transfers between devices with their start and end apart: 31, of which 15 were waited for; matrix products, arithmetic and copies ran while one was open for 0% of the time, Pallas kernels for 24%

profile of v9, /device:TPU:0, one launch (start us, length us, event | category | flops | bytes accessed | tf_op | source)
XLA Modules:
  0.0 146.3 jit_solution(872300744529864333)
XLA Ops:
  0.6 9.6 %tiles_0_0.1 = (bf16[128,2176]{1,0:T(8,128)(2,1)S(1)}, bf16[128,2048]{1,0:T(8,128)(2,1)S(1)}, bf16[128,2048]{1,0:T(8,128)(2,1)S(1)}, bf16[128,2048]{1,0:T(8,128)...) custom-call(s32[2,1,1,64]{3,2,1,0:T(1,128)} %refs_0_.7, ...), custom_call_target="tpu_custom_call" | custom-call | flops 16000000000 | bytes 65536 | tf_op jit(solution)/shard_map/tiles_0_0/pallas_call | solution.py:319
  10.3 3.0 %collective-permute-start.4 = (bf16[128,2176]{1,0:T(8,128)(2,1)S(1)}, bf16[128,2176]{1,0:T(8,128)(2,1)S(1)}, u32[]{:S(2)}, u32[]{:S(2)}) collective-permute-start(bf16[128,2176]{1,0:T(8,128)(2,1)S(1)} %get-tuple-element.95.refs_4_.refs_6_), channel_id=1, source_target_pairs={{0,1},{1,0},{2,3},{3,2},{4,5},{5,4},{6,7},{7,6},{8,9},{9,8},{10,11... | collective-permute-start | bytes 1671176 | tf_op jit(solution)/shard_map/ppermute | solution.py:470
  13.3 7.2 %tiles_0_1.1 = (bf16[128,2048]{1,0:T(8,128)(2,1)S(1)}, bf16[128,2048]{1,0:T(8,128)(2,1)S(1)}, bf16[128,2048]{1,0:T(8,128)(2,1)S(1)}, bf16[128,2048]{1,0:T(8,128)...) custom-call(s32[2,1,1,64]{3,2,1,0:T(1,128)} %refs_0_.7, ...), custom_call_target="tpu_custom_call" | custom-call | flops 16000000000 | bytes 65536 | tf_op jit(solution)/shard_map/tiles_0_1/pallas_call | solution.py:319
  20.4 2.3 %collective-permute-start = (bf16[128,2048]{1,0:T(8,128)(2,1)S(1)}, bf16[128,2048]{1,0:T(8,128)(2,1)S(1)}, u32[]{:S(2)}, u32[]{:S(2)}) collective-permute-start(bf16[128,2048]{1,0:T(8,128)(2,1)S(1)} %get-tuple-element.82), channel_id=1, source_target_pairs={{0,1},{1,0},{2,3},{3,2},{4,5},{5,4},{6,7},{7,6},{8,9},{9,8},{10,11... | collective-permute-start | bytes 1572872 | tf_op jit(solution)/shard_map/ppermute | solution.py:470
  22.8 2.0 %collective-permute-start.5 = (bf16[128,2048]{1,0:T(8,128)(2,1)S(1)}, bf16[128,2048]{1,0:T(8,128)(2,1)S(1)}, u32[]{:S(2)}, u32[]{:S(2)}) collective-permute-start(bf16[128,2048]{1,0:T(8,128)(2,1)S(1)} %get-tuple-element.98), channel_id=1, source_target_pairs={{0,2},{1,3},{2,0},{3,1},{4,6},{5,7},{6,4},{7,5},{8,10},{9,11},{10,... | collective-permute-start | bytes 1572872 | tf_op jit(solution)/shard_map/ppermute | solution.py:470
  24.8 12.2 %collective-permute-done.refs_1_ = bf16[128,2048]{1,0:T(8,128)(2,1)S(1)} collective-permute-done((bf16[128,2048]{1,0:T(8,128)(2,1)S(1)}, bf16[128,2048]{1,0:T(8,128)(2,1)S(1)}, u32[]{:S(2)}, u32[]{:S(2)}) %collective-permute-start) | collective-permute-done | bytes 524320 | tf_op jit(solution)/shard_map/ppermute | solution.py:470
  37.0 0.6 collective-permute-done.1.refs_3_.refs_4_
  37.8 1.0 collective-permute-start.2
  38.8 1.7 %collective-permute-start.3 = (bf16[128,1024]{1,0:T(8,128)(2,1)S(1)}, bf16[128,1024]{1,0:T(8,128)(2,1)S(1)}, u32[]{:S(2)}, u32[]{:S(2)}) collective-permute-start(bf16[128,1024]{1,0:T(8,128)(2,1)S(1)} %get-tuple-element.88), channel_id=1, source_target_pairs={{0,1},{1,0},{2,3},{3,2},{4,5},{5,4},{6,7},{7,6},{8,9},{9,8},{10,11... | collective-permute-start | bytes 786440 | tf_op jit(solution)/shard_map/ppermute | solution.py:470
  40.6 8.3 %collective-permute-done.5.refs_3_.refs_4_ = bf16[128,2048]{1,0:T(8,128)(2,1)S(1)} collective-permute-done((bf16[128,2048]{1,0:T(8,128)(2,1)S(1)}, bf16[128,2048]{1,0:T(8,128)(2,1)S(1)}, u32[]{:S(2)}, u32[]{:S(2)}) %collective-permute-start.5) | collective-permute-done | bytes 524320 | tf_op jit(solution)/shard_map/ppermute | solution.py:470
  48.9 0.1 mid_0_0_0.1
  49.1 1.3 collective-permute-start.7
  50.4 4.8 %users_0.1 = (f32[2048,128]{1,0:T(8,128)S(1)}, bf16[2048,128]{1,0:T(8,128)(2,1)S(1)}, bf16[128,2048]{1,0:T(8,128)(2,1)S(1)}, bf16[128,128]{1,0:T(8,128)(2,1)S(1)}) custom-call(s32[1,2]{1,0:T(1,128)S(1)} %bitcast.6, f32[2048,128]{1,0:T(8,128)S(1)} %copy-done, f32[128,2048]{1,0:T(8,128)S(1)} %get-tuple-element.74.grad, ...), custom_call_target="tpu_custom_call" | custom-call | flops 10000000000 | bytes 65536 | tf_op jit(solution)/shard_map/users_0/pallas_call | solution.py:358
  55.2 0.3 collective-permute-done.7.refs_5_
  55.5 1.8 %collective-permute-done.6.refs_2_.refs_8_ = bf16[128,1152]{1,0:T(8,128)(2,1)S(1)} collective-permute-done((bf16[128,1152]{1,0:T(8,128)(2,1)S(1)}, bf16[128,1152]{1,0:T(8,128)(2,1)S(1)}, u32[]{:S(2)}, u32[]{:S(2)}) %collective-permute-start.6) | collective-permute-done | bytes 294944 | tf_op jit(solution)/shard_map/ppermute | solution.py:470
  57.3 0.6 items_0_0.1
  58.0 2.7 %collective-permute-start.15 = (bf16[128,2048]{1,0:T(8,128)(2,1)S(1)}, bf16[128,2048]{1,0:T(8,128)(2,1)S(1)}, u32[]{:S(2)}, u32[]{:S(2)}) collective-permute-start(bf16[128,2048]{1,0:T(8,128)(2,1)S(1)} %get-tuple-element.107), channel_id=1, source_target_pairs={{0,6},{1,7},{2,4},{3,5},{4,10},{5,11},{6,8},{7,9},{8,14},{9,15},{1... | collective-permute-start | bytes 1572872 | tf_op jit(solution)/shard_map/ppermute | solution.py:480
  60.7 0.6 items_0_1.1
  61.4 4.9 %collective-permute-start.10 = (bf16[128,2048]{1,0:T(8,128)(2,1)S(1)}, bf16[128,2048]{1,0:T(8,128)(2,1)S(1)}, u32[]{:S(2)}, u32[]{:S(2)}) collective-permute-start(bf16[128,2048]{1,0:T(8,128)(2,1)S(1)} %items_0_1.1), channel_id=1, source_target_pairs={{0,6},{1,7},{2,4},{3,5},{4,10},{5,11},{6,8},{7,9},{8,14},{9,15},{1... | collective-permute-start | bytes 1572872 | tf_op jit(solution)/shard_map/ppermute | solution.py:480
  66.3 4.0 %collective-permute-done.14.refs_9_.refs_1_ = bf16[128,2048]{1,0:T(8,128)(2,1)S(1)} collective-permute-done((bf16[128,2048]{1,0:T(8,128)(2,1)S(1)}, bf16[128,2048]{1,0:T(8,128)(2,1)S(1)}, u32[]{:S(2)}, u32[]{:S(2)}) %collective-permute-start.14) | collective-permute-done | bytes 524320 | tf_op jit(solution)/shard_map/ppermute | solution.py:480
  70.3 1.4 collective-permute-start.16
  71.7 5.0 %collective-permute-done.15.refs_10_.refs_2_ = bf16[128,2048]{1,0:T(8,128)(2,1)S(1)} collective-permute-done((bf16[128,2048]{1,0:T(8,128)(2,1)S(1)}, bf16[128,2048]{1,0:T(8,128)(2,1)S(1)}, u32[]{:S(2)}, u32[]{:S(2)}) %collective-permute-start.15) | collective-permute-done | bytes 524320 | tf_op jit(solution)/shard_map/ppermute | solution.py:480
  76.7 0.3 collective-permute-start.17
  77.0 6.2 %collective-permute-done.9.refs_9_.refs_6_ = bf16[128,2048]{1,0:T(8,128)(2,1)S(1)} collective-permute-done((bf16[128,2048]{1,0:T(8,128)(2,1)S(1)}, bf16[128,2048]{1,0:T(8,128)(2,1)S(1)}, u32[]{:S(2)}, u32[]{:S(2)}) %collective-permute-start.9) | collective-permute-done | bytes 524320 | tf_op jit(solution)/shard_map/ppermute | solution.py:480
  83.2 3.1 %collective-permute-start.8 = (bf16[128,2048]{1,0:T(8,128)(2,1)S(1)}, bf16[128,2048]{1,0:T(8,128)(2,1)S(1)}, u32[]{:S(2)}, u32[]{:S(2)}) collective-permute-start(bf16[128,2048]{1,0:T(8,128)(2,1)S(1)} %items_0_1.1), channel_id=1, source_target_pairs={{0,4},{1,5},{2,6},{3,7},{4,8},{5,9},{6,10},{7,11},{8,12},{9,13},{1... | collective-permute-start | bytes 1572872 | tf_op jit(solution)/shard_map/ppermute | solution.py:480
  86.3 1.7 %collective-permute-done.10.refs_10_.refs_7_ = bf16[128,2048]{1,0:T(8,128)(2,1)S(1)} collective-permute-done((bf16[128,2048]{1,0:T(8,128)(2,1)S(1)}, bf16[128,2048]{1,0:T(8,128)(2,1)S(1)}, u32[]{:S(2)}, u32[]{:S(2)}) %collective-permute-start.10) | collective-permute-done | bytes 524320 | tf_op jit(solution)/shard_map/ppermute | solution.py:480
  88.0 0.6 collective-permute-start.11
  88.6 3.8 %collective-permute-done.13.refs_8_.refs_0_.items = bf16[128,2048]{1,0:T(8,128)(2,1)S(1)} collective-permute-done((bf16[128,2048]{1,0:T(8,128)(2,1)S(1)}, bf16[128,2048]{1,0:T(8,128)(2,1)S(1)}, u32[]{:S(2)}, u32[]{:S(2)}) %collective-permute-start.13) | collective-permute-done | bytes 524320 | tf_op jit(solution)/shard_map/ppermute | solution.py:480
  92.5 0.4 collective-permute-start.12
  92.9 2.1 %collective-permute-start.22 = (bf16[128,2048]{1,0:T(8,128)(2,1)S(1)}, bf16[128,2048]{1,0:T(8,128)(2,1)S(1)}, u32[]{:S(2)}, u32[]{:S(2)}) collective-permute-start(bf16[128,2048]{1,0:T(8,128)(2,1)S(1)} %items_0_1.1), channel_id=1, source_target_pairs={{0,8},{1,9},{2,10},{3,11},{4,12},{5,13},{6,14},{7,15},{8,16},{9,17... | collective-permute-start | bytes 1572872 | tf_op jit(solution)/shard_map/ppermute | solution.py:480
  94.9 7.2 %tiles_1_0.1 = (bf16[128,2176]{1,0:T(8,128)(2,1)S(1)}, bf16[128,2048]{1,0:T(8,128)(2,1)S(1)}, bf16[128,2048]{1,0:T(8,128)(2,1)S(1)}, bf16[128,2048]{1,0:T(8,128)(2,1)S(1)}, f32[128,2048]{1,0:T(8,128)S(1)}) custom-call(s32[2,1,1,64]{3,2,1,0:T(1,128)} %refs_0_.7, s32[2,1,1,64]{3,2,1,0:T(1,128)} %refs_1_.7, s32[1,2]{1,0:T(1,128)} %bitcast.10, s32[1,2]{1,0:T(1,128)} %bitcast.4, ...), custom_call_target="tpu_custom_call" | custom-call | flops 16000000000 | bytes 65536 | tf_op jit(solution)/shard_map/tiles_1_0/pallas_call | solution.py:319
  102.2 2.1 %collective-permute-start.23 = (bf16[128,2048]{1,0:T(8,128)(2,1)S(1)}, bf16[128,2048]{1,0:T(8,128)(2,1)S(1)}, u32[]{:S(2)}, u32[]{:S(2)}) collective-permute-start(bf16[128,2048]{1,0:T(8,128)(2,1)S(1)} %get-tuple-element.132), channel_id=1, source_target_pairs={{0,2},{1,3},{2,0},{3,1},{4,6},{5,7},{6,4},{7,5},{8,10},{9,11},{10,... | collective-permute-start | bytes 1572872 | tf_op jit(solution)/shard_map/ppermute | solution.py:470
  104.3 8.3 %tiles_1_1.1 = (bf16[128,1024]{1,0:T(8,128)(2,1)S(1)}, bf16[128,1024]{1,0:T(8,128)(2,1)S(1)}, bf16[128,1024]{1,0:T(8,128)(2,1)S(1)}, bf16[128,1024]{1,0:T(8,128)...) custom-call(s32[2,1,1,64]{3,2,1,0:T(1,128)} %refs_0_.7, ...), custom_call_target="tpu_custom_call" | custom-call | flops 16000000000 | bytes 65536 | tf_op jit(solution)/shard_map/tiles_1_1/pallas_call | solution.py:319
  112.8 2.0 %collective-permute-done.23.refs_3_.refs_4_ = bf16[128,2048]{1,0:T(8,128)(2,1)S(1)} collective-permute-done((bf16[128,2048]{1,0:T(8,128)(2,1)S(1)}, bf16[128,2048]{1,0:T(8,128)(2,1)S(1)}, u32[]{:S(2)}, u32[]{:S(2)}) %collective-permute-start.23) | collective-permute-done | bytes 524320 | tf_op jit(solution)/shard_map/ppermute | solution.py:470
  114.8 1.7 %collective-permute-start.20 = (bf16[128,1024]{1,0:T(8,128)(2,1)S(1)}, bf16[128,1024]{1,0:T(8,128)(2,1)S(1)}, u32[]{:S(2)}, u32[]{:S(2)}) collective-permute-start(bf16[128,1024]{1,0:T(8,128)(2,1)S(1)} %get-tuple-element.120), channel_id=1, source_target_pairs={{0,2},{1,3},{2,0},{3,1},{4,6},{5,7},{6,4},{7,5},{8,10},{9,11},{10,... | collective-permute-start | bytes 786440 | tf_op jit(solution)/shard_map/ppermute | solution.py:470
  116.6 0.4 collective-permute-start.24
  117.0 1.7 %collective-permute-start.25 = (bf16[128,1024]{1,0:T(8,128)(2,1)S(1)}, bf16[128,1024]{1,0:T(8,128)(2,1)S(1)}, u32[]{:S(2)}, u32[]{:S(2)}) collective-permute-start(bf16[128,1024]{1,0:T(8,128)(2,1)S(1)} %get-tuple-element.136), channel_id=1, source_target_pairs={{0,1},{1,0},{2,3},{3,2},{4,5},{5,4},{6,7},{7,6},{8,9},{9,8},{10,11... | collective-permute-start | bytes 786440 | tf_op jit(solution)/shard_map/ppermute | solution.py:470
  118.8 3.2 %collective-permute-done.18.refs_1_ = bf16[128,1024]{1,0:T(8,128)(2,1)S(1)} collective-permute-done((bf16[128,1024]{1,0:T(8,128)(2,1)S(1)}, bf16[128,1024]{1,0:T(8,128)(2,1)S(1)}, u32[]{:S(2)}, u32[]{:S(2)}) %collective-permute-start.18) | collective-permute-done | bytes 262176 | tf_op jit(solution)/shard_map/ppermute | solution.py:470
  121.9 2.1 %collective-permute-done.20.refs_3_ = bf16[128,1024]{1,0:T(8,128)(2,1)S(1)} collective-permute-done((bf16[128,1024]{1,0:T(8,128)(2,1)S(1)}, bf16[128,1024]{1,0:T(8,128)(2,1)S(1)}, u32[]{:S(2)}, u32[]{:S(2)}) %collective-permute-start.20) | collective-permute-done | bytes 262176 | tf_op jit(solution)/shard_map/ppermute | solution.py:470
  124.0 0.5 collective-permute-start.29
  124.7 2.3 %collective-permute-start.28 = (bf16[128,1024]{1,0:T(8,128)(2,1)S(1)}, bf16[128,1024]{1,0:T(8,128)(2,1)S(1)}, u32[]{:S(2)}, u32[]{:S(2)}) collective-permute-start(bf16[128,1024]{1,0:T(8,128)(2,1)S(1)} %get-tuple-element.123), channel_id=1, source_target_pairs={{0,6},{1,7},{2,4},{3,5},{4,10},{5,11},{6,8},{7,9},{8,14},{9,15},{1... | collective-permute-start | bytes 786440 | tf_op jit(solution)/shard_map/ppermute | solution.py:480
  127.0 0.6 collective-permute-start.30
  127.6 1.1 items_1_0.1
  128.7 3.3 %collective-permute-start.26 = (bf16[2176,128]{1,0:T(8,128)(2,1)S(1)}, bf16[2176,128]{1,0:T(8,128)(2,1)S(1)}, u32[]{:S(2)}, u32[]{:S(2)}) collective-permute-start(bf16[2176,128]{1,0:T(8,128)(2,1)S(1)} %get-tuple-element.137), channel_id=1, source_target_pairs={{0,4},{1,5},{2,6},{3,7},{4,8},{5,9},{6,10},{7,11},{8,12},{9,13},{1... | collective-permute-start | bytes 1671176 | tf_op jit(solution)/shard_map/ppermute | solution.py:480
  132.0 5.3 %users_1.1 = f32[2048,128]{1,0:T(8,128)} custom-call(s32[1,2]{1,0:T(1,128)S(1)} %bitcast.7, f32[2048,128]{1,0:T(8,128)S(1)} %get-tuple-element.77.users, f32[128,2048]{1,0:T(8,128)S(1)} %get-tuple-element.125.grad, bf16[128,2048]{1,0:T(8,128)(2,1)S(1)} %collective-permute-done.13.refs_8_.refs_0_.items, ...), custom_call_target="tpu_custom_call" | custom-call | flops 10000000000 | bytes 65536 | tf_op jit(solution)/shard_map/users_1/pallas_call | solution.py:358
  137.3 1.6 %collective-permute-done.30.refs_6_ = bf16[128,1024]{1,0:T(8,128)(2,1)S(1)} collective-permute-done((bf16[128,1024]{1,0:T(8,128)(2,1)S(1)}, bf16[128,1024]{1,0:T(8,128)(2,1)S(1)}, u32[]{:S(2)}, u32[]{:S(2)}) %collective-permute-start.30) | collective-permute-done | bytes 262176 | tf_op jit(solution)/shard_map/ppermute | solution.py:480
  138.9 5.5 %collective-permute-done.26.refs_0_ = bf16[2176,128]{1,0:T(8,128)(2,1)S(1)} collective-permute-done((bf16[2176,128]{1,0:T(8,128)(2,1)S(1)}, bf16[2176,128]{1,0:T(8,128)(2,1)S(1)}, u32[]{:S(2)}, u32[]{:S(2)}) %collective-permute-start.26) | collective-permute-done | bytes 557088 | tf_op jit(solution)/shard_map/ppermute | solution.py:480
  144.4 1.7 %items_final.1 = f32[4096,128]{1,0:T(8,128)} custom-call(bf16[2176,128]{1,0:T(8,128)(2,1)S(1)} %collective-permute-done.26.refs_0_, bf16[128,2048]{1,0:T(8,128)(2,1)S(1)} %collective-permute-done.22.refs_1_, bf16[128,2048]{1,0:T(8,128)(2,1)S(1)} %collective-permute-done.19.refs_2_, bf16[128,1024]{1,0:T(8,128)(2,1)S(1)} %collective-permute-done.27.refs_3_, ...), custom_call_target="tpu_custom_call" | custom-call | flops 1200000000 | bytes 65536 | tf_op jit(solution)/shard_map/items_final/pallas_call | solution.py:579
  (38 shorter events, 1.0 us)
Async XLA Ops:
  10.3 38.6 %collective-permute-start.4 = (bf16[128,2176]{1,0:T(8,128)(2,1)S(1)}, bf16[128,2176]{1,0:T(8,128)(2,1)S(1)}, u32[]{:S(2)}, u32[]{:S(2)}) collective-permute-start(bf16[128,2176]{1,0:T(8,128)(2,1)S(1)} %get-tuple-element.95.refs_4_.refs_6_), channel_id=1, source_target_pairs={{0,1},{1,0},{2,3},{3,2},{4,5},{5,4},{6,7},{7,6},{8,9},{9,8},{10,11... | collective-permute-start | bytes 1671176 | tf_op jit(solution)/shard_map/ppermute | solution.py:470
  20.4 16.6 %collective-permute-start = (bf16[128,2048]{1,0:T(8,128)(2,1)S(1)}, bf16[128,2048]{1,0:T(8,128)(2,1)S(1)}, u32[]{:S(2)}, u32[]{:S(2)}) collective-permute-start(bf16[128,2048]{1,0:T(8,128)(2,1)S(1)} %get-tuple-element.82), channel_id=1, source_target_pairs={{0,1},{1,0},{2,3},{3,2},{4,5},{5,4},{6,7},{7,6},{8,9},{9,8},{10,11... | collective-permute-start | bytes 1572872 | tf_op jit(solution)/shard_map/ppermute | solution.py:470
  22.8 14.9 %collective-permute-start.1 = (bf16[128,2048]{1,0:T(8,128)(2,1)S(1)}, bf16[128,2048]{1,0:T(8,128)(2,1)S(1)}, u32[]{:S(2)}, u32[]{:S(2)}) collective-permute-start(bf16[128,2048]{1,0:T(8,128)(2,1)S(1)} %get-tuple-element.85), channel_id=1, source_target_pairs={{0,2},{1,3},{2,0},{3,1},{4,6},{5,7},{6,4},{7,5},{8,10},{9,11},{10,... | collective-permute-start | bytes 1572872 | tf_op jit(solution)/shard_map/ppermute | solution.py:470
  22.8 26.1 %collective-permute-start.5 = (bf16[128,2048]{1,0:T(8,128)(2,1)S(1)}, bf16[128,2048]{1,0:T(8,128)(2,1)S(1)}, u32[]{:S(2)}, u32[]{:S(2)}) collective-permute-start(bf16[128,2048]{1,0:T(8,128)(2,1)S(1)} %get-tuple-element.98), channel_id=1, source_target_pairs={{0,2},{1,3},{2,0},{3,1},{4,6},{5,7},{6,4},{7,5},{8,10},{9,11},{10,... | collective-permute-start | bytes 1572872 | tf_op jit(solution)/shard_map/ppermute | solution.py:470
  37.8 12.7 %copy-start = (f32[2048,128]{1,0:T(8,128)S(1)}, f32[2048,128]{1,0:T(8,128)}, u32[]{:S(2)}) copy-start(f32[2048,128]{1,0:T(8,128)} %users.1) | copy-start | bytes 3145732
  37.8 12.7 %copy-start.1 = (s32[2,1]{0,1:T(1,128)S(1)}, s32[2,1]{0,1:T(1,128)}, u32[]{:S(2)}) copy-start(s32[2,1]{0,1:T(1,128)} %param.13) | copy-start | bytes 28
  37.8 22.9 %collective-permute-start.2 = (bf16[128,1024]{1,0:T(8,128)(2,1)S(1)}, bf16[128,1024]{1,0:T(8,128)(2,1)S(1)}, u32[]{:S(2)}, u32[]{:S(2)}) collective-permute-start(bf16[128,1024]{1,0:T(8,128)(2,1)S(1)} %get-tuple-element.87), channel_id=1, source_target_pairs={{0,2},{1,3},{2,0},{3,1},{4,6},{5,7},{6,4},{7,5},{8,10},{9,11},{10,... | collective-permute-start | bytes 786440 | tf_op jit(solution)/shard_map/ppermute | solution.py:470
  38.8 21.8 %collective-permute-start.3 = (bf16[128,1024]{1,0:T(8,128)(2,1)S(1)}, bf16[128,1024]{1,0:T(8,128)(2,1)S(1)}, u32[]{:S(2)}, u32[]{:S(2)}) collective-permute-start(bf16[128,1024]{1,0:T(8,128)(2,1)S(1)} %get-tuple-element.88), channel_id=1, source_target_pairs={{0,1},{1,0},{2,3},{3,2},{4,5},{5,4},{6,7},{7,6},{8,9},{9,8},{10,11... | collective-permute-start | bytes 786440 | tf_op jit(solution)/shard_map/ppermute | solution.py:470
  49.0 8.3 %collective-permute-start.6 = (bf16[128,1152]{1,0:T(8,128)(2,1)S(1)}, bf16[128,1152]{1,0:T(8,128)(2,1)S(1)}, u32[]{:S(2)}, u32[]{:S(2)}) collective-permute-start(bf16[128,1152]{1,0:T(8,128)(2,1)S(1)} %get-tuple-element.100), channel_id=1, source_target_pairs={{0,2},{1,3},{2,0},{3,1},{4,6},{5,7},{6,4},{7,5},{8,10},{9,11},{10,... | collective-permute-start | bytes 884744 | tf_op jit(solution)/shard_map/ppermute | solution.py:470
  49.1 6.4 %collective-permute-start.7 = (bf16[128,1024]{1,0:T(8,128)(2,1)S(1)}, bf16[128,1024]{1,0:T(8,128)(2,1)S(1)}, u32[]{:S(2)}, u32[]{:S(2)}) collective-permute-start(bf16[128,1024]{1,0:T(8,128)(2,1)S(1)} %get-tuple-element.101), channel_id=1, source_target_pairs={{0,1},{1,0},{2,3},{3,2},{4,5},{5,4},{6,7},{7,6},{8,9},{9,8},{10,11... | collective-permute-start | bytes 786440 | tf_op jit(solution)/shard_map/ppermute | solution.py:470
  57.9 12.4 %collective-permute-start.14 = (bf16[128,2048]{1,0:T(8,128)(2,1)S(1)}, bf16[128,2048]{1,0:T(8,128)(2,1)S(1)}, u32[]{:S(2)}, u32[]{:S(2)}) collective-permute-start(bf16[128,2048]{1,0:T(8,128)(2,1)S(1)} %get-tuple-element.107), channel_id=1, source_target_pairs={{0,5},{1,4},{2,7},{3,6},{4,9},{5,8},{6,11},{7,10},{8,13},{9,12},{1... | collective-permute-start | bytes 1572872 | tf_op jit(solution)/shard_map/ppermute | solution.py:480
  58.0 18.7 %collective-permute-start.15 = (bf16[128,2048]{1,0:T(8,128)(2,1)S(1)}, bf16[128,2048]{1,0:T(8,128)(2,1)S(1)}, u32[]{:S(2)}, u32[]{:S(2)}) collective-permute-start(bf16[128,2048]{1,0:T(8,128)(2,1)S(1)} %get-tuple-element.107), channel_id=1, source_target_pairs={{0,6},{1,7},{2,4},{3,5},{4,10},{5,11},{6,8},{7,9},{8,14},{9,15},{1... | collective-permute-start | bytes 1572872 | tf_op jit(solution)/shard_map/ppermute | solution.py:480
  61.2 21.9 %collective-permute-start.9 = (bf16[128,2048]{1,0:T(8,128)(2,1)S(1)}, bf16[128,2048]{1,0:T(8,128)(2,1)S(1)}, u32[]{:S(2)}, u32[]{:S(2)}) collective-permute-start(bf16[128,2048]{1,0:T(8,128)(2,1)S(1)} %items_0_1.1), channel_id=1, source_target_pairs={{0,5},{1,4},{2,7},{3,6},{4,9},{5,8},{6,11},{7,10},{8,13},{9,12},{1... | collective-permute-start | bytes 1572872 | tf_op jit(solution)/shard_map/ppermute | solution.py:480
  61.4 26.7 %collective-permute-start.10 = (bf16[128,2048]{1,0:T(8,128)(2,1)S(1)}, bf16[128,2048]{1,0:T(8,128)(2,1)S(1)}, u32[]{:S(2)}, u32[]{:S(2)}) collective-permute-start(bf16[128,2048]{1,0:T(8,128)(2,1)S(1)} %items_0_1.1), channel_id=1, source_target_pairs={{0,6},{1,7},{2,4},{3,5},{4,10},{5,11},{6,8},{7,9},{8,14},{9,15},{1... | collective-permute-start | bytes 1572872 | tf_op jit(solution)/shard_map/ppermute | solution.py:480
  66.3 26.2 %collective-permute-start.13 = (bf16[128,2048]{1,0:T(8,128)(2,1)S(1)}, bf16[128,2048]{1,0:T(8,128)(2,1)S(1)}, u32[]{:S(2)}, u32[]{:S(2)}) collective-permute-start(bf16[128,2048]{1,0:T(8,128)(2,1)S(1)} %get-tuple-element.107), channel_id=1, source_target_pairs={{0,4},{1,5},{2,6},{3,7},{4,8},{5,9},{6,10},{7,11},{8,12},{9,13},{1... | collective-permute-start | bytes 1572872 | tf_op jit(solution)/shard_map/ppermute | solution.py:480
  70.3 22.5 %collective-permute-start.16 = (bf16[128,1024]{1,0:T(8,128)(2,1)S(1)}, bf16[128,1024]{1,0:T(8,128)(2,1)S(1)}, u32[]{:S(2)}, u32[]{:S(2)}) collective-permute-start(bf16[128,1024]{1,0:T(8,128)(2,1)S(1)} %slice.18), channel_id=1, source_target_pairs={{0,2},{1,3},{2,0},{3,1},{4,6},{5,7},{6,4},{7,5},{8,10},{9,11},{10,... | collective-permute-start | bytes 786440 | tf_op jit(solution)/shard_map/ppermute | solution.py:470
  76.7 18.2 %collective-permute-start.17 = (bf16[128,1024]{1,0:T(8,128)(2,1)S(1)}, bf16[128,1024]{1,0:T(8,128)(2,1)S(1)}, u32[]{:S(2)}, u32[]{:S(2)}) collective-permute-start(bf16[128,1024]{1,0:T(8,128)(2,1)S(1)} %slice.19), channel_id=1, source_target_pairs={{0,1},{1,0},{2,3},{3,2},{4,5},{5,4},{6,7},{7,6},{8,9},{9,8},{10,11... | collective-permute-start | bytes 786440 | tf_op jit(solution)/shard_map/ppermute | solution.py:470
  83.2 19.1 %collective-permute-start.8 = (bf16[128,2048]{1,0:T(8,128)(2,1)S(1)}, bf16[128,2048]{1,0:T(8,128)(2,1)S(1)}, u32[]{:S(2)}, u32[]{:S(2)}) collective-permute-start(bf16[128,2048]{1,0:T(8,128)(2,1)S(1)} %items_0_1.1), channel_id=1, source_target_pairs={{0,4},{1,5},{2,6},{3,7},{4,8},{5,9},{6,10},{7,11},{8,12},{9,13},{1... | collective-permute-start | bytes 1572872 | tf_op jit(solution)/shard_map/ppermute | solution.py:480
  88.0 16.3 %collective-permute-start.11 = (bf16[128,1024]{1,0:T(8,128)(2,1)S(1)}, bf16[128,1024]{1,0:T(8,128)(2,1)S(1)}, u32[]{:S(2)}, u32[]{:S(2)}) collective-permute-start(bf16[128,1024]{1,0:T(8,128)(2,1)S(1)} %slice.16), channel_id=1, source_target_pairs={{0,2},{1,3},{2,0},{3,1},{4,6},{5,7},{6,4},{7,5},{8,10},{9,11},{10,... | collective-permute-start | bytes 786440 | tf_op jit(solution)/shard_map/ppermute | solution.py:470
  92.5 11.9 %collective-permute-start.12 = (bf16[128,1024]{1,0:T(8,128)(2,1)S(1)}, bf16[128,1024]{1,0:T(8,128)(2,1)S(1)}, u32[]{:S(2)}, u32[]{:S(2)}) collective-permute-start(bf16[128,1024]{1,0:T(8,128)(2,1)S(1)} %slice.17), channel_id=1, source_target_pairs={{0,1},{1,0},{2,3},{3,2},{4,5},{5,4},{6,7},{7,6},{8,9},{9,8},{10,11... | collective-permute-start | bytes 786440 | tf_op jit(solution)/shard_map/ppermute | solution.py:470
  92.9 23.6 %collective-permute-start.22 = (bf16[128,2048]{1,0:T(8,128)(2,1)S(1)}, bf16[128,2048]{1,0:T(8,128)(2,1)S(1)}, u32[]{:S(2)}, u32[]{:S(2)}) collective-permute-start(bf16[128,2048]{1,0:T(8,128)(2,1)S(1)} %items_0_1.1), channel_id=1, source_target_pairs={{0,8},{1,9},{2,10},{3,11},{4,12},{5,13},{6,14},{7,15},{8,16},{9,17... | collective-permute-start | bytes 1572872 | tf_op jit(solution)/shard_map/ppermute | solution.py:480
  102.2 14.3 %collective-permute-start.21 = (bf16[128,2176]{1,0:T(8,128)(2,1)S(1)}, bf16[128,2176]{1,0:T(8,128)(2,1)S(1)}, u32[]{:S(2)}, u32[]{:S(2)}) collective-permute-start(bf16[128,2176]{1,0:T(8,128)(2,1)S(1)} %get-tuple-element.127.refs_4_.refs_6_), channel_id=1, source_target_pairs={{0,1},{1,0},{2,3},{3,2},{4,5},{5,4},{6,7},{7,6},{8,9},{9,8},{10,11... | collective-permute-start | bytes 1671176 | tf_op jit(solution)/shard_map/ppermute | solution.py:470
  102.2 12.6 %collective-permute-start.23 = (bf16[128,2048]{1,0:T(8,128)(2,1)S(1)}, bf16[128,2048]{1,0:T(8,128)(2,1)S(1)}, u32[]{:S(2)}, u32[]{:S(2)}) collective-permute-start(bf16[128,2048]{1,0:T(8,128)(2,1)S(1)} %get-tuple-element.132), channel_id=1, source_target_pairs={{0,2},{1,3},{2,0},{3,1},{4,6},{5,7},{6,4},{7,5},{8,10},{9,11},{10,... | collective-permute-start | bytes 1572872 | tf_op jit(solution)/shard_map/ppermute | solution.py:470
  112.7 11.9 %collective-permute-start.19 = (bf16[128,2048]{1,0:T(8,128)(2,1)S(1)}, bf16[128,2048]{1,0:T(8,128)(2,1)S(1)}, u32[]{:S(2)}, u32[]{:S(2)}) collective-permute-start(bf16[128,2048]{1,0:T(8,128)(2,1)S(1)} %get-tuple-element.117), channel_id=1, source_target_pairs={{0,4},{1,5},{2,6},{3,7},{4,8},{5,9},{6,10},{7,11},{8,12},{9,13},{1... | collective-permute-start | bytes 1572872 | tf_op jit(solution)/shard_map/ppermute | solution.py:480
  112.7 9.2 %collective-permute-start.18 = (bf16[128,1024]{1,0:T(8,128)(2,1)S(1)}, bf16[128,1024]{1,0:T(8,128)(2,1)S(1)}, u32[]{:S(2)}, u32[]{:S(2)}) collective-permute-start(bf16[128,1024]{1,0:T(8,128)(2,1)S(1)} %get-tuple-element.115), channel_id=1, source_target_pairs={{0,1},{1,0},{2,3},{3,2},{4,5},{5,4},{6,7},{7,6},{8,9},{9,8},{10,11... | collective-permute-start | bytes 786440 | tf_op jit(solution)/shard_map/ppermute | solution.py:470
  114.8 9.2 %collective-permute-start.20 = (bf16[128,1024]{1,0:T(8,128)(2,1)S(1)}, bf16[128,1024]{1,0:T(8,128)(2,1)S(1)}, u32[]{:S(2)}, u32[]{:S(2)}) collective-permute-start(bf16[128,1024]{1,0:T(8,128)(2,1)S(1)} %get-tuple-element.120), channel_id=1, source_target_pairs={{0,2},{1,3},{2,0},{3,1},{4,6},{5,7},{6,4},{7,5},{8,10},{9,11},{10,... | collective-permute-start | bytes 786440 | tf_op jit(solution)/shard_map/ppermute | solution.py:470
  116.6 11.0 %collective-permute-start.24 = (bf16[128,1152]{1,0:T(8,128)(2,1)S(1)}, bf16[128,1152]{1,0:T(8,128)(2,1)S(1)}, u32[]{:S(2)}, u32[]{:S(2)}) collective-permute-start(bf16[128,1152]{1,0:T(8,128)(2,1)S(1)} %get-tuple-element.135), channel_id=1, source_target_pairs={{0,2},{1,3},{2,0},{3,1},{4,6},{5,7},{6,4},{7,5},{8,10},{9,11},{10,... | collective-permute-start | bytes 884744 | tf_op jit(solution)/shard_map/ppermute | solution.py:470
  117.0 9.9 %collective-permute-start.25 = (bf16[128,1024]{1,0:T(8,128)(2,1)S(1)}, bf16[128,1024]{1,0:T(8,128)(2,1)S(1)}, u32[]{:S(2)}, u32[]{:S(2)}) collective-permute-start(bf16[128,1024]{1,0:T(8,128)(2,1)S(1)} %get-tuple-element.136), channel_id=1, source_target_pairs={{0,1},{1,0},{2,3},{3,2},{4,5},{5,4},{6,7},{7,6},{8,9},{9,8},{10,11... | collective-permute-start | bytes 786440 | tf_op jit(solution)/shard_map/ppermute | solution.py:470
  121.9 15.4 %collective-permute-start.27 = (bf16[128,1024]{1,0:T(8,128)(2,1)S(1)}, bf16[128,1024]{1,0:T(8,128)(2,1)S(1)}, u32[]{:S(2)}, u32[]{:S(2)}) collective-permute-start(bf16[128,1024]{1,0:T(8,128)(2,1)S(1)} %get-tuple-element.138), channel_id=1, source_target_pairs={{0,5},{1,4},{2,7},{3,6},{4,9},{5,8},{6,11},{7,10},{8,13},{9,12},{1... | collective-permute-start | bytes 786440 | tf_op jit(solution)/shard_map/ppermute | solution.py:480
  124.0 13.2 %collective-permute-start.29 = (bf16[128,1024]{1,0:T(8,128)(2,1)S(1)}, bf16[128,1024]{1,0:T(8,128)(2,1)S(1)}, u32[]{:S(2)}, u32[]{:S(2)}) collective-permute-start(bf16[128,1024]{1,0:T(8,128)(2,1)S(1)} %get-tuple-element.139), channel_id=1, source_target_pairs={{0,6},{1,7},{2,4},{3,5},{4,10},{5,11},{6,8},{7,9},{8,14},{9,15},{1... | collective-permute-start | bytes 786440 | tf_op jit(solution)/shard_map/ppermute | solution.py:480
  124.7 12.6 %collective-permute-start.28 = (bf16[128,1024]{1,0:T(8,128)(2,1)S(1)}, bf16[128,1024]{1,0:T(8,128)(2,1)S(1)}, u32[]{:S(2)}, u32[]{:S(2)}) collective-permute-start(bf16[128,1024]{1,0:T(8,128)(2,1)S(1)} %get-tuple-element.123), channel_id=1, source_target_pairs={{0,6},{1,7},{2,4},{3,5},{4,10},{5,11},{6,8},{7,9},{8,14},{9,15},{1... | collective-permute-start | bytes 786440 | tf_op jit(solution)/shard_map/ppermute | solution.py:480
  127.0 5.0 %copy-start.2 = (s32[2,1]{0,1:T(1,128)S(1)}, s32[2,1]{0,1:T(1,128)}, u32[]{:S(2)}) copy-start(s32[2,1]{0,1:T(1,128)} %param.13) | copy-start | bytes 28
  127.0 12.0 %collective-permute-start.30 = (bf16[128,1024]{1,0:T(8,128)(2,1)S(1)}, bf16[128,1024]{1,0:T(8,128)(2,1)S(1)}, u32[]{:S(2)}, u32[]{:S(2)}) collective-permute-start(bf16[128,1024]{1,0:T(8,128)(2,1)S(1)} %get-tuple-element.124), channel_id=1, source_target_pairs={{0,5},{1,4},{2,7},{3,6},{4,9},{5,8},{6,11},{7,10},{8,13},{9,12},{1... | collective-permute-start | bytes 786440 | tf_op jit(solution)/shard_map/ppermute | solution.py:480
  128.7 15.7 %collective-permute-start.26 = (bf16[2176,128]{1,0:T(8,128)(2,1)S(1)}, bf16[2176,128]{1,0:T(8,128)(2,1)S(1)}, u32[]{:S(2)}, u32[]{:S(2)}) collective-permute-start(bf16[2176,128]{1,0:T(8,128)(2,1)S(1)} %get-tuple-element.137), channel_id=1, source_target_pairs={{0,4},{1,5},{2,6},{3,7},{4,8},{5,9},{6,10},{7,11},{8,12},{9,13},{1... | collective-permute-start | bytes 1671176 | tf_op jit(solution)/shard_map/ppermute | solution.py:480

commit v10 on v8

--- a/solution.py
+++ b/solution.py
@@ -678,9 +678,8 @@
             if last:
                 if c == 0:
                     ahead = exchanged(outs[1], members)
-                    arrived = [tied(array, kept) for array in arrived]
                 else:
-                    arrived = [tied(array, grad_user) for array in ahead]
+                    arrived = [tied(array, grad_user, kept) for array in ahead]
             reduce = scattered_direct if last and c + 1 == CHUNKS else scattered
             reduced.append(
                 reduce(epoch, c, outs[c], arrived, members, (rows // 2, rows - rows // 2))

time: 134 us -> 134 us (level)
  starting transfers between devices: 26.4 us -> 35.8 us
  Pallas kernels: 49 us -> 40.6 us
    pallas_call x4, Pallas kernels: 34.5 us -> 26 us  [tile_call(): pl.pallas_call(functools.partial(tile_kernel, epoch, chunk, direct, membe...]
    ppermute x13, waiting for transfers between devices: 37.2 us -> 30.9 us  [moved(): return lax.ppermute(value, ('blk', 'grp'), pairs)]
    ppermute x18, starting transfers between devices: 15.9 us -> 22.1 us  [swapped(): return lax.ppermute(value, 'grp', [(i, i ^ bit) for i in range(length)])]
    ppermute x18, waiting for transfers between devices: 20.1 us -> 25.5 us  [swapped(): return lax.ppermute(value, 'grp', [(i, i ^ bit) for i in range(length)])]
    ppermute x13, starting transfers between devices: 10.5 us -> 13.7 us  [moved(): return lax.ppermute(value, ('blk', 'grp'), pairs)]
  transfers between devices with their start and end apart: 31 -> 31, of which waited for: 17 -> 17; matrix products, arithmetic and copies ran while one was open for 0% -> 0% of each run, Pallas kernels for 27% -> 24%
where the time goes in v10:
time: 134 us
  waiting for transfers between devices  56.4 us (42%)
  Pallas kernels  40.6 us (30%)
  starting transfers between devices  35.8 us (27%)
    ppermute x13, waiting for transfers between devices, moved(): return lax.ppermute(value, ('blk', 'grp'), pairs)  30.9 us
    pallas_call x4, Pallas kernels, tile_call(): pl.pallas_call(functools.partial(tile_kernel, epoch, chunk, direct, membe...  26 us
    ppermute x18, waiting for transfers between devices, swapped(): return lax.ppermute(value, 'grp', [(i, i ^ bit) for i in range(length)])  25.5 us
    ppermute x18, starting transfers between devices, swapped(): return lax.ppermute(value, 'grp', [(i, i ^ bit) for i in range(length)])  22.1 us
    ppermute x13, starting transfers between devices, moved(): return lax.ppermute(value, ('blk', 'grp'), pairs)  13.7 us
    pallas_call x2, Pallas kernels, user_call(): pl.pallas_call(functools.partial(user_kernel, epoch, block_rows), out_sha...  10.1 us
  transfers between devices with their start and end apart: 31, of which 17 were waited for; matrix products, arithmetic and copies ran while one was open for 0% of the time, Pallas kernels for 24%

profile of v10, /device:TPU:0, one launch (start us, length us, event | category | flops | bytes accessed | tf_op | source)
XLA Modules:
  0.0 133.8 jit_solution(2771544252927477091)
XLA Ops:
  0.6 6.5 %tiles_0_0.1 = (bf16[128,2176]{1,0:T(8,128)(2,1)S(1)}, bf16[128,2048]{1,0:T(8,128)(2,1)S(1)}, bf16[128,2048]{1,0:T(8,128)(2,1)S(1)}, bf16[128,2048]{1,0:T(8,128)...) custom-call(s32[2,1,1,64]{3,2,1,0:T(1,128)} %refs_0_.7, ...), custom_call_target="tpu_custom_call" | custom-call | flops 16000000000 | bytes 65536 | tf_op jit(solution)/shard_map/tiles_0_0/pallas_call | solution.py:319
  7.1 5.1 %collective-permute-start.4 = (bf16[128,2176]{1,0:T(8,128)(2,1)S(1)}, bf16[128,2176]{1,0:T(8,128)(2,1)S(1)}, u32[]{:S(2)}, u32[]{:S(2)}) collective-permute-start(bf16[128,2176]{1,0:T(8,128)(2,1)S(1)} %get-tuple-element.93.refs_4_.refs_6_), channel_id=1, source_target_pairs={{0,1},{1,0},{2,3},{3,2},{4,5},{5,4},{6,7},{7,6},{8,9},{9,8},{10,11... | collective-permute-start | bytes 1671176 | tf_op jit(solution)/shard_map/ppermute | solution.py:470
  12.2 2.6 %collective-permute-start.5 = (bf16[128,2048]{1,0:T(8,128)(2,1)S(1)}, bf16[128,2048]{1,0:T(8,128)(2,1)S(1)}, u32[]{:S(2)}, u32[]{:S(2)}) collective-permute-start(bf16[128,2048]{1,0:T(8,128)(2,1)S(1)} %get-tuple-element.96), channel_id=1, source_target_pairs={{0,2},{1,3},{2,0},{3,1},{4,6},{5,7},{6,4},{7,5},{8,10},{9,11},{10,... | collective-permute-start | bytes 1572872 | tf_op jit(solution)/shard_map/ppermute | solution.py:470
  14.8 7.2 %tiles_0_1.1 = (bf16[128,2048]{1,0:T(8,128)(2,1)S(1)}, bf16[128,2048]{1,0:T(8,128)(2,1)S(1)}, bf16[128,2048]{1,0:T(8,128)(2,1)S(1)}, bf16[128,2048]{1,0:T(8,128)...) custom-call(s32[2,1,1,64]{3,2,1,0:T(1,128)} %refs_0_.7, ...), custom_call_target="tpu_custom_call" | custom-call | flops 16000000000 | bytes 65536 | tf_op jit(solution)/shard_map/tiles_0_1/pallas_call | solution.py:319
  22.1 1.7 %collective-permute-start.1 = (bf16[128,2048]{1,0:T(8,128)(2,1)S(1)}, bf16[128,2048]{1,0:T(8,128)(2,1)S(1)}, u32[]{:S(2)}, u32[]{:S(2)}) collective-permute-start(bf16[128,2048]{1,0:T(8,128)(2,1)S(1)} %get-tuple-element.83), channel_id=1, source_target_pairs={{0,2},{1,3},{2,0},{3,1},{4,6},{5,7},{6,4},{7,5},{8,10},{9,11},{10,... | collective-permute-start | bytes 1572872 | tf_op jit(solution)/shard_map/ppermute | solution.py:470
  23.8 3.6 %collective-permute-done.5.refs_3_.refs_4_ = bf16[128,2048]{1,0:T(8,128)(2,1)S(1)} collective-permute-done((bf16[128,2048]{1,0:T(8,128)(2,1)S(1)}, bf16[128,2048]{1,0:T(8,128)(2,1)S(1)}, u32[]{:S(2)}, u32[]{:S(2)}) %collective-permute-start.5) | collective-permute-done | bytes 524320 | tf_op jit(solution)/shard_map/ppermute | solution.py:470
  27.7 0.7 collective-permute-start.7
  28.4 4.8 %users_0.1 = (f32[2048,128]{1,0:T(8,128)S(1)}, bf16[2048,128]{1,0:T(8,128)(2,1)S(1)}, bf16[128,2048]{1,0:T(8,128)(2,1)S(1)}, bf16[128,128]{1,0:T(8,128)(2,1)S(1)}) custom-call(s32[1,2]{1,0:T(1,128)S(1)} %bitcast.6, f32[2048,128]{1,0:T(8,128)S(1)} %copy-done, f32[128,2048]{1,0:T(8,128)S(1)} %get-tuple-element.72.grad, ...), custom_call_target="tpu_custom_call" | custom-call | flops 10000000000 | bytes 65536 | tf_op jit(solution)/shard_map/users_0/pallas_call | solution.py:358
  33.1 3.8 %collective-permute-done.refs_1_ = bf16[128,2048]{1,0:T(8,128)(2,1)S(1)} collective-permute-done((bf16[128,2048]{1,0:T(8,128)(2,1)S(1)}, bf16[128,2048]{1,0:T(8,128)(2,1)S(1)}, u32[]{:S(2)}, u32[]{:S(2)}) %collective-permute-start) | collective-permute-done | bytes 524320 | tf_op jit(solution)/shard_map/ppermute | solution.py:470
  36.9 1.8 %collective-permute-done.1.refs_3_.refs_4_ = bf16[128,2048]{1,0:T(8,128)(2,1)S(1)} collective-permute-done((bf16[128,2048]{1,0:T(8,128)(2,1)S(1)}, bf16[128,2048]{1,0:T(8,128)(2,1)S(1)}, u32[]{:S(2)}, u32[]{:S(2)}) %collective-permute-start.1) | collective-permute-done | bytes 524320 | tf_op jit(solution)/shard_map/ppermute | solution.py:470
  38.9 0.1 collective-permute-start.3
  39.0 3.5 %collective-permute-done.7.refs_5_ = bf16[128,1024]{1,0:T(8,128)(2,1)S(1)} collective-permute-done((bf16[128,1024]{1,0:T(8,128)(2,1)S(1)}, bf16[128,1024]{1,0:T(8,128)(2,1)S(1)}, u32[]{:S(2)}, u32[]{:S(2)}) %collective-permute-start.7) | collective-permute-done | bytes 262176 | tf_op jit(solution)/shard_map/ppermute | solution.py:470
  42.5 2.5 %collective-permute-done.6.refs_2_.refs_8_ = bf16[128,1152]{1,0:T(8,128)(2,1)S(1)} collective-permute-done((bf16[128,1152]{1,0:T(8,128)(2,1)S(1)}, bf16[128,1152]{1,0:T(8,128)(2,1)S(1)}, u32[]{:S(2)}, u32[]{:S(2)}) %collective-permute-start.6) | collective-permute-done | bytes 294944 | tf_op jit(solution)/shard_map/ppermute | solution.py:470
  45.0 0.6 items_0_0.1
  45.7 3.7 %collective-permute-start.15 = (bf16[128,2048]{1,0:T(8,128)(2,1)S(1)}, bf16[128,2048]{1,0:T(8,128)(2,1)S(1)}, u32[]{:S(2)}, u32[]{:S(2)}) collective-permute-start(bf16[128,2048]{1,0:T(8,128)(2,1)S(1)} %get-tuple-element.105), channel_id=1, source_target_pairs={{0,6},{1,7},{2,4},{3,5},{4,10},{5,11},{6,8},{7,9},{8,14},{9,15},{1... | collective-permute-start | bytes 1572872 | tf_op jit(solution)/shard_map/ppermute | solution.py:480
  49.3 1.0 collective-permute-done.2.refs_2_
  50.3 0.6 items_0_1.1
  50.9 0.1 collective-permute-start.9
  51.1 2.7 %collective-permute-start.10 = (bf16[128,2048]{1,0:T(8,128)(2,1)S(1)}, bf16[128,2048]{1,0:T(8,128)(2,1)S(1)}, u32[]{:S(2)}, u32[]{:S(2)}) collective-permute-start(bf16[128,2048]{1,0:T(8,128)(2,1)S(1)} %items_0_1.1), channel_id=1, source_target_pairs={{0,6},{1,7},{2,4},{3,5},{4,10},{5,11},{6,8},{7,9},{8,14},{9,15},{1... | collective-permute-start | bytes 1572872 | tf_op jit(solution)/shard_map/ppermute | solution.py:480
  53.8 5.2 %collective-permute-done.14.refs_9_.refs_1_ = bf16[128,2048]{1,0:T(8,128)(2,1)S(1)} collective-permute-done((bf16[128,2048]{1,0:T(8,128)(2,1)S(1)}, bf16[128,2048]{1,0:T(8,128)(2,1)S(1)}, u32[]{:S(2)}, u32[]{:S(2)}) %collective-permute-start.14) | collective-permute-done | bytes 524320 | tf_op jit(solution)/shard_map/ppermute | solution.py:480
  58.9 0.8 collective-permute-start.16
  59.8 2.3 %collective-permute-done.15.refs_10_.refs_2_ = bf16[128,2048]{1,0:T(8,128)(2,1)S(1)} collective-permute-done((bf16[128,2048]{1,0:T(8,128)(2,1)S(1)}, bf16[128,2048]{1,0:T(8,128)(2,1)S(1)}, u32[]{:S(2)}, u32[]{:S(2)}) %collective-permute-start.15) | collective-permute-done | bytes 524320 | tf_op jit(solution)/shard_map/ppermute | solution.py:480
  62.1 0.4 collective-permute-start.17
  62.6 10.4 %collective-permute-done.9.refs_9_.refs_6_ = bf16[128,2048]{1,0:T(8,128)(2,1)S(1)} collective-permute-done((bf16[128,2048]{1,0:T(8,128)(2,1)S(1)}, bf16[128,2048]{1,0:T(8,128)(2,1)S(1)}, u32[]{:S(2)}, u32[]{:S(2)}) %collective-permute-start.9) | collective-permute-done | bytes 524320 | tf_op jit(solution)/shard_map/ppermute | solution.py:480
  73.0 0.3 collective-permute-start.8
  73.3 2.4 %collective-permute-done.10.refs_10_.refs_7_ = bf16[128,2048]{1,0:T(8,128)(2,1)S(1)} collective-permute-done((bf16[128,2048]{1,0:T(8,128)(2,1)S(1)}, bf16[128,2048]{1,0:T(8,128)(2,1)S(1)}, u32[]{:S(2)}, u32[]{:S(2)}) %collective-permute-start.10) | collective-permute-done | bytes 524320 | tf_op jit(solution)/shard_map/ppermute | solution.py:480
  75.7 1.5 %collective-permute-start.11 = (bf16[128,1024]{1,0:T(8,128)(2,1)S(1)}, bf16[128,1024]{1,0:T(8,128)(2,1)S(1)}, u32[]{:S(2)}, u32[]{:S(2)}) collective-permute-start(bf16[128,1024]{1,0:T(8,128)(2,1)S(1)} %slice.16), channel_id=1, source_target_pairs={{0,2},{1,3},{2,0},{3,1},{4,6},{5,7},{6,4},{7,5},{8,10},{9,11},{10,... | collective-permute-start | bytes 786440 | tf_op jit(solution)/shard_map/ppermute | solution.py:470
  77.2 1.0 collective-permute-done.13.refs_8_.refs_0_.items
  78.2 2.0 %collective-permute-start.12 = (bf16[128,1024]{1,0:T(8,128)(2,1)S(1)}, bf16[128,1024]{1,0:T(8,128)(2,1)S(1)}, u32[]{:S(2)}, u32[]{:S(2)}) collective-permute-start(bf16[128,1024]{1,0:T(8,128)(2,1)S(1)} %slice.17), channel_id=1, source_target_pairs={{0,1},{1,0},{2,3},{3,2},{4,5},{5,4},{6,7},{7,6},{8,9},{9,8},{10,11... | collective-permute-start | bytes 786440 | tf_op jit(solution)/shard_map/ppermute | solution.py:470
  80.2 0.3 collective-permute-done.16.refs_11_.refs_3_
  80.5 5.6 %tiles_1_0.1 = (bf16[128,2176]{1,0:T(8,128)(2,1)S(1)}, bf16[128,2048]{1,0:T(8,128)(2,1)S(1)}, bf16[128,2048]{1,0:T(8,128)(2,1)S(1)}, bf16[128,2048]{1,0:T(8,128)(2,1)S(1)}, f32[128,2048]{1,0:T(8,128)S(1)}) custom-call(s32[2,1,1,64]{3,2,1,0:T(1,128)} %refs_0_.7, s32[2,1,1,64]{3,2,1,0:T(1,128)} %refs_1_.7, s32[1,2]{1,0:T(1,128)} %bitcast.10, s32[1,2]{1,0:T(1,128)} %bitcast.4, ...), custom_call_target="tpu_custom_call" | custom-call | flops 16000000000 | bytes 65536 | tf_op jit(solution)/shard_map/tiles_1_0/pallas_call | solution.py:319
  86.1 2.3 %collective-permute-start.22 = (bf16[128,2176]{1,0:T(8,128)(2,1)S(1)}, bf16[128,2176]{1,0:T(8,128)(2,1)S(1)}, u32[]{:S(2)}, u32[]{:S(2)}) collective-permute-start(bf16[128,2176]{1,0:T(8,128)(2,1)S(1)} %get-tuple-element.126.refs_4_.refs_6_), channel_id=1, source_target_pairs={{0,1},{1,0},{2,3},{3,2},{4,5},{5,4},{6,7},{7,6},{8,9},{9,8},{10,11... | collective-permute-start | bytes 1671176 | tf_op jit(solution)/shard_map/ppermute | solution.py:470
  88.4 6.8 %tiles_1_1.1 = (bf16[128,1024]{1,0:T(8,128)(2,1)S(1)}, bf16[128,1024]{1,0:T(8,128)(2,1)S(1)}, bf16[128,1024]{1,0:T(8,128)(2,1)S(1)}, bf16[128,1024]{1,0:T(8,128)...) custom-call(s32[2,1,1,64]{3,2,1,0:T(1,128)} %refs_0_.7, ...), custom_call_target="tpu_custom_call" | custom-call | flops 16000000000 | bytes 65536 | tf_op jit(solution)/shard_map/tiles_1_1/pallas_call | solution.py:319
  95.2 1.8 %collective-permute-start.20 = (bf16[128,2048]{1,0:T(8,128)(2,1)S(1)}, bf16[128,2048]{1,0:T(8,128)(2,1)S(1)}, u32[]{:S(2)}, u32[]{:S(2)}) collective-permute-start(bf16[128,2048]{1,0:T(8,128)(2,1)S(1)} %get-tuple-element.116), channel_id=1, source_target_pairs={{0,4},{1,5},{2,6},{3,7},{4,8},{5,9},{6,10},{7,11},{8,12},{9,13},{1... | collective-permute-start | bytes 1572872 | tf_op jit(solution)/shard_map/ppermute | solution.py:480
  97.0 0.9 collective-permute-start.18
  97.9 2.6 %collective-permute-done.23.refs_3_.refs_4_ = bf16[128,2048]{1,0:T(8,128)(2,1)S(1)} collective-permute-done((bf16[128,2048]{1,0:T(8,128)(2,1)S(1)}, bf16[128,2048]{1,0:T(8,128)(2,1)S(1)}, u32[]{:S(2)}, u32[]{:S(2)}) %collective-permute-start.23) | collective-permute-done | bytes 524320 | tf_op jit(solution)/shard_map/ppermute | solution.py:470
  100.6 1.1 collective-permute-start.21
  101.8 1.0 collective-permute-start.24
  102.8 2.8 %collective-permute-done.18.refs_1_ = bf16[128,1024]{1,0:T(8,128)(2,1)S(1)} collective-permute-done((bf16[128,1024]{1,0:T(8,128)(2,1)S(1)}, bf16[128,1024]{1,0:T(8,128)(2,1)S(1)}, u32[]{:S(2)}, u32[]{:S(2)}) %collective-permute-start.18) | collective-permute-done | bytes 262176 | tf_op jit(solution)/shard_map/ppermute | solution.py:470
  105.6 1.6 %collective-permute-start.25 = (bf16[128,1024]{1,0:T(8,128)(2,1)S(1)}, bf16[128,1024]{1,0:T(8,128)(2,1)S(1)}, u32[]{:S(2)}, u32[]{:S(2)}) collective-permute-start(bf16[128,1024]{1,0:T(8,128)(2,1)S(1)} %get-tuple-element.132), channel_id=1, source_target_pairs={{0,1},{1,0},{2,3},{3,2},{4,5},{5,4},{6,7},{7,6},{8,9},{9,8},{10,11... | collective-permute-start | bytes 786440 | tf_op jit(solution)/shard_map/ppermute | solution.py:470
  107.2 4.1 %collective-permute-done.20.refs_2_ = bf16[128,2048]{1,0:T(8,128)(2,1)S(1)} collective-permute-done((bf16[128,2048]{1,0:T(8,128)(2,1)S(1)}, bf16[128,2048]{1,0:T(8,128)(2,1)S(1)}, u32[]{:S(2)}, u32[]{:S(2)}) %collective-permute-start.20) | collective-permute-done | bytes 524320 | tf_op jit(solution)/shard_map/ppermute | solution.py:480
  111.4 1.1 collective-permute-start.28
  112.5 3.6 %collective-permute-done.25.refs_5_ = bf16[128,1024]{1,0:T(8,128)(2,1)S(1)} collective-permute-done((bf16[128,1024]{1,0:T(8,128)(2,1)S(1)}, bf16[128,1024]{1,0:T(8,128)(2,1)S(1)}, u32[]{:S(2)}, u32[]{:S(2)}) %collective-permute-start.25) | collective-permute-done | bytes 262176 | tf_op jit(solution)/shard_map/ppermute | solution.py:470
  116.1 1.1 items_1_0.1
  117.2 3.8 %collective-permute-start.26 = (bf16[2176,128]{1,0:T(8,128)(2,1)S(1)}, bf16[2176,128]{1,0:T(8,128)(2,1)S(1)}, u32[]{:S(2)}, u32[]{:S(2)}) collective-permute-start(bf16[2176,128]{1,0:T(8,128)(2,1)S(1)} %get-tuple-element.133), channel_id=1, source_target_pairs={{0,4},{1,5},{2,6},{3,7},{4,8},{5,9},{6,10},{7,11},{8,12},{9,13},{1... | collective-permute-start | bytes 1671176 | tf_op jit(solution)/shard_map/ppermute | solution.py:480
  121.0 5.3 %users_1.1 = f32[2048,128]{1,0:T(8,128)} custom-call(s32[1,2]{1,0:T(1,128)S(1)} %bitcast.7, f32[2048,128]{1,0:T(8,128)S(1)} %get-tuple-element.75.users, f32[128,2048]{1,0:T(8,128)S(1)} %get-tuple-element.124.grad, bf16[128,2048]{1,0:T(8,128)(2,1)S(1)} %collective-permute-done.13.refs_8_.refs_0_.items, ...), custom_call_target="tpu_custom_call" | custom-call | flops 10000000000 | bytes 65536 | tf_op jit(solution)/shard_map/users_1/pallas_call | solution.py:358
  126.4 5.6 %collective-permute-done.26.refs_0_ = bf16[2176,128]{1,0:T(8,128)(2,1)S(1)} collective-permute-done((bf16[2176,128]{1,0:T(8,128)(2,1)S(1)}, bf16[2176,128]{1,0:T(8,128)(2,1)S(1)}, u32[]{:S(2)}, u32[]{:S(2)}) %collective-permute-start.26) | collective-permute-done | bytes 557088 | tf_op jit(solution)/shard_map/ppermute | solution.py:480
  131.9 1.7 %items_final.1 = f32[4096,128]{1,0:T(8,128)} custom-call(bf16[2176,128]{1,0:T(8,128)(2,1)S(1)} %collective-permute-done.26.refs_0_, bf16[128,2048]{1,0:T(8,128)(2,1)S(1)} %collective-permute-done.19.refs_1_, bf16[128,2048]{1,0:T(8,128)(2,1)S(1)} %collective-permute-done.20.refs_2_, bf16[128,1024]{1,0:T(8,128)(2,1)S(1)} %collective-permute-done.27.refs_3_, ...), custom_call_target="tpu_custom_call" | custom-call | flops 1200000000 | bytes 65536 | tf_op jit(solution)/shard_map/items_final/pallas_call | solution.py:579
  (38 shorter events, 1.0 us)
Async XLA Ops:
  7.1 20.4 %collective-permute-start.4 = (bf16[128,2176]{1,0:T(8,128)(2,1)S(1)}, bf16[128,2176]{1,0:T(8,128)(2,1)S(1)}, u32[]{:S(2)}, u32[]{:S(2)}) collective-permute-start(bf16[128,2176]{1,0:T(8,128)(2,1)S(1)} %get-tuple-element.93.refs_4_.refs_6_), channel_id=1, source_target_pairs={{0,1},{1,0},{2,3},{3,2},{4,5},{5,4},{6,7},{7,6},{8,9},{9,8},{10,11... | collective-permute-start | bytes 1671176 | tf_op jit(solution)/shard_map/ppermute | solution.py:470
  12.2 15.3 %collective-permute-start.5 = (bf16[128,2048]{1,0:T(8,128)(2,1)S(1)}, bf16[128,2048]{1,0:T(8,128)(2,1)S(1)}, u32[]{:S(2)}, u32[]{:S(2)}) collective-permute-start(bf16[128,2048]{1,0:T(8,128)(2,1)S(1)} %get-tuple-element.96), channel_id=1, source_target_pairs={{0,2},{1,3},{2,0},{3,1},{4,6},{5,7},{6,4},{7,5},{8,10},{9,11},{10,... | collective-permute-start | bytes 1572872 | tf_op jit(solution)/shard_map/ppermute | solution.py:470
  22.0 6.4 %copy-start = (f32[2048,128]{1,0:T(8,128)S(1)}, f32[2048,128]{1,0:T(8,128)}, u32[]{:S(2)}) copy-start(f32[2048,128]{1,0:T(8,128)} %users.1) | copy-start | bytes 3145732
  22.0 6.4 %copy-start.1 = (s32[2,1]{0,1:T(1,128)S(1)}, s32[2,1]{0,1:T(1,128)}, u32[]{:S(2)}) copy-start(s32[2,1]{0,1:T(1,128)} %param.13) | copy-start | bytes 28
  22.0 14.9 %collective-permute-start = (bf16[128,2048]{1,0:T(8,128)(2,1)S(1)}, bf16[128,2048]{1,0:T(8,128)(2,1)S(1)}, u32[]{:S(2)}, u32[]{:S(2)}) collective-permute-start(bf16[128,2048]{1,0:T(8,128)(2,1)S(1)} %get-tuple-element.80), channel_id=1, source_target_pairs={{0,1},{1,0},{2,3},{3,2},{4,5},{5,4},{6,7},{7,6},{8,9},{9,8},{10,11... | collective-permute-start | bytes 1572872 | tf_op jit(solution)/shard_map/ppermute | solution.py:470
  22.1 16.6 %collective-permute-start.1 = (bf16[128,2048]{1,0:T(8,128)(2,1)S(1)}, bf16[128,2048]{1,0:T(8,128)(2,1)S(1)}, u32[]{:S(2)}, u32[]{:S(2)}) collective-permute-start(bf16[128,2048]{1,0:T(8,128)(2,1)S(1)} %get-tuple-element.83), channel_id=1, source_target_pairs={{0,2},{1,3},{2,0},{3,1},{4,6},{5,7},{6,4},{7,5},{8,10},{9,11},{10,... | collective-permute-start | bytes 1572872 | tf_op jit(solution)/shard_map/ppermute | solution.py:470
  27.6 17.4 %collective-permute-start.6 = (bf16[128,1152]{1,0:T(8,128)(2,1)S(1)}, bf16[128,1152]{1,0:T(8,128)(2,1)S(1)}, u32[]{:S(2)}, u32[]{:S(2)}) collective-permute-start(bf16[128,1152]{1,0:T(8,128)(2,1)S(1)} %get-tuple-element.98), channel_id=1, source_target_pairs={{0,2},{1,3},{2,0},{3,1},{4,6},{5,7},{6,4},{7,5},{8,10},{9,11},{10,... | collective-permute-start | bytes 884744 | tf_op jit(solution)/shard_map/ppermute | solution.py:470
  27.7 14.9 %collective-permute-start.7 = (bf16[128,1024]{1,0:T(8,128)(2,1)S(1)}, bf16[128,1024]{1,0:T(8,128)(2,1)S(1)}, u32[]{:S(2)}, u32[]{:S(2)}) collective-permute-start(bf16[128,1024]{1,0:T(8,128)(2,1)S(1)} %get-tuple-element.99), channel_id=1, source_target_pairs={{0,1},{1,0},{2,3},{3,2},{4,5},{5,4},{6,7},{7,6},{8,9},{9,8},{10,11... | collective-permute-start | bytes 786440 | tf_op jit(solution)/shard_map/ppermute | solution.py:470
  38.8 11.5 %collective-permute-start.2 = (bf16[128,1024]{1,0:T(8,128)(2,1)S(1)}, bf16[128,1024]{1,0:T(8,128)(2,1)S(1)}, u32[]{:S(2)}, u32[]{:S(2)}) collective-permute-start(bf16[128,1024]{1,0:T(8,128)(2,1)S(1)} %get-tuple-element.85), channel_id=1, source_target_pairs={{0,2},{1,3},{2,0},{3,1},{4,6},{5,7},{6,4},{7,5},{8,10},{9,11},{10,... | collective-permute-start | bytes 786440 | tf_op jit(solution)/shard_map/ppermute | solution.py:470
  38.9 11.4 %collective-permute-start.3 = (bf16[128,1024]{1,0:T(8,128)(2,1)S(1)}, bf16[128,1024]{1,0:T(8,128)(2,1)S(1)}, u32[]{:S(2)}, u32[]{:S(2)}) collective-permute-start(bf16[128,1024]{1,0:T(8,128)(2,1)S(1)} %get-tuple-element.86), channel_id=1, source_target_pairs={{0,1},{1,0},{2,3},{3,2},{4,5},{5,4},{6,7},{7,6},{8,9},{9,8},{10,11... | collective-permute-start | bytes 786440 | tf_op jit(solution)/shard_map/ppermute | solution.py:470
  45.6 13.3 %collective-permute-start.14 = (bf16[128,2048]{1,0:T(8,128)(2,1)S(1)}, bf16[128,2048]{1,0:T(8,128)(2,1)S(1)}, u32[]{:S(2)}, u32[]{:S(2)}) collective-permute-start(bf16[128,2048]{1,0:T(8,128)(2,1)S(1)} %get-tuple-element.105), channel_id=1, source_target_pairs={{0,5},{1,4},{2,7},{3,6},{4,9},{5,8},{6,11},{7,10},{8,13},{9,12},{1... | collective-permute-start | bytes 1572872 | tf_op jit(solution)/shard_map/ppermute | solution.py:480
  45.7 16.4 %collective-permute-start.15 = (bf16[128,2048]{1,0:T(8,128)(2,1)S(1)}, bf16[128,2048]{1,0:T(8,128)(2,1)S(1)}, u32[]{:S(2)}, u32[]{:S(2)}) collective-permute-start(bf16[128,2048]{1,0:T(8,128)(2,1)S(1)} %get-tuple-element.105), channel_id=1, source_target_pairs={{0,6},{1,7},{2,4},{3,5},{4,10},{5,11},{6,8},{7,9},{8,14},{9,15},{1... | collective-permute-start | bytes 1572872 | tf_op jit(solution)/shard_map/ppermute | solution.py:480
  50.9 22.0 %collective-permute-start.9 = (bf16[128,2048]{1,0:T(8,128)(2,1)S(1)}, bf16[128,2048]{1,0:T(8,128)(2,1)S(1)}, u32[]{:S(2)}, u32[]{:S(2)}) collective-permute-start(bf16[128,2048]{1,0:T(8,128)(2,1)S(1)} %items_0_1.1), channel_id=1, source_target_pairs={{0,5},{1,4},{2,7},{3,6},{4,9},{5,8},{6,11},{7,10},{8,13},{9,12},{1... | collective-permute-start | bytes 1572872 | tf_op jit(solution)/shard_map/ppermute | solution.py:480
  51.1 24.6 %collective-permute-start.10 = (bf16[128,2048]{1,0:T(8,128)(2,1)S(1)}, bf16[128,2048]{1,0:T(8,128)(2,1)S(1)}, u32[]{:S(2)}, u32[]{:S(2)}) collective-permute-start(bf16[128,2048]{1,0:T(8,128)(2,1)S(1)} %items_0_1.1), channel_id=1, source_target_pairs={{0,6},{1,7},{2,4},{3,5},{4,10},{5,11},{6,8},{7,9},{8,14},{9,15},{1... | collective-permute-start | bytes 1572872 | tf_op jit(solution)/shard_map/ppermute | solution.py:480
  53.7 24.5 %collective-permute-start.13 = (bf16[128,2048]{1,0:T(8,128)(2,1)S(1)}, bf16[128,2048]{1,0:T(8,128)(2,1)S(1)}, u32[]{:S(2)}, u32[]{:S(2)}) collective-permute-start(bf16[128,2048]{1,0:T(8,128)(2,1)S(1)} %get-tuple-element.105), channel_id=1, source_target_pairs={{0,4},{1,5},{2,6},{3,7},{4,8},{5,9},{6,10},{7,11},{8,12},{9,13},{1... | collective-permute-start | bytes 1572872 | tf_op jit(solution)/shard_map/ppermute | solution.py:480
  58.9 21.5 %collective-permute-start.16 = (bf16[128,1024]{1,0:T(8,128)(2,1)S(1)}, bf16[128,1024]{1,0:T(8,128)(2,1)S(1)}, u32[]{:S(2)}, u32[]{:S(2)}) collective-permute-start(bf16[128,1024]{1,0:T(8,128)(2,1)S(1)} %slice.18), channel_id=1, source_target_pairs={{0,2},{1,3},{2,0},{3,1},{4,6},{5,7},{6,4},{7,5},{8,10},{9,11},{10,... | collective-permute-start | bytes 786440 | tf_op jit(solution)/shard_map/ppermute | solution.py:470
  62.1 18.4 %collective-permute-start.17 = (bf16[128,1024]{1,0:T(8,128)(2,1)S(1)}, bf16[128,1024]{1,0:T(8,128)(2,1)S(1)}, u32[]{:S(2)}, u32[]{:S(2)}) collective-permute-start(bf16[128,1024]{1,0:T(8,128)(2,1)S(1)} %slice.19), channel_id=1, source_target_pairs={{0,1},{1,0},{2,3},{3,2},{4,5},{5,4},{6,7},{7,6},{8,9},{9,8},{10,11... | collective-permute-start | bytes 786440 | tf_op jit(solution)/shard_map/ppermute | solution.py:470
  73.0 15.4 %collective-permute-start.8 = (bf16[128,2048]{1,0:T(8,128)(2,1)S(1)}, bf16[128,2048]{1,0:T(8,128)(2,1)S(1)}, u32[]{:S(2)}, u32[]{:S(2)}) collective-permute-start(bf16[128,2048]{1,0:T(8,128)(2,1)S(1)} %items_0_1.1), channel_id=1, source_target_pairs={{0,4},{1,5},{2,6},{3,7},{4,8},{5,9},{6,10},{7,11},{8,12},{9,13},{1... | collective-permute-start | bytes 1572872 | tf_op jit(solution)/shard_map/ppermute | solution.py:480
  75.7 12.7 %collective-permute-start.11 = (bf16[128,1024]{1,0:T(8,128)(2,1)S(1)}, bf16[128,1024]{1,0:T(8,128)(2,1)S(1)}, u32[]{:S(2)}, u32[]{:S(2)}) collective-permute-start(bf16[128,1024]{1,0:T(8,128)(2,1)S(1)} %slice.16), channel_id=1, source_target_pairs={{0,2},{1,3},{2,0},{3,1},{4,6},{5,7},{6,4},{7,5},{8,10},{9,11},{10,... | collective-permute-start | bytes 786440 | tf_op jit(solution)/shard_map/ppermute | solution.py:470
  78.2 10.2 %collective-permute-start.12 = (bf16[128,1024]{1,0:T(8,128)(2,1)S(1)}, bf16[128,1024]{1,0:T(8,128)(2,1)S(1)}, u32[]{:S(2)}, u32[]{:S(2)}) collective-permute-start(bf16[128,1024]{1,0:T(8,128)(2,1)S(1)} %slice.17), channel_id=1, source_target_pairs={{0,1},{1,0},{2,3},{3,2},{4,5},{5,4},{6,7},{7,6},{8,9},{9,8},{10,11... | collective-permute-start | bytes 786440 | tf_op jit(solution)/shard_map/ppermute | solution.py:470
  86.1 15.5 %collective-permute-start.22 = (bf16[128,2176]{1,0:T(8,128)(2,1)S(1)}, bf16[128,2176]{1,0:T(8,128)(2,1)S(1)}, u32[]{:S(2)}, u32[]{:S(2)}) collective-permute-start(bf16[128,2176]{1,0:T(8,128)(2,1)S(1)} %get-tuple-element.126.refs_4_.refs_6_), channel_id=1, source_target_pairs={{0,1},{1,0},{2,3},{3,2},{4,5},{5,4},{6,7},{7,6},{8,9},{9,8},{10,11... | collective-permute-start | bytes 1671176 | tf_op jit(solution)/shard_map/ppermute | solution.py:470
  88.4 12.2 %collective-permute-start.23 = (bf16[128,2048]{1,0:T(8,128)(2,1)S(1)}, bf16[128,2048]{1,0:T(8,128)(2,1)S(1)}, u32[]{:S(2)}, u32[]{:S(2)}) collective-permute-start(bf16[128,2048]{1,0:T(8,128)(2,1)S(1)} %get-tuple-element.129), channel_id=1, source_target_pairs={{0,2},{1,3},{2,0},{3,1},{4,6},{5,7},{6,4},{7,5},{8,10},{9,11},{10,... | collective-permute-start | bytes 1572872 | tf_op jit(solution)/shard_map/ppermute | solution.py:470
  95.2 12.0 %collective-permute-start.19 = (bf16[128,2048]{1,0:T(8,128)(2,1)S(1)}, bf16[128,2048]{1,0:T(8,128)(2,1)S(1)}, u32[]{:S(2)}, u32[]{:S(2)}) collective-permute-start(bf16[128,2048]{1,0:T(8,128)(2,1)S(1)} %collective-permute-done.8.refs_8_.refs_5_), channel_id=1, source_target_pairs={{0,4},{1,5},{2,6},{3,7},{4,8},{5,9},{6,10},{7,11},{8,12},{9,13},{1... | collective-permute-start | bytes 1572872 | tf_op jit(solution)/shard_map/ppermute | solution.py:480
  95.2 16.0 %collective-permute-start.20 = (bf16[128,2048]{1,0:T(8,128)(2,1)S(1)}, bf16[128,2048]{1,0:T(8,128)(2,1)S(1)}, u32[]{:S(2)}, u32[]{:S(2)}) collective-permute-start(bf16[128,2048]{1,0:T(8,128)(2,1)S(1)} %get-tuple-element.116), channel_id=1, source_target_pairs={{0,4},{1,5},{2,6},{3,7},{4,8},{5,9},{6,10},{7,11},{8,12},{9,13},{1... | collective-permute-start | bytes 1572872 | tf_op jit(solution)/shard_map/ppermute | solution.py:480
  97.0 8.5 %collective-permute-start.18 = (bf16[128,1024]{1,0:T(8,128)(2,1)S(1)}, bf16[128,1024]{1,0:T(8,128)(2,1)S(1)}, u32[]{:S(2)}, u32[]{:S(2)}) collective-permute-start(bf16[128,1024]{1,0:T(8,128)(2,1)S(1)} %get-tuple-element.113), channel_id=1, source_target_pairs={{0,1},{1,0},{2,3},{3,2},{4,5},{5,4},{6,7},{7,6},{8,9},{9,8},{10,11... | collective-permute-start | bytes 786440 | tf_op jit(solution)/shard_map/ppermute | solution.py:470
  100.6 10.7 %collective-permute-start.21 = (bf16[128,1024]{1,0:T(8,128)(2,1)S(1)}, bf16[128,1024]{1,0:T(8,128)(2,1)S(1)}, u32[]{:S(2)}, u32[]{:S(2)}) collective-permute-start(bf16[128,1024]{1,0:T(8,128)(2,1)S(1)} %get-tuple-element.119), channel_id=1, source_target_pairs={{0,2},{1,3},{2,0},{3,1},{4,6},{5,7},{6,4},{7,5},{8,10},{9,11},{10,... | collective-permute-start | bytes 786440 | tf_op jit(solution)/shard_map/ppermute | solution.py:470
  101.8 14.3 %collective-permute-start.24 = (bf16[128,1152]{1,0:T(8,128)(2,1)S(1)}, bf16[128,1152]{1,0:T(8,128)(2,1)S(1)}, u32[]{:S(2)}, u32[]{:S(2)}) collective-permute-start(bf16[128,1152]{1,0:T(8,128)(2,1)S(1)} %get-tuple-element.131), channel_id=1, source_target_pairs={{0,2},{1,3},{2,0},{3,1},{4,6},{5,7},{6,4},{7,5},{8,10},{9,11},{10,... | collective-permute-start | bytes 884744 | tf_op jit(solution)/shard_map/ppermute | solution.py:470
  105.6 10.5 %collective-permute-start.25 = (bf16[128,1024]{1,0:T(8,128)(2,1)S(1)}, bf16[128,1024]{1,0:T(8,128)(2,1)S(1)}, u32[]{:S(2)}, u32[]{:S(2)}) collective-permute-start(bf16[128,1024]{1,0:T(8,128)(2,1)S(1)} %get-tuple-element.132), channel_id=1, source_target_pairs={{0,1},{1,0},{2,3},{3,2},{4,5},{5,4},{6,7},{7,6},{8,9},{9,8},{10,11... | collective-permute-start | bytes 786440 | tf_op jit(solution)/shard_map/ppermute | solution.py:470
  107.2 19.2 %collective-permute-start.27 = (bf16[128,1024]{1,0:T(8,128)(2,1)S(1)}, bf16[128,1024]{1,0:T(8,128)(2,1)S(1)}, u32[]{:S(2)}, u32[]{:S(2)}) collective-permute-start(bf16[128,1024]{1,0:T(8,128)(2,1)S(1)} %get-tuple-element.134), channel_id=1, source_target_pairs={{0,5},{1,4},{2,7},{3,6},{4,9},{5,8},{6,11},{7,10},{8,13},{9,12},{1... | collective-permute-start | bytes 786440 | tf_op jit(solution)/shard_map/ppermute | solution.py:480
  111.2 15.1 %collective-permute-start.29 = (bf16[128,1024]{1,0:T(8,128)(2,1)S(1)}, bf16[128,1024]{1,0:T(8,128)(2,1)S(1)}, u32[]{:S(2)}, u32[]{:S(2)}) collective-permute-start(bf16[128,1024]{1,0:T(8,128)(2,1)S(1)} %get-tuple-element.135), channel_id=1, source_target_pairs={{0,6},{1,7},{2,4},{3,5},{4,10},{5,11},{6,8},{7,9},{8,14},{9,15},{1... | collective-permute-start | bytes 786440 | tf_op jit(solution)/shard_map/ppermute | solution.py:480
  111.4 15.0 %collective-permute-start.28 = (bf16[128,1024]{1,0:T(8,128)(2,1)S(1)}, bf16[128,1024]{1,0:T(8,128)(2,1)S(1)}, u32[]{:S(2)}, u32[]{:S(2)}) collective-permute-start(bf16[128,1024]{1,0:T(8,128)(2,1)S(1)} %get-tuple-element.122), channel_id=1, source_target_pairs={{0,6},{1,7},{2,4},{3,5},{4,10},{5,11},{6,8},{7,9},{8,14},{9,15},{1... | collective-permute-start | bytes 786440 | tf_op jit(solution)/shard_map/ppermute | solution.py:480
  112.5 8.5 %copy-start.2 = (s32[2,1]{0,1:T(1,128)S(1)}, s32[2,1]{0,1:T(1,128)}, u32[]{:S(2)}) copy-start(s32[2,1]{0,1:T(1,128)} %param.13) | copy-start | bytes 28
  116.1 10.3 %collective-permute-start.30 = (bf16[128,1024]{1,0:T(8,128)(2,1)S(1)}, bf16[128,1024]{1,0:T(8,128)(2,1)S(1)}, u32[]{:S(2)}, u32[]{:S(2)}) collective-permute-start(bf16[128,1024]{1,0:T(8,128)(2,1)S(1)} %get-tuple-element.123), channel_id=1, source_target_pairs={{0,5},{1,4},{2,7},{3,6},{4,9},{5,8},{6,11},{7,10},{8,13},{9,12},{1... | collective-permute-start | bytes 786440 | tf_op jit(solution)/shard_map/ppermute | solution.py:480
  117.2 14.7 %collective-permute-start.26 = (bf16[2176,128]{1,0:T(8,128)(2,1)S(1)}, bf16[2176,128]{1,0:T(8,128)(2,1)S(1)}, u32[]{:S(2)}, u32[]{:S(2)}) collective-permute-start(bf16[2176,128]{1,0:T(8,128)(2,1)S(1)} %get-tuple-element.133), channel_id=1, source_target_pairs={{0,4},{1,5},{2,6},{3,7},{4,8},{5,9},{6,10},{7,11},{8,12},{9,13},{1... | collective-permute-start | bytes 1671176 | tf_op jit(solution)/shard_map/ppermute | solution.py:480

commit v11 on v8

--- a/solution.py
+++ b/solution.py
@@ -647,6 +647,8 @@
                 sources = [(item_factors, None)]
             else:
                 sources = gathers[c]
+                if epoch + 1 == SUB and c + 1 == CHUNKS:
+                    kept = moved(tied(sources[0][0], grad_user), 0)
             direct = epoch + 1 == SUB and c + 1 == CHUNKS
             out = tile_call(
                 epoch, c, direct, members, scalars, ratings, row_mask, users, sources, grad_user,
@@ -663,8 +665,6 @@
                 pieces += [array for array, _ in sources]
                 olds.append(sources[0][0])
         last = epoch + 1 == SUB
-        if last:
-            kept = moved(tied(olds[-1], grad_user), 0)
         if not last:
             new_users = user_call(epoch, block_rows, owners, full_users, grad_user, pieces)
             full_users = new_users[0]

time: 134 us -> 136 us (1.015)
  starting transfers between devices: 26.4 us -> 37.7 us
  waiting for transfers between devices: 57.2 us -> 51.3 us
  Pallas kernels: 49 us -> 45.9 us
    ppermute x18, starting transfers between devices: 15.9 us -> 26.1 us  [swapped(): return lax.ppermute(value, 'grp', [(i, i ^ bit) for i in range(length)])]
    ppermute x13, waiting for transfers between devices: 37.2 us -> 27.1 us  [moved(): return lax.ppermute(value, ('blk', 'grp'), pairs)]
    ppermute x18, waiting for transfers between devices: 20.1 us -> 24.3 us  [swapped(): return lax.ppermute(value, 'grp', [(i, i ^ bit) for i in range(length)])]
    pallas_call x4, Pallas kernels: 34.5 us -> 31.4 us  [tile_call(): pl.pallas_call(functools.partial(tile_kernel, epoch, chunk, direct, membe...]
  transfers between devices with their start and end apart: 31 -> 31, of which waited for: 17 -> 16; matrix products, arithmetic and copies ran while one was open for 0% -> 0% of each run, Pallas kernels for 27% -> 26%
where the time goes in v11:
time: 136 us
  waiting for transfers between devices  51.3 us (38%)
  Pallas kernels  45.9 us (34%)
  starting transfers between devices  37.7 us (28%)
    pallas_call x4, Pallas kernels, tile_call(): pl.pallas_call(functools.partial(tile_kernel, epoch, chunk, direct, membe...  31.4 us
    ppermute x13, waiting for transfers between devices, moved(): return lax.ppermute(value, ('blk', 'grp'), pairs)  27.1 us
    ppermute x18, starting transfers between devices, swapped(): return lax.ppermute(value, 'grp', [(i, i ^ bit) for i in range(length)])  26.1 us
    ppermute x18, waiting for transfers between devices, swapped(): return lax.ppermute(value, 'grp', [(i, i ^ bit) for i in range(length)])  24.3 us
    ppermute x13, starting transfers between devices, moved(): return lax.ppermute(value, ('blk', 'grp'), pairs)  11.6 us
    pallas_call x2, Pallas kernels, user_call(): pl.pallas_call(functools.partial(user_kernel, epoch, block_rows), out_sha...  10.1 us
  transfers between devices with their start and end apart: 31, of which 16 were waited for; matrix products, arithmetic and copies ran while one was open for 0% of the time, Pallas kernels for 26%

profile of v11, /device:TPU:0, one launch (start us, length us, event | category | flops | bytes accessed | tf_op | source)
XLA Modules:
  0.0 136.0 jit_solution(7550375963751578365)
XLA Ops:
  0.6 9.1 %tiles_0_0.1 = (bf16[128,2176]{1,0:T(8,128)(2,1)S(1)}, bf16[128,2048]{1,0:T(8,128)(2,1)S(1)}, bf16[128,2048]{1,0:T(8,128)(2,1)S(1)}, bf16[128,2048]{1,0:T(8,128)...) custom-call(s32[2,1,1,64]{3,2,1,0:T(1,128)} %refs_0_.7, ...), custom_call_target="tpu_custom_call" | custom-call | flops 16000000000 | bytes 65536 | tf_op jit(solution)/shard_map/tiles_0_0/pallas_call | solution.py:319
  9.7 3.5 %collective-permute-start.4 = (bf16[128,2176]{1,0:T(8,128)(2,1)S(1)}, bf16[128,2176]{1,0:T(8,128)(2,1)S(1)}, u32[]{:S(2)}, u32[]{:S(2)}) collective-permute-start(bf16[128,2176]{1,0:T(8,128)(2,1)S(1)} %get-tuple-element.95.refs_4_.refs_6_), channel_id=1, source_target_pairs={{0,1},{1,0},{2,3},{3,2},{4,5},{5,4},{6,7},{7,6},{8,9},{9,8},{10,11... | collective-permute-start | bytes 1671176 | tf_op jit(solution)/shard_map/ppermute | solution.py:470
  13.2 2.0 %collective-permute-start.5 = (bf16[128,2048]{1,0:T(8,128)(2,1)S(1)}, bf16[128,2048]{1,0:T(8,128)(2,1)S(1)}, u32[]{:S(2)}, u32[]{:S(2)}) collective-permute-start(bf16[128,2048]{1,0:T(8,128)(2,1)S(1)} %get-tuple-element.98), channel_id=1, source_target_pairs={{0,2},{1,3},{2,0},{3,1},{4,6},{5,7},{6,4},{7,5},{8,10},{9,11},{10,... | collective-permute-start | bytes 1572872 | tf_op jit(solution)/shard_map/ppermute | solution.py:470
  15.3 8.9 %tiles_0_1.1 = (bf16[128,2048]{1,0:T(8,128)(2,1)S(1)}, bf16[128,2048]{1,0:T(8,128)(2,1)S(1)}, bf16[128,2048]{1,0:T(8,128)(2,1)S(1)}, bf16[128,2048]{1,0:T(8,128)...) custom-call(s32[2,1,1,64]{3,2,1,0:T(1,128)} %refs_0_.7, ...), custom_call_target="tpu_custom_call" | custom-call | flops 16000000000 | bytes 65536 | tf_op jit(solution)/shard_map/tiles_0_1/pallas_call | solution.py:319
  24.4 3.7 %collective-permute-done.5.refs_3_.refs_4_ = bf16[128,2048]{1,0:T(8,128)(2,1)S(1)} collective-permute-done((bf16[128,2048]{1,0:T(8,128)(2,1)S(1)}, bf16[128,2048]{1,0:T(8,128)(2,1)S(1)}, u32[]{:S(2)}, u32[]{:S(2)}) %collective-permute-start.5) | collective-permute-done | bytes 524320 | tf_op jit(solution)/shard_map/ppermute | solution.py:470
  28.1 0.1 mid_0_0_0.1
  28.2 2.1 %collective-permute-start.6 = (bf16[128,1152]{1,0:T(8,128)(2,1)S(1)}, bf16[128,1152]{1,0:T(8,128)(2,1)S(1)}, u32[]{:S(2)}, u32[]{:S(2)}) collective-permute-start(bf16[128,1152]{1,0:T(8,128)(2,1)S(1)} %get-tuple-element.100), channel_id=1, source_target_pairs={{0,2},{1,3},{2,0},{3,1},{4,6},{5,7},{6,4},{7,5},{8,10},{9,11},{10,... | collective-permute-start | bytes 884744 | tf_op jit(solution)/shard_map/ppermute | solution.py:470
  30.3 0.7 collective-permute-start.7
  31.0 4.8 %users_0.1 = (f32[2048,128]{1,0:T(8,128)S(1)}, bf16[2048,128]{1,0:T(8,128)(2,1)S(1)}, bf16[128,2048]{1,0:T(8,128)(2,1)S(1)}, bf16[128,128]{1,0:T(8,128)(2,1)S(1)}) custom-call(s32[1,2]{1,0:T(1,128)S(1)} %bitcast.6, f32[2048,128]{1,0:T(8,128)S(1)} %copy-done, f32[128,2048]{1,0:T(8,128)S(1)} %get-tuple-element.74.grad, ...), custom_call_target="tpu_custom_call" | custom-call | flops 10000000000 | bytes 65536 | tf_op jit(solution)/shard_map/users_0/pallas_call | solution.py:358
  35.7 3.4 %collective-permute-done.refs_1_ = bf16[128,2048]{1,0:T(8,128)(2,1)S(1)} collective-permute-done((bf16[128,2048]{1,0:T(8,128)(2,1)S(1)}, bf16[128,2048]{1,0:T(8,128)(2,1)S(1)}, u32[]{:S(2)}, u32[]{:S(2)}) %collective-permute-start) | collective-permute-done | bytes 524320 | tf_op jit(solution)/shard_map/ppermute | solution.py:470
  39.1 0.2 collective-permute-done.1.refs_3_.refs_4_
  39.4 2.1 %collective-permute-start.2 = (bf16[128,1024]{1,0:T(8,128)(2,1)S(1)}, bf16[128,1024]{1,0:T(8,128)(2,1)S(1)}, u32[]{:S(2)}, u32[]{:S(2)}) collective-permute-start(bf16[128,1024]{1,0:T(8,128)(2,1)S(1)} %get-tuple-element.87), channel_id=1, source_target_pairs={{0,2},{1,3},{2,0},{3,1},{4,6},{5,7},{6,4},{7,5},{8,10},{9,11},{10,... | collective-permute-start | bytes 786440 | tf_op jit(solution)/shard_map/ppermute | solution.py:470
  41.5 0.7 collective-permute-start.3
  42.2 1.4 %collective-permute-done.7.refs_5_ = bf16[128,1024]{1,0:T(8,128)(2,1)S(1)} collective-permute-done((bf16[128,1024]{1,0:T(8,128)(2,1)S(1)}, bf16[128,1024]{1,0:T(8,128)(2,1)S(1)}, u32[]{:S(2)}, u32[]{:S(2)}) %collective-permute-start.7) | collective-permute-done | bytes 262176 | tf_op jit(solution)/shard_map/ppermute | solution.py:470
  43.7 2.0 %collective-permute-done.6.refs_2_.refs_8_ = bf16[128,1152]{1,0:T(8,128)(2,1)S(1)} collective-permute-done((bf16[128,1152]{1,0:T(8,128)(2,1)S(1)}, bf16[128,1152]{1,0:T(8,128)(2,1)S(1)}, u32[]{:S(2)}, u32[]{:S(2)}) %collective-permute-start.6) | collective-permute-done | bytes 294944 | tf_op jit(solution)/shard_map/ppermute | solution.py:470
  45.6 0.6 items_0_0.1
  46.3 1.8 %collective-permute-start.15 = (bf16[128,2048]{1,0:T(8,128)(2,1)S(1)}, bf16[128,2048]{1,0:T(8,128)(2,1)S(1)}, u32[]{:S(2)}, u32[]{:S(2)}) collective-permute-start(bf16[128,2048]{1,0:T(8,128)(2,1)S(1)} %get-tuple-element.107), channel_id=1, source_target_pairs={{0,6},{1,7},{2,4},{3,5},{4,10},{5,11},{6,8},{7,9},{8,14},{9,15},{1... | collective-permute-start | bytes 1572872 | tf_op jit(solution)/shard_map/ppermute | solution.py:480
  48.0 2.1 %collective-permute-done.2.refs_2_ = bf16[128,1024]{1,0:T(8,128)(2,1)S(1)} collective-permute-done((bf16[128,1024]{1,0:T(8,128)(2,1)S(1)}, bf16[128,1024]{1,0:T(8,128)(2,1)S(1)}, u32[]{:S(2)}, u32[]{:S(2)}) %collective-permute-start.2) | collective-permute-done | bytes 262176 | tf_op jit(solution)/shard_map/ppermute | solution.py:470
  50.1 0.6 items_0_1.1
  50.8 2.0 %collective-permute-start.10 = (bf16[128,2048]{1,0:T(8,128)(2,1)S(1)}, bf16[128,2048]{1,0:T(8,128)(2,1)S(1)}, u32[]{:S(2)}, u32[]{:S(2)}) collective-permute-start(bf16[128,2048]{1,0:T(8,128)(2,1)S(1)} %items_0_1.1), channel_id=1, source_target_pairs={{0,6},{1,7},{2,4},{3,5},{4,10},{5,11},{6,8},{7,9},{8,14},{9,15},{1... | collective-permute-start | bytes 1572872 | tf_op jit(solution)/shard_map/ppermute | solution.py:480
  52.7 5.8 %collective-permute-done.14.refs_9_.refs_1_ = bf16[128,2048]{1,0:T(8,128)(2,1)S(1)} collective-permute-done((bf16[128,2048]{1,0:T(8,128)(2,1)S(1)}, bf16[128,2048]{1,0:T(8,128)(2,1)S(1)}, u32[]{:S(2)}, u32[]{:S(2)}) %collective-permute-start.14) | collective-permute-done | bytes 524320 | tf_op jit(solution)/shard_map/ppermute | solution.py:480
  58.6 2.4 %collective-permute-start.16 = (bf16[128,1024]{1,0:T(8,128)(2,1)S(1)}, bf16[128,1024]{1,0:T(8,128)(2,1)S(1)}, u32[]{:S(2)}, u32[]{:S(2)}) collective-permute-start(bf16[128,1024]{1,0:T(8,128)(2,1)S(1)} %slice.18), channel_id=1, source_target_pairs={{0,2},{1,3},{2,0},{3,1},{4,6},{5,7},{6,4},{7,5},{8,10},{9,11},{10,... | collective-permute-start | bytes 786440 | tf_op jit(solution)/shard_map/ppermute | solution.py:470
  61.0 2.4 %collective-permute-done.15.refs_10_.refs_2_ = bf16[128,2048]{1,0:T(8,128)(2,1)S(1)} collective-permute-done((bf16[128,2048]{1,0:T(8,128)(2,1)S(1)}, bf16[128,2048]{1,0:T(8,128)(2,1)S(1)}, u32[]{:S(2)}, u32[]{:S(2)}) %collective-permute-start.15) | collective-permute-done | bytes 524320 | tf_op jit(solution)/shard_map/ppermute | solution.py:480
  63.4 2.1 %collective-permute-start.17 = (bf16[128,1024]{1,0:T(8,128)(2,1)S(1)}, bf16[128,1024]{1,0:T(8,128)(2,1)S(1)}, u32[]{:S(2)}, u32[]{:S(2)}) collective-permute-start(bf16[128,1024]{1,0:T(8,128)(2,1)S(1)} %slice.19), channel_id=1, source_target_pairs={{0,1},{1,0},{2,3},{3,2},{4,5},{5,4},{6,7},{7,6},{8,9},{9,8},{10,11... | collective-permute-start | bytes 786440 | tf_op jit(solution)/shard_map/ppermute | solution.py:470
  65.5 5.7 %collective-permute-done.9.refs_9_.refs_6_ = bf16[128,2048]{1,0:T(8,128)(2,1)S(1)} collective-permute-done((bf16[128,2048]{1,0:T(8,128)(2,1)S(1)}, bf16[128,2048]{1,0:T(8,128)(2,1)S(1)}, u32[]{:S(2)}, u32[]{:S(2)}) %collective-permute-start.9) | collective-permute-done | bytes 524320 | tf_op jit(solution)/shard_map/ppermute | solution.py:480
  71.2 3.8 %collective-permute-start.8 = (bf16[128,2048]{1,0:T(8,128)(2,1)S(1)}, bf16[128,2048]{1,0:T(8,128)(2,1)S(1)}, u32[]{:S(2)}, u32[]{:S(2)}) collective-permute-start(bf16[128,2048]{1,0:T(8,128)(2,1)S(1)} %items_0_1.1), channel_id=1, source_target_pairs={{0,4},{1,5},{2,6},{3,7},{4,8},{5,9},{6,10},{7,11},{8,12},{9,13},{1... | collective-permute-start | bytes 1572872 | tf_op jit(solution)/shard_map/ppermute | solution.py:480
  75.1 1.4 %collective-permute-start.11 = (bf16[128,1024]{1,0:T(8,128)(2,1)S(1)}, bf16[128,1024]{1,0:T(8,128)(2,1)S(1)}, u32[]{:S(2)}, u32[]{:S(2)}) collective-permute-start(bf16[128,1024]{1,0:T(8,128)(2,1)S(1)} %slice.16), channel_id=1, source_target_pairs={{0,2},{1,3},{2,0},{3,1},{4,6},{5,7},{6,4},{7,5},{8,10},{9,11},{10,... | collective-permute-start | bytes 786440 | tf_op jit(solution)/shard_map/ppermute | solution.py:470
  76.5 4.1 %collective-permute-done.13.refs_8_.refs_0_.items = bf16[128,2048]{1,0:T(8,128)(2,1)S(1)} collective-permute-done((bf16[128,2048]{1,0:T(8,128)(2,1)S(1)}, bf16[128,2048]{1,0:T(8,128)(2,1)S(1)}, u32[]{:S(2)}, u32[]{:S(2)}) %collective-permute-start.13) | collective-permute-done | bytes 524320 | tf_op jit(solution)/shard_map/ppermute | solution.py:480
  80.6 0.2 collective-permute-start.12
  80.8 6.7 %tiles_1_0.1 = (bf16[128,2176]{1,0:T(8,128)(2,1)S(1)}, bf16[128,2048]{1,0:T(8,128)(2,1)S(1)}, bf16[128,2048]{1,0:T(8,128)(2,1)S(1)}, bf16[128,2048]{1,0:T(8,128)(2,1)S(1)}, f32[128,2048]{1,0:T(8,128)S(1)}) custom-call(s32[2,1,1,64]{3,2,1,0:T(1,128)} %refs_0_.7, s32[2,1,1,64]{3,2,1,0:T(1,128)} %refs_1_.7, s32[1,2]{1,0:T(1,128)} %bitcast.10, s32[1,2]{1,0:T(1,128)} %bitcast.4, ...), custom_call_target="tpu_custom_call" | custom-call | flops 16000000000 | bytes 65536 | tf_op jit(solution)/shard_map/tiles_1_0/pallas_call | solution.py:319
  87.5 3.0 %collective-permute-start.21 = (bf16[128,2176]{1,0:T(8,128)(2,1)S(1)}, bf16[128,2176]{1,0:T(8,128)(2,1)S(1)}, u32[]{:S(2)}, u32[]{:S(2)}) collective-permute-start(bf16[128,2176]{1,0:T(8,128)(2,1)S(1)} %get-tuple-element.127.refs_4_.refs_6_), channel_id=1, source_target_pairs={{0,1},{1,0},{2,3},{3,2},{4,5},{5,4},{6,7},{7,6},{8,9},{9,8},{10,11... | collective-permute-start | bytes 1671176 | tf_op jit(solution)/shard_map/ppermute | solution.py:470
  90.5 6.7 %tiles_1_1.1 = (bf16[128,1024]{1,0:T(8,128)(2,1)S(1)}, bf16[128,1024]{1,0:T(8,128)(2,1)S(1)}, bf16[128,1024]{1,0:T(8,128)(2,1)S(1)}, bf16[128,1024]{1,0:T(8,128)...) custom-call(s32[2,1,1,64]{3,2,1,0:T(1,128)} %refs_0_.7, ...), custom_call_target="tpu_custom_call" | custom-call | flops 16000000000 | bytes 65536 | tf_op jit(solution)/shard_map/tiles_1_1/pallas_call | solution.py:319
  97.3 1.7 %collective-permute-start.18 = (bf16[128,1024]{1,0:T(8,128)(2,1)S(1)}, bf16[128,1024]{1,0:T(8,128)(2,1)S(1)}, u32[]{:S(2)}, u32[]{:S(2)}) collective-permute-start(bf16[128,1024]{1,0:T(8,128)(2,1)S(1)} %get-tuple-element.115), channel_id=1, source_target_pairs={{0,1},{1,0},{2,3},{3,2},{4,5},{5,4},{6,7},{7,6},{8,9},{9,8},{10,11... | collective-permute-start | bytes 786440 | tf_op jit(solution)/shard_map/ppermute | solution.py:470
  99.0 4.4 %collective-permute-done.23.refs_3_.refs_4_ = bf16[128,2048]{1,0:T(8,128)(2,1)S(1)} collective-permute-done((bf16[128,2048]{1,0:T(8,128)(2,1)S(1)}, bf16[128,2048]{1,0:T(8,128)(2,1)S(1)}, u32[]{:S(2)}, u32[]{:S(2)}) %collective-permute-start.23) | collective-permute-done | bytes 524320 | tf_op jit(solution)/shard_map/ppermute | solution.py:470
  103.5 0.8 collective-permute-start.20
  104.3 0.1 mid_1_0_0.1
  104.4 1.3 collective-permute-start.24
  105.7 1.9 %collective-permute-start.25 = (bf16[128,1024]{1,0:T(8,128)(2,1)S(1)}, bf16[128,1024]{1,0:T(8,128)(2,1)S(1)}, u32[]{:S(2)}, u32[]{:S(2)}) collective-permute-start(bf16[128,1024]{1,0:T(8,128)(2,1)S(1)} %get-tuple-element.136), channel_id=1, source_target_pairs={{0,1},{1,0},{2,3},{3,2},{4,5},{5,4},{6,7},{7,6},{8,9},{9,8},{10,11... | collective-permute-start | bytes 786440 | tf_op jit(solution)/shard_map/ppermute | solution.py:470
  107.6 5.1 %collective-permute-done.20.refs_3_ = bf16[128,1024]{1,0:T(8,128)(2,1)S(1)} collective-permute-done((bf16[128,1024]{1,0:T(8,128)(2,1)S(1)}, bf16[128,1024]{1,0:T(8,128)(2,1)S(1)}, u32[]{:S(2)}, u32[]{:S(2)}) %collective-permute-start.20) | collective-permute-done | bytes 262176 | tf_op jit(solution)/shard_map/ppermute | solution.py:470
  112.8 1.7 %collective-permute-start.28 = (bf16[128,1024]{1,0:T(8,128)(2,1)S(1)}, bf16[128,1024]{1,0:T(8,128)(2,1)S(1)}, u32[]{:S(2)}, u32[]{:S(2)}) collective-permute-start(bf16[128,1024]{1,0:T(8,128)(2,1)S(1)} %get-tuple-element.123), channel_id=1, source_target_pairs={{0,6},{1,7},{2,4},{3,5},{4,10},{5,11},{6,8},{7,9},{8,14},{9,15},{1... | collective-permute-start | bytes 786440 | tf_op jit(solution)/shard_map/ppermute | solution.py:480
  114.5 2.0 %collective-permute-done.25.refs_5_ = bf16[128,1024]{1,0:T(8,128)(2,1)S(1)} collective-permute-done((bf16[128,1024]{1,0:T(8,128)(2,1)S(1)}, bf16[128,1024]{1,0:T(8,128)(2,1)S(1)}, u32[]{:S(2)}, u32[]{:S(2)}) %collective-permute-start.25) | collective-permute-done | bytes 262176 | tf_op jit(solution)/shard_map/ppermute | solution.py:470
  116.5 1.1 items_1_0.1
  117.6 2.2 %collective-permute-start.26 = (bf16[2176,128]{1,0:T(8,128)(2,1)S(1)}, bf16[2176,128]{1,0:T(8,128)(2,1)S(1)}, u32[]{:S(2)}, u32[]{:S(2)}) collective-permute-start(bf16[2176,128]{1,0:T(8,128)(2,1)S(1)} %get-tuple-element.137), channel_id=1, source_target_pairs={{0,4},{1,5},{2,6},{3,7},{4,8},{5,9},{6,10},{7,11},{8,12},{9,13},{1... | collective-permute-start | bytes 1671176 | tf_op jit(solution)/shard_map/ppermute | solution.py:480
  119.8 5.3 %users_1.1 = f32[2048,128]{1,0:T(8,128)} custom-call(s32[1,2]{1,0:T(1,128)S(1)} %bitcast.7, f32[2048,128]{1,0:T(8,128)S(1)} %get-tuple-element.77.users, f32[128,2048]{1,0:T(8,128)S(1)} %get-tuple-element.125.grad, bf16[128,2048]{1,0:T(8,128)(2,1)S(1)} %collective-permute-done.13.refs_8_.refs_0_.items, ...), custom_call_target="tpu_custom_call" | custom-call | flops 10000000000 | bytes 65536 | tf_op jit(solution)/shard_map/users_1/pallas_call | solution.py:358
  125.1 1.6 %collective-permute-done.28.refs_4_ = bf16[128,1024]{1,0:T(8,128)(2,1)S(1)} collective-permute-done((bf16[128,1024]{1,0:T(8,128)(2,1)S(1)}, bf16[128,1024]{1,0:T(8,128)(2,1)S(1)}, u32[]{:S(2)}, u32[]{:S(2)}) %collective-permute-start.28) | collective-permute-done | bytes 262176 | tf_op jit(solution)/shard_map/ppermute | solution.py:480
  126.7 0.3 collective-permute-done.30.refs_6_
  127.0 7.1 %collective-permute-done.26.refs_0_ = bf16[2176,128]{1,0:T(8,128)(2,1)S(1)} collective-permute-done((bf16[2176,128]{1,0:T(8,128)(2,1)S(1)}, bf16[2176,128]{1,0:T(8,128)(2,1)S(1)}, u32[]{:S(2)}, u32[]{:S(2)}) %collective-permute-start.26) | collective-permute-done | bytes 557088 | tf_op jit(solution)/shard_map/ppermute | solution.py:480
  134.1 1.7 %items_final.1 = f32[4096,128]{1,0:T(8,128)} custom-call(bf16[2176,128]{1,0:T(8,128)(2,1)S(1)} %collective-permute-done.26.refs_0_, bf16[128,2048]{1,0:T(8,128)(2,1)S(1)} %collective-permute-done.22.refs_1_, bf16[128,2048]{1,0:T(8,128)(2,1)S(1)} %collective-permute-done.19.refs_2_, bf16[128,1024]{1,0:T(8,128)(2,1)S(1)} %collective-permute-done.27.refs_3_, ...), custom_call_target="tpu_custom_call" | custom-call | flops 1200000000 | bytes 65536 | tf_op jit(solution)/shard_map/items_final/pallas_call | solution.py:579
  (38 shorter events, 0.7 us)
Async XLA Ops:
  9.7 18.4 %collective-permute-start.4 = (bf16[128,2176]{1,0:T(8,128)(2,1)S(1)}, bf16[128,2176]{1,0:T(8,128)(2,1)S(1)}, u32[]{:S(2)}, u32[]{:S(2)}) collective-permute-start(bf16[128,2176]{1,0:T(8,128)(2,1)S(1)} %get-tuple-element.95.refs_4_.refs_6_), channel_id=1, source_target_pairs={{0,1},{1,0},{2,3},{3,2},{4,5},{5,4},{6,7},{7,6},{8,9},{9,8},{10,11... | collective-permute-start | bytes 1671176 | tf_op jit(solution)/shard_map/ppermute | solution.py:470
  13.2 14.8 %collective-permute-start.5 = (bf16[128,2048]{1,0:T(8,128)(2,1)S(1)}, bf16[128,2048]{1,0:T(8,128)(2,1)S(1)}, u32[]{:S(2)}, u32[]{:S(2)}) collective-permute-start(bf16[128,2048]{1,0:T(8,128)(2,1)S(1)} %get-tuple-element.98), channel_id=1, source_target_pairs={{0,2},{1,3},{2,0},{3,1},{4,6},{5,7},{6,4},{7,5},{8,10},{9,11},{10,... | collective-permute-start | bytes 1572872 | tf_op jit(solution)/shard_map/ppermute | solution.py:470
  24.2 6.8 %copy-start = (f32[2048,128]{1,0:T(8,128)S(1)}, f32[2048,128]{1,0:T(8,128)}, u32[]{:S(2)}) copy-start(f32[2048,128]{1,0:T(8,128)} %users.1) | copy-start | bytes 3145732
  24.2 6.8 %copy-start.1 = (s32[2,1]{0,1:T(1,128)S(1)}, s32[2,1]{0,1:T(1,128)}, u32[]{:S(2)}) copy-start(s32[2,1]{0,1:T(1,128)} %param.13) | copy-start | bytes 28
  24.2 14.9 %collective-permute-start = (bf16[128,2048]{1,0:T(8,128)(2,1)S(1)}, bf16[128,2048]{1,0:T(8,128)(2,1)S(1)}, u32[]{:S(2)}, u32[]{:S(2)}) collective-permute-start(bf16[128,2048]{1,0:T(8,128)(2,1)S(1)} %get-tuple-element.82), channel_id=1, source_target_pairs={{0,1},{1,0},{2,3},{3,2},{4,5},{5,4},{6,7},{7,6},{8,9},{9,8},{10,11... | collective-permute-start | bytes 1572872 | tf_op jit(solution)/shard_map/ppermute | solution.py:470
  24.3 15.0 %collective-permute-start.1 = (bf16[128,2048]{1,0:T(8,128)(2,1)S(1)}, bf16[128,2048]{1,0:T(8,128)(2,1)S(1)}, u32[]{:S(2)}, u32[]{:S(2)}) collective-permute-start(bf16[128,2048]{1,0:T(8,128)(2,1)S(1)} %get-tuple-element.85), channel_id=1, source_target_pairs={{0,2},{1,3},{2,0},{3,1},{4,6},{5,7},{6,4},{7,5},{8,10},{9,11},{10,... | collective-permute-start | bytes 1572872 | tf_op jit(solution)/shard_map/ppermute | solution.py:470
  28.2 17.4 %collective-permute-start.6 = (bf16[128,1152]{1,0:T(8,128)(2,1)S(1)}, bf16[128,1152]{1,0:T(8,128)(2,1)S(1)}, u32[]{:S(2)}, u32[]{:S(2)}) collective-permute-start(bf16[128,1152]{1,0:T(8,128)(2,1)S(1)} %get-tuple-element.100), channel_id=1, source_target_pairs={{0,2},{1,3},{2,0},{3,1},{4,6},{5,7},{6,4},{7,5},{8,10},{9,11},{10,... | collective-permute-start | bytes 884744 | tf_op jit(solution)/shard_map/ppermute | solution.py:470
  30.3 13.3 %collective-permute-start.7 = (bf16[128,1024]{1,0:T(8,128)(2,1)S(1)}, bf16[128,1024]{1,0:T(8,128)(2,1)S(1)}, u32[]{:S(2)}, u32[]{:S(2)}) collective-permute-start(bf16[128,1024]{1,0:T(8,128)(2,1)S(1)} %get-tuple-element.101), channel_id=1, source_target_pairs={{0,1},{1,0},{2,3},{3,2},{4,5},{5,4},{6,7},{7,6},{8,9},{9,8},{10,11... | collective-permute-start | bytes 786440 | tf_op jit(solution)/shard_map/ppermute | solution.py:470
  39.4 10.7 %collective-permute-start.2 = (bf16[128,1024]{1,0:T(8,128)(2,1)S(1)}, bf16[128,1024]{1,0:T(8,128)(2,1)S(1)}, u32[]{:S(2)}, u32[]{:S(2)}) collective-permute-start(bf16[128,1024]{1,0:T(8,128)(2,1)S(1)} %get-tuple-element.87), channel_id=1, source_target_pairs={{0,2},{1,3},{2,0},{3,1},{4,6},{5,7},{6,4},{7,5},{8,10},{9,11},{10,... | collective-permute-start | bytes 786440 | tf_op jit(solution)/shard_map/ppermute | solution.py:470
  41.5 8.6 %collective-permute-start.3 = (bf16[128,1024]{1,0:T(8,128)(2,1)S(1)}, bf16[128,1024]{1,0:T(8,128)(2,1)S(1)}, u32[]{:S(2)}, u32[]{:S(2)}) collective-permute-start(bf16[128,1024]{1,0:T(8,128)(2,1)S(1)} %get-tuple-element.88), channel_id=1, source_target_pairs={{0,1},{1,0},{2,3},{3,2},{4,5},{5,4},{6,7},{7,6},{8,9},{9,8},{10,11... | collective-permute-start | bytes 786440 | tf_op jit(solution)/shard_map/ppermute | solution.py:470
  46.2 12.4 %collective-permute-start.14 = (bf16[128,2048]{1,0:T(8,128)(2,1)S(1)}, bf16[128,2048]{1,0:T(8,128)(2,1)S(1)}, u32[]{:S(2)}, u32[]{:S(2)}) collective-permute-start(bf16[128,2048]{1,0:T(8,128)(2,1)S(1)} %get-tuple-element.107), channel_id=1, source_target_pairs={{0,5},{1,4},{2,7},{3,6},{4,9},{5,8},{6,11},{7,10},{8,13},{9,12},{1... | collective-permute-start | bytes 1572872 | tf_op jit(solution)/shard_map/ppermute | solution.py:480
  46.3 17.1 %collective-permute-start.15 = (bf16[128,2048]{1,0:T(8,128)(2,1)S(1)}, bf16[128,2048]{1,0:T(8,128)(2,1)S(1)}, u32[]{:S(2)}, u32[]{:S(2)}) collective-permute-start(bf16[128,2048]{1,0:T(8,128)(2,1)S(1)} %get-tuple-element.107), channel_id=1, source_target_pairs={{0,6},{1,7},{2,4},{3,5},{4,10},{5,11},{6,8},{7,9},{8,14},{9,15},{1... | collective-permute-start | bytes 1572872 | tf_op jit(solution)/shard_map/ppermute | solution.py:480
  50.7 20.5 %collective-permute-start.9 = (bf16[128,2048]{1,0:T(8,128)(2,1)S(1)}, bf16[128,2048]{1,0:T(8,128)(2,1)S(1)}, u32[]{:S(2)}, u32[]{:S(2)}) collective-permute-start(bf16[128,2048]{1,0:T(8,128)(2,1)S(1)} %items_0_1.1), channel_id=1, source_target_pairs={{0,5},{1,4},{2,7},{3,6},{4,9},{5,8},{6,11},{7,10},{8,13},{9,12},{1... | collective-permute-start | bytes 1572872 | tf_op jit(solution)/shard_map/ppermute | solution.py:480
  50.8 24.3 %collective-permute-start.10 = (bf16[128,2048]{1,0:T(8,128)(2,1)S(1)}, bf16[128,2048]{1,0:T(8,128)(2,1)S(1)}, u32[]{:S(2)}, u32[]{:S(2)}) collective-permute-start(bf16[128,2048]{1,0:T(8,128)(2,1)S(1)} %items_0_1.1), channel_id=1, source_target_pairs={{0,6},{1,7},{2,4},{3,5},{4,10},{5,11},{6,8},{7,9},{8,14},{9,15},{1... | collective-permute-start | bytes 1572872 | tf_op jit(solution)/shard_map/ppermute | solution.py:480
  52.7 27.9 %collective-permute-start.13 = (bf16[128,2048]{1,0:T(8,128)(2,1)S(1)}, bf16[128,2048]{1,0:T(8,128)(2,1)S(1)}, u32[]{:S(2)}, u32[]{:S(2)}) collective-permute-start(bf16[128,2048]{1,0:T(8,128)(2,1)S(1)} %get-tuple-element.107), channel_id=1, source_target_pairs={{0,4},{1,5},{2,6},{3,7},{4,8},{5,9},{6,10},{7,11},{8,12},{9,13},{1... | collective-permute-start | bytes 1572872 | tf_op jit(solution)/shard_map/ppermute | solution.py:480
  58.6 22.2 %collective-permute-start.16 = (bf16[128,1024]{1,0:T(8,128)(2,1)S(1)}, bf16[128,1024]{1,0:T(8,128)(2,1)S(1)}, u32[]{:S(2)}, u32[]{:S(2)}) collective-permute-start(bf16[128,1024]{1,0:T(8,128)(2,1)S(1)} %slice.18), channel_id=1, source_target_pairs={{0,2},{1,3},{2,0},{3,1},{4,6},{5,7},{6,4},{7,5},{8,10},{9,11},{10,... | collective-permute-start | bytes 786440 | tf_op jit(solution)/shard_map/ppermute | solution.py:470
  63.4 17.4 %collective-permute-start.17 = (bf16[128,1024]{1,0:T(8,128)(2,1)S(1)}, bf16[128,1024]{1,0:T(8,128)(2,1)S(1)}, u32[]{:S(2)}, u32[]{:S(2)}) collective-permute-start(bf16[128,1024]{1,0:T(8,128)(2,1)S(1)} %slice.19), channel_id=1, source_target_pairs={{0,1},{1,0},{2,3},{3,2},{4,5},{5,4},{6,7},{7,6},{8,9},{9,8},{10,11... | collective-permute-start | bytes 786440 | tf_op jit(solution)/shard_map/ppermute | solution.py:470
  71.2 19.3 %collective-permute-start.8 = (bf16[128,2048]{1,0:T(8,128)(2,1)S(1)}, bf16[128,2048]{1,0:T(8,128)(2,1)S(1)}, u32[]{:S(2)}, u32[]{:S(2)}) collective-permute-start(bf16[128,2048]{1,0:T(8,128)(2,1)S(1)} %items_0_1.1), channel_id=1, source_target_pairs={{0,4},{1,5},{2,6},{3,7},{4,8},{5,9},{6,10},{7,11},{8,12},{9,13},{1... | collective-permute-start | bytes 1572872 | tf_op jit(solution)/shard_map/ppermute | solution.py:480
  75.1 15.4 %collective-permute-start.11 = (bf16[128,1024]{1,0:T(8,128)(2,1)S(1)}, bf16[128,1024]{1,0:T(8,128)(2,1)S(1)}, u32[]{:S(2)}, u32[]{:S(2)}) collective-permute-start(bf16[128,1024]{1,0:T(8,128)(2,1)S(1)} %slice.16), channel_id=1, source_target_pairs={{0,2},{1,3},{2,0},{3,1},{4,6},{5,7},{6,4},{7,5},{8,10},{9,11},{10,... | collective-permute-start | bytes 786440 | tf_op jit(solution)/shard_map/ppermute | solution.py:470
  80.6 9.9 %collective-permute-start.12 = (bf16[128,1024]{1,0:T(8,128)(2,1)S(1)}, bf16[128,1024]{1,0:T(8,128)(2,1)S(1)}, u32[]{:S(2)}, u32[]{:S(2)}) collective-permute-start(bf16[128,1024]{1,0:T(8,128)(2,1)S(1)} %slice.17), channel_id=1, source_target_pairs={{0,1},{1,0},{2,3},{3,2},{4,5},{5,4},{6,7},{7,6},{8,9},{9,8},{10,11... | collective-permute-start | bytes 786440 | tf_op jit(solution)/shard_map/ppermute | solution.py:470
  87.5 16.8 %collective-permute-start.21 = (bf16[128,2176]{1,0:T(8,128)(2,1)S(1)}, bf16[128,2176]{1,0:T(8,128)(2,1)S(1)}, u32[]{:S(2)}, u32[]{:S(2)}) collective-permute-start(bf16[128,2176]{1,0:T(8,128)(2,1)S(1)} %get-tuple-element.127.refs_4_.refs_6_), channel_id=1, source_target_pairs={{0,1},{1,0},{2,3},{3,2},{4,5},{5,4},{6,7},{7,6},{8,9},{9,8},{10,11... | collective-permute-start | bytes 1671176 | tf_op jit(solution)/shard_map/ppermute | solution.py:470
  90.5 13.8 %collective-permute-start.22 = (bf16[128,2048]{1,0:T(8,128)(2,1)S(1)}, bf16[128,2048]{1,0:T(8,128)(2,1)S(1)}, u32[]{:S(2)}, u32[]{:S(2)}) collective-permute-start(bf16[128,2048]{1,0:T(8,128)(2,1)S(1)} %collective-permute-done.8.refs_8_.refs_5_), channel_id=1, source_target_pairs={{0,4},{1,5},{2,6},{3,7},{4,8},{5,9},{6,10},{7,11},{8,12},{9,13},{1... | collective-permute-start | bytes 1572872 | tf_op jit(solution)/shard_map/ppermute | solution.py:480
  90.5 13.0 %collective-permute-start.23 = (bf16[128,2048]{1,0:T(8,128)(2,1)S(1)}, bf16[128,2048]{1,0:T(8,128)(2,1)S(1)}, u32[]{:S(2)}, u32[]{:S(2)}) collective-permute-start(bf16[128,2048]{1,0:T(8,128)(2,1)S(1)} %get-tuple-element.132), channel_id=1, source_target_pairs={{0,2},{1,3},{2,0},{3,1},{4,6},{5,7},{6,4},{7,5},{8,10},{9,11},{10,... | collective-permute-start | bytes 1572872 | tf_op jit(solution)/shard_map/ppermute | solution.py:470
  97.2 15.5 %collective-permute-start.19 = (bf16[128,2048]{1,0:T(8,128)(2,1)S(1)}, bf16[128,2048]{1,0:T(8,128)(2,1)S(1)}, u32[]{:S(2)}, u32[]{:S(2)}) collective-permute-start(bf16[128,2048]{1,0:T(8,128)(2,1)S(1)} %get-tuple-element.117), channel_id=1, source_target_pairs={{0,4},{1,5},{2,6},{3,7},{4,8},{5,9},{6,10},{7,11},{8,12},{9,13},{1... | collective-permute-start | bytes 1572872 | tf_op jit(solution)/shard_map/ppermute | solution.py:480
  97.3 10.3 %collective-permute-start.18 = (bf16[128,1024]{1,0:T(8,128)(2,1)S(1)}, bf16[128,1024]{1,0:T(8,128)(2,1)S(1)}, u32[]{:S(2)}, u32[]{:S(2)}) collective-permute-start(bf16[128,1024]{1,0:T(8,128)(2,1)S(1)} %get-tuple-element.115), channel_id=1, source_target_pairs={{0,1},{1,0},{2,3},{3,2},{4,5},{5,4},{6,7},{7,6},{8,9},{9,8},{10,11... | collective-permute-start | bytes 786440 | tf_op jit(solution)/shard_map/ppermute | solution.py:470
  103.5 9.2 %collective-permute-start.20 = (bf16[128,1024]{1,0:T(8,128)(2,1)S(1)}, bf16[128,1024]{1,0:T(8,128)(2,1)S(1)}, u32[]{:S(2)}, u32[]{:S(2)}) collective-permute-start(bf16[128,1024]{1,0:T(8,128)(2,1)S(1)} %get-tuple-element.120), channel_id=1, source_target_pairs={{0,2},{1,3},{2,0},{3,1},{4,6},{5,7},{6,4},{7,5},{8,10},{9,11},{10,... | collective-permute-start | bytes 786440 | tf_op jit(solution)/shard_map/ppermute | solution.py:470
  104.4 12.1 %collective-permute-start.24 = (bf16[128,1152]{1,0:T(8,128)(2,1)S(1)}, bf16[128,1152]{1,0:T(8,128)(2,1)S(1)}, u32[]{:S(2)}, u32[]{:S(2)}) collective-permute-start(bf16[128,1152]{1,0:T(8,128)(2,1)S(1)} %get-tuple-element.135), channel_id=1, source_target_pairs={{0,2},{1,3},{2,0},{3,1},{4,6},{5,7},{6,4},{7,5},{8,10},{9,11},{10,... | collective-permute-start | bytes 884744 | tf_op jit(solution)/shard_map/ppermute | solution.py:470
  105.7 10.8 %collective-permute-start.25 = (bf16[128,1024]{1,0:T(8,128)(2,1)S(1)}, bf16[128,1024]{1,0:T(8,128)(2,1)S(1)}, u32[]{:S(2)}, u32[]{:S(2)}) collective-permute-start(bf16[128,1024]{1,0:T(8,128)(2,1)S(1)} %get-tuple-element.136), channel_id=1, source_target_pairs={{0,1},{1,0},{2,3},{3,2},{4,5},{5,4},{6,7},{7,6},{8,9},{9,8},{10,11... | collective-permute-start | bytes 786440 | tf_op jit(solution)/shard_map/ppermute | solution.py:470
  107.6 17.4 %collective-permute-start.27 = (bf16[128,1024]{1,0:T(8,128)(2,1)S(1)}, bf16[128,1024]{1,0:T(8,128)(2,1)S(1)}, u32[]{:S(2)}, u32[]{:S(2)}) collective-permute-start(bf16[128,1024]{1,0:T(8,128)(2,1)S(1)} %get-tuple-element.138), channel_id=1, source_target_pairs={{0,5},{1,4},{2,7},{3,6},{4,9},{5,8},{6,11},{7,10},{8,13},{9,12},{1... | collective-permute-start | bytes 786440 | tf_op jit(solution)/shard_map/ppermute | solution.py:480
  112.7 12.4 %collective-permute-start.29 = (bf16[128,1024]{1,0:T(8,128)(2,1)S(1)}, bf16[128,1024]{1,0:T(8,128)(2,1)S(1)}, u32[]{:S(2)}, u32[]{:S(2)}) collective-permute-start(bf16[128,1024]{1,0:T(8,128)(2,1)S(1)} %get-tuple-element.139), channel_id=1, source_target_pairs={{0,6},{1,7},{2,4},{3,5},{4,10},{5,11},{6,8},{7,9},{8,14},{9,15},{1... | collective-permute-start | bytes 786440 | tf_op jit(solution)/shard_map/ppermute | solution.py:480
  112.8 13.9 %collective-permute-start.28 = (bf16[128,1024]{1,0:T(8,128)(2,1)S(1)}, bf16[128,1024]{1,0:T(8,128)(2,1)S(1)}, u32[]{:S(2)}, u32[]{:S(2)}) collective-permute-start(bf16[128,1024]{1,0:T(8,128)(2,1)S(1)} %get-tuple-element.123), channel_id=1, source_target_pairs={{0,6},{1,7},{2,4},{3,5},{4,10},{5,11},{6,8},{7,9},{8,14},{9,15},{1... | collective-permute-start | bytes 786440 | tf_op jit(solution)/shard_map/ppermute | solution.py:480
  114.5 5.3 %copy-start.2 = (s32[2,1]{0,1:T(1,128)S(1)}, s32[2,1]{0,1:T(1,128)}, u32[]{:S(2)}) copy-start(s32[2,1]{0,1:T(1,128)} %param.13) | copy-start | bytes 28
  116.5 10.5 %collective-permute-start.30 = (bf16[128,1024]{1,0:T(8,128)(2,1)S(1)}, bf16[128,1024]{1,0:T(8,128)(2,1)S(1)}, u32[]{:S(2)}, u32[]{:S(2)}) collective-permute-start(bf16[128,1024]{1,0:T(8,128)(2,1)S(1)} %get-tuple-element.124), channel_id=1, source_target_pairs={{0,5},{1,4},{2,7},{3,6},{4,9},{5,8},{6,11},{7,10},{8,13},{9,12},{1... | collective-permute-start | bytes 786440 | tf_op jit(solution)/shard_map/ppermute | solution.py:480
  117.6 16.5 %collective-permute-start.26 = (bf16[2176,128]{1,0:T(8,128)(2,1)S(1)}, bf16[2176,128]{1,0:T(8,128)(2,1)S(1)}, u32[]{:S(2)}, u32[]{:S(2)}) collective-permute-start(bf16[2176,128]{1,0:T(8,128)(2,1)S(1)} %get-tuple-element.137), channel_id=1, source_target_pairs={{0,4},{1,5},{2,6},{3,7},{4,8},{5,9},{6,10},{7,11},{8,12},{9,13},{1... | collective-permute-start | bytes 1671176 | tf_op jit(solution)/shard_map/ppermute | solution.py:480

commit v12 on v10

--- a/solution.py
+++ b/solution.py
@@ -152,7 +152,7 @@
         here = ((col >> bits_tile) & (CHUNKS - 1)) == chunk
         return found + jnp.where(here & (t < count), 1, 0).astype(jnp.int32)
 
-    total = lax.fori_loop(0, col_ref.shape[3], pick, jnp.int32(0), unroll=8)
+    total = lax.fori_loop(0, col_ref.shape[3], pick, jnp.int32(0), unroll=16)
 
     def fetch(i):
         return pltpu.make_async_copy(ratings.at[epoch, 0, 0, slots[i]], held.at[i], sem_tile.at[i])
@@ -250,7 +250,11 @@
         add(adds)
         return 0
 
-    lax.fori_loop(0, groups, step, 0)
+    lax.fori_loop(0, groups - 1, step, 0)
+
+    @pl.when(total > 0)
+    def _():
+        add(back(groups - 1))
 
     for out, columns in zip(outs, chunk_columns(members, rows, direct)):
         at = 0

time: 134 us -> 134 us (level)
  waiting for transfers between devices: 56.4 us -> 47 us
  starting transfers between devices: 35.8 us -> 42.3 us
  Pallas kernels: 40.6 us -> 44.3 us
    ppermute x18, waiting for transfers between devices: 25.5 us -> 16.3 us  [swapped(): return lax.ppermute(value, 'grp', [(i, i ^ bit) for i in range(length)])]
    ppermute x13, starting transfers between devices: 13.7 us -> 18.6 us  [moved(): return lax.ppermute(value, ('blk', 'grp'), pairs)]
    pallas_call x4, Pallas kernels: 26 us -> 29.7 us  [tile_call(): pl.pallas_call(functools.partial(tile_kernel, epoch, chunk, direct, membe...]
    ppermute x18, starting transfers between devices: 22.1 us -> 23.7 us  [swapped(): return lax.ppermute(value, 'grp', [(i, i ^ bit) for i in range(length)])]
  transfers between devices with their start and end apart: 31 -> 31, of which waited for: 17 -> 16; matrix products, arithmetic and copies ran while one was open for 0% -> 0% of each run, Pallas kernels for 24% -> 25%
where the time goes in v12:
time: 134 us; the launch traced here: 135 us
  waiting for transfers between devices  47 us (35%)
  Pallas kernels  44.3 us (33%)
  starting transfers between devices  42.3 us (32%)
    ppermute x13, waiting for transfers between devices, moved(): return lax.ppermute(value, ('blk', 'grp'), pairs)  30.7 us
    pallas_call x4, Pallas kernels, tile_call(): pl.pallas_call(functools.partial(tile_kernel, epoch, chunk, direct, membe...  29.7 us
    ppermute x18, starting transfers between devices, swapped(): return lax.ppermute(value, 'grp', [(i, i ^ bit) for i in range(length)])  23.7 us
    ppermute x13, starting transfers between devices, moved(): return lax.ppermute(value, ('blk', 'grp'), pairs)  18.6 us
    ppermute x18, waiting for transfers between devices, swapped(): return lax.ppermute(value, 'grp', [(i, i ^ bit) for i in range(length)])  16.3 us
    pallas_call x2, Pallas kernels, user_call(): pl.pallas_call(functools.partial(user_kernel, epoch, block_rows), out_sha...  10.1 us
  transfers between devices with their start and end apart: 31, of which 16 were waited for; matrix products, arithmetic and copies ran while one was open for 0% of the time, Pallas kernels for 25%

profile of v12, /device:TPU:0, one launch (start us, length us, event | category | flops | bytes accessed | tf_op | source)
XLA Modules:
  0.0 134.6 jit_solution(2318248220567648597)
XLA Ops:
  0.6 8.4 %tiles_0_0.1 = (bf16[128,2176]{1,0:T(8,128)(2,1)S(1)}, bf16[128,2048]{1,0:T(8,128)(2,1)S(1)}, bf16[128,2048]{1,0:T(8,128)(2,1)S(1)}, bf16[128,2048]{1,0:T(8,128)...) custom-call(s32[2,1,1,64]{3,2,1,0:T(1,128)} %refs_0_.7, ...), custom_call_target="tpu_custom_call" | custom-call | flops 16000000000 | bytes 65536 | tf_op jit(solution)/shard_map/tiles_0_0/pallas_call | solution.py:323
  9.0 2.0 %collective-permute-start.4 = (bf16[128,2176]{1,0:T(8,128)(2,1)S(1)}, bf16[128,2176]{1,0:T(8,128)(2,1)S(1)}, u32[]{:S(2)}, u32[]{:S(2)}) collective-permute-start(bf16[128,2176]{1,0:T(8,128)(2,1)S(1)} %get-tuple-element.93.refs_4_.refs_6_), channel_id=1, source_target_pairs={{0,1},{1,0},{2,3},{3,2},{4,5},{5,4},{6,7},{7,6},{8,9},{9,8},{10,11... | collective-permute-start | bytes 1671176 | tf_op jit(solution)/shard_map/ppermute | solution.py:474
  11.0 2.6 %collective-permute-start.5 = (bf16[128,2048]{1,0:T(8,128)(2,1)S(1)}, bf16[128,2048]{1,0:T(8,128)(2,1)S(1)}, u32[]{:S(2)}, u32[]{:S(2)}) collective-permute-start(bf16[128,2048]{1,0:T(8,128)(2,1)S(1)} %get-tuple-element.96), channel_id=1, source_target_pairs={{0,2},{1,3},{2,0},{3,1},{4,6},{5,7},{6,4},{7,5},{8,10},{9,11},{10,... | collective-permute-start | bytes 1572872 | tf_op jit(solution)/shard_map/ppermute | solution.py:474
  13.6 7.6 %tiles_0_1.1 = (bf16[128,2048]{1,0:T(8,128)(2,1)S(1)}, bf16[128,2048]{1,0:T(8,128)(2,1)S(1)}, bf16[128,2048]{1,0:T(8,128)(2,1)S(1)}, bf16[128,2048]{1,0:T(8,128)...) custom-call(s32[2,1,1,64]{3,2,1,0:T(1,128)} %refs_0_.7, ...), custom_call_target="tpu_custom_call" | custom-call | flops 16000000000 | bytes 65536 | tf_op jit(solution)/shard_map/tiles_0_1/pallas_call | solution.py:323
  21.3 1.2 collective-permute-start.1
  22.5 3.9 %collective-permute-done.5.refs_3_.refs_4_ = bf16[128,2048]{1,0:T(8,128)(2,1)S(1)} collective-permute-done((bf16[128,2048]{1,0:T(8,128)(2,1)S(1)}, bf16[128,2048]{1,0:T(8,128)(2,1)S(1)}, u32[]{:S(2)}, u32[]{:S(2)}) %collective-permute-start.5) | collective-permute-done | bytes 524320 | tf_op jit(solution)/shard_map/ppermute | solution.py:474
  26.5 2.1 %collective-permute-start.6 = (bf16[128,1152]{1,0:T(8,128)(2,1)S(1)}, bf16[128,1152]{1,0:T(8,128)(2,1)S(1)}, u32[]{:S(2)}, u32[]{:S(2)}) collective-permute-start(bf16[128,1152]{1,0:T(8,128)(2,1)S(1)} %get-tuple-element.98), channel_id=1, source_target_pairs={{0,2},{1,3},{2,0},{3,1},{4,6},{5,7},{6,4},{7,5},{8,10},{9,11},{10,... | collective-permute-start | bytes 884744 | tf_op jit(solution)/shard_map/ppermute | solution.py:474
  28.6 0.7 collective-permute-start.7
  29.3 4.8 %users_0.1 = (f32[2048,128]{1,0:T(8,128)S(1)}, bf16[2048,128]{1,0:T(8,128)(2,1)S(1)}, bf16[128,2048]{1,0:T(8,128)(2,1)S(1)}, bf16[128,128]{1,0:T(8,128)(2,1)S(1)}) custom-call(s32[1,2]{1,0:T(1,128)S(1)} %bitcast.6, f32[2048,128]{1,0:T(8,128)S(1)} %copy-done, f32[128,2048]{1,0:T(8,128)S(1)} %get-tuple-element.72.grad, ...), custom_call_target="tpu_custom_call" | custom-call | flops 10000000000 | bytes 65536 | tf_op jit(solution)/shard_map/users_0/pallas_call | solution.py:362
  34.1 2.0 %collective-permute-done.refs_1_ = bf16[128,2048]{1,0:T(8,128)(2,1)S(1)} collective-permute-done((bf16[128,2048]{1,0:T(8,128)(2,1)S(1)}, bf16[128,2048]{1,0:T(8,128)(2,1)S(1)}, u32[]{:S(2)}, u32[]{:S(2)}) %collective-permute-start) | collective-permute-done | bytes 524320 | tf_op jit(solution)/shard_map/ppermute | solution.py:474
  36.1 1.5 %collective-permute-done.1.refs_3_.refs_4_ = bf16[128,2048]{1,0:T(8,128)(2,1)S(1)} collective-permute-done((bf16[128,2048]{1,0:T(8,128)(2,1)S(1)}, bf16[128,2048]{1,0:T(8,128)(2,1)S(1)}, u32[]{:S(2)}, u32[]{:S(2)}) %collective-permute-start.1) | collective-permute-done | bytes 524320 | tf_op jit(solution)/shard_map/ppermute | solution.py:474
  37.7 2.2 %collective-permute-start.2 = (bf16[128,1024]{1,0:T(8,128)(2,1)S(1)}, bf16[128,1024]{1,0:T(8,128)(2,1)S(1)}, u32[]{:S(2)}, u32[]{:S(2)}) collective-permute-start(bf16[128,1024]{1,0:T(8,128)(2,1)S(1)} %get-tuple-element.85), channel_id=1, source_target_pairs={{0,2},{1,3},{2,0},{3,1},{4,6},{5,7},{6,4},{7,5},{8,10},{9,11},{10,... | collective-permute-start | bytes 786440 | tf_op jit(solution)/shard_map/ppermute | solution.py:474
  39.8 0.7 collective-permute-start.3
  40.6 1.2 collective-permute-done.7.refs_5_
  41.7 2.2 %collective-permute-done.6.refs_2_.refs_8_ = bf16[128,1152]{1,0:T(8,128)(2,1)S(1)} collective-permute-done((bf16[128,1152]{1,0:T(8,128)(2,1)S(1)}, bf16[128,1152]{1,0:T(8,128)(2,1)S(1)}, u32[]{:S(2)}, u32[]{:S(2)}) %collective-permute-start.6) | collective-permute-done | bytes 294944 | tf_op jit(solution)/shard_map/ppermute | solution.py:474
  43.9 0.6 items_0_0.1
  44.7 3.2 %collective-permute-start.15 = (bf16[128,2048]{1,0:T(8,128)(2,1)S(1)}, bf16[128,2048]{1,0:T(8,128)(2,1)S(1)}, u32[]{:S(2)}, u32[]{:S(2)}) collective-permute-start(bf16[128,2048]{1,0:T(8,128)(2,1)S(1)} %get-tuple-element.105), channel_id=1, source_target_pairs={{0,6},{1,7},{2,4},{3,5},{4,10},{5,11},{6,8},{7,9},{8,14},{9,15},{1... | collective-permute-start | bytes 1572872 | tf_op jit(solution)/shard_map/ppermute | solution.py:484
  47.9 1.4 %collective-permute-done.2.refs_2_ = bf16[128,1024]{1,0:T(8,128)(2,1)S(1)} collective-permute-done((bf16[128,1024]{1,0:T(8,128)(2,1)S(1)}, bf16[128,1024]{1,0:T(8,128)(2,1)S(1)}, u32[]{:S(2)}, u32[]{:S(2)}) %collective-permute-start.2) | collective-permute-done | bytes 262176 | tf_op jit(solution)/shard_map/ppermute | solution.py:474
  49.3 0.6 items_0_1.1
  49.9 0.5 collective-permute-start.9
  50.3 2.1 %collective-permute-start.10 = (bf16[128,2048]{1,0:T(8,128)(2,1)S(1)}, bf16[128,2048]{1,0:T(8,128)(2,1)S(1)}, u32[]{:S(2)}, u32[]{:S(2)}) collective-permute-start(bf16[128,2048]{1,0:T(8,128)(2,1)S(1)} %items_0_1.1), channel_id=1, source_target_pairs={{0,6},{1,7},{2,4},{3,5},{4,10},{5,11},{6,8},{7,9},{8,14},{9,15},{1... | collective-permute-start | bytes 1572872 | tf_op jit(solution)/shard_map/ppermute | solution.py:484
  52.5 5.2 %collective-permute-done.14.refs_9_.refs_1_ = bf16[128,2048]{1,0:T(8,128)(2,1)S(1)} collective-permute-done((bf16[128,2048]{1,0:T(8,128)(2,1)S(1)}, bf16[128,2048]{1,0:T(8,128)(2,1)S(1)}, u32[]{:S(2)}, u32[]{:S(2)}) %collective-permute-start.14) | collective-permute-done | bytes 524320 | tf_op jit(solution)/shard_map/ppermute | solution.py:484
  57.7 1.3 collective-permute-start.16
  59.0 3.1 %collective-permute-done.15.refs_10_.refs_2_ = bf16[128,2048]{1,0:T(8,128)(2,1)S(1)} collective-permute-done((bf16[128,2048]{1,0:T(8,128)(2,1)S(1)}, bf16[128,2048]{1,0:T(8,128)(2,1)S(1)}, u32[]{:S(2)}, u32[]{:S(2)}) %collective-permute-start.15) | collective-permute-done | bytes 524320 | tf_op jit(solution)/shard_map/ppermute | solution.py:484
  62.1 1.7 %collective-permute-start.17 = (bf16[128,1024]{1,0:T(8,128)(2,1)S(1)}, bf16[128,1024]{1,0:T(8,128)(2,1)S(1)}, u32[]{:S(2)}, u32[]{:S(2)}) collective-permute-start(bf16[128,1024]{1,0:T(8,128)(2,1)S(1)} %slice.19), channel_id=1, source_target_pairs={{0,1},{1,0},{2,3},{3,2},{4,5},{5,4},{6,7},{7,6},{8,9},{9,8},{10,11... | collective-permute-start | bytes 786440 | tf_op jit(solution)/shard_map/ppermute | solution.py:474
  63.8 8.0 %collective-permute-done.9.refs_9_.refs_6_ = bf16[128,2048]{1,0:T(8,128)(2,1)S(1)} collective-permute-done((bf16[128,2048]{1,0:T(8,128)(2,1)S(1)}, bf16[128,2048]{1,0:T(8,128)(2,1)S(1)}, u32[]{:S(2)}, u32[]{:S(2)}) %collective-permute-start.9) | collective-permute-done | bytes 524320 | tf_op jit(solution)/shard_map/ppermute | solution.py:484
  71.7 0.7 collective-permute-start.8
  72.4 1.8 %collective-permute-done.10.refs_10_.refs_7_ = bf16[128,2048]{1,0:T(8,128)(2,1)S(1)} collective-permute-done((bf16[128,2048]{1,0:T(8,128)(2,1)S(1)}, bf16[128,2048]{1,0:T(8,128)(2,1)S(1)}, u32[]{:S(2)}, u32[]{:S(2)}) %collective-permute-start.10) | collective-permute-done | bytes 524320 | tf_op jit(solution)/shard_map/ppermute | solution.py:484
  74.2 1.8 %collective-permute-start.11 = (bf16[128,1024]{1,0:T(8,128)(2,1)S(1)}, bf16[128,1024]{1,0:T(8,128)(2,1)S(1)}, u32[]{:S(2)}, u32[]{:S(2)}) collective-permute-start(bf16[128,1024]{1,0:T(8,128)(2,1)S(1)} %slice.16), channel_id=1, source_target_pairs={{0,2},{1,3},{2,0},{3,1},{4,6},{5,7},{6,4},{7,5},{8,10},{9,11},{10,... | collective-permute-start | bytes 786440 | tf_op jit(solution)/shard_map/ppermute | solution.py:474
  76.0 1.5 %collective-permute-done.13.refs_8_.refs_0_.items = bf16[128,2048]{1,0:T(8,128)(2,1)S(1)} collective-permute-done((bf16[128,2048]{1,0:T(8,128)(2,1)S(1)}, bf16[128,2048]{1,0:T(8,128)(2,1)S(1)}, u32[]{:S(2)}, u32[]{:S(2)}) %collective-permute-start.13) | collective-permute-done | bytes 524320 | tf_op jit(solution)/shard_map/ppermute | solution.py:484
  77.6 1.5 %collective-permute-start.12 = (bf16[128,1024]{1,0:T(8,128)(2,1)S(1)}, bf16[128,1024]{1,0:T(8,128)(2,1)S(1)}, u32[]{:S(2)}, u32[]{:S(2)}) collective-permute-start(bf16[128,1024]{1,0:T(8,128)(2,1)S(1)} %slice.17), channel_id=1, source_target_pairs={{0,1},{1,0},{2,3},{3,2},{4,5},{5,4},{6,7},{7,6},{8,9},{9,8},{10,11... | collective-permute-start | bytes 786440 | tf_op jit(solution)/shard_map/ppermute | solution.py:474
  79.0 0.3 collective-permute-done.16.refs_11_.refs_3_
  79.3 8.3 %tiles_1_0.1 = (bf16[128,2176]{1,0:T(8,128)(2,1)S(1)}, bf16[128,2048]{1,0:T(8,128)(2,1)S(1)}, bf16[128,2048]{1,0:T(8,128)(2,1)S(1)}, bf16[128,2048]{1,0:T(8,128)(2,1)S(1)}, f32[128,2048]{1,0:T(8,128)S(1)}) custom-call(s32[2,1,1,64]{3,2,1,0:T(1,128)} %refs_0_.7, s32[2,1,1,64]{3,2,1,0:T(1,128)} %refs_1_.7, s32[1,2]{1,0:T(1,128)} %bitcast.10, s32[1,2]{1,0:T(1,128)} %bitcast.4, ...), custom_call_target="tpu_custom_call" | custom-call | flops 16000000000 | bytes 65536 | tf_op jit(solution)/shard_map/tiles_1_0/pallas_call | solution.py:323
  87.7 1.3 collective-permute-start.23
  89.1 5.5 %tiles_1_1.1 = (bf16[128,1024]{1,0:T(8,128)(2,1)S(1)}, bf16[128,1024]{1,0:T(8,128)(2,1)S(1)}, bf16[128,1024]{1,0:T(8,128)(2,1)S(1)}, bf16[128,1024]{1,0:T(8,128)...) custom-call(s32[2,1,1,64]{3,2,1,0:T(1,128)} %refs_0_.7, ...), custom_call_target="tpu_custom_call" | custom-call | flops 16000000000 | bytes 65536 | tf_op jit(solution)/shard_map/tiles_1_1/pallas_call | solution.py:323
  94.6 3.1 %collective-permute-start.20 = (bf16[128,2048]{1,0:T(8,128)(2,1)S(1)}, bf16[128,2048]{1,0:T(8,128)(2,1)S(1)}, u32[]{:S(2)}, u32[]{:S(2)}) collective-permute-start(bf16[128,2048]{1,0:T(8,128)(2,1)S(1)} %get-tuple-element.116), channel_id=1, source_target_pairs={{0,4},{1,5},{2,6},{3,7},{4,8},{5,9},{6,10},{7,11},{8,12},{9,13},{1... | collective-permute-start | bytes 1572872 | tf_op jit(solution)/shard_map/ppermute | solution.py:484
  97.7 2.2 %collective-permute-start.18 = (bf16[128,1024]{1,0:T(8,128)(2,1)S(1)}, bf16[128,1024]{1,0:T(8,128)(2,1)S(1)}, u32[]{:S(2)}, u32[]{:S(2)}) collective-permute-start(bf16[128,1024]{1,0:T(8,128)(2,1)S(1)} %get-tuple-element.113), channel_id=1, source_target_pairs={{0,1},{1,0},{2,3},{3,2},{4,5},{5,4},{6,7},{7,6},{8,9},{9,8},{10,11... | collective-permute-start | bytes 786440 | tf_op jit(solution)/shard_map/ppermute | solution.py:474
  100.2 2.0 %collective-permute-start.24 = (bf16[128,1152]{1,0:T(8,128)(2,1)S(1)}, bf16[128,1152]{1,0:T(8,128)(2,1)S(1)}, u32[]{:S(2)}, u32[]{:S(2)}) collective-permute-start(bf16[128,1152]{1,0:T(8,128)(2,1)S(1)} %get-tuple-element.131), channel_id=1, source_target_pairs={{0,2},{1,3},{2,0},{3,1},{4,6},{5,7},{6,4},{7,5},{8,10},{9,11},{10,... | collective-permute-start | bytes 884744 | tf_op jit(solution)/shard_map/ppermute | solution.py:474
  102.1 3.8 %collective-permute-done.18.refs_1_ = bf16[128,1024]{1,0:T(8,128)(2,1)S(1)} collective-permute-done((bf16[128,1024]{1,0:T(8,128)(2,1)S(1)}, bf16[128,1024]{1,0:T(8,128)(2,1)S(1)}, u32[]{:S(2)}, u32[]{:S(2)}) %collective-permute-start.18) | collective-permute-done | bytes 262176 | tf_op jit(solution)/shard_map/ppermute | solution.py:474
  106.0 0.3 collective-permute-start.25
  106.4 4.3 %collective-permute-done.20.refs_2_ = bf16[128,2048]{1,0:T(8,128)(2,1)S(1)} collective-permute-done((bf16[128,2048]{1,0:T(8,128)(2,1)S(1)}, bf16[128,2048]{1,0:T(8,128)(2,1)S(1)}, u32[]{:S(2)}, u32[]{:S(2)}) %collective-permute-start.20) | collective-permute-done | bytes 524320 | tf_op jit(solution)/shard_map/ppermute | solution.py:484
  110.8 2.4 %collective-permute-start.28 = (bf16[128,1024]{1,0:T(8,128)(2,1)S(1)}, bf16[128,1024]{1,0:T(8,128)(2,1)S(1)}, u32[]{:S(2)}, u32[]{:S(2)}) collective-permute-start(bf16[128,1024]{1,0:T(8,128)(2,1)S(1)} %get-tuple-element.122), channel_id=1, source_target_pairs={{0,6},{1,7},{2,4},{3,5},{4,10},{5,11},{6,8},{7,9},{8,14},{9,15},{1... | collective-permute-start | bytes 786440 | tf_op jit(solution)/shard_map/ppermute | solution.py:484
  113.2 1.1 items_1_0.1
  114.3 6.3 %collective-permute-start.26 = (bf16[2176,128]{1,0:T(8,128)(2,1)S(1)}, bf16[2176,128]{1,0:T(8,128)(2,1)S(1)}, u32[]{:S(2)}, u32[]{:S(2)}) collective-permute-start(bf16[2176,128]{1,0:T(8,128)(2,1)S(1)} %get-tuple-element.133), channel_id=1, source_target_pairs={{0,4},{1,5},{2,6},{3,7},{4,8},{5,9},{6,10},{7,11},{8,12},{9,13},{1... | collective-permute-start | bytes 1671176 | tf_op jit(solution)/shard_map/ppermute | solution.py:484
  120.6 5.3 %users_1.1 = f32[2048,128]{1,0:T(8,128)} custom-call(s32[1,2]{1,0:T(1,128)S(1)} %bitcast.7, f32[2048,128]{1,0:T(8,128)S(1)} %get-tuple-element.75.users, f32[128,2048]{1,0:T(8,128)S(1)} %get-tuple-element.124.grad, bf16[128,2048]{1,0:T(8,128)(2,1)S(1)} %collective-permute-done.13.refs_8_.refs_0_.items, ...), custom_call_target="tpu_custom_call" | custom-call | flops 10000000000 | bytes 65536 | tf_op jit(solution)/shard_map/users_1/pallas_call | solution.py:362
  125.9 0.6 collective-permute-done.30.refs_6_
  126.5 6.2 %collective-permute-done.26.refs_0_ = bf16[2176,128]{1,0:T(8,128)(2,1)S(1)} collective-permute-done((bf16[2176,128]{1,0:T(8,128)(2,1)S(1)}, bf16[2176,128]{1,0:T(8,128)(2,1)S(1)}, u32[]{:S(2)}, u32[]{:S(2)}) %collective-permute-start.26) | collective-permute-done | bytes 557088 | tf_op jit(solution)/shard_map/ppermute | solution.py:484
  132.7 1.7 %items_final.1 = f32[4096,128]{1,0:T(8,128)} custom-call(bf16[2176,128]{1,0:T(8,128)(2,1)S(1)} %collective-permute-done.26.refs_0_, bf16[128,2048]{1,0:T(8,128)(2,1)S(1)} %collective-permute-done.19.refs_1_, bf16[128,2048]{1,0:T(8,128)(2,1)S(1)} %collective-permute-done.20.refs_2_, bf16[128,1024]{1,0:T(8,128)(2,1)S(1)} %collective-permute-done.27.refs_3_, ...), custom_call_target="tpu_custom_call" | custom-call | flops 1200000000 | bytes 65536 | tf_op jit(solution)/shard_map/items_final/pallas_call | solution.py:583
  (38 shorter events, 1.3 us)
Async XLA Ops:
  9.0 17.3 %collective-permute-start.4 = (bf16[128,2176]{1,0:T(8,128)(2,1)S(1)}, bf16[128,2176]{1,0:T(8,128)(2,1)S(1)}, u32[]{:S(2)}, u32[]{:S(2)}) collective-permute-start(bf16[128,2176]{1,0:T(8,128)(2,1)S(1)} %get-tuple-element.93.refs_4_.refs_6_), channel_id=1, source_target_pairs={{0,1},{1,0},{2,3},{3,2},{4,5},{5,4},{6,7},{7,6},{8,9},{9,8},{10,11... | collective-permute-start | bytes 1671176 | tf_op jit(solution)/shard_map/ppermute | solution.py:474
  11.0 15.4 %collective-permute-start.5 = (bf16[128,2048]{1,0:T(8,128)(2,1)S(1)}, bf16[128,2048]{1,0:T(8,128)(2,1)S(1)}, u32[]{:S(2)}, u32[]{:S(2)}) collective-permute-start(bf16[128,2048]{1,0:T(8,128)(2,1)S(1)} %get-tuple-element.96), channel_id=1, source_target_pairs={{0,2},{1,3},{2,0},{3,1},{4,6},{5,7},{6,4},{7,5},{8,10},{9,11},{10,... | collective-permute-start | bytes 1572872 | tf_op jit(solution)/shard_map/ppermute | solution.py:474
  21.1 8.2 %copy-start = (f32[2048,128]{1,0:T(8,128)S(1)}, f32[2048,128]{1,0:T(8,128)}, u32[]{:S(2)}) copy-start(f32[2048,128]{1,0:T(8,128)} %users.1) | copy-start | bytes 3145732
  21.2 8.2 %copy-start.1 = (s32[2,1]{0,1:T(1,128)S(1)}, s32[2,1]{0,1:T(1,128)}, u32[]{:S(2)}) copy-start(s32[2,1]{0,1:T(1,128)} %param.13) | copy-start | bytes 28
  21.2 14.9 %collective-permute-start = (bf16[128,2048]{1,0:T(8,128)(2,1)S(1)}, bf16[128,2048]{1,0:T(8,128)(2,1)S(1)}, u32[]{:S(2)}, u32[]{:S(2)}) collective-permute-start(bf16[128,2048]{1,0:T(8,128)(2,1)S(1)} %get-tuple-element.80), channel_id=1, source_target_pairs={{0,1},{1,0},{2,3},{3,2},{4,5},{5,4},{6,7},{7,6},{8,9},{9,8},{10,11... | collective-permute-start | bytes 1572872 | tf_op jit(solution)/shard_map/ppermute | solution.py:474
  21.3 16.3 %collective-permute-start.1 = (bf16[128,2048]{1,0:T(8,128)(2,1)S(1)}, bf16[128,2048]{1,0:T(8,128)(2,1)S(1)}, u32[]{:S(2)}, u32[]{:S(2)}) collective-permute-start(bf16[128,2048]{1,0:T(8,128)(2,1)S(1)} %get-tuple-element.83), channel_id=1, source_target_pairs={{0,2},{1,3},{2,0},{3,1},{4,6},{5,7},{6,4},{7,5},{8,10},{9,11},{10,... | collective-permute-start | bytes 1572872 | tf_op jit(solution)/shard_map/ppermute | solution.py:474
  26.5 17.4 %collective-permute-start.6 = (bf16[128,1152]{1,0:T(8,128)(2,1)S(1)}, bf16[128,1152]{1,0:T(8,128)(2,1)S(1)}, u32[]{:S(2)}, u32[]{:S(2)}) collective-permute-start(bf16[128,1152]{1,0:T(8,128)(2,1)S(1)} %get-tuple-element.98), channel_id=1, source_target_pairs={{0,2},{1,3},{2,0},{3,1},{4,6},{5,7},{6,4},{7,5},{8,10},{9,11},{10,... | collective-permute-start | bytes 884744 | tf_op jit(solution)/shard_map/ppermute | solution.py:474
  28.6 13.1 %collective-permute-start.7 = (bf16[128,1024]{1,0:T(8,128)(2,1)S(1)}, bf16[128,1024]{1,0:T(8,128)(2,1)S(1)}, u32[]{:S(2)}, u32[]{:S(2)}) collective-permute-start(bf16[128,1024]{1,0:T(8,128)(2,1)S(1)} %get-tuple-element.99), channel_id=1, source_target_pairs={{0,1},{1,0},{2,3},{3,2},{4,5},{5,4},{6,7},{7,6},{8,9},{9,8},{10,11... | collective-permute-start | bytes 786440 | tf_op jit(solution)/shard_map/ppermute | solution.py:474
  37.7 11.6 %collective-permute-start.2 = (bf16[128,1024]{1,0:T(8,128)(2,1)S(1)}, bf16[128,1024]{1,0:T(8,128)(2,1)S(1)}, u32[]{:S(2)}, u32[]{:S(2)}) collective-permute-start(bf16[128,1024]{1,0:T(8,128)(2,1)S(1)} %get-tuple-element.85), channel_id=1, source_target_pairs={{0,2},{1,3},{2,0},{3,1},{4,6},{5,7},{6,4},{7,5},{8,10},{9,11},{10,... | collective-permute-start | bytes 786440 | tf_op jit(solution)/shard_map/ppermute | solution.py:474
  39.8 9.4 %collective-permute-start.3 = (bf16[128,1024]{1,0:T(8,128)(2,1)S(1)}, bf16[128,1024]{1,0:T(8,128)(2,1)S(1)}, u32[]{:S(2)}, u32[]{:S(2)}) collective-permute-start(bf16[128,1024]{1,0:T(8,128)(2,1)S(1)} %get-tuple-element.86), channel_id=1, source_target_pairs={{0,1},{1,0},{2,3},{3,2},{4,5},{5,4},{6,7},{7,6},{8,9},{9,8},{10,11... | collective-permute-start | bytes 786440 | tf_op jit(solution)/shard_map/ppermute | solution.py:474
  44.5 13.2 %collective-permute-start.14 = (bf16[128,2048]{1,0:T(8,128)(2,1)S(1)}, bf16[128,2048]{1,0:T(8,128)(2,1)S(1)}, u32[]{:S(2)}, u32[]{:S(2)}) collective-permute-start(bf16[128,2048]{1,0:T(8,128)(2,1)S(1)} %get-tuple-element.105), channel_id=1, source_target_pairs={{0,5},{1,4},{2,7},{3,6},{4,9},{5,8},{6,11},{7,10},{8,13},{9,12},{1... | collective-permute-start | bytes 1572872 | tf_op jit(solution)/shard_map/ppermute | solution.py:484
  44.7 17.4 %collective-permute-start.15 = (bf16[128,2048]{1,0:T(8,128)(2,1)S(1)}, bf16[128,2048]{1,0:T(8,128)(2,1)S(1)}, u32[]{:S(2)}, u32[]{:S(2)}) collective-permute-start(bf16[128,2048]{1,0:T(8,128)(2,1)S(1)} %get-tuple-element.105), channel_id=1, source_target_pairs={{0,6},{1,7},{2,4},{3,5},{4,10},{5,11},{6,8},{7,9},{8,14},{9,15},{1... | collective-permute-start | bytes 1572872 | tf_op jit(solution)/shard_map/ppermute | solution.py:484
  49.9 21.9 %collective-permute-start.9 = (bf16[128,2048]{1,0:T(8,128)(2,1)S(1)}, bf16[128,2048]{1,0:T(8,128)(2,1)S(1)}, u32[]{:S(2)}, u32[]{:S(2)}) collective-permute-start(bf16[128,2048]{1,0:T(8,128)(2,1)S(1)} %items_0_1.1), channel_id=1, source_target_pairs={{0,5},{1,4},{2,7},{3,6},{4,9},{5,8},{6,11},{7,10},{8,13},{9,12},{1... | collective-permute-start | bytes 1572872 | tf_op jit(solution)/shard_map/ppermute | solution.py:484
  50.3 23.9 %collective-permute-start.10 = (bf16[128,2048]{1,0:T(8,128)(2,1)S(1)}, bf16[128,2048]{1,0:T(8,128)(2,1)S(1)}, u32[]{:S(2)}, u32[]{:S(2)}) collective-permute-start(bf16[128,2048]{1,0:T(8,128)(2,1)S(1)} %items_0_1.1), channel_id=1, source_target_pairs={{0,6},{1,7},{2,4},{3,5},{4,10},{5,11},{6,8},{7,9},{8,14},{9,15},{1... | collective-permute-start | bytes 1572872 | tf_op jit(solution)/shard_map/ppermute | solution.py:484
  52.5 25.1 %collective-permute-start.13 = (bf16[128,2048]{1,0:T(8,128)(2,1)S(1)}, bf16[128,2048]{1,0:T(8,128)(2,1)S(1)}, u32[]{:S(2)}, u32[]{:S(2)}) collective-permute-start(bf16[128,2048]{1,0:T(8,128)(2,1)S(1)} %get-tuple-element.105), channel_id=1, source_target_pairs={{0,4},{1,5},{2,6},{3,7},{4,8},{5,9},{6,10},{7,11},{8,12},{9,13},{1... | collective-permute-start | bytes 1572872 | tf_op jit(solution)/shard_map/ppermute | solution.py:484
  57.7 21.6 %collective-permute-start.16 = (bf16[128,1024]{1,0:T(8,128)(2,1)S(1)}, bf16[128,1024]{1,0:T(8,128)(2,1)S(1)}, u32[]{:S(2)}, u32[]{:S(2)}) collective-permute-start(bf16[128,1024]{1,0:T(8,128)(2,1)S(1)} %slice.18), channel_id=1, source_target_pairs={{0,2},{1,3},{2,0},{3,1},{4,6},{5,7},{6,4},{7,5},{8,10},{9,11},{10,... | collective-permute-start | bytes 786440 | tf_op jit(solution)/shard_map/ppermute | solution.py:474
  62.1 17.2 %collective-permute-start.17 = (bf16[128,1024]{1,0:T(8,128)(2,1)S(1)}, bf16[128,1024]{1,0:T(8,128)(2,1)S(1)}, u32[]{:S(2)}, u32[]{:S(2)}) collective-permute-start(bf16[128,1024]{1,0:T(8,128)(2,1)S(1)} %slice.19), channel_id=1, source_target_pairs={{0,1},{1,0},{2,3},{3,2},{4,5},{5,4},{6,7},{7,6},{8,9},{9,8},{10,11... | collective-permute-start | bytes 786440 | tf_op jit(solution)/shard_map/ppermute | solution.py:474
  71.7 17.3 %collective-permute-start.8 = (bf16[128,2048]{1,0:T(8,128)(2,1)S(1)}, bf16[128,2048]{1,0:T(8,128)(2,1)S(1)}, u32[]{:S(2)}, u32[]{:S(2)}) collective-permute-start(bf16[128,2048]{1,0:T(8,128)(2,1)S(1)} %items_0_1.1), channel_id=1, source_target_pairs={{0,4},{1,5},{2,6},{3,7},{4,8},{5,9},{6,10},{7,11},{8,12},{9,13},{1... | collective-permute-start | bytes 1572872 | tf_op jit(solution)/shard_map/ppermute | solution.py:484
  74.2 14.8 %collective-permute-start.11 = (bf16[128,1024]{1,0:T(8,128)(2,1)S(1)}, bf16[128,1024]{1,0:T(8,128)(2,1)S(1)}, u32[]{:S(2)}, u32[]{:S(2)}) collective-permute-start(bf16[128,1024]{1,0:T(8,128)(2,1)S(1)} %slice.16), channel_id=1, source_target_pairs={{0,2},{1,3},{2,0},{3,1},{4,6},{5,7},{6,4},{7,5},{8,10},{9,11},{10,... | collective-permute-start | bytes 786440 | tf_op jit(solution)/shard_map/ppermute | solution.py:474
  77.6 11.5 %collective-permute-start.12 = (bf16[128,1024]{1,0:T(8,128)(2,1)S(1)}, bf16[128,1024]{1,0:T(8,128)(2,1)S(1)}, u32[]{:S(2)}, u32[]{:S(2)}) collective-permute-start(bf16[128,1024]{1,0:T(8,128)(2,1)S(1)} %slice.17), channel_id=1, source_target_pairs={{0,1},{1,0},{2,3},{3,2},{4,5},{5,4},{6,7},{7,6},{8,9},{9,8},{10,11... | collective-permute-start | bytes 786440 | tf_op jit(solution)/shard_map/ppermute | solution.py:474
  87.6 12.4 %collective-permute-start.22 = (bf16[128,2176]{1,0:T(8,128)(2,1)S(1)}, bf16[128,2176]{1,0:T(8,128)(2,1)S(1)}, u32[]{:S(2)}, u32[]{:S(2)}) collective-permute-start(bf16[128,2176]{1,0:T(8,128)(2,1)S(1)} %get-tuple-element.126.refs_4_.refs_6_), channel_id=1, source_target_pairs={{0,1},{1,0},{2,3},{3,2},{4,5},{5,4},{6,7},{7,6},{8,9},{9,8},{10,11... | collective-permute-start | bytes 1671176 | tf_op jit(solution)/shard_map/ppermute | solution.py:474
  87.7 12.2 %collective-permute-start.23 = (bf16[128,2048]{1,0:T(8,128)(2,1)S(1)}, bf16[128,2048]{1,0:T(8,128)(2,1)S(1)}, u32[]{:S(2)}, u32[]{:S(2)}) collective-permute-start(bf16[128,2048]{1,0:T(8,128)(2,1)S(1)} %get-tuple-element.129), channel_id=1, source_target_pairs={{0,2},{1,3},{2,0},{3,1},{4,6},{5,7},{6,4},{7,5},{8,10},{9,11},{10,... | collective-permute-start | bytes 1572872 | tf_op jit(solution)/shard_map/ppermute | solution.py:474
  94.6 11.7 %collective-permute-start.19 = (bf16[128,2048]{1,0:T(8,128)(2,1)S(1)}, bf16[128,2048]{1,0:T(8,128)(2,1)S(1)}, u32[]{:S(2)}, u32[]{:S(2)}) collective-permute-start(bf16[128,2048]{1,0:T(8,128)(2,1)S(1)} %collective-permute-done.8.refs_8_.refs_5_), channel_id=1, source_target_pairs={{0,4},{1,5},{2,6},{3,7},{4,8},{5,9},{6,10},{7,11},{8,12},{9,13},{1... | collective-permute-start | bytes 1572872 | tf_op jit(solution)/shard_map/ppermute | solution.py:484
  94.6 16.0 %collective-permute-start.20 = (bf16[128,2048]{1,0:T(8,128)(2,1)S(1)}, bf16[128,2048]{1,0:T(8,128)(2,1)S(1)}, u32[]{:S(2)}, u32[]{:S(2)}) collective-permute-start(bf16[128,2048]{1,0:T(8,128)(2,1)S(1)} %get-tuple-element.116), channel_id=1, source_target_pairs={{0,4},{1,5},{2,6},{3,7},{4,8},{5,9},{6,10},{7,11},{8,12},{9,13},{1... | collective-permute-start | bytes 1572872 | tf_op jit(solution)/shard_map/ppermute | solution.py:484
  97.7 8.3 %collective-permute-start.18 = (bf16[128,1024]{1,0:T(8,128)(2,1)S(1)}, bf16[128,1024]{1,0:T(8,128)(2,1)S(1)}, u32[]{:S(2)}, u32[]{:S(2)}) collective-permute-start(bf16[128,1024]{1,0:T(8,128)(2,1)S(1)} %get-tuple-element.113), channel_id=1, source_target_pairs={{0,1},{1,0},{2,3},{3,2},{4,5},{5,4},{6,7},{7,6},{8,9},{9,8},{10,11... | collective-permute-start | bytes 786440 | tf_op jit(solution)/shard_map/ppermute | solution.py:474
  99.9 10.7 %collective-permute-start.21 = (bf16[128,1024]{1,0:T(8,128)(2,1)S(1)}, bf16[128,1024]{1,0:T(8,128)(2,1)S(1)}, u32[]{:S(2)}, u32[]{:S(2)}) collective-permute-start(bf16[128,1024]{1,0:T(8,128)(2,1)S(1)} %get-tuple-element.119), channel_id=1, source_target_pairs={{0,2},{1,3},{2,0},{3,1},{4,6},{5,7},{6,4},{7,5},{8,10},{9,11},{10,... | collective-permute-start | bytes 786440 | tf_op jit(solution)/shard_map/ppermute | solution.py:474
  100.2 13.0 %collective-permute-start.24 = (bf16[128,1152]{1,0:T(8,128)(2,1)S(1)}, bf16[128,1152]{1,0:T(8,128)(2,1)S(1)}, u32[]{:S(2)}, u32[]{:S(2)}) collective-permute-start(bf16[128,1152]{1,0:T(8,128)(2,1)S(1)} %get-tuple-element.131), channel_id=1, source_target_pairs={{0,2},{1,3},{2,0},{3,1},{4,6},{5,7},{6,4},{7,5},{8,10},{9,11},{10,... | collective-permute-start | bytes 884744 | tf_op jit(solution)/shard_map/ppermute | solution.py:474
  106.0 7.2 %collective-permute-start.25 = (bf16[128,1024]{1,0:T(8,128)(2,1)S(1)}, bf16[128,1024]{1,0:T(8,128)(2,1)S(1)}, u32[]{:S(2)}, u32[]{:S(2)}) collective-permute-start(bf16[128,1024]{1,0:T(8,128)(2,1)S(1)} %get-tuple-element.132), channel_id=1, source_target_pairs={{0,1},{1,0},{2,3},{3,2},{4,5},{5,4},{6,7},{7,6},{8,9},{9,8},{10,11... | collective-permute-start | bytes 786440 | tf_op jit(solution)/shard_map/ppermute | solution.py:474
  106.3 19.6 %collective-permute-start.27 = (bf16[128,1024]{1,0:T(8,128)(2,1)S(1)}, bf16[128,1024]{1,0:T(8,128)(2,1)S(1)}, u32[]{:S(2)}, u32[]{:S(2)}) collective-permute-start(bf16[128,1024]{1,0:T(8,128)(2,1)S(1)} %get-tuple-element.134), channel_id=1, source_target_pairs={{0,5},{1,4},{2,7},{3,6},{4,9},{5,8},{6,11},{7,10},{8,13},{9,12},{1... | collective-permute-start | bytes 786440 | tf_op jit(solution)/shard_map/ppermute | solution.py:484
  110.6 15.3 %collective-permute-start.29 = (bf16[128,1024]{1,0:T(8,128)(2,1)S(1)}, bf16[128,1024]{1,0:T(8,128)(2,1)S(1)}, u32[]{:S(2)}, u32[]{:S(2)}) collective-permute-start(bf16[128,1024]{1,0:T(8,128)(2,1)S(1)} %get-tuple-element.135), channel_id=1, source_target_pairs={{0,6},{1,7},{2,4},{3,5},{4,10},{5,11},{6,8},{7,9},{8,14},{9,15},{1... | collective-permute-start | bytes 786440 | tf_op jit(solution)/shard_map/ppermute | solution.py:484
  110.8 15.1 %collective-permute-start.28 = (bf16[128,1024]{1,0:T(8,128)(2,1)S(1)}, bf16[128,1024]{1,0:T(8,128)(2,1)S(1)}, u32[]{:S(2)}, u32[]{:S(2)}) collective-permute-start(bf16[128,1024]{1,0:T(8,128)(2,1)S(1)} %get-tuple-element.122), channel_id=1, source_target_pairs={{0,6},{1,7},{2,4},{3,5},{4,10},{5,11},{6,8},{7,9},{8,14},{9,15},{1... | collective-permute-start | bytes 786440 | tf_op jit(solution)/shard_map/ppermute | solution.py:484
  113.2 7.4 %copy-start.2 = (s32[2,1]{0,1:T(1,128)S(1)}, s32[2,1]{0,1:T(1,128)}, u32[]{:S(2)}) copy-start(s32[2,1]{0,1:T(1,128)} %param.13) | copy-start | bytes 28
  113.2 13.3 %collective-permute-start.30 = (bf16[128,1024]{1,0:T(8,128)(2,1)S(1)}, bf16[128,1024]{1,0:T(8,128)(2,1)S(1)}, u32[]{:S(2)}, u32[]{:S(2)}) collective-permute-start(bf16[128,1024]{1,0:T(8,128)(2,1)S(1)} %get-tuple-element.123), channel_id=1, source_target_pairs={{0,5},{1,4},{2,7},{3,6},{4,9},{5,8},{6,11},{7,10},{8,13},{9,12},{1... | collective-permute-start | bytes 786440 | tf_op jit(solution)/shard_map/ppermute | solution.py:484
  114.3 18.4 %collective-permute-start.26 = (bf16[2176,128]{1,0:T(8,128)(2,1)S(1)}, bf16[2176,128]{1,0:T(8,128)(2,1)S(1)}, u32[]{:S(2)}, u32[]{:S(2)}) collective-permute-start(bf16[2176,128]{1,0:T(8,128)(2,1)S(1)} %get-tuple-element.133), channel_id=1, source_target_pairs={{0,4},{1,5},{2,6},{3,7},{4,8},{5,9},{6,10},{7,11},{8,12},{9,13},{1... | collective-permute-start | bytes 1671176 | tf_op jit(solution)/shard_map/ppermute | solution.py:484
